TPU v7x, 32 devices: a whole 2x2x4 slice. The times are simulated.
32 devices in a mesh: dp: 2 (over y), ctx: 4 (over x, core), mp: 4 (over z).
Axes of the slice: x: 2, y: 2, z: 4, core: 2. Of those that a mesh axis runs over, the one named last changes fastest.
Arguments:
- tokens: bfloat16 [4, 512, 2048], P('dp', 'ctx'), may hold values from -6 to 6
- segments: int32 [4, 512], P('dp', 'ctx'), may hold values from 0 to 5, never falling along the last dimension, each value on 1 to 256 neighbouring positions
- cotangent: bfloat16 [4, 512, 2048], P('dp', 'ctx'), may hold values from -6 to 6
- first_gain: float32 [2, 2048], replicated, may hold values from 0.1 to 1.9
- first_bias: float32 [2, 2048], replicated, may hold values from -1.5 to 1.5
- qkv_weight: bfloat16 [2, 2048, 3, 2048], P(None, ('dp', 'ctx'), None, 'mp'), may hold values from -0.125 to 0.125
- qkv_bias: float32 [2, 3, 2048], P(None, None, 'mp'), may hold values from -2.5 to 2.5
- out_weight: bfloat16 [2, 2048, 2048], P(None, ('dp', 'ctx'), 'mp'), may hold values from -1 to 1
- second_gain: float32 [2, 2048], replicated, may hold values from 0.1 to 1.9
- second_bias: float32 [2, 2048], replicated, may hold values from -1.5 to 1.5
- gate_up_weight: bfloat16 [2, 2048, 2, 5632], P(None, ('dp', 'ctx'), None, 'mp'), may hold values from -0.125 to 0.125
- down_weight: bfloat16 [2, 2048, 5632], P(None, ('dp', 'ctx'), 'mp'), may hold values from -0.078125 to 0.078125
Outputs:
- activations: bfloat16 [4, 512, 2048], P('dp', 'ctx')
- tokens_grad: float32 [4, 512, 2048], P('dp', 'ctx')
- first_gain_grad: float32 [2, 2048], replicated
- first_bias_grad: float32 [2, 2048], replicated
- qkv_weight_grad: float32 [2, 2048, 3, 2048], P(None, ('dp', 'ctx'), None, 'mp')
- qkv_bias_grad: float32 [2, 3, 2048], P(None, None, 'mp')
- out_weight_grad: float32 [2, 2048, 2048], P(None, ('dp', 'ctx'), 'mp')
- second_gain_grad: float32 [2, 2048], replicated
- second_bias_grad: float32 [2, 2048], replicated
- gate_up_grad: float32 [2, 2048, 2, 5632], P(None, ('dp', 'ctx'), None, 'mp')
- down_grad: float32 [2, 2048, 5632], P(None, ('dp', 'ctx'), 'mp')
Inputs may be any that keep to these rules, and one draw needn't show every extreme that they name: `segments`: in each sequence the document numbers never fall, and each document has 1 to 256 tokens.
All inputs are finite; a program needn't handle non-finite values.
Results may differ from a plain program's by a relative error of at most 0.03.
Values may be sent and summed in bfloat16 or wider, within the bound.
No kernel may reach another device: no remote copies, remote signals or barrier semaphores. Data moves between devices by JAX's collectives and lax.ppermute only.
A program may use at most 256 MiB of HBM per device.

v0:
```python
import math

import jax
import jax.numpy as jnp
from jax import lax
from jax.sharding import PartitionSpec as P

HEAD = 64
ROT = 16
LAYERS = 2
MICRO = 2


NORM_EPS = 1e-05
MASK_FILL = -1e30


def as_sent(shard):

    def short(part):
        return part.astype(jnp.bfloat16) if part.dtype == jnp.float32 else part

    return jax.tree.map(short, shard)


def frequencies():
    return jnp.exp(jnp.arange(ROT // 2, dtype=jnp.float32) * (-2.0 * math.log(10000.0) / ROT))


def layer_norm(values, gain_vec, offset):
    center = values - jnp.mean(values, axis=-1, keepdims=True)
    inverse = lax.rsqrt(jnp.mean(center * center, axis=-1, keepdims=True) + NORM_EPS)
    normed = center * inverse
    return (normed * gain_vec + offset, normed, inverse)


def norm_back(upstream, normed, inverse, gain_vec):
    scaled = upstream * gain_vec
    return inverse * (
        scaled
        - jnp.mean(scaled, axis=-1, keepdims=True)
        - normed * jnp.mean(scaled * normed, axis=-1, keepdims=True)
    )


def rotate(tensor, cosine_table, sine_table):
    half_rot = ROT // 2
    first_part = tensor[..., :half_rot]
    second_part = tensor[..., half_rot:ROT]
    cos_b = cosine_table[:, :, None, :]
    sin_b = sine_table[:, :, None, :]
    return jnp.concatenate(
        [
            first_part * cos_b - second_part * sin_b,
            second_part * cos_b + first_part * sin_b,
            tensor[..., ROT:],
        ],
        axis=-1,
    )


def rotate_back(tensor, cosine_table, sine_table):
    half_rot = ROT // 2
    first_part = tensor[..., :half_rot]
    second_part = tensor[..., half_rot:ROT]
    cos_b = cosine_table[:, :, None, :]
    sin_b = sine_table[:, :, None, :]
    return jnp.concatenate(
        [
            first_part * cos_b + second_part * sin_b,
            second_part * cos_b - first_part * sin_b,
            tensor[..., ROT:],
        ],
        axis=-1,
    )


def geometry(whole_seg, local_len):
    total_len = whole_seg.shape[1]
    places = jnp.arange(total_len, dtype=jnp.int32)
    starts = jnp.sum((whole_seg[:, None, :] < whole_seg[:, :, None]).astype(jnp.int32), axis=2)
    offset = lax.axis_index("ctx") * local_len
    local_pos = lax.dynamic_slice_in_dim(places[None, :] - starts, offset, local_len, 1).astype(
        jnp.float32
    )
    local_seg = lax.dynamic_slice_in_dim(whole_seg, offset, local_len, 1)
    query_place = offset + jnp.arange(local_len, dtype=jnp.int32)
    angles = local_pos[:, :, None] * frequencies()[None, None, :]
    allowed = (local_seg[:, :, None] == whole_seg[:, None, :]) & (
        places[None, None, :] <= query_place[None, :, None]
    )
    return (jnp.cos(angles), jnp.sin(angles), allowed)


def model_sum(partial_sum):
    return lax.psum(partial_sum.astype(jnp.bfloat16), "mp").astype(jnp.float32)


def masked_scores(queries, key_all, allowed):
    products = jnp.einsum(
        "bqhe,bkhe->bhqk", queries, key_all, preferred_element_type=jnp.float32
    ) * (1.0 / math.sqrt(HEAD))
    return jnp.where(allowed[:, None], products, MASK_FILL)


def layer_forward(rows_in, weights, smalls, geometry_loc):
    w_qkv, w_gate_up, w_out, w_down = weights
    gain_one, bias_one, bias_qkv, gain_two, bias_two = smalls
    cosine_table, sine_table, allowed = geometry_loc
    batch_seqs, local_len = (cosine_table.shape[0], cosine_table.shape[1])
    width_loc = w_qkv.shape[2]
    head_shape = (batch_seqs, local_len, width_loc // HEAD, HEAD)
    normed_out_one, normed_one, inverse_one = layer_norm(rows_in, gain_one, bias_one)
    input_one = normed_out_one.astype(jnp.bfloat16)
    projected = (
        jnp.einsum("rd,dcf->rcf", input_one, w_qkv, preferred_element_type=jnp.float32) + bias_qkv
    )
    queries = rotate(projected[:, 0].reshape(head_shape), cosine_table, sine_table).astype(
        jnp.bfloat16
    )
    key_loc = (
        rotate(projected[:, 1].reshape(head_shape), cosine_table, sine_table)
        .astype(jnp.bfloat16)
        .reshape(batch_seqs, local_len, width_loc)
    )
    value_loc = projected[:, 2].astype(jnp.bfloat16).reshape(batch_seqs, local_len, width_loc)
    key_all, value_all = (
        lax.all_gather(key_loc, "ctx", axis=1, tiled=True),
        lax.all_gather(value_loc, "ctx", axis=1, tiled=True),
    )
    total_len = key_all.shape[1]
    all_shape = (batch_seqs, total_len, width_loc // HEAD, HEAD)
    key_all = key_all.reshape(all_shape)
    value_all = value_all.reshape(all_shape)
    scores = masked_scores(queries, key_all, allowed)
    highest = jnp.max(scores, axis=-1, keepdims=True)
    exponent = jnp.exp(scores - highest)
    denominator = jnp.sum(exponent, axis=-1, keepdims=True)
    log_total = highest + jnp.log(denominator)
    weights_low = (exponent / denominator).astype(jnp.bfloat16)
    mixed_heads = jnp.einsum(
        "bhqk,bkhe->bqhe", weights_low, value_all, preferred_element_type=jnp.float32
    )
    mixed_heads = mixed_heads.reshape(-1, width_loc).astype(jnp.bfloat16)
    attended = model_sum(
        jnp.einsum("re,oe->ro", mixed_heads, w_out, preferred_element_type=jnp.float32)
    )
    middle = rows_in + attended
    normed_out_two, normed_two, inverse_two = layer_norm(middle, gain_two, bias_two)
    input_two = normed_out_two.astype(jnp.bfloat16)
    gate_up = jnp.einsum("rd,dcf->rcf", input_two, w_gate_up, preferred_element_type=jnp.float32)
    hidden = (jax.nn.silu(gate_up[:, 0]) * gate_up[:, 1]).astype(jnp.bfloat16)
    branch = model_sum(jnp.einsum("rf,df->rd", hidden, w_down, preferred_element_type=jnp.float32))
    saved_state = (
        input_one,
        normed_one,
        inverse_one,
        queries,
        key_all,
        value_all,
        log_total,
        mixed_heads,
        input_two,
        normed_two,
        inverse_two,
        gate_up,
        hidden,
    )
    return (middle + branch, saved_state)


def layer_backward(upstream, weights, smalls, geometry_loc, saved_state):
    w_qkv, w_gate_up, w_out, w_down = weights
    gain_one, bias_one, bias_qkv, gain_two, bias_two = smalls
    cosine_table, sine_table, allowed = geometry_loc
    (
        input_one,
        normed_one,
        inverse_one,
        queries,
        key_all,
        value_all,
        log_total,
        mixed_heads,
        input_two,
        normed_two,
        inverse_two,
        gate_up,
        hidden,
    ) = saved_state
    batch_seqs, local_len = (cosine_table.shape[0], cosine_table.shape[1])
    width_loc = w_qkv.shape[2]
    total_len = key_all.shape[1]
    head_shape = (batch_seqs, local_len, width_loc // HEAD, HEAD)
    upstream_low = upstream.astype(jnp.bfloat16)
    grad_down = jnp.einsum("rd,rf->df", upstream_low, hidden, preferred_element_type=jnp.float32)
    grad_hidden = jnp.einsum("rd,df->rf", upstream_low, w_down, preferred_element_type=jnp.float32)
    gate_half = gate_up[:, 0]
    upper_half = gate_up[:, 1]
    sigmoid_gate = jax.nn.sigmoid(gate_half)
    grad_gate = grad_hidden * upper_half * sigmoid_gate * (1.0 + gate_half * (1.0 - sigmoid_gate))
    grad_upper = grad_hidden * gate_half * sigmoid_gate
    grad_pre = jnp.stack([grad_gate, grad_upper], axis=1).astype(jnp.bfloat16)
    grad_gate_up = jnp.einsum(
        "rd,rcf->dcf", input_two, grad_pre, preferred_element_type=jnp.float32
    )
    grad_two = model_sum(
        jnp.einsum("rcf,dcf->rd", grad_pre, w_gate_up, preferred_element_type=jnp.float32)
    )
    gain_two_grad = jnp.sum(grad_two * normed_two, axis=0)
    bias_two_grad = jnp.sum(grad_two, axis=0)
    grad_middle = upstream + norm_back(grad_two, normed_two, inverse_two, gain_two)
    middle_low = grad_middle.astype(jnp.bfloat16)
    grad_out = jnp.einsum("ro,re->oe", middle_low, mixed_heads, preferred_element_type=jnp.float32)
    grad_mixed = (
        jnp.einsum("ro,oe->re", middle_low, w_out, preferred_element_type=jnp.float32)
        .astype(jnp.bfloat16)
        .reshape(head_shape)
    )
    scores = masked_scores(queries, key_all, allowed)
    probabilities = jnp.exp(scores - log_total)
    grad_probs = jnp.einsum(
        "bqhe,bkhe->bhqk", grad_mixed, value_all, preferred_element_type=jnp.float32
    )
    grad_value_all = jnp.einsum(
        "bhqk,bqhe->bkhe",
        probabilities.astype(jnp.bfloat16),
        grad_mixed,
        preferred_element_type=jnp.float32,
    )
    grad_scores = (
        probabilities * (grad_probs - jnp.sum(probabilities * grad_probs, axis=-1, keepdims=True))
    ).astype(jnp.bfloat16)
    score_scale = 1.0 / math.sqrt(HEAD)
    grad_query = (
        jnp.einsum("bhqk,bkhe->bqhe", grad_scores, key_all, preferred_element_type=jnp.float32)
        * score_scale
    )
    grad_key_all = (
        jnp.einsum("bhqk,bqhe->bkhe", grad_scores, queries, preferred_element_type=jnp.float32)
        * score_scale
    )
    flat_shape = (batch_seqs, total_len, width_loc)
    grad_key, grad_value = (
        lax.psum_scatter(
            grad_key_all.reshape(flat_shape).astype(jnp.bfloat16),
            "ctx",
            scatter_dimension=1,
            tiled=True,
        ).astype(jnp.float32),
        lax.psum_scatter(
            grad_value_all.reshape(flat_shape).astype(jnp.bfloat16),
            "ctx",
            scatter_dimension=1,
            tiled=True,
        ).astype(jnp.float32),
    )
    grad_query = rotate_back(grad_query, cosine_table, sine_table).reshape(-1, width_loc)
    grad_key = rotate_back(grad_key.reshape(head_shape), cosine_table, sine_table).reshape(
        -1, width_loc
    )
    grad_proj = jnp.stack([grad_query, grad_key, grad_value.reshape(-1, width_loc)], axis=1).astype(
        jnp.bfloat16
    )
    bias_qkv_grad = jnp.sum(grad_proj.astype(jnp.float32), axis=0)
    grad_qkv = jnp.einsum("rd,rcf->dcf", input_one, grad_proj, preferred_element_type=jnp.float32)
    grad_one = model_sum(
        jnp.einsum("rcf,dcf->rd", grad_proj, w_qkv, preferred_element_type=jnp.float32)
    )
    gain_one_grad = jnp.sum(grad_one * normed_one, axis=0)
    bias_one_grad = jnp.sum(grad_one, axis=0)
    grad_rows = grad_middle + norm_back(grad_one, normed_one, inverse_one, gain_one)
    return (
        grad_rows,
        (grad_qkv, grad_gate_up, grad_out, grad_down),
        (gain_one_grad, bias_one_grad, bias_qkv_grad, gain_two_grad, bias_two_grad),
    )


def on_device(
    tokens,
    segments,
    cotangent,
    first_gain,
    first_bias,
    qkv_weight,
    qkv_bias,
    out_weight,
    second_gain,
    second_bias,
    gate_up_weight,
    down_weight,
):
    seq_dev, local_len, width = tokens.shape
    per_batch = seq_dev // MICRO
    rows_batch = per_batch * local_len
    whole_seg = lax.all_gather(segments, "ctx", axis=1, tiled=True)
    cosine_table, sine_table, allowed = geometry(whole_seg, local_len)

    def fetch_weights(layer_no):
        return (
            lax.all_gather(qkv_weight[layer_no], ("dp", "ctx"), axis=0, tiled=True),
            lax.all_gather(gate_up_weight[layer_no], ("dp", "ctx"), axis=0, tiled=True),
            lax.all_gather(out_weight[layer_no], ("dp", "ctx"), axis=0, tiled=True),
            lax.all_gather(down_weight[layer_no], ("dp", "ctx"), axis=0, tiled=True),
        )

    def spread(gradients):
        return jax.tree.map(
            lambda part: part.astype(jnp.float32),
            lax.psum_scatter(as_sent(gradients), ("dp", "ctx"), scatter_dimension=0, tiled=True),
        )

    smalls = [
        (
            first_gain[layer_no],
            first_bias[layer_no],
            qkv_bias[layer_no],
            second_gain[layer_no],
            second_bias[layer_no],
        )
        for layer_no in range(LAYERS)
    ]
    shard_grads = [
        tuple(
            (
                jnp.zeros(array_in.shape[1:], jnp.float32)
                for array_in in (qkv_weight, gate_up_weight, out_weight, down_weight)
            )
        )
        for layer_no in range(LAYERS)
    ]
    full_grads = [None] * LAYERS
    small_grads = [
        tuple(
            (
                jnp.zeros(array_in.shape[1:], jnp.float32)
                for array_in in (first_gain, first_bias, qkv_bias, second_gain, second_bias)
            )
        )
        for layer_no in range(LAYERS)
    ]
    outputs = []
    input_grads = []
    for batch_no in range(MICRO):
        first_seq = batch_no * per_batch
        geometry_loc = (
            cosine_table[first_seq : first_seq + per_batch],
            sine_table[first_seq : first_seq + per_batch],
            allowed[first_seq : first_seq + per_batch],
        )
        values = (
            tokens[first_seq : first_seq + per_batch].astype(jnp.float32).reshape(rows_batch, width)
        )
        saved = []
        for layer_no in range(LAYERS):
            weights = fetch_weights(layer_no)
            values, saved_state = layer_forward(values, weights, smalls[layer_no], geometry_loc)
            saved.append(saved_state)
        outputs.append(values.astype(jnp.bfloat16).reshape(per_batch, local_len, width))
        upstream = (
            cotangent[first_seq : first_seq + per_batch]
            .astype(jnp.float32)
            .reshape(rows_batch, width)
        )
        for layer_no in reversed(range(LAYERS)):
            weights = fetch_weights(layer_no)
            upstream, weight_terms, small_terms = layer_backward(
                upstream, weights, smalls[layer_no], geometry_loc, saved[layer_no]
            )
            small_grads[layer_no] = tuple(
                (running + fresh for running, fresh in zip(small_grads[layer_no], small_terms))
            )
            if full_grads[layer_no] is None:
                full_grads[layer_no] = weight_terms
            else:
                full_grads[layer_no] = tuple(
                    (running + fresh for running, fresh in zip(full_grads[layer_no], weight_terms))
                )
        input_grads.append(upstream.reshape(per_batch, local_len, width))
    shard_grads = [spread(full_grads[layer_no]) for layer_no in range(LAYERS)]
    stacked_small = tuple(
        (
            jnp.stack([small_grads[layer_no][member_no] for layer_no in range(LAYERS)])
            for member_no in range(5)
        )
    )
    summed_small = jax.tree.map(
        lambda part: part.astype(jnp.float32), lax.psum(as_sent(stacked_small), ("dp", "ctx"))
    )
    stacked_weights = tuple(
        (
            jnp.stack([shard_grads[layer_no][member_no] for layer_no in range(LAYERS)])
            for member_no in range(4)
        )
    )
    return (
        jnp.concatenate(outputs, axis=0),
        jnp.concatenate(input_grads, axis=0),
        summed_small[0],
        summed_small[1],
        stacked_weights[0],
        summed_small[2],
        stacked_weights[2],
        summed_small[3],
        summed_small[4],
        stacked_weights[1],
        stacked_weights[3],
    )


def solution(mesh):
    return jax.shard_map(
        on_device,
        mesh=mesh,
        in_specs=(
            P("dp", "ctx", None),
            P("dp", "ctx"),
            P("dp", "ctx", None),
            P(),
            P(),
            P(None, ("dp", "ctx"), None, "mp"),
            P(None, None, "mp"),
            P(None, ("dp", "ctx"), "mp"),
            P(),
            P(),
            P(None, ("dp", "ctx"), None, "mp"),
            P(None, ("dp", "ctx"), "mp"),
        ),
        out_specs=(
            P("dp", "ctx", None),
            P("dp", "ctx", None),
            P(),
            P(),
            P(None, ("dp", "ctx"), None, "mp"),
            P(None, None, "mp"),
            P(None, ("dp", "ctx"), "mp"),
            P(),
            P(),
            P(None, ("dp", "ctx"), None, "mp"),
            P(None, ("dp", "ctx"), "mp"),
        ),
        check_vma=False,
    )
```

profile of v0, /device:TPU:0, one launch (start us, length us, event | category | flops | bytes accessed | tf_op | source)
XLA Modules:
  0.0 1712.5 jit_solution(3707837928637207378)
XLA Ops:
  12.2 6.0 all_gather.36
  19.3 39.5 %all-gather.21.cloned.1.call-done = bf16[1,2048,3,512]{3,1,2,0:T(8,128)(2,1)} async-done(((bf16[1,256,3,512]{3,1,2,0:T(8,128)(2,1)}), bf16[1,2048,3,512]{3,1,2,0:T(8,128)(2,1)}) %all-gather.21.cloned.1.call-update) | async-done | bytes 6291472 | tf_op jit(solution)/shard_map/all_gather | solution.py:302
  62.6 7.2 all-gather.1
  71.3 7.3 all_gather.37
  81.4 7.7 all-gather.23.cloned.1.call-done
  92.5 38.4 %all-reduce.16.cloned.1.call-done = bf16[128,2048]{1,0:T(8,128)(2,1)} async-done(((bf16[128,2048]{1,0:T(8,128)(2,1)}), bf16[128,2048]{1,0:T(8,128)(2,1)}) %all-reduce.16.cloned.1.call-update) | async-done | bytes 524304 | tf_op jit(solution)/shard_map/psum | solution.py:96
  132.3 3.8 fusion.164
  136.2 7.1 all-gather.10
  144.8 7.3 all_gather.89
  157.5 4.7 fusion.382
  166.6 28.7 %all-reduce.18.cloned.1.call-done = bf16[128,2048]{1,0:T(8,128)(2,1)} async-done(((bf16[128,2048]{1,0:T(8,128)(2,1)}), bf16[128,2048]{1,0:T(8,128)(2,1)}) %all-reduce.18.cloned.1.call-update) | async-done | bytes 524304 | tf_op jit(solution)/shard_map/psum | solution.py:96
  197.2 68.1 %all-gather.25.cloned.1.call-done = bf16[1,2048,2,1408]{3,1,2,0:T(8,128)(2,1)} async-done(((bf16[1,256,2,1408]{3,1,2,0:T(8,128)(2,1)}), bf16[1,2048,2,1408]{3,1,2,0:T(8,128)(2,1)}) %all-gather.25.cloned.1.call-update) | async-done | bytes 11534352 | tf_op jit(solution)/shard_map/all_gather | solution.py:303
  265.3 6.2 fusion.14
  276.5 34.4 %all-gather.27.cloned.1.call-done = bf16[1,2048,1408]{2,1,0:T(8,128)(2,1)} async-done(((bf16[1,256,1408]{2,1,0:T(8,128)(2,1)}), bf16[1,2048,1408]{2,1,0:T(8,128)(2,1)}) %all-gather.27.cloned.1.call-update) | async-done | bytes 5767184 | tf_op jit(solution)/shard_map/all_gather | solution.py:305
  311.0 5.5 fusion.97
  320.9 50.8 %all-reduce.30.cloned.1.call-done = (bf16[128,2048]{1,0:T(8,128)(2,1)}, bf16[128,2048]{1,0:T(8,128)(2,1)}) async-done(((bf16[128,2048]{1,0:T(8,128)(2,1)}, bf16[128,2048]{1,0:T(8,128)(2,1)}), (bf16[128,2048]{1,0:T(8,128)(2,1)}, bf16[128,2048]{1,0:T(8,128)(2,1)})) %all-reduce.30.cloned.1.call-update) | async-done | bytes 1048592 | tf_op jit(solution)/shard_map/psum | solution.py:96
  375.6 43.6 %all-gather.29.cloned.1.call-done = bf16[1,2048,3,512]{3,1,2,0:T(8,128)(2,1)} async-done(((bf16[1,256,3,512]{3,1,2,0:T(8,128)(2,1)}), bf16[1,2048,3,512]{3,1,2,0:T(8,128)(2,1)}) %all-gather.29.cloned.1.call-update) | async-done | bytes 6291472 | tf_op jit(solution)/shard_map/all_gather | solution.py:302
  419.2 4.0 fusion.167
  424.0 7.6 all-gather.6
  433.1 7.4 all-gather.11
  445.8 7.3 all_gather.84
  453.2 7.5 all_gather.91
  474.6 49.1 %all-reduce.28.cloned.1.call-done = (bf16[128,2048]{1,0:T(8,128)(2,1)}, bf16[128,2048]{1,0:T(8,128)(2,1)}) async-done(((bf16[128,2048]{1,0:T(8,128)(2,1)}, bf16[128,2048]{1,0:T(8,128)(2,1)}), (bf16[128,2048]{1,0:T(8,128)(2,1)}, bf16[128,2048]{1,0:T(8,128)(2,1)})) %all-reduce.28.cloned.1.call-update) | async-done | bytes 1048592 | tf_op jit(solution)/shard_map/psum | solution.py:96
  528.4 64.4 %all-gather.33.cloned.1.call-done = bf16[1,2048,2,1408]{3,1,2,0:T(8,128)(2,1)} async-done(((bf16[1,256,2,1408]{3,1,2,0:T(8,128)(2,1)}), bf16[1,2048,2,1408]{3,1,2,0:T(8,128)(2,1)}) %all-gather.33.cloned.1.call-update) | async-done | bytes 11534352 | tf_op jit(solution)/shard_map/all_gather | solution.py:303
  592.8 7.3 fusion.6
  603.7 34.2 %all-gather.35.cloned.1.call-done = bf16[1,2048,1408]{2,1,0:T(8,128)(2,1)} async-done(((bf16[1,256,1408]{2,1,0:T(8,128)(2,1)}), bf16[1,2048,1408]{2,1,0:T(8,128)(2,1)}) %all-gather.35.cloned.1.call-update) | async-done | bytes 5767184 | tf_op jit(solution)/shard_map/all_gather | solution.py:305
  637.9 4.4 fusion.308
  642.3 4.9 fusion.309
  647.3 4.6 fusion.76
  651.9 4.6 fusion.73
  659.3 49.5 %all-reduce.26.cloned.1.call-done = (bf16[128,2048]{1,0:T(8,128)(2,1)}, bf16[128,2048]{1,0:T(8,128)(2,1)}) async-done(((bf16[128,2048]{1,0:T(8,128)(2,1)}, bf16[128,2048]{1,0:T(8,128)(2,1)}), (bf16[128,2048]{1,0:T(8,128)(2,1)}, bf16[128,2048]{1,0:T(8,128)(2,1)})) %all-reduce.26.cloned.1.call-update) | async-done | bytes 1048592 | tf_op jit(solution)/shard_map/psum | solution.py:96
  768.1 5.4 reduce-scatter.53.cloned.1.call-done
  794.5 3.8 reduce-scatter.25.cloned.1.call-done
  798.3 5.9 fusion.88
  804.3 18.6 %reduce-scatter.29.cloned.1.call-done = bf16[1,128,512]{2,1,0:T(8,128)(2,1)} async-done(((bf16[1,512,512]{2,1,0:T(8,128)(2,1)}), bf16[1,128,512]{2,1,0:T(8,128)(2,1)}) %reduce-scatter.29.cloned.1.call-update) | async-done | bytes 131088 | tf_op jit(solution)/shard_map/reduce_scatter | solution.py:251
  822.9 5.9 fusion.85
  829.3 51.9 %all-reduce.24.cloned.1.call-done = (bf16[128,2048]{1,0:T(8,128)(2,1)}, bf16[128,2048]{1,0:T(8,128)(2,1)}) async-done(((bf16[128,2048]{1,0:T(8,128)(2,1)}, bf16[128,2048]{1,0:T(8,128)(2,1)}), (bf16[128,2048]{1,0:T(8,128)(2,1)}, bf16[128,2048]{1,0:T(8,128)(2,1)})) %all-reduce.24.cloned.1.call-update) | async-done | bytes 1048592 | tf_op jit(solution)/shard_map/psum | solution.py:96
  888.9 4.7 fusion.306
  893.7 4.1 fusion.307
  897.9 4.6 fusion.82
  902.5 4.6 fusion.79
  909.9 48.9 %all-reduce.22.cloned.1.call-done = (bf16[128,2048]{1,0:T(8,128)(2,1)}, bf16[128,2048]{1,0:T(8,128)(2,1)}) async-done(((bf16[128,2048]{1,0:T(8,128)(2,1)}, bf16[128,2048]{1,0:T(8,128)(2,1)}), (bf16[128,2048]{1,0:T(8,128)(2,1)}, bf16[128,2048]{1,0:T(8,128)(2,1)})) %all-reduce.22.cloned.1.call-update) | async-done | bytes 1048592 | tf_op jit(solution)/shard_map/psum | solution.py:96
  996.4 6.0 fusion.106
  1006.0 6.0 fusion.103
  1050.9 5.9 fusion.94
  1056.9 18.8 %reduce-scatter.31.cloned.1.call-done = bf16[1,128,512]{2,1,0:T(8,128)(2,1)} async-done(((bf16[1,512,512]{2,1,0:T(8,128)(2,1)}), bf16[1,128,512]{2,1,0:T(8,128)(2,1)}) %reduce-scatter.31.cloned.1.call-update) | async-done | bytes 131088 | tf_op jit(solution)/shard_map/reduce_scatter | solution.py:251
  1075.7 5.9 fusion.91
  1093.6 4.3 fusion.16
  1101.5 4.2 add_convert_fusion.5
  1110.0 4.6 add_convert_fusion.2
  1118.6 4.6 add_convert_fusion.3
  1123.8 10.8 fusion.291
  1134.6 13.7 add_convert_fusion
  1149.0 12.2 fusion.290
  1161.3 15.4 add_convert_fusion.1
  1188.2 24.3 %all-reduce = (bf16[2,3,512]{2,1,0:T(4,128)(2,1)S(1)}, bf16[2,2048]{1,0:T(2,128)(2,1)S(1)}, bf16[2,2048]{1,0:T(2,128)(2,1)S(1)}, bf16[2,2048]{1,0:T(2,128)(2,1)S(1)}, bf16[2,2048]{1,0:T(2,128)(2,1)S(1)}) all-reduce(bf16[2,3,512]{2,1,0:T(4,128)(2,1)S(1)} %pad_maximum_fusion.44, ...), channel_id=1, replica_groups=mesh['dp'=2,'ctx'=4,'mp'=4] {'dp','ctx'}, use_global_device_ids=true, to_apply=%region_85.86 | all-reduce | flops 19456 | bytes 77824 | tf_op jit(solution)/shard_map/psum | solution.py:389
  1215.6 44.0 %reduce-scatter.37.cloned.1.call-done = bf16[256,512]{1,0:T(8,128)(2,1)} async-done(((bf16[2048,512]{1,0:T(8,128)(2,1)}), bf16[256,512]{1,0:T(8,128)(2,1)}) %reduce-scatter.37.cloned.1.call-update) | async-done | bytes 262160 | tf_op jit(solution)/shard_map/reduce_scatter | solution.py:311
  1267.5 55.0 %reduce-scatter.47.cloned.1.call-done = bf16[256,1408]{1,0:T(8,128)(2,1)} async-done(((bf16[2048,1408]{1,0:T(8,128)(2,1)}), bf16[256,1408]{1,0:T(8,128)(2,1)}) %reduce-scatter.47.cloned.1.call-update) | async-done | bytes 720912 | tf_op jit(solution)/shard_map/reduce_scatter | solution.py:311
  1322.5 62.9 %reduce-scatter.45.cloned.1.call-done = bf16[256,1408]{1,0:T(8,128)(2,1)} async-done(((bf16[2048,1408]{1,0:T(8,128)(2,1)}), bf16[256,1408]{1,0:T(8,128)(2,1)}) %reduce-scatter.45.cloned.1.call-update) | async-done | bytes 720912 | tf_op jit(solution)/shard_map/reduce_scatter | solution.py:311
  1388.5 62.1 %reduce-scatter.35.cloned.1.call-done = bf16[256,3,512]{2,0,1:T(8,128)(2,1)} async-done(((bf16[2048,3,512]{2,0,1:T(8,128)(2,1)}), bf16[256,3,512]{2,0,1:T(8,128)(2,1)}) %reduce-scatter.35.cloned.1.call-update) | async-done | bytes 786448 | tf_op jit(solution)/shard_map/reduce_scatter | solution.py:311
  1450.5 65.4 %reduce-scatter.33.cloned.1.call-done = bf16[256,3,512]{2,0,1:T(8,128)(2,1)} async-done(((bf16[2048,3,512]{2,0,1:T(8,128)(2,1)}), bf16[256,3,512]{2,0,1:T(8,128)(2,1)}) %reduce-scatter.33.cloned.1.call-update) | async-done | bytes 786448 | tf_op jit(solution)/shard_map/reduce_scatter | solution.py:311
  1519.2 87.1 %reduce-scatter.43.cloned.1.call-done = bf16[256,2,1408]{2,0,1:T(8,128)(2,1)} async-done(((bf16[2048,2,1408]{2,0,1:T(8,128)(2,1)}), bf16[256,2,1408]{2,0,1:T(8,128)(2,1)}) %reduce-scatter.43.cloned.1.call-update) | async-done | bytes 1441808 | tf_op jit(solution)/shard_map/reduce_scatter | solution.py:311
  1606.2 90.3 %reduce-scatter.41.cloned.1.call-done = bf16[256,2,1408]{2,0,1:T(8,128)(2,1)} async-done(((bf16[2048,2,1408]{2,0,1:T(8,128)(2,1)}), bf16[256,2,1408]{2,0,1:T(8,128)(2,1)}) %reduce-scatter.41.cloned.1.call-update) | async-done | bytes 1441808 | tf_op jit(solution)/shard_map/reduce_scatter | solution.py:311
  1698.7 7.0 copy.209
  (783 shorter events, 302.6 us)
Async XLA Ops:
  7.2 51.6 %all-gather.21.cloned.1.call-start = ((), (), s32[]{:S(2)}) async-start(), calls=%async_computation.30 | async-start | bytes 7077888 | tf_op jit(solution)/shard_map/all_gather | solution.py:302
  10.1 79.1 %all-gather.23.cloned.1.call-start = ((), (), s32[]{:S(2)}) async-start(), calls=%async_computation.31 | async-start | bytes 2359296 | tf_op jit(solution)/shard_map/all_gather | solution.py:304
  11.0 119.9 %all-reduce.16.cloned.1.call-start = ((), (), s32[]{:S(2)}) async-start(), calls=%async_computation.16 | async-start | bytes 1048576 | tf_op jit(solution)/shard_map/psum | solution.py:96
  11.9 50.7 %copy-start.205 = (f32[128]{0:T(128)}, f32[128]{0:T(128)S(1)}, u32[]{:S(2)}) copy-start(f32[128]{0:T(128)S(1)} %broadcast_multiply_fusion.23) | copy-start | bytes 1540
  18.8 52.4 %copy-start.144 = (f32[128,8]{0,1:T(8,128)}, f32[128,8]{0,1:T(8,128)S(1)}, u32[]{:S(2)}) copy-start(f32[128,8]{0,1:T(8,128)S(1)} %get-tuple-element.222) | copy-start | bytes 12292
  18.8 125.9 %copy-start.140 = (f32[128,8]{0,1:T(8,128)}, f32[128,8]{0,1:T(8,128)S(1)}, u32[]{:S(2)}) copy-start(f32[128,8]{0,1:T(8,128)S(1)} %get-tuple-element.221) | copy-start | bytes 12292
  18.8 52.4 %copy-start.145 = (f32[128,8]{0,1:T(8,128)}, f32[128,8]{0,1:T(8,128)S(1)}, u32[]{:S(2)}) copy-start(f32[128,8]{0,1:T(8,128)S(1)} %get-tuple-element.220) | copy-start | bytes 12292
  18.8 125.9 %copy-start.142 = (f32[128,8]{0,1:T(8,128)}, f32[128,8]{0,1:T(8,128)S(1)}, u32[]{:S(2)}) copy-start(f32[128,8]{0,1:T(8,128)S(1)} %get-tuple-element.219) | copy-start | bytes 12292
  19.1 59.5 %copy-start.111 = (pred[128,512]{1,0:T(8,128)(4,1)}, pred[128,512]{1,0:T(8,128)(4,1)S(1)}, u32[]{:S(2)}) copy-start(pred[128,512]{1,0:T(8,128)(4,1)S(1)} %get-tuple-element.189) | copy-start | bytes 196612
  19.1 133.0 %copy-start.109 = (pred[128,512]{1,0:T(8,128)(4,1)}, pred[128,512]{1,0:T(8,128)(4,1)S(1)}, u32[]{:S(2)}) copy-start(pred[128,512]{1,0:T(8,128)(4,1)S(1)} %get-tuple-element.188) | copy-start | bytes 196612
  19.2 43.4 %copy-start.208 = (f32[128]{0:T(128)}, f32[128]{0:T(128)S(1)}, u32[]{:S(2)}) copy-start(f32[128]{0:T(128)S(1)} %add_rsqrt_fusion.7) | copy-start | bytes 1540
  19.2 113.1 %copy-start.146 = (f32[1,2048]{1,0:T(1,128)}, f32[1,2048]{1,0:T(1,128)S(1)}, u32[]{:S(2)}) copy-start(f32[1,2048]{1,0:T(1,128)S(1)} %get-tuple-element.197) | copy-start | bytes 24580
  19.3 113.0 %copy-start.122 = (f32[1,2048]{1,0:T(1,128)}, f32[1,2048]{1,0:T(1,128)S(1)}, u32[]{:S(2)}) copy-start(f32[1,2048]{1,0:T(1,128)S(1)} %get-tuple-element.195) | copy-start | bytes 24580
  81.4 50.8 %copy-start.121 = (bf16[8,64,128]{2,1,0:T(8,128)(2,1)}, bf16[8,64,128]{2,1,0:T(8,128)(2,1)S(1)}, u32[]{:S(2)}) copy-start(bf16[8,64,128]{2,1,0:T(8,128)(2,1)S(1)} %convolution_convert_fusion.11) | copy-start | bytes 393220
  92.4 102.8 %all-reduce.18.cloned.1.call-start = ((), (), s32[]{:S(2)}) async-start(), calls=%async_computation.17 | async-start | bytes 1048576 | tf_op jit(solution)/shard_map/psum | solution.py:96
  92.5 43.7 %copy-start.202 = (f32[128]{0:T(128)}, f32[128]{0:T(128)S(1)}, u32[]{:S(2)}) copy-start(f32[128]{0:T(128)S(1)} %broadcast_multiply_fusion.19) | copy-start | bytes 1540
  157.4 107.9 %all-gather.25.cloned.1.call-start = ((), (), s32[]{:S(2)}) async-start(), calls=%async_computation.32 | async-start | bytes 12976128 | tf_op jit(solution)/shard_map/all_gather | solution.py:303
  163.4 31.8 %copy-start.18 = (bf16[128,2048]{1,0:T(8,128)(2,1)S(1)}, bf16[128,2048]{1,0:T(8,128)(2,1)}, u32[]{:S(2)}) copy-start(bf16[128,2048]{1,0:T(8,128)(2,1)} %all-reduce.16.cloned.1.call-done) | copy-start | bytes 1572868
  163.5 147.5 %all-gather.27.cloned.1.call-start = ((), (), s32[]{:S(2)}) async-start(), calls=%async_computation.33 | async-start | bytes 6488064 | tf_op jit(solution)/shard_map/all_gather | solution.py:305
  166.0 205.7 %all-reduce.30.cloned.1.call-start = ((), (), s32[]{:S(2)}) async-start(), calls=%async_computation.47 | async-start | bytes 2097152 | tf_op jit(solution)/shard_map/psum | solution.py:96
  166.5 106.4 %copy-start.94 = (f32[1,2048]{1,0:T(1,128)}, f32[1,2048]{1,0:T(1,128)S(1)}, u32[]{:S(2)}) copy-start(f32[1,2048]{1,0:T(1,128)S(1)} %get-tuple-element.193) | copy-start | bytes 24580
  166.6 105.0 %copy-start.159 = (f32[128]{0:T(128)}, f32[128]{0:T(128)S(1)}, u32[]{:S(2)}) copy-start(f32[128]{0:T(128)S(1)} %broadcast_multiply_fusion.22) | copy-start | bytes 1540
  196.8 76.1 %copy-start.166 = (f32[128]{0:T(128)}, f32[128]{0:T(128)S(1)}, u32[]{:S(2)}) copy-start(f32[128]{0:T(128)S(1)} %broadcast_multiply_fusion.18) | copy-start | bytes 1540
  197.1 74.4 %copy-start.163 = (f32[128]{0:T(128)}, f32[128]{0:T(128)S(1)}, u32[]{:S(2)}) copy-start(f32[128]{0:T(128)S(1)} %add_rsqrt_fusion.6) | copy-start | bytes 1540
  197.2 75.8 %copy-start.189 = (f32[128]{0:T(128)}, f32[128]{0:T(128)S(1)}, u32[]{:S(2)}) copy-start(f32[128]{0:T(128)S(1)} %add_rsqrt_fusion.2) | copy-start | bytes 1540
  273.4 37.6 %copy-start.58 = (bf16[128,1408]{1,0:T(8,128)(2,1)}, bf16[128,1408]{1,0:T(8,128)(2,1)S(1)}, u32[]{:S(2)}) copy-start(bf16[128,1408]{1,0:T(8,128)(2,1)S(1)} %multiply_convert_fusion.11) | copy-start | bytes 1081348
  319.3 99.9 %all-gather.29.cloned.1.call-start = ((), (), s32[]{:S(2)}) async-start(), calls=%async_computation.34 | async-start | bytes 7077888 | tf_op jit(solution)/shard_map/all_gather | solution.py:302
  320.1 146.2 %all-gather.31.cloned.1.call-start = ((), (), s32[]{:S(2)}) async-start(), calls=%async_computation.35 | async-start | bytes 2359296 | tf_op jit(solution)/shard_map/all_gather | solution.py:304
  320.8 203.0 %all-reduce.28.cloned.1.call-start = ((), (), s32[]{:S(2)}) async-start(), calls=%async_computation.46 | async-start | bytes 2097152 | tf_op jit(solution)/shard_map/psum | solution.py:96
  374.2 49.1 %copy-start.16 = (f32[128,2048]{1,0:T(8,128)}, f32[128,2048]{1,0:T(8,128)S(1)}, u32[]{:S(2)}) copy-start(f32[128,2048]{1,0:T(8,128)S(1)} %get-tuple-element.123) | copy-start | bytes 3145732
  374.2 57.7 %copy-start.13 = (f32[128,2048]{1,0:T(8,128)}, f32[128,2048]{1,0:T(8,128)S(1)}, u32[]{:S(2)}) copy-start(f32[128,2048]{1,0:T(8,128)S(1)} %get-tuple-element.145) | copy-start | bytes 3145732
  419.2 12.4 copy-start.215
  419.2 12.7 copy-start.26
  444.6 16.1 copy-start.112
  445.7 15.6 copy-start.136
  445.7 15.6 copy-start.138
  445.8 16.3 copy-start.132
  445.8 16.3 copy-start.134
  471.3 121.5 %all-gather.33.cloned.1.call-start = ((), (), s32[]{:S(2)}) async-start(), calls=%async_computation.36 | async-start | bytes 12976128 | tf_op jit(solution)/shard_map/all_gather | solution.py:303
  474.0 163.9 %all-gather.35.cloned.1.call-start = ((), (), s32[]{:S(2)}) async-start(), calls=%async_computation.37 | async-start | bytes 6488064 | tf_op jit(solution)/shard_map/all_gather | solution.py:305
  474.6 234.3 %all-reduce.26.cloned.1.call-start = ((), (), s32[]{:S(2)}) async-start(), calls=%async_computation.45 | async-start | bytes 2097152 | tf_op jit(solution)/shard_map/psum | solution.py:96
  656.5 104.3 %reduce-scatter.49.cloned.1.call-start = ((), (), s32[]{:S(2)}) async-start(), calls=%async_computation.38 | async-start | bytes 655360
  728.3 45.2 %reduce-scatter.53.cloned.1.call-start = ((), (), s32[]{:S(2)}) async-start(), calls=%async_computation.40 | async-start | bytes 655360
  744.1 54.3 %reduce-scatter.25.cloned.1.call-start = ((), (), s32[]{:S(2)}) async-start(), calls=%async_computation.18 | async-start | bytes 655360 | tf_op jit(solution)/shard_map/reduce_scatter | solution.py:251
  749.1 73.8 %reduce-scatter.29.cloned.1.call-start = ((), (), s32[]{:S(2)}) async-start(), calls=%async_computation.20 | async-start | bytes 655360 | tf_op jit(solution)/shard_map/reduce_scatter | solution.py:251
  760.7 120.5 %all-reduce.24.cloned.1.call-start = ((), (), s32[]{:S(2)}) async-start(), calls=%async_computation.44 | async-start | bytes 2097152 | tf_op jit(solution)/shard_map/psum | solution.py:96
  828.9 130.0 %all-reduce.22.cloned.1.call-start = ((), (), s32[]{:S(2)}) async-start(), calls=%async_computation.43 | async-start | bytes 2097152 | tf_op jit(solution)/shard_map/psum | solution.py:96
  907.1 113.6 %reduce-scatter.51.cloned.1.call-start = ((), (), s32[]{:S(2)}) async-start(), calls=%async_computation.39 | async-start | bytes 655360
  980.6 47.5 %reduce-scatter.55.cloned.1.call-start = ((), (), s32[]{:S(2)}) async-start(), calls=%async_computation.41 | async-start | bytes 655360
  996.4 54.6 %reduce-scatter.27.cloned.1.call-start = ((), (), s32[]{:S(2)}) async-start(), calls=%async_computation.19 | async-start | bytes 655360 | tf_op jit(solution)/shard_map/reduce_scatter | solution.py:251
  1005.9 69.8 %reduce-scatter.31.cloned.1.call-start = ((), (), s32[]{:S(2)}) async-start(), calls=%async_computation.21 | async-start | bytes 655360 | tf_op jit(solution)/shard_map/reduce_scatter | solution.py:251
  1020.5 165.3 %all-reduce.20.cloned.1.call-start = ((), (), s32[]{:S(2)}) async-start(), calls=%async_computation.42 | async-start | bytes 4194304 | tf_op jit(solution)/shard_map/psum | solution.py:96
  1081.6 134.0 %reduce-scatter.39.cloned.1.call-start = ((), (), s32[]{:S(2)}) async-start(), calls=%async_computation.25 | async-start | bytes 2359296 | tf_op jit(solution)/shard_map/reduce_scatter | solution.py:311
  1085.9 173.7 %reduce-scatter.37.cloned.1.call-start = ((), (), s32[]{:S(2)}) async-start(), calls=%async_computation.24 | async-start | bytes 2359296 | tf_op jit(solution)/shard_map/reduce_scatter | solution.py:311
  1090.2 232.3 %reduce-scatter.47.cloned.1.call-start = ((), (), s32[]{:S(2)}) async-start(), calls=%async_computation.29 | async-start | bytes 6488064 | tf_op jit(solution)/shard_map/reduce_scatter | solution.py:311
  1098.0 287.4 %reduce-scatter.45.cloned.1.call-start = ((), (), s32[]{:S(2)}) async-start(), calls=%async_computation.28 | async-start | bytes 6488064 | tf_op jit(solution)/shard_map/reduce_scatter | solution.py:311
  1105.8 344.8 %reduce-scatter.35.cloned.1.call-start = ((), (), s32[]{:S(2)}) async-start(), calls=%async_computation.23 | async-start | bytes 7077888 | tf_op jit(solution)/shard_map/reduce_scatter | solution.py:311
  1114.7 401.2 %reduce-scatter.33.cloned.1.call-start = ((), (), s32[]{:S(2)}) async-start(), calls=%async_computation.22 | async-start | bytes 7077888 | tf_op jit(solution)/shard_map/reduce_scatter | solution.py:311
  1123.2 11.4 copy-start.69
  1123.2 483.0 %reduce-scatter.43.cloned.1.call-start = ((), (), s32[]{:S(2)}) async-start(), calls=%async_computation.27 | async-start | bytes 12976128 | tf_op jit(solution)/shard_map/reduce_scatter | solution.py:311
  1148.4 12.9 copy-start.72
  1148.4 12.9 copy-start.168
  1148.4 12.9 copy-start.191
  1148.4 548.2 %reduce-scatter.41.cloned.1.call-start = ((), (), s32[]{:S(2)}) async-start(), calls=%async_computation.26 | async-start | bytes 12976128 | tf_op jit(solution)/shard_map/reduce_scatter | solution.py:311
  (190 other events, 601.6 us)
Sparse Core Ops, SparseCore 0:
  10.5 48.2 all-gather.20
  61.2 27.8 all-gather.22
  92.5 38.2 all-reduce.15
  157.6 37.6 all-reduce.17
  197.6 67.6 all-gather.24
  267.6 43.3 all-gather.26
  319.4 52.2 all-reduce.29
  374.3 44.8 all-gather.28
  421.3 28.0 all-gather.30
  471.4 52.2 all-reduce.27
  525.6 67.0 all-gather.32
  594.5 43.3 all-gather.34
  656.6 52.1 all-reduce.25
  728.4 21.0 reduce-scatter.48
  751.8 21.6 reduce-scatter.52
  776.6 21.6 reduce-scatter.24
  801.2 21.6 reduce-scatter.28
  829.0 52.2 all-reduce.23
  907.3 51.5 all-reduce.21
  980.7 21.0 reduce-scatter.50
  1004.3 21.6 reduce-scatter.54
  1029.2 21.6 reduce-scatter.26
  1054.0 21.6 reduce-scatter.30
  1081.8 88.0 all-reduce.19
  1173.7 40.4 reduce-scatter.38
  1218.3 41.2 reduce-scatter.36
  1263.4 59.0 reduce-scatter.46
  1326.3 58.9 reduce-scatter.44
  1388.8 61.7 reduce-scatter.34
  1454.1 61.7 reduce-scatter.32
  1519.4 86.7 reduce-scatter.42
  1609.7 86.7 reduce-scatter.40
where the time goes:
time: 1720 us; the launch traced here: 1710 us
  waiting for transfers between devices  1130 us (66%)
  matrix products  257 us (15%)
  local copies, waits for them, and re-layouts  126 us (7%)
  other arithmetic  93.2 us (5%)
  blocking collectives  89.1 us (5%)
  between operations  17.5 us (1%)
    reduce_scatter x8, waiting for transfers between devices, spread(): lax.psum_scatter(as_sent(gradients), ('dp', 'ctx'), scatter_dimension=0,...  467 us
    psum x8, waiting for transfers between devices, model_sum(): return lax.psum(partial_sum.astype(jnp.bfloat16), 'mp').astype(jnp.float32)  317 us
    all_gather x2, waiting for transfers between devices, fetch_weights(): lax.all_gather(gate_up_weight[layer_no], ('dp', 'ctx'), axis=0, tiled=True)  132 us
    all_gather x2, waiting for transfers between devices, fetch_weights(): lax.all_gather(qkv_weight[layer_no], ('dp', 'ctx'), axis=0, tiled=True)  83.1 us
    unnamed x466, local copies, waits for them, and re-layouts  71.5 us
    all_gather x2, waiting for transfers between devices, fetch_weights(): lax.all_gather(down_weight[layer_no], ('dp', 'ctx'), axis=0, tiled=True)  68.6 us
    dot_general x4, matrix products, layer_backward(): jnp.einsum('rd,rcf->dcf', input_two, grad_pre, preferred_element_type=jnp...  52.2 us
    reduce_scatter x4, waiting for transfers between devices, layer_backward(): lax.psum_scatter(grad_value_all.reshape(flat_shape).astype(jnp.bfloat16),...  43.2 us
  transfers between devices with their start and end apart: 32, of which 26 were waited for; matrix products, arithmetic and copies ran while one was open for 19% of the time, Pallas kernels for 0%

commit v1 on v0

v1 whole, which is shorter than its diff:
```python
import math

import jax
import jax.numpy as jnp
from jax import lax
from jax.sharding import Mesh
from jax.sharding import PartitionSpec as P

HEAD = 64
ROT = 16
LAYERS = 2
NORM_EPS = 1e-05
MASK_FILL = -1e30
LOW = jnp.bfloat16
F32 = jnp.float32


def dot(a, b, dims):
    return lax.dot_general(a, b, (dims, ((), ())), preferred_element_type=F32)


def nn(a, b):
    return dot(a, b, ((1,), (0,)))


def nt(a, b):
    return dot(a, b, ((1,), (1,)))


def tn(a, b):
    return dot(a, b, ((0,), (0,)))


def normalize(values):
    center = values - jnp.mean(values, axis=-1, keepdims=True)
    inverse = lax.rsqrt(jnp.mean(center * center, axis=-1, keepdims=True) + NORM_EPS)
    return center * inverse, inverse


def norm_back(upstream, normed, inverse, gain_vec):
    scaled = upstream * gain_vec
    return inverse * (
        scaled
        - jnp.mean(scaled, axis=-1, keepdims=True)
        - normed * jnp.mean(scaled * normed, axis=-1, keepdims=True)
    )


def make_program(n_dp, n_chi, n_clo, n_mp):
    dp_bits = [("dp", 1 << k) for k in range(int(math.log2(n_dp)))]
    chi_bits = [("chi", 1 << k) for k in range(int(math.log2(n_chi)))]
    group_bits = chi_bits + dp_bits
    n_groups = n_dp * n_chi
    sizes = {"dp": n_dp, "chi": n_chi, "clo": n_clo, "mp": n_mp}

    def swap(value, axis, bit):
        return lax.ppermute(value, axis, [(i, i ^ bit) for i in range(sizes[axis])])

    def bit_set(axis, bit):
        return (lax.axis_index(axis) & bit) != 0

    def relative(value, axis):
        rest = value.shape[:axis]
        width = value.shape[axis]
        tail = value.shape[axis + 1 :]
        for k, (name, bit) in enumerate(group_bits):
            inner = width // n_groups << k
            parts = value.reshape(rest + (width // (2 * inner), 2, inner) + tail)
            flipped = jnp.flip(parts, len(rest) + 1)
            value = jnp.where(bit_set(name, bit), flipped, parts).reshape(
                rest + (width,) + tail
            )
        return value

    def gather_half(part, order):
        blocks = {0: part}
        for k in order:
            name, bit = group_bits[k]
            fresh = {r | (1 << k): swap(block, name, bit) for r, block in blocks.items()}
            blocks.update(fresh)
        return [blocks[r] for r in range(n_groups)]

    def reduce_half(blocks, order):
        blocks = dict(enumerate(blocks))
        for k in order:
            name, bit = group_bits[k]
            for r in [r for r in blocks if r & (1 << k)]:
                moved = swap(blocks.pop(r).astype(LOW), name, bit)
                blocks[r ^ (1 << k)] = blocks[r ^ (1 << k)] + moved.astype(F32)
        return blocks[0]

    up_order = list(range(len(group_bits)))
    down_order = up_order[::-1]

    def fetch(low_cols, high_cols):
        odd = bit_set("clo", 1)
        keep = jnp.where(odd, high_cols, low_cols)
        other = swap(jnp.where(odd, low_cols, high_cols), "clo", 1)
        first, second = jnp.where(odd, other, keep), jnp.where(odd, keep, other)
        first = gather_half(first, up_order)
        second = gather_half(second, down_order)
        return jnp.concatenate([x for pair in zip(first, second) for x in pair], axis=0)

    def spread(grad):
        rows = grad.shape[0] // (2 * n_groups)
        parts = [grad[i * rows : (i + 1) * rows] for i in range(2 * n_groups)]
        first = reduce_half(parts[0::2], down_order)
        second = reduce_half(parts[1::2], up_order)
        odd = bit_set("clo", 1)
        keep = jnp.where(odd, second, first)
        other = swap(jnp.where(odd, first, second).astype(LOW), "clo", 1).astype(F32)
        return jnp.where(odd, other, keep), jnp.where(odd, keep, other)

    def token_gather(own):
        half = [own] + [swap(own, "mp", r) for r in range(1, n_mp)]
        half = jnp.concatenate(half, axis=0)
        return jnp.concatenate([half, swap(half, "clo", 1)], axis=0)

    def token_reduce(partial):
        rows = partial.shape[0] // 2
        moved = swap(partial[rows:].astype(LOW), "clo", 1)
        half = partial[:rows] + moved.astype(F32)
        own = rows // n_mp
        total = half[:own]
        for r in range(1, n_mp):
            total = total + swap(half[r * own : (r + 1) * own].astype(LOW), "mp", r).astype(F32)
        return total

    def own_tokens(value):
        seqs, block, width = value.shape
        sub = block * n_chi // n_mp
        per_block = block // sub
        place = lax.axis_index("mp") % per_block
        mine = lax.dynamic_slice_in_dim(value, place * sub, sub, 1)
        chi = lax.axis_index("chi")
        here = lax.dynamic_index_in_dim(mine, chi, 0, keepdims=False)
        there = swap(lax.dynamic_index_in_dim(mine, 1 - chi, 0, keepdims=False), "chi", 1)
        return jnp.where(lax.axis_index("mp") // per_block == chi, here, there)

    def tokens_out(own, block):
        sub, width = own.shape
        per_block = block // sub
        chi, mp = lax.axis_index("chi"), lax.axis_index("mp")
        parts = jnp.stack([own] + [swap(own, "mp", r) for r in range(1, n_mp)])
        parts = parts.reshape(n_chi, per_block, sub, width)
        parts = jnp.where(mp % per_block == 1, jnp.flip(parts, 1), parts)
        parts = parts.reshape(n_chi, block, width)
        here = (mp // per_block) == chi
        mine = jnp.where(here, parts[0], parts[1])
        moved = swap(jnp.where(here, parts[1], parts[0]), "chi", 1)
        return jnp.where(chi == 0, jnp.stack([mine, moved]), jnp.stack([moved, mine]))

    def on_device(
        tokens, segments, cotangent, first_gain, first_bias, qkv_weight, qkv_bias,
        out_weight, second_gain, second_bias, gate_up_weight, down_weight,
    ):
        n_seq, block, width = tokens.shape
        rows_dev = qkv_weight.shape[1]
        half_in = qkv_weight.shape[3] // 2
        half_ff = down_weight.shape[2] // 2
        heads = half_in // HEAD
        total = block * n_chi * n_clo
        sub = total // (n_clo * n_mp)
        mp, clo, chi = (lax.axis_index(a) for a in ("mp", "clo", "chi"))

        x_own = relative(own_tokens(tokens), 1).astype(F32)
        dx = relative(own_tokens(cotangent), 1)

        weights = []
        for l in range(LAYERS):
            qkv = qkv_weight[l]
            gu = gate_up_weight[l]
            weights.append(
                (
                    fetch(
                        qkv[:, :, :half_in].reshape(rows_dev, -1),
                        qkv[:, :, half_in:].reshape(rows_dev, -1),
                    ),
                    fetch(out_weight[l][:, :half_in], out_weight[l][:, half_in:]),
                    fetch(
                        gu[:, :, :half_ff].reshape(rows_dev, -1),
                        gu[:, :, half_ff:].reshape(rows_dev, -1),
                    ),
                    fetch(down_weight[l][:, :half_ff], down_weight[l][:, half_ff:]),
                )
            )
        gains = relative(
            jnp.stack([first_gain, first_bias, second_gain, second_bias]), 2
        )
        half_bias = jnp.where(clo == 1, qkv_bias[:, :, half_in:], qkv_bias[:, :, :half_in])

        there = swap(lax.dynamic_index_in_dim(segments, 1 - chi, 0, keepdims=False), "chi", 1)
        here = lax.dynamic_index_in_dim(segments, chi, 0, keepdims=False)
        pair = jnp.stack([jnp.where(chi == 0, here, there), jnp.where(chi == 0, there, here)])
        other = swap(pair, "clo", 1)
        whole = jnp.stack(
            [jnp.where(clo == 0, pair, other), jnp.where(clo == 0, other, pair)], axis=1
        ).reshape(total)
        core_of = jnp.arange(n_clo, dtype=jnp.int32) ^ clo
        mp_of = jnp.arange(n_mp, dtype=jnp.int32) ^ mp
        per_block = block // sub
        place = (
            (mp_of // per_block * (n_clo * block) + mp_of % per_block * sub)[None, :, None]
            + (core_of * block)[:, None, None]
            + jnp.arange(sub, dtype=jnp.int32)[None, None, :]
        ).reshape(total)
        match = place[:, None] == jnp.arange(total, dtype=jnp.int32)[None, :]
        seg = jnp.sum(jnp.where(match, whole[None, :], 0), axis=1)
        starts = jnp.sum((seg[None, :] < seg[:, None]).astype(jnp.int32), axis=1)
        freq = jnp.exp(
            jnp.arange(ROT // 2, dtype=F32) * (-2.0 * math.log(10000.0) / ROT)
        )
        angles = (place - starts).astype(F32)[:, None] * freq[None, :]
        cos_t, sin_t = jnp.cos(angles)[:, None, :], jnp.sin(angles)[:, None, :]
        allowed = (seg[:, None] == seg[None, :]) & (place[None, :] <= place[:, None])

        def rotate(value, sign):
            a, b = value[..., : ROT // 2], value[..., ROT // 2 : ROT]
            return jnp.concatenate(
                [a * cos_t - sign * b * sin_t, b * cos_t + sign * a * sin_t, value[..., ROT:]],
                axis=-1,
            )

        scale = 1.0 / math.sqrt(HEAD)

        def scores_of(q, k):
            s = jnp.einsum("qhe,khe->hqk", q, k, preferred_element_type=F32) * scale
            return jnp.where(allowed[None], s, MASK_FILL)

        saved = []
        for l in range(LAYERS):
            w_qkv, w_out, w_gu, w_down = weights[l]
            n1, inv1 = normalize(x_own)
            h1 = token_gather((n1 * gains[0, l] + gains[1, l]).astype(LOW))
            p = nn(h1, w_qkv).reshape(total, 3, heads, HEAD) + half_bias[l].reshape(
                1, 3, heads, HEAD
            )
            q = rotate(p[:, 0], 1.0).astype(LOW)
            k = rotate(p[:, 1], 1.0).astype(LOW)
            v = p[:, 2].astype(LOW)
            s = scores_of(q, k)
            top = jnp.max(s, axis=-1, keepdims=True)
            e = jnp.exp(s - top)
            den = jnp.sum(e, axis=-1, keepdims=True)
            log_total = top + jnp.log(den)
            w = (e / den).astype(LOW)
            o = jnp.einsum("hqk,khe->qhe", w, v, preferred_element_type=F32)
            o = o.reshape(total, half_in).astype(LOW)
            y_own = x_own + token_reduce(nt(o, w_out))
            n2, inv2 = normalize(y_own)
            h2 = token_gather((n2 * gains[2, l] + gains[3, l]).astype(LOW))
            gu = nn(h2, w_gu)
            g, u = gu[:, :half_ff], gu[:, half_ff:]
            z = (jax.nn.silu(g) * u).astype(LOW)
            x_own = y_own + token_reduce(nt(z, w_down))
            saved.append((h1, n1, inv1, q, k, v, log_total, o, h2, n2, inv2, gu, z))

        activations = tokens_out(relative(x_own.astype(LOW), 1), block)

        dx = dx.astype(F32)
        weight_grads = [None] * LAYERS
        small_grads = [None] * LAYERS
        for l in reversed(range(LAYERS)):
            w_qkv, w_out, w_gu, w_down = weights[l]
            h1, n1, inv1, q, k, v, log_total, o, h2, n2, inv2, gu, z = saved[l]
            dm = token_gather(dx.astype(LOW))
            dz = nn(dm, w_down)
            g, u = gu[:, :half_ff], gu[:, half_ff:]
            sig = jax.nn.sigmoid(g)
            dg = dz * u * sig * (1.0 + g * (1.0 - sig))
            du = dz * g * sig
            dp2 = jnp.concatenate([dg.astype(LOW), du.astype(LOW)], axis=1)
            dh2 = token_reduce(nt(dp2, w_gu))
            g_down = spread(tn(dm, z))
            g_gu = spread(tn(h2, dp2))
            dy = dx + norm_back(dh2, n2, inv2, gains[2, l])
            da = token_gather(dy.astype(LOW))
            do = nn(da, w_out).astype(LOW).reshape(total, heads, HEAD)
            prob = jnp.exp(scores_of(q, k) - log_total)
            dw = jnp.einsum("qhe,khe->hqk", do, v, preferred_element_type=F32)
            dv = jnp.einsum("hqk,qhe->khe", prob.astype(LOW), do, preferred_element_type=F32)
            ds = (prob * (dw - jnp.sum(prob * dw, axis=-1, keepdims=True))).astype(LOW)
            dq = jnp.einsum("hqk,khe->qhe", ds, k, preferred_element_type=F32) * scale
            dk = jnp.einsum("hqk,qhe->khe", ds, q, preferred_element_type=F32) * scale
            dp1 = jnp.stack([rotate(dq, -1.0), rotate(dk, -1.0), dv], axis=1).astype(LOW)
            dp1 = dp1.reshape(total, 3 * half_in)
            dh1 = token_reduce(nt(dp1, w_qkv))
            g_out = spread(tn(da, o))
            g_qkv = spread(tn(h1, dp1))
            dx = dy + norm_back(dh1, n1, inv1, gains[0, l])
            weight_grads[l] = (g_qkv, g_out, g_gu, g_down)
            small_grads[l] = (
                jnp.sum(dh1 * n1, axis=0),
                jnp.sum(dh1, axis=0),
                jnp.sum(dh2 * n2, axis=0),
                jnp.sum(dh2, axis=0),
                jnp.sum(dp1.astype(F32), axis=0),
            )
        tokens_grad = tokens_out(relative(dx.astype(LOW), 1), block).astype(F32)

        norms = relative(
            jnp.stack([jnp.stack([small_grads[l][i] for l in range(LAYERS)]) for i in range(4)]), 2
        )
        bias = jnp.stack([small_grads[l][4] for l in range(LAYERS)]).reshape(LAYERS, 3, half_in)
        for name, bit in [("mp", 1 << k) for k in range(int(math.log2(n_mp)))] + [("clo", 1)]:
            norms = norms + swap(norms, name, bit)
        for name, bit in group_bits:
            norms = norms + swap(norms, name, bit)
            bias = bias + swap(bias, name, bit)
        bias_other = swap(bias, "clo", 1)
        bias = jnp.concatenate(
            [jnp.where(clo == 0, bias, bias_other), jnp.where(clo == 0, bias_other, bias)], axis=2
        )

        def joined(i, parts):
            return jnp.stack(
                [
                    jnp.concatenate(
                        [
                            piece.reshape((rows_dev,) + parts + (-1,))
                            for piece in weight_grads[l][i]
                        ],
                        axis=-1,
                    )
                    for l in range(LAYERS)
                ]
            )

        return (
            activations, tokens_grad, norms[0], norms[1], joined(0, (3,)), bias,
            joined(1, ()), norms[2], norms[3], joined(2, (2,)), joined(3, ()),
        )

    return on_device


def solution(mesh):
    n_dp, n_ctx, n_mp = (mesh.shape[a] for a in ("dp", "ctx", "mp"))
    n_clo = 2
    n_chi = n_ctx // n_clo
    fine = Mesh(mesh.devices.reshape(n_dp, n_chi, n_clo, n_mp), ("dp", "chi", "clo", "mp"))
    rows = ("dp", "chi", "clo")
    ctx = ("chi", "clo")
    return jax.shard_map(
        make_program(n_dp, n_chi, n_clo, n_mp),
        mesh=fine,
        in_specs=(
            P("dp", ctx, None),
            P("dp", ctx),
            P("dp", ctx, None),
            P(),
            P(),
            P(None, rows, None, "mp"),
            P(None, None, "mp"),
            P(None, rows, "mp"),
            P(),
            P(),
            P(None, rows, None, "mp"),
            P(None, rows, "mp"),
        ),
        out_specs=(
            P("dp", ctx, None),
            P("dp", ctx, None),
            P(),
            P(),
            P(None, rows, None, "mp"),
            P(None, None, "mp"),
            P(None, rows, "mp"),
            P(),
            P(),
            P(None, rows, None, "mp"),
            P(None, rows, "mp"),
        ),
        check_vma=False,
    )
```

time: 1720 us -> 1040 us (0.60)
  waiting for transfers between devices: 1130 us -> 461 us
  starting transfers between devices: 3.37 us -> 221 us
  matrix products: 257 us -> 79.9 us
  blocking collectives: 89.1 us -> 0 us
  other arithmetic: 93.2 us -> 124 us
    reduce_scatter x12 -> x0, waiting for transfers between devices: 510 us -> none  [the longest x8 467 us: spread(): lax.psum_scatter(as_sent(gradients), ('dp', 'ctx'), scatter_dimension=0,...]
    ppermute x0 -> x196, waiting for transfers between devices: none -> 461 us  [swap(): return lax.ppermute(value, axis, [(i, i ^ bit) for i in range(sizes[axis])])]
    psum x8 -> x0, waiting for transfers between devices: 317 us -> none  [model_sum(): return lax.psum(partial_sum.astype(jnp.bfloat16), 'mp').astype(jnp.float32)]
    all_gather x8 -> x0, waiting for transfers between devices: 292 us -> none  [the longest x2 132 us: fetch_weights(): lax.all_gather(gate_up_weight[layer_no], ('dp', 'ctx'), axis=0, tiled=True)]
    ppermute x0 -> x196, starting transfers between devices: none -> 221 us  [swap(): return lax.ppermute(value, axis, [(i, i ^ bit) for i in range(sizes[axis])])]
    dot_general x72 -> x36, matrix products: 257 us -> 79.9 us  [the longest x24 69.6 us: dot(): return lax.dot_general(a, b, (dims, ((), ())), preferred_element_type=F32)]
    all_gather x9 -> x0, blocking collectives: 64.8 us -> none  [the longest x4 29.4 us: layer_forward(): lax.all_gather(value_loc, 'ctx', axis=1, tiled=True)]
    select_n x0 -> x39, other arithmetic: none -> 35.6 us  [the longest x8 15.9 us: spread(): return (jnp.where(odd, other, keep), jnp.where(odd, keep, other))]
  transfers between devices with their start and end apart: 32 -> 196, of which waited for: 26 -> 71; matrix products, arithmetic and copies ran while one was open for 19% -> 25% of each run, Pallas kernels for 0% -> 0%
where the time goes in v1:
time: 1040 us; the launch traced here: 1030 us
  waiting for transfers between devices  461 us (44%)
  starting transfers between devices  221 us (21%)
  local copies, waits for them, and re-layouts  138 us (13%)
  other arithmetic  124 us (12%)
  matrix products  79.9 us (8%)
    ppermute x196, waiting for transfers between devices, swap(): return lax.ppermute(value, axis, [(i, i ^ bit) for i in range(sizes[axis])])  461 us
    ppermute x196, starting transfers between devices, swap(): return lax.ppermute(value, axis, [(i, i ^ bit) for i in range(sizes[axis])])  221 us
    dot_general x24, matrix products, dot(): return lax.dot_general(a, b, (dims, ((), ())), preferred_element_type=F32)  69.6 us
    unnamed x380, local copies, waits for them, and re-layouts  43.6 us
  transfers between devices with their start and end apart: 196, of which 71 were waited for; matrix products, arithmetic and copies ran while one was open for 25% of the time, Pallas kernels for 0%

profile of v1, /device:TPU:0, one launch (start us, length us, event | category | flops | bytes accessed | tf_op | source)
XLA Modules:
  0.0 1029.1 jit_solution(3775704071552942751)
XLA Ops:
  10.1 3.7 slice_bitcast_fusion
  107.2 7.4 collective-permute-done.1
  116.2 6.9 collective-permute-done.2
  128.6 17.0 %collective-permute-done.97 = bf16[64,2048]{1,0:T(8,128)(2,1)S(1)} collective-permute-done((bf16[64,2048]{1,0:T(8,128)(2,1)S(1)}, bf16[64,2048]{1,0:T(8,128)(2,1)S(1)}, u32[]{:S(2)}, u32[]{:S(2)}) %collective-permute-start.97) | collective-permute-done | bytes 262176 | tf_op jit(solution)/shard_map/ppermute | solution.py:57
  154.6 12.0 %collective-permute-done.9 = bf16[256,768]{0,1:T(8,128)(2,1)S(1)} collective-permute-done((bf16[256,768]{0,1:T(8,128)(2,1)S(1)}, bf16[256,768]{0,1:T(8,128)(2,1)S(1)}, u32[]{:S(2)}, u32[]{:S(2)}) %collective-permute-start.9) | collective-permute-done | bytes 393248 | tf_op jit(solution)/shard_map/ppermute | solution.py:57
  168.9 6.2 collective-permute-done.10
  192.1 7.7 collective-permute-done.41
  201.4 12.3 %collective-permute-done.42 = bf16[256,704]{0,1:T(8,128)(2,1)S(1)} collective-permute-done((bf16[256,704]{0,1:T(8,128)(2,1)S(1)}, bf16[256,704]{0,1:T(8,128)(2,1)S(1)}, u32[]{:S(2)}, u32[]{:S(2)}) %collective-permute-start.42) | collective-permute-done | bytes 360480 | tf_op jit(solution)/shard_map/ppermute | solution.py:57
  214.2 4.1 collective-permute-start.24
  218.3 5.7 collective-permute-start.23
  227.8 10.2 collective-permute-done.23
  237.9 11.1 %fusion.122 = (f32[64]{0:T(128)S(1)}, f32[64,2048]{1,0:T(8,128)S(1)}) fusion(f32[64,2048]{1,0:T(8,128)S(1)} %bitcast.251, bf16[64,2048]{1,0:T(8,128)(2,1)S(1)} %collective-permute-done.24, bf16[64,2048]{1,0:T(8,128)(2,1)S(1)} %collective-permute-done.23, bf16[64,2048]{1,0:T(8,128)(2,1)S(1)} %collective-permute-done.22, f32[256,2048]{1,0:T(8,128)S(1)} %get-tuple-element.107), kind=kLoop, calls=%fused_computation.536 | loop fusion | flops 1048512 | bytes 2359552 | tf_op jit(solution)/shard_map/reduce_sum | solution.py:35
  255.8 5.6 collective-permute-done.25
  261.4 9.4 collective-permute-done.26
  277.0 5.8 fusion.158
  297.0 4.9 collective-permute-done.46
  303.4 14.0 %collective-permute-done.45 = bf16[64,2048]{1,0:T(8,128)(2,1)S(1)} collective-permute-done((bf16[64,2048]{1,0:T(8,128)(2,1)S(1)}, bf16[64,2048]{1,0:T(8,128)(2,1)S(1)}, u32[]{:S(2)}, u32[]{:S(2)}) %collective-permute-start.45) | collective-permute-done | bytes 262176 | tf_op jit(solution)/shard_map/ppermute | solution.py:57
  324.9 4.6 collective-permute-done.55
  333.6 7.5 collective-permute-done.48
  346.1 13.9 %collective-permute-done.57 = bf16[256,768]{0,1:T(8,128)(2,1)S(1)} collective-permute-done((bf16[256,768]{0,1:T(8,128)(2,1)S(1)}, bf16[256,768]{0,1:T(8,128)(2,1)S(1)}, u32[]{:S(2)}, u32[]{:S(2)}) %collective-permute-start.57) | collective-permute-done | bytes 393248 | tf_op jit(solution)/shard_map/ppermute | solution.py:57
  371.0 10.1 collective-permute-done.86
  384.2 4.7 collective-permute-done.76
  393.0 11.3 %collective-permute-done.77 = bf16[256,1408]{0,1:T(8,128)(2,1)S(1)} collective-permute-done((bf16[256,1408]{0,1:T(8,128)(2,1)S(1)}, bf16[256,1408]{0,1:T(8,128)(2,1)S(1)}, u32[]{:S(2)}, u32[]{:S(2)}) %collective-permute-start.77) | collective-permute-done | bytes 720928 | tf_op jit(solution)/shard_map/ppermute | solution.py:57
  407.4 8.0 collective-permute-done.67
  424.0 5.7 collective-permute-done.69
  429.8 10.2 collective-permute-done.70
  453.0 3.5 fusion.152
  465.8 5.9 collective-permute-done.193
  473.4 6.9 collective-permute-done.189
  483.8 18.0 %collective-permute-done.191 = bf16[256,704]{0,1:T(8,128)(2,1)S(1)} collective-permute-done((bf16[256,704]{0,1:T(8,128)(2,1)S(1)}, bf16[256,704]{0,1:T(8,128)(2,1)S(1)}, u32[]{:S(2)}, u32[]{:S(2)}) %collective-permute-start.191) | collective-permute-done | bytes 360480 | tf_op jit(solution)/shard_map/ppermute | solution.py:57
  515.8 11.7 %collective-permute-start.88 = (bf16[64,2048]{1,0:T(8,128)(2,1)S(1)}, bf16[64,2048]{1,0:T(8,128)(2,1)S(1)}, u32[]{:S(2)}, u32[]{:S(2)}) collective-permute-start(bf16[64,2048]{1,0:T(8,128)(2,1)S(1)} %get-tuple-element.219), channel_id=1, source_target_pairs={{0,1},{1,0},{2,3},{3,2},{4,5},{5,4},{6,7},{7,6},{8,9},{9,8},{10,11... | collective-permute-start | bytes 786440 | tf_op jit(solution)/shard_map/ppermute | solution.py:57
  528.9 14.5 %collective-permute-done.102 = bf16[64,2048]{1,0:T(8,128)(2,1)S(1)} collective-permute-done((bf16[64,2048]{1,0:T(8,128)(2,1)S(1)}, bf16[64,2048]{1,0:T(8,128)(2,1)S(1)}, u32[]{:S(2)}, u32[]{:S(2)}) %collective-permute-start.102) | collective-permute-done | bytes 262176 | tf_op jit(solution)/shard_map/ppermute | solution.py:57
  546.0 8.5 collective-permute-done.89
  574.1 3.5 collective-permute-done.177
  584.8 17.7 %collective-permute-done.105 = bf16[64,2048]{1,0:T(8,128)(2,1)S(1)} collective-permute-done((bf16[64,2048]{1,0:T(8,128)(2,1)}, bf16[64,2048]{1,0:T(8,128)(2,1)S(1)}, u32[]{:S(2)}, u32[]{:S(2)}) %collective-permute-start.105) | collective-permute-done | bytes 262176 | tf_op jit(solution)/shard_map/ppermute | solution.py:57
  605.1 13.0 %collective-permute-done.92 = bf16[64,2048]{1,0:T(8,128)(2,1)S(1)} collective-permute-done((bf16[64,2048]{1,0:T(8,128)(2,1)}, bf16[64,2048]{1,0:T(8,128)(2,1)S(1)}, u32[]{:S(2)}, u32[]{:S(2)}) %collective-permute-start.92) | collective-permute-done | bytes 262176 | tf_op jit(solution)/shard_map/ppermute | solution.py:57
  622.7 4.5 convert_select_fusion.1
  627.2 3.6 copy.93
  630.8 3.7 copy.92
  658.8 4.5 fusion.148
  686.0 3.8 collective-permute-done.111
  689.8 10.7 %collective-permute-done.110 = bf16[64,2048]{1,0:T(8,128)(2,1)S(1)} collective-permute-done((bf16[64,2048]{1,0:T(8,128)(2,1)S(1)}, bf16[64,2048]{1,0:T(8,128)(2,1)S(1)}, u32[]{:S(2)}, u32[]{:S(2)}) %collective-permute-start.110) | collective-permute-done | bytes 262176 | tf_op jit(solution)/shard_map/ppermute | solution.py:57
  714.1 10.2 collective-permute-done.113
  736.4 4.1 multiply_convert_fusion.3
  742.3 5.1 fusion.153
  753.1 5.7 fusion.34
  759.1 16.1 %collective-permute-done.186 = bf16[256,704]{0,1:T(8,128)(2,1)S(1)} collective-permute-done((bf16[256,704]{0,1:T(8,128)(2,1)S(1)}, bf16[256,704]{0,1:T(8,128)(2,1)S(1)}, u32[]{:S(2)}, u32[]{:S(2)}) %collective-permute-start.186) | collective-permute-done | bytes 360480 | tf_op jit(solution)/shard_map/ppermute | solution.py:57
  781.2 5.3 collective-permute-done.182
  789.0 7.1 collective-permute-done.184
  811.1 15.7 %collective-permute-done.118 = bf16[64,2048]{1,0:T(8,128)(2,1)} collective-permute-done((bf16[64,2048]{1,0:T(8,128)(2,1)}, bf16[64,2048]{1,0:T(8,128)(2,1)}, u32[]{:S(2)}, u32[]{:S(2)}) %collective-permute-start.118) | collective-permute-done | bytes 262176 | tf_op jit(solution)/shard_map/ppermute | solution.py:57
  835.6 9.5 collective-permute-done.173
  847.8 4.7 collective-permute-done.121
  855.7 3.9 convert_select_fusion.3
  861.8 3.6 copy.90
  865.4 6.4 maximum_bitcast_fusion
  871.8 5.2 pad_maximum_fusion
  888.8 3.9 fusion.165
  892.7 4.5 fusion.149
  915.3 7.6 collective-permute-done.154
  940.2 4.2 collective-permute-start.126
  948.9 16.0 %collective-permute-done.126 = bf16[64,2048]{1,0:T(8,128)(2,1)S(1)} collective-permute-done((bf16[64,2048]{1,0:T(8,128)(2,1)S(1)}, bf16[64,2048]{1,0:T(8,128)(2,1)S(1)}, u32[]{:S(2)}, u32[]{:S(2)}) %collective-permute-start.126) | collective-permute-done | bytes 262176 | tf_op jit(solution)/shard_map/ppermute | solution.py:57
  978.6 10.6 %collective-permute-done.133 = f32[4,2,2048]{2,1,0:T(2,128)S(1)} collective-permute-done((f32[4,2,2048]{2,1,0:T(2,128)S(1)}, f32[4,2,2048]{2,1,0:T(2,128)S(1)}, u32[]{:S(2)}, u32[]{:S(2)}) %collective-permute-start.133) | collective-permute-done | bytes 65568 | tf_op jit(solution)/shard_map/ppermute | solution.py:57
  1007.4 10.2 collective-permute-done.94
  1018.7 8.5 collective-permute-done.131
  (1036 shorter events, 502.4 us)
Async XLA Ops:
  2.4 54.6 %collective-permute-start = (bf16[64,2048]{1,0:T(8,128)(2,1)}, bf16[64,2048]{1,0:T(8,128)(2,1)}, u32[]{:S(2)}, u32[]{:S(2)}) collective-permute-start(bf16[64,2048]{1,0:T(8,128)(2,1)} %dynamic-slice_bitcast_fusion.1), channel_id=1, source_target_pairs={{0,8},{8,0},{1,9},{9,1},{2,10},{10,2},{3,11},{11,3},{4,12},{12,4},... | collective-permute-start | bytes 786440 | tf_op jit(solution)/shard_map/ppermute | solution.py:57
  8.6 95.6 %collective-permute-start.5 = (bf16[256,768]{0,1:T(8,128)(2,1)}, bf16[256,768]{0,1:T(8,128)(2,1)}, u32[]{:S(2)}, u32[]{:S(2)}) collective-permute-start(bf16[256,768]{0,1:T(8,128)(2,1)} %bitcast.5), channel_id=1, source_target_pairs={{0,4},{4,0},{1,5},{5,1},{2,6},{6,2},{3,7},{7,3},{8,12},{12,8},{9,1... | collective-permute-start | bytes 1179656 | tf_op jit(solution)/shard_map/ppermute | solution.py:57
  8.6 26.9 %collective-permute-start.12 = (s32[128]{0:T(128)S(1)}, s32[128]{0:T(128)S(1)}, u32[]{:S(2)}, u32[]{:S(2)}) collective-permute-start(s32[128]{0:T(128)S(1)} %fusion.94), channel_id=1, source_target_pairs={{0,8},{8,0},{1,9},{9,1},{2,10},{10,2},{3,11},{11,3},{4,12},{12,4},... | collective-permute-start | bytes 1544 | tf_op jit(solution)/shard_map/ppermute | solution.py:57
  9.6 41.3 %collective-permute-start.14 = (bf16[256,256]{0,1:T(8,128)(2,1)}, bf16[256,256]{0,1:T(8,128)(2,1)}, u32[]{:S(2)}, u32[]{:S(2)}) collective-permute-start(bf16[256,256]{0,1:T(8,128)(2,1)} %broadcast_select_fusion.43), channel_id=1, source_target_pairs={{0,4},{4,0},{1,5},{5,1},{2,6},{6,2},{3,7},{7,3},{8,12},{12,8},{9,1... | collective-permute-start | bytes 393224 | tf_op jit(solution)/shard_map/ppermute | solution.py:57
  19.7 128.1 %collective-permute-start.29 = (bf16[256,1408]{0,1:T(8,128)(2,1)}, bf16[256,1408]{0,1:T(8,128)(2,1)}, u32[]{:S(2)}, u32[]{:S(2)}) collective-permute-start(bf16[256,1408]{0,1:T(8,128)(2,1)} %bitcast.24), channel_id=1, source_target_pairs={{0,4},{4,0},{1,5},{5,1},{2,6},{6,2},{3,7},{7,3},{8,12},{12,8},{9,1... | collective-permute-start | bytes 2162696 | tf_op jit(solution)/shard_map/ppermute | solution.py:57
  48.6 40.3 %collective-permute-start.36 = (bf16[256,704]{0,1:T(8,128)(2,1)}, bf16[256,704]{0,1:T(8,128)(2,1)S(1)}, u32[]{:S(2)}, u32[]{:S(2)}) collective-permute-start(bf16[256,704]{0,1:T(8,128)(2,1)} %broadcast_select_fusion.33), channel_id=1, source_target_pairs={{0,4},{4,0},{1,5},{5,1},{2,6},{6,2},{3,7},{7,3},{8,12},{12,8},{9,1... | collective-permute-start | bytes 1081352 | tf_op jit(solution)/shard_map/ppermute | solution.py:57
  114.6 31.0 %collective-permute-start.97 = (bf16[64,2048]{1,0:T(8,128)(2,1)S(1)}, bf16[64,2048]{1,0:T(8,128)(2,1)S(1)}, u32[]{:S(2)}, u32[]{:S(2)}) collective-permute-start(bf16[64,2048]{1,0:T(8,128)(2,1)S(1)} %bitcast.279), channel_id=1, source_target_pairs={{0,2},{1,3},{2,0},{3,1},{4,6},{5,7},{6,4},{7,5},{8,10},{9,11},{10,... | collective-permute-start | bytes 786440 | tf_op jit(solution)/shard_map/ppermute | solution.py:57
  148.4 31.9 %collective-permute-start.4 = (bf16[256,2048]{1,0:T(8,128)(2,1)S(1)}, bf16[256,2048]{1,0:T(8,128)(2,1)S(1)}, u32[]{:S(2)}, u32[]{:S(2)}) collective-permute-start(bf16[256,2048]{1,0:T(8,128)(2,1)S(1)} %pad_maximum_fusion.5), channel_id=1, source_target_pairs={{0,4},{4,0},{1,5},{5,1},{2,6},{6,2},{3,7},{7,3},{8,12},{12,8},{9,1... | collective-permute-start | bytes 3145736 | tf_op jit(solution)/shard_map/ppermute | solution.py:57
  149.6 25.4 %collective-permute-start.10 = (bf16[256,768]{0,1:T(8,128)(2,1)S(1)}, bf16[256,768]{0,1:T(8,128)(2,1)S(1)}, u32[]{:S(2)}, u32[]{:S(2)}) collective-permute-start(bf16[256,768]{0,1:T(8,128)(2,1)S(1)} %collective-permute-done.6), channel_id=1, source_target_pairs={{0,16},{16,0},{1,17},{17,1},{2,18},{18,2},{3,19},{19,3},{4,20},{20... | collective-permute-start | bytes 1179656 | tf_op jit(solution)/shard_map/ppermute | solution.py:57
  153.3 35.6 %collective-permute-start.39 = (bf16[256,704]{0,1:T(8,128)(2,1)S(1)}, bf16[256,704]{0,1:T(8,128)(2,1)S(1)}, u32[]{:S(2)}, u32[]{:S(2)}) collective-permute-start(bf16[256,704]{0,1:T(8,128)(2,1)S(1)} %get-tuple-element.101), channel_id=1, source_target_pairs={{0,16},{16,0},{1,17},{17,1},{2,18},{18,2},{3,19},{19,3},{4,20},{20... | collective-permute-start | bytes 1081352 | tf_op jit(solution)/shard_map/ppermute | solution.py:57
  178.7 45.3 %collective-permute-start.30 = (bf16[256,1408]{0,1:T(8,128)(2,1)S(1)}, bf16[256,1408]{0,1:T(8,128)(2,1)S(1)}, u32[]{:S(2)}, u32[]{:S(2)}) collective-permute-start(bf16[256,1408]{0,1:T(8,128)(2,1)S(1)} %get-tuple-element.192), channel_id=1, source_target_pairs={{0,8},{8,0},{1,9},{9,1},{2,10},{10,2},{3,11},{11,3},{4,12},{12,4},... | collective-permute-start | bytes 2162696 | tf_op jit(solution)/shard_map/ppermute | solution.py:57
  180.3 44.3 %collective-permute-start.31 = (bf16[256,1408]{0,1:T(8,128)(2,1)S(1)}, bf16[256,1408]{0,1:T(8,128)(2,1)S(1)}, u32[]{:S(2)}, u32[]{:S(2)}) collective-permute-start(bf16[256,1408]{0,1:T(8,128)(2,1)S(1)} %get-tuple-element.191), channel_id=1, source_target_pairs={{0,8},{8,0},{1,9},{9,1},{2,10},{10,2},{3,11},{11,3},{4,12},{12,4},... | collective-permute-start | bytes 2162696 | tf_op jit(solution)/shard_map/ppermute | solution.py:57
  188.8 25.0 %collective-permute-start.21 = (bf16[256,2048]{1,0:T(8,128)(2,1)S(1)}, bf16[256,2048]{1,0:T(8,128)(2,1)S(1)}, u32[]{:S(2)}, u32[]{:S(2)}) collective-permute-start(bf16[256,2048]{1,0:T(8,128)(2,1)S(1)} %slice.1439), channel_id=1, source_target_pairs={{0,4},{4,0},{1,5},{5,1},{2,6},{6,2},{3,7},{7,3},{8,12},{12,8},{9,1... | collective-permute-start | bytes 3145736 | tf_op jit(solution)/shard_map/ppermute | solution.py:57
  199.8 25.1 %collective-permute-start.33 = (bf16[256,1408]{0,1:T(8,128)(2,1)S(1)}, bf16[256,1408]{0,1:T(8,128)(2,1)S(1)}, u32[]{:S(2)}, u32[]{:S(2)}) collective-permute-start(bf16[256,1408]{0,1:T(8,128)(2,1)S(1)} %get-tuple-element.191), channel_id=1, source_target_pairs={{0,16},{16,0},{1,17},{17,1},{2,18},{18,2},{3,19},{19,3},{4,20},{20... | collective-permute-start | bytes 2162696 | tf_op jit(solution)/shard_map/ppermute | solution.py:57
  224.6 28.2 %collective-permute-start.32 = (bf16[256,1408]{0,1:T(8,128)(2,1)S(1)}, bf16[256,1408]{0,1:T(8,128)(2,1)S(1)}, u32[]{:S(2)}, u32[]{:S(2)}) collective-permute-start(bf16[256,1408]{0,1:T(8,128)(2,1)S(1)} %get-tuple-element.192), channel_id=1, source_target_pairs={{0,16},{16,0},{1,17},{17,1},{2,18},{18,2},{3,19},{19,3},{4,20},{20... | collective-permute-start | bytes 2162696 | tf_op jit(solution)/shard_map/ppermute | solution.py:57
  224.9 47.6 %collective-permute-start.34 = (bf16[256,1408]{0,1:T(8,128)(2,1)S(1)}, bf16[256,1408]{0,1:T(8,128)(2,1)S(1)}, u32[]{:S(2)}, u32[]{:S(2)}) collective-permute-start(bf16[256,1408]{0,1:T(8,128)(2,1)S(1)} %collective-permute-done.30), channel_id=1, source_target_pairs={{0,16},{16,0},{1,17},{17,1},{2,18},{18,2},{3,19},{19,3},{4,20},{20... | collective-permute-start | bytes 2162696 | tf_op jit(solution)/shard_map/ppermute | solution.py:57
  226.8 46.6 %collective-permute-start.35 = (bf16[256,1408]{0,1:T(8,128)(2,1)S(1)}, bf16[256,1408]{0,1:T(8,128)(2,1)S(1)}, u32[]{:S(2)}, u32[]{:S(2)}) collective-permute-start(bf16[256,1408]{0,1:T(8,128)(2,1)S(1)} %collective-permute-done.33), channel_id=1, source_target_pairs={{0,8},{8,0},{1,9},{9,1},{2,10},{10,2},{3,11},{11,3},{4,12},{12,4},... | collective-permute-start | bytes 2162696 | tf_op jit(solution)/shard_map/ppermute | solution.py:57
  261.4 27.9 %collective-permute-start.73 = (bf16[256,1408]{0,1:T(8,128)(2,1)S(1)}, bf16[256,1408]{0,1:T(8,128)(2,1)S(1)}, u32[]{:S(2)}, u32[]{:S(2)}) collective-permute-start(bf16[256,1408]{0,1:T(8,128)(2,1)S(1)} %bitcast.310), channel_id=1, source_target_pairs={{0,4},{4,0},{1,5},{5,1},{2,6},{6,2},{3,7},{7,3},{8,12},{12,8},{9,1... | collective-permute-start | bytes 2162696 | tf_op jit(solution)/shard_map/ppermute | solution.py:57
  285.6 34.0 %collective-permute-start.52 = (bf16[256,768]{0,1:T(8,128)(2,1)S(1)}, bf16[256,768]{0,1:T(8,128)(2,1)S(1)}, u32[]{:S(2)}, u32[]{:S(2)}) collective-permute-start(bf16[256,768]{0,1:T(8,128)(2,1)S(1)} %get-tuple-element.232), channel_id=1, source_target_pairs={{0,8},{8,0},{1,9},{9,1},{2,10},{10,2},{3,11},{11,3},{4,12},{12,4},... | collective-permute-start | bytes 1179656 | tf_op jit(solution)/shard_map/ppermute | solution.py:57
  287.5 35.2 %collective-permute-start.53 = (bf16[256,768]{0,1:T(8,128)(2,1)S(1)}, bf16[256,768]{0,1:T(8,128)(2,1)S(1)}, u32[]{:S(2)}, u32[]{:S(2)}) collective-permute-start(bf16[256,768]{0,1:T(8,128)(2,1)S(1)} %get-tuple-element.231), channel_id=1, source_target_pairs={{0,8},{8,0},{1,9},{9,1},{2,10},{10,2},{3,11},{11,3},{4,12},{12,4},... | collective-permute-start | bytes 1179656 | tf_op jit(solution)/shard_map/ppermute | solution.py:57
  292.7 24.8 %collective-permute-start.45 = (bf16[64,2048]{1,0:T(8,128)(2,1)S(1)}, bf16[64,2048]{1,0:T(8,128)(2,1)S(1)}, u32[]{:S(2)}, u32[]{:S(2)}) collective-permute-start(bf16[64,2048]{1,0:T(8,128)(2,1)S(1)} %get-tuple-element.227), channel_id=1, source_target_pairs={{0,2},{1,3},{2,0},{3,1},{4,6},{5,7},{6,4},{7,5},{8,10},{9,11},{10,... | collective-permute-start | bytes 786440 | tf_op jit(solution)/shard_map/ppermute | solution.py:57
  294.7 24.2 %collective-permute-start.44 = (bf16[64,2048]{1,0:T(8,128)(2,1)S(1)}, bf16[64,2048]{1,0:T(8,128)(2,1)S(1)}, u32[]{:S(2)}, u32[]{:S(2)}) collective-permute-start(bf16[64,2048]{1,0:T(8,128)(2,1)S(1)} %get-tuple-element.225), channel_id=1, source_target_pairs={{0,1},{1,0},{2,3},{3,2},{4,5},{5,4},{6,7},{7,6},{8,9},{9,8},{10,11... | collective-permute-start | bytes 786440 | tf_op jit(solution)/shard_map/ppermute | solution.py:57
  332.5 49.4 %collective-permute-start.74 = (bf16[256,1408]{0,1:T(8,128)(2,1)S(1)}, bf16[256,1408]{0,1:T(8,128)(2,1)S(1)}, u32[]{:S(2)}, u32[]{:S(2)}) collective-permute-start(bf16[256,1408]{0,1:T(8,128)(2,1)S(1)} %get-tuple-element.188), channel_id=1, source_target_pairs={{0,8},{8,0},{1,9},{9,1},{2,10},{10,2},{3,11},{11,3},{4,12},{12,4},... | collective-permute-start | bytes 2162696 | tf_op jit(solution)/shard_map/ppermute | solution.py:57
  342.6 39.8 %collective-permute-start.75 = (bf16[256,1408]{0,1:T(8,128)(2,1)S(1)}, bf16[256,1408]{0,1:T(8,128)(2,1)S(1)}, u32[]{:S(2)}, u32[]{:S(2)}) collective-permute-start(bf16[256,1408]{0,1:T(8,128)(2,1)S(1)} %get-tuple-element.187), channel_id=1, source_target_pairs={{0,8},{8,0},{1,9},{9,1},{2,10},{10,2},{3,11},{11,3},{4,12},{12,4},... | collective-permute-start | bytes 2162696 | tf_op jit(solution)/shard_map/ppermute | solution.py:57
  344.6 25.3 %collective-permute-start.85 = (bf16[256,704]{0,1:T(8,128)(2,1)S(1)}, bf16[256,704]{0,1:T(8,128)(2,1)S(1)}, u32[]{:S(2)}, u32[]{:S(2)}) collective-permute-start(bf16[256,704]{0,1:T(8,128)(2,1)S(1)} %collective-permute-done.81), channel_id=1, source_target_pairs={{0,16},{16,0},{1,17},{17,1},{2,18},{18,2},{3,19},{19,3},{4,20},{20... | collective-permute-start | bytes 1081352 | tf_op jit(solution)/shard_map/ppermute | solution.py:57
  381.1 25.4 %collective-permute-start.99 = (bf16[256,2048]{1,0:T(8,128)(2,1)S(1)}, bf16[256,2048]{1,0:T(8,128)(2,1)S(1)}, u32[]{:S(2)}, u32[]{:S(2)}) collective-permute-start(bf16[256,2048]{1,0:T(8,128)(2,1)S(1)} %pad_maximum_fusion.10), channel_id=1, source_target_pairs={{0,4},{4,0},{1,5},{5,1},{2,6},{6,2},{3,7},{7,3},{8,12},{12,8},{9,1... | collective-permute-start | bytes 3145736 | tf_op jit(solution)/shard_map/ppermute | solution.py:57
  382.4 41.5 %collective-permute-start.78 = (bf16[256,1408]{0,1:T(8,128)(2,1)S(1)}, bf16[256,1408]{0,1:T(8,128)(2,1)S(1)}, u32[]{:S(2)}, u32[]{:S(2)}) collective-permute-start(bf16[256,1408]{0,1:T(8,128)(2,1)S(1)} %collective-permute-done.74), channel_id=1, source_target_pairs={{0,16},{16,0},{1,17},{17,1},{2,18},{18,2},{3,19},{19,3},{4,20},{20... | collective-permute-start | bytes 2162696 | tf_op jit(solution)/shard_map/ppermute | solution.py:57
  391.3 24.1 %collective-permute-start.67 = (bf16[64,2048]{1,0:T(8,128)(2,1)S(1)}, bf16[64,2048]{1,0:T(8,128)(2,1)S(1)}, u32[]{:S(2)}, u32[]{:S(2)}) collective-permute-start(bf16[64,2048]{1,0:T(8,128)(2,1)S(1)} %get-tuple-element.224), channel_id=1, source_target_pairs={{0,2},{1,3},{2,0},{3,1},{4,6},{5,7},{6,4},{7,5},{8,10},{9,11},{10,... | collective-permute-start | bytes 786440 | tf_op jit(solution)/shard_map/ppermute | solution.py:57
  406.5 33.7 %collective-permute-start.79 = (bf16[256,1408]{0,1:T(8,128)(2,1)S(1)}, bf16[256,1408]{0,1:T(8,128)(2,1)S(1)}, u32[]{:S(2)}, u32[]{:S(2)}) collective-permute-start(bf16[256,1408]{0,1:T(8,128)(2,1)S(1)} %collective-permute-done.77), channel_id=1, source_target_pairs={{0,8},{8,0},{1,9},{9,1},{2,10},{10,2},{3,11},{11,3},{4,12},{12,4},... | collective-permute-start | bytes 2162696 | tf_op jit(solution)/shard_map/ppermute | solution.py:57
  456.7 47.4 %collective-permute-start.100 = (bf16[256,2048]{1,0:T(8,128)(2,1)S(1)}, bf16[256,2048]{1,0:T(8,128)(2,1)S(1)}, u32[]{:S(2)}, u32[]{:S(2)}) collective-permute-start(bf16[256,2048]{1,0:T(8,128)(2,1)S(1)} %slice.1435), channel_id=1, source_target_pairs={{0,4},{4,0},{1,5},{5,1},{2,6},{6,2},{3,7},{7,3},{8,12},{12,8},{9,1... | collective-permute-start | bytes 3145736 | tf_op jit(solution)/shard_map/ppermute | solution.py:57
  471.7 30.9 %collective-permute-start.179 = (bf16[256,1408]{0,1:T(8,128)(2,1)S(1)}, bf16[256,1408]{0,1:T(8,128)(2,1)S(1)}, u32[]{:S(2)}, u32[]{:S(2)}) collective-permute-start(bf16[256,1408]{0,1:T(8,128)(2,1)S(1)} %get-tuple-element.145), channel_id=1, source_target_pairs={{0,8},{8,0},{1,9},{9,1},{2,10},{10,2},{3,11},{11,3},{4,12},{12,4},... | collective-permute-start | bytes 2162696 | tf_op jit(solution)/shard_map/ppermute | solution.py:57
  472.5 30.1 %collective-permute-start.176 = (bf16[256,1408]{0,1:T(8,128)(2,1)S(1)}, bf16[256,1408]{0,1:T(8,128)(2,1)S(1)}, u32[]{:S(2)}, u32[]{:S(2)}) collective-permute-start(bf16[256,1408]{0,1:T(8,128)(2,1)S(1)} %get-tuple-element.146), channel_id=1, source_target_pairs={{0,16},{16,0},{1,17},{17,1},{2,18},{18,2},{3,19},{19,3},{4,20},{20... | collective-permute-start | bytes 2162696 | tf_op jit(solution)/shard_map/ppermute | solution.py:57
  507.0 36.3 %collective-permute-start.102 = (bf16[64,2048]{1,0:T(8,128)(2,1)S(1)}, bf16[64,2048]{1,0:T(8,128)(2,1)S(1)}, u32[]{:S(2)}, u32[]{:S(2)}) collective-permute-start(bf16[64,2048]{1,0:T(8,128)(2,1)S(1)} %get-tuple-element.216), channel_id=1, source_target_pairs={{0,2},{1,3},{2,0},{3,1},{4,6},{5,7},{6,4},{7,5},{8,10},{9,11},{10,... | collective-permute-start | bytes 786440 | tf_op jit(solution)/shard_map/ppermute | solution.py:57
  510.1 33.9 %collective-permute-start.101 = (bf16[64,2048]{1,0:T(8,128)(2,1)S(1)}, bf16[64,2048]{1,0:T(8,128)(2,1)S(1)}, u32[]{:S(2)}, u32[]{:S(2)}) collective-permute-start(bf16[64,2048]{1,0:T(8,128)(2,1)S(1)} %get-tuple-element.214), channel_id=1, source_target_pairs={{0,1},{1,0},{2,3},{3,2},{4,5},{5,4},{6,7},{7,6},{8,9},{9,8},{10,11... | collective-permute-start | bytes 786440 | tf_op jit(solution)/shard_map/ppermute | solution.py:57
  510.6 34.4 %collective-permute-start.90 = (bf16[64,2048]{1,0:T(8,128)(2,1)S(1)}, bf16[64,2048]{1,0:T(8,128)(2,1)S(1)}, u32[]{:S(2)}, u32[]{:S(2)}) collective-permute-start(bf16[64,2048]{1,0:T(8,128)(2,1)S(1)} %get-tuple-element.220), channel_id=1, source_target_pairs={{0,3},{1,2},{2,1},{3,0},{4,7},{5,6},{6,5},{7,4},{8,11},{9,10},{10,... | collective-permute-start | bytes 786440 | tf_op jit(solution)/shard_map/ppermute | solution.py:57
  513.0 41.5 %collective-permute-start.89 = (bf16[64,2048]{1,0:T(8,128)(2,1)S(1)}, bf16[64,2048]{1,0:T(8,128)(2,1)S(1)}, u32[]{:S(2)}, u32[]{:S(2)}) collective-permute-start(bf16[64,2048]{1,0:T(8,128)(2,1)S(1)} %get-tuple-element.221), channel_id=1, source_target_pairs={{0,2},{1,3},{2,0},{3,1},{4,6},{5,7},{6,4},{7,5},{8,10},{9,11},{10,... | collective-permute-start | bytes 786440 | tf_op jit(solution)/shard_map/ppermute | solution.py:57
  515.8 39.4 %collective-permute-start.88 = (bf16[64,2048]{1,0:T(8,128)(2,1)S(1)}, bf16[64,2048]{1,0:T(8,128)(2,1)S(1)}, u32[]{:S(2)}, u32[]{:S(2)}) collective-permute-start(bf16[64,2048]{1,0:T(8,128)(2,1)S(1)} %get-tuple-element.219), channel_id=1, source_target_pairs={{0,1},{1,0},{2,3},{3,2},{4,5},{5,4},{6,7},{7,6},{8,9},{9,8},{10,11... | collective-permute-start | bytes 786440 | tf_op jit(solution)/shard_map/ppermute | solution.py:57
  543.4 26.3 %collective-permute-start.175 = (bf16[256,1408]{0,1:T(8,128)(2,1)}, bf16[256,1408]{0,1:T(8,128)(2,1)S(1)}, u32[]{:S(2)}, u32[]{:S(2)}) collective-permute-start(bf16[256,1408]{0,1:T(8,128)(2,1)} %get-tuple-element.147), channel_id=1, source_target_pairs={{0,16},{16,0},{1,17},{17,1},{2,18},{18,2},{3,19},{19,3},{4,20},{20... | collective-permute-start | bytes 2162696 | tf_op jit(solution)/shard_map/ppermute | solution.py:57
  544.0 28.5 %collective-permute-start.178 = (bf16[256,1408]{0,1:T(8,128)(2,1)}, bf16[256,1408]{0,1:T(8,128)(2,1)}, u32[]{:S(2)}, u32[]{:S(2)}) collective-permute-start(bf16[256,1408]{0,1:T(8,128)(2,1)} %get-tuple-element.144), channel_id=1, source_target_pairs={{0,8},{8,0},{1,9},{9,1},{2,10},{10,2},{3,11},{11,3},{4,12},{12,4},... | collective-permute-start | bytes 2162696 | tf_op jit(solution)/shard_map/ppermute | solution.py:57
  545.0 32.5 %collective-permute-start.177 = (bf16[256,1408]{0,1:T(8,128)(2,1)}, bf16[256,1408]{0,1:T(8,128)(2,1)}, u32[]{:S(2)}, u32[]{:S(2)}) collective-permute-start(bf16[256,1408]{0,1:T(8,128)(2,1)} %get-tuple-element.123), channel_id=1, source_target_pairs={{0,8},{8,0},{1,9},{9,1},{2,10},{10,2},{3,11},{11,3},{4,12},{12,4},... | collective-permute-start | bytes 2162696 | tf_op jit(solution)/shard_map/ppermute | solution.py:57
  554.5 25.3 %collective-permute-start.180 = (bf16[256,1408]{0,1:T(8,128)(2,1)}, bf16[256,1408]{0,1:T(8,128)(2,1)}, u32[]{:S(2)}, u32[]{:S(2)}) collective-permute-start(bf16[256,1408]{0,1:T(8,128)(2,1)} %get-tuple-element.122), channel_id=1, source_target_pairs={{0,16},{16,0},{1,17},{17,1},{2,18},{18,2},{3,19},{19,3},{4,20},{20... | collective-permute-start | bytes 2162696 | tf_op jit(solution)/shard_map/ppermute | solution.py:57
  569.7 32.8 %collective-permute-start.105 = (bf16[64,2048]{1,0:T(8,128)(2,1)}, bf16[64,2048]{1,0:T(8,128)(2,1)S(1)}, u32[]{:S(2)}, u32[]{:S(2)}) collective-permute-start(bf16[64,2048]{1,0:T(8,128)(2,1)} %get-tuple-element.71), channel_id=1, source_target_pairs={{0,2},{1,3},{2,0},{3,1},{4,6},{5,7},{6,4},{7,5},{8,10},{9,11},{10,... | collective-permute-start | bytes 786440 | tf_op jit(solution)/shard_map/ppermute | solution.py:57
  572.5 30.0 %collective-permute-start.106 = (bf16[64,2048]{1,0:T(8,128)(2,1)}, bf16[64,2048]{1,0:T(8,128)(2,1)S(1)}, u32[]{:S(2)}, u32[]{:S(2)}) collective-permute-start(bf16[64,2048]{1,0:T(8,128)(2,1)} %get-tuple-element.71), channel_id=1, source_target_pairs={{0,3},{1,2},{2,1},{3,0},{4,7},{5,6},{6,5},{7,4},{8,11},{9,10},{10,... | collective-permute-start | bytes 786440 | tf_op jit(solution)/shard_map/ppermute | solution.py:57
  577.5 27.6 %collective-permute-start.93 = (bf16[64,2048]{1,0:T(8,128)(2,1)}, bf16[64,2048]{1,0:T(8,128)(2,1)S(1)}, u32[]{:S(2)}, u32[]{:S(2)}) collective-permute-start(bf16[64,2048]{1,0:T(8,128)(2,1)} %bitcast.316), channel_id=1, source_target_pairs={{0,3},{1,2},{2,1},{3,0},{4,7},{5,6},{6,5},{7,4},{8,11},{9,10},{10,... | collective-permute-start | bytes 786440 | tf_op jit(solution)/shard_map/ppermute | solution.py:57
  579.8 38.3 %collective-permute-start.92 = (bf16[64,2048]{1,0:T(8,128)(2,1)}, bf16[64,2048]{1,0:T(8,128)(2,1)S(1)}, u32[]{:S(2)}, u32[]{:S(2)}) collective-permute-start(bf16[64,2048]{1,0:T(8,128)(2,1)} %bitcast.317), channel_id=1, source_target_pairs={{0,2},{1,3},{2,0},{3,1},{4,6},{5,7},{6,4},{7,5},{8,10},{9,11},{10,... | collective-permute-start | bytes 786440 | tf_op jit(solution)/shard_map/ppermute | solution.py:57
  579.8 38.3 %collective-permute-start.91 = (bf16[64,2048]{1,0:T(8,128)(2,1)}, bf16[64,2048]{1,0:T(8,128)(2,1)S(1)}, u32[]{:S(2)}, u32[]{:S(2)}) collective-permute-start(bf16[64,2048]{1,0:T(8,128)(2,1)} %bitcast.318), channel_id=1, source_target_pairs={{0,1},{1,0},{2,3},{3,2},{4,5},{5,4},{6,7},{7,6},{8,9},{9,8},{10,11... | collective-permute-start | bytes 786440 | tf_op jit(solution)/shard_map/ppermute | solution.py:57
  604.6 29.9 %collective-permute-start.107 = (bf16[256,2048]{1,0:T(8,128)(2,1)}, bf16[256,2048]{1,0:T(8,128)(2,1)}, u32[]{:S(2)}, u32[]{:S(2)}) collective-permute-start(bf16[256,2048]{1,0:T(8,128)(2,1)} %pad_maximum_fusion.11), channel_id=1, source_target_pairs={{0,4},{4,0},{1,5},{5,1},{2,6},{6,2},{3,7},{7,3},{8,12},{12,8},{9,1... | collective-permute-start | bytes 3145736 | tf_op jit(solution)/shard_map/ppermute | solution.py:57
  671.9 32.2 %collective-permute-start.144 = (bf16[256,768]{0,1:T(8,128)(2,1)S(1)}, bf16[256,768]{0,1:T(8,128)(2,1)S(1)}, u32[]{:S(2)}, u32[]{:S(2)}) collective-permute-start(bf16[256,768]{0,1:T(8,128)(2,1)S(1)} %get-tuple-element.159), channel_id=1, source_target_pairs={{0,16},{16,0},{1,17},{17,1},{2,18},{18,2},{3,19},{19,3},{4,20},{20... | collective-permute-start | bytes 1179656 | tf_op jit(solution)/shard_map/ppermute | solution.py:57
  674.3 29.9 %collective-permute-start.147 = (bf16[256,768]{0,1:T(8,128)(2,1)}, bf16[256,768]{0,1:T(8,128)(2,1)S(1)}, u32[]{:S(2)}, u32[]{:S(2)}) collective-permute-start(bf16[256,768]{0,1:T(8,128)(2,1)} %get-tuple-element.156), channel_id=1, source_target_pairs={{0,8},{8,0},{1,9},{9,1},{2,10},{10,2},{3,11},{11,3},{4,12},{12,4},... | collective-permute-start | bytes 1179656 | tf_op jit(solution)/shard_map/ppermute | solution.py:57
  689.8 35.5 %collective-permute-start.167 = (bf16[256,256]{0,1:T(8,128)(2,1)S(1)}, bf16[256,256]{0,1:T(8,128)(2,1)S(1)}, u32[]{:S(2)}, u32[]{:S(2)}) collective-permute-start(bf16[256,256]{0,1:T(8,128)(2,1)S(1)} %select_convert_fusion.6), channel_id=1, source_target_pairs={{0,4},{4,0},{1,5},{5,1},{2,6},{6,2},{3,7},{7,3},{8,12},{12,8},{9,1... | collective-permute-start | bytes 393224 | tf_op jit(solution)/shard_map/ppermute | solution.py:57
  748.9 29.0 %collective-permute-start.172 = (bf16[256,1408]{0,1:T(8,128)(2,1)S(1)}, bf16[256,1408]{0,1:T(8,128)(2,1)S(1)}, u32[]{:S(2)}, u32[]{:S(2)}) collective-permute-start(bf16[256,1408]{0,1:T(8,128)(2,1)S(1)} %get-tuple-element.141), channel_id=1, source_target_pairs={{0,8},{8,0},{1,9},{9,1},{2,10},{10,2},{3,11},{11,3},{4,12},{12,4},... | collective-permute-start | bytes 2162696 | tf_op jit(solution)/shard_map/ppermute | solution.py:57
  749.5 29.7 %collective-permute-start.169 = (bf16[256,1408]{0,1:T(8,128)(2,1)S(1)}, bf16[256,1408]{0,1:T(8,128)(2,1)S(1)}, u32[]{:S(2)}, u32[]{:S(2)}) collective-permute-start(bf16[256,1408]{0,1:T(8,128)(2,1)S(1)} %get-tuple-element.142), channel_id=1, source_target_pairs={{0,16},{16,0},{1,17},{17,1},{2,18},{18,2},{3,19},{19,3},{4,20},{20... | collective-permute-start | bytes 2162696 | tf_op jit(solution)/shard_map/ppermute | solution.py:57
  751.5 23.7 %collective-permute-start.186 = (bf16[256,704]{0,1:T(8,128)(2,1)S(1)}, bf16[256,704]{0,1:T(8,128)(2,1)S(1)}, u32[]{:S(2)}, u32[]{:S(2)}) collective-permute-start(bf16[256,704]{0,1:T(8,128)(2,1)S(1)} %get-tuple-element.161), channel_id=1, source_target_pairs={{0,8},{8,0},{1,9},{9,1},{2,10},{10,2},{3,11},{11,3},{4,12},{12,4},... | collective-permute-start | bytes 1081352 | tf_op jit(solution)/shard_map/ppermute | solution.py:57
  752.9 24.1 %collective-permute-start.183 = (bf16[256,704]{0,1:T(8,128)(2,1)S(1)}, bf16[256,704]{0,1:T(8,128)(2,1)S(1)}, u32[]{:S(2)}, u32[]{:S(2)}) collective-permute-start(bf16[256,704]{0,1:T(8,128)(2,1)S(1)} %get-tuple-element.162), channel_id=1, source_target_pairs={{0,16},{16,0},{1,17},{17,1},{2,18},{18,2},{3,19},{19,3},{4,20},{20... | collective-permute-start | bytes 1081352 | tf_op jit(solution)/shard_map/ppermute | solution.py:57
  759.0 37.4 %collective-permute-start.116 = (bf16[256,2048]{1,0:T(8,128)(2,1)S(1)}, bf16[256,2048]{1,0:T(8,128)(2,1)S(1)}, u32[]{:S(2)}, u32[]{:S(2)}) collective-permute-start(bf16[256,2048]{1,0:T(8,128)(2,1)S(1)} %slice.1433), channel_id=1, source_target_pairs={{0,4},{4,0},{1,5},{5,1},{2,6},{6,2},{3,7},{7,3},{8,12},{12,8},{9,1... | collective-permute-start | bytes 3145736 | tf_op jit(solution)/shard_map/ppermute | solution.py:57
  786.5 44.7 %collective-permute-start.168 = (bf16[256,1408]{0,1:T(8,128)(2,1)}, bf16[256,1408]{0,1:T(8,128)(2,1)}, u32[]{:S(2)}, u32[]{:S(2)}) collective-permute-start(bf16[256,1408]{0,1:T(8,128)(2,1)} %get-tuple-element.143), channel_id=1, source_target_pairs={{0,16},{16,0},{1,17},{17,1},{2,18},{18,2},{3,19},{19,3},{4,20},{20... | collective-permute-start | bytes 2162696 | tf_op jit(solution)/shard_map/ppermute | solution.py:57
  788.3 45.6 %collective-permute-start.171 = (bf16[256,1408]{0,1:T(8,128)(2,1)}, bf16[256,1408]{0,1:T(8,128)(2,1)}, u32[]{:S(2)}, u32[]{:S(2)}) collective-permute-start(bf16[256,1408]{0,1:T(8,128)(2,1)} %get-tuple-element.140), channel_id=1, source_target_pairs={{0,8},{8,0},{1,9},{9,1},{2,10},{10,2},{3,11},{11,3},{4,12},{12,4},... | collective-permute-start | bytes 2162696 | tf_op jit(solution)/shard_map/ppermute | solution.py:57
  801.0 25.7 %collective-permute-start.118 = (bf16[64,2048]{1,0:T(8,128)(2,1)}, bf16[64,2048]{1,0:T(8,128)(2,1)}, u32[]{:S(2)}, u32[]{:S(2)}) collective-permute-start(bf16[64,2048]{1,0:T(8,128)(2,1)} %get-tuple-element.210), channel_id=1, source_target_pairs={{0,2},{1,3},{2,0},{3,1},{4,6},{5,7},{6,4},{7,5},{8,10},{9,11},{10,... | collective-permute-start | bytes 786440 | tf_op jit(solution)/shard_map/ppermute | solution.py:57
  810.4 25.2 %collective-permute-start.170 = (bf16[256,1408]{0,1:T(8,128)(2,1)}, bf16[256,1408]{0,1:T(8,128)(2,1)S(1)}, u32[]{:S(2)}, u32[]{:S(2)}) collective-permute-start(bf16[256,1408]{0,1:T(8,128)(2,1)} %get-tuple-element.121), channel_id=1, source_target_pairs={{0,8},{8,0},{1,9},{9,1},{2,10},{10,2},{3,11},{11,3},{4,12},{12,4},... | collective-permute-start | bytes 2162696 | tf_op jit(solution)/shard_map/ppermute | solution.py:57
  853.6 23.5 %collective-permute-start.123 = (bf16[256,2048]{1,0:T(8,128)(2,1)}, bf16[256,2048]{1,0:T(8,128)(2,1)}, u32[]{:S(2)}, u32[]{:S(2)}) collective-permute-start(bf16[256,2048]{1,0:T(8,128)(2,1)} %pad_maximum_fusion.13), channel_id=1, source_target_pairs={{0,4},{4,0},{1,5},{5,1},{2,6},{6,2},{3,7},{7,3},{8,12},{12,8},{9,1... | collective-permute-start | bytes 3145736 | tf_op jit(solution)/shard_map/ppermute | solution.py:57
  940.2 24.7 %collective-permute-start.126 = (bf16[64,2048]{1,0:T(8,128)(2,1)S(1)}, bf16[64,2048]{1,0:T(8,128)(2,1)S(1)}, u32[]{:S(2)}, u32[]{:S(2)}) collective-permute-start(bf16[64,2048]{1,0:T(8,128)(2,1)S(1)} %get-tuple-element.207), channel_id=1, source_target_pairs={{0,2},{1,3},{2,0},{3,1},{4,6},{5,7},{6,4},{7,5},{8,10},{9,11},{10,... | collective-permute-start | bytes 786440 | tf_op jit(solution)/shard_map/ppermute | solution.py:57
  947.2 42.2 %collective-permute-start.143 = (bf16[256,768]{0,1:T(8,128)(2,1)S(1)}, bf16[256,768]{0,1:T(8,128)(2,1)}, u32[]{:S(2)}, u32[]{:S(2)}) collective-permute-start(bf16[256,768]{0,1:T(8,128)(2,1)S(1)} %select_convert_fusion.3), channel_id=1, source_target_pairs={{0,4},{4,0},{1,5},{5,1},{2,6},{6,2},{3,7},{7,3},{8,12},{12,8},{9,1... | collective-permute-start | bytes 1179656 | tf_op jit(solution)/shard_map/ppermute | solution.py:57
  974.2 26.0 %collective-permute-start.130 = (bf16[64,2048]{1,0:T(8,128)(2,1)}, bf16[64,2048]{1,0:T(8,128)(2,1)}, u32[]{:S(2)}, u32[]{:S(2)}) collective-permute-start(bf16[64,2048]{1,0:T(8,128)(2,1)} %bitcast.119), channel_id=1, source_target_pairs={{0,3},{1,2},{2,1},{3,0},{4,7},{5,6},{6,5},{7,4},{8,11},{9,10},{10,... | collective-permute-start | bytes 786440 | tf_op jit(solution)/shard_map/ppermute | solution.py:57
  976.0 24.8 %collective-permute-start.129 = (bf16[64,2048]{1,0:T(8,128)(2,1)}, bf16[64,2048]{1,0:T(8,128)(2,1)}, u32[]{:S(2)}, u32[]{:S(2)}) collective-permute-start(bf16[64,2048]{1,0:T(8,128)(2,1)} %bitcast.119), channel_id=1, source_target_pairs={{0,2},{1,3},{2,0},{3,1},{4,6},{5,7},{6,4},{7,5},{8,10},{9,11},{10,... | collective-permute-start | bytes 786440 | tf_op jit(solution)/shard_map/ppermute | solution.py:57
  (278 other events, 4300.4 us)

commit v2 on v1

v2 whole, which is shorter than its diff:
```python
import functools
import math

import jax
import jax.numpy as jnp
from jax import lax
from jax.experimental import pallas as pl
from jax.experimental.pallas import tpu as pltpu
from jax.sharding import Mesh
from jax.sharding import PartitionSpec as P

HEAD = 64
ROT = 16
LAYERS = 2
NORM_EPS = 1e-05
MASK_FILL = -1e30
LOW = jnp.bfloat16
F32 = jnp.float32
VMEM_LIMIT = 44 * 1024 * 1024
ANY = pl.BlockSpec(memory_space=pl.ANY)
VMEM = pl.BlockSpec(memory_space=pltpu.VMEM)


def dot(a, b, dims):
    return lax.dot_general(a, b, (dims, ((), ())), preferred_element_type=F32)


def nn(a, b):
    return dot(a, b, ((1,), (0,)))


def nt(a, b):
    return dot(a, b, ((1,), (1,)))


def tn(a, b):
    return dot(a, b, ((0,), (0,)))


def shape(dims, kind):
    return jax.ShapeDtypeStruct(dims, kind)


def call(body, n_any, args, outs, scratch, flops):
    moved = sum(a.size * a.dtype.itemsize for a in args)
    moved += sum(math.prod(o.shape) * jnp.dtype(o.dtype).itemsize for o in outs)
    return pl.pallas_call(
        body,
        out_shape=tuple(outs),
        in_specs=[ANY] * n_any + [VMEM] * (len(args) - n_any),
        out_specs=tuple([VMEM] * len(outs)),
        scratch_shapes=scratch,
        compiler_params=pltpu.CompilerParams(vmem_limit_bytes=VMEM_LIMIT),
        cost_estimate=pl.CostEstimate(flops=flops, bytes_accessed=moved, transcendentals=0),
    )(*args)


def into_rows(pieces, whole, sems, first):
    copies, row = [], 0
    for i, piece in enumerate(pieces):
        rows = piece.shape[0]
        copies.append(
            pltpu.make_async_copy(piece, whole.at[pl.ds(row, rows)], sems.at[first + i])
        )
        row += rows
    return copies


def start_all(copies):
    for c in copies:
        c.start()


def wait_all(copies):
    for c in copies:
        c.wait()


def rolled(value, cos_t, sa, sb, sign):
    width = value.shape[1]
    ahead = pltpu.roll(value, width - ROT // 2, 1)
    behind = pltpu.roll(value, ROT // 2, 1)
    return value * cos_t + sign * (ahead * sa + behind * sb)


def allowed_of(pc, sc, pr, sr):
    return (sc == sr) & (pr <= pc)


def put_halves(tile, cols, own_ref, send_ref):
    half = own_ref.shape[0]
    own_ref[:, cols] = tile[:half]
    send_ref[:, cols] = tile[half:].astype(LOW)


def softmax_of(q_h, k, allowed, scale):
    s = jnp.where(allowed, nt(q_h, k) * scale, MASK_FILL)
    top = jnp.max(s, axis=-1, keepdims=True)
    e = jnp.exp(s - top)
    return e / jnp.sum(e, axis=-1, keepdims=True)


def attn_forward(n_h, n_w, heads, *refs):
    h_parts, w_parts, refs = refs[:n_h], refs[n_h : n_h + n_w], refs[n_h + n_w :]
    bias, pc, sc, pr, sr, cos_t, sa, sb = refs[:8]
    q_o, k_o, v_o, o_o, own_o, send_o, h_s, w_s, acc, sems = refs[8:]
    width = heads * HEAD
    copies = into_rows(h_parts, h_s, sems, 0)
    w_copies = into_rows(w_parts, w_s, sems, n_h)
    start_all(copies + w_copies)
    wait_all(copies)
    block = w_s.shape[0] // (n_w // 2)
    for r in range(n_w // 2):
        wait_all(w_copies[2 * r : 2 * r + 2])
        rows = slice(r * block, (r + 1) * block)
        for c in range(3):
            cols = slice(c * width, (c + 1) * width)
            part = nn(h_s[:, rows], w_s[rows, cols])
            acc[:, cols] = part + (bias[:, cols] if r == 0 else acc[:, cols])
    q_o[...] = rolled(acc[:, :width], cos_t[...], sa[...], sb[...], 1.0).astype(LOW)
    k_o[...] = rolled(acc[:, width : 2 * width], cos_t[...], sa[...], sb[...], 1.0).astype(LOW)
    v_o[...] = acc[:, 2 * width :].astype(LOW)
    lane = lax.broadcasted_iota(jnp.int32, (1, width), 1) // HEAD
    allowed = allowed_of(pc[...], sc[...], pr[...], sr[...])
    k, v, q = k_o[...], v_o[...], q_o[...]
    zero = jnp.zeros((), LOW)
    o = None
    for h in range(heads):
        mine = lane == h
        w = softmax_of(jnp.where(mine, q, zero), k, allowed, 1.0 / math.sqrt(HEAD))
        part = nn(w.astype(LOW), jnp.where(mine, v, zero))
        o = part if o is None else o + part
    o_o[...] = o.astype(LOW)
    o = o_o[...]
    for r in range(n_w // 2):
        rows = slice(r * block, (r + 1) * block)
        put_halves(nt(o, w_s[rows, 3 * width :]), rows, own_o, send_o)


def attn_backward(n_h, n_w, heads, *refs):
    d_parts, w_parts, refs = refs[:n_h], refs[n_h : n_h + n_w], refs[n_h + n_w :]
    q_i, k_i, v_i, pc, sc, pr, sr, cos_t, sa, sb = refs[:10]
    dp_o, bias_o, own_o, send_o, d_s, w_s, acc, sems = refs[10:]
    width = heads * HEAD
    copies = into_rows(d_parts, d_s, sems, 0)
    w_copies = into_rows(w_parts, w_s, sems, n_h)
    start_all(copies + w_copies)
    wait_all(copies)
    block = w_s.shape[0] // (n_w // 2)
    for r in range(n_w // 2):
        wait_all(w_copies[2 * r : 2 * r + 2])
        rows = slice(r * block, (r + 1) * block)
        part = nn(d_s[:, rows], w_s[rows, 3 * width :])
        acc[...] = part if r == 0 else acc[...] + part
    do = acc[...].astype(LOW)
    q, k, v = q_i[...], k_i[...], v_i[...]
    lane = lax.broadcasted_iota(jnp.int32, (1, width), 1) // HEAD
    allowed = allowed_of(pc[...], sc[...], pr[...], sr[...])
    zero = jnp.zeros((), LOW)
    scale = 1.0 / math.sqrt(HEAD)
    dq = dk = dv = None
    for h in range(heads):
        mine = lane == h
        q_h = jnp.where(mine, q, zero)
        do_h = jnp.where(mine, do, zero)
        w = softmax_of(q_h, k, allowed, scale)
        dw = nt(do_h, v)
        ds = (w * (dw - jnp.sum(w * dw, axis=-1, keepdims=True))).astype(LOW)
        dv_h = tn(w.astype(LOW), do_h)
        dq_h = nn(ds, jnp.where(mine, k, zero))
        dk_h = tn(ds, q_h)
        dq, dk, dv = (
            (dq_h, dk_h, dv_h) if h == 0 else (dq + dq_h, dk + dk_h, dv + dv_h)
        )
    dp_o[:, :width] = rolled(dq * scale, cos_t[...], sa[...], sb[...], -1.0).astype(LOW)
    dp_o[:, width : 2 * width] = rolled(
        dk * scale, cos_t[...], sa[...], sb[...], -1.0
    ).astype(LOW)
    dp_o[:, 2 * width :] = dv.astype(LOW)
    bias_o[...] = jnp.sum(dp_o[...].astype(F32), axis=0, keepdims=True)
    for r in range(n_w // 2):
        rows = slice(r * block, (r + 1) * block)
        put_halves(nt(dp_o[...], w_s[rows, : 3 * width]), rows, own_o, send_o)


def to_front(value, units):
    return value[:, units : 2 * units]


def mlp_forward(n_h, n_w, *refs):
    h_parts, w_parts, refs = refs[:n_h], refs[n_h : n_h + n_w], refs[n_h + n_w :]
    gu_o, z_o, own_o, send_o, h_s, w_s, sems = refs
    units = z_o.shape[1]
    copies = into_rows(h_parts, h_s, sems, 0)
    w_copies = into_rows(w_parts, w_s, sems, n_h)
    start_all(copies + w_copies)
    wait_all(copies)
    block = w_s.shape[0] // (n_w // 2)
    for r in range(n_w // 2):
        wait_all(w_copies[2 * r : 2 * r + 2])
        rows = slice(r * block, (r + 1) * block)
        part = nn(h_s[:, rows], w_s[rows, : 2 * units])
        gu_o[...] = part if r == 0 else gu_o[...] + part
    g = gu_o[:, :units]
    u = to_front(gu_o, units)
    z_o[...] = (g * u / (1.0 + jnp.exp(-g))).astype(LOW)
    z = z_o[...]
    for r in range(n_w // 2):
        rows = slice(r * block, (r + 1) * block)
        put_halves(nt(z, w_s[rows, 2 * units :]), rows, own_o, send_o)


def mlp_backward(n_h, n_w, *refs):
    d_parts, w_parts, refs = refs[:n_h], refs[n_h : n_h + n_w], refs[n_h + n_w :]
    gu_i, dp_o, own_o, send_o, d_s, w_s, acc, sems = refs
    units = acc.shape[1]
    copies = into_rows(d_parts, d_s, sems, 0)
    w_copies = into_rows(w_parts, w_s, sems, n_h)
    start_all(copies + w_copies)
    wait_all(copies)
    block = w_s.shape[0] // (n_w // 2)
    for r in range(n_w // 2):
        wait_all(w_copies[2 * r : 2 * r + 2])
        rows = slice(r * block, (r + 1) * block)
        part = nn(d_s[:, rows], w_s[rows, 2 * units :])
        acc[...] = part if r == 0 else acc[...] + part
    g = gu_i[:, :units]
    u = to_front(gu_i, units)
    sig = 1.0 / (1.0 + jnp.exp(-g))
    dz = acc[...]
    dp_o[:, :units] = (dz * u * sig * (1.0 + g * (1.0 - sig))).astype(LOW)
    dp_o[:, units:] = (dz * g * sig).astype(LOW)
    dp = dp_o[...]
    for r in range(n_w // 2):
        rows = slice(r * block, (r + 1) * block)
        put_halves(nt(dp, w_s[rows, : 2 * units]), rows, own_o, send_o)


def weight_grads(n_h, n_w, *refs):
    a_parts, b_parts, refs = refs[:n_h], refs[n_h : 2 * n_h], refs[2 * n_h :]
    da, db = refs[:2]
    outs, (a_s, b_s, sems) = refs[2 : 2 + n_w], refs[2 + n_w :]
    copies = into_rows(a_parts, a_s, sems, 0) + into_rows(b_parts, b_s, sems, n_h)
    start_all(copies)
    wait_all(copies)
    block = a_s.shape[1] // (n_w // 2)
    half = block // 2
    split = da.shape[1]
    for r in range(n_w // 2):
        cols = slice(r * block, (r + 1) * block)
        first = tn(a_s[:, cols], da[...]).astype(LOW)
        second = tn(b_s[:, cols], db[...]).astype(LOW)
        for i in range(2):
            rows = slice(i * half, (i + 1) * half)
            outs[2 * r + i][:, :split] = first[rows]
            outs[2 * r + i][:, split:] = second[rows]


def middle(own_i, moved_i, own_o, *sends):
    rows = own_o.shape[0]
    own_o[...] = own_i[:rows] + moved_i[:rows].astype(F32)
    for r, send in enumerate(sends):
        at = slice((r + 1) * rows, (r + 2) * rows)
        send[...] = (own_i[at] + moved_i[at].astype(F32)).astype(LOW)


def norm_of(value):
    center = value - jnp.mean(value, axis=-1, keepdims=True)
    inverse = lax.rsqrt(jnp.mean(center * center, axis=-1, keepdims=True) + NORM_EPS)
    return center * inverse, inverse


def norm_forward(x_i, gain, offset, *refs):
    terms, (x_o, h_o) = refs[:-2], refs[-2:]
    x = x_i[...]
    for t in terms:
        x = x + t[...].astype(F32)
    x_o[...] = x
    h_o[...] = (norm_of(x)[0] * gain[...] + offset[...]).astype(LOW)


def norm_backward(dx_i, y_i, gain, *refs):
    terms, (dy_o, low_o, small_o) = refs[:-3], refs[-3:]
    dh = terms[0][...]
    for t in terms[1:]:
        dh = dh + t[...].astype(F32)
    n, inverse = norm_of(y_i[...])
    small_o[0:1] = jnp.sum(dh * n, axis=0, keepdims=True)
    small_o[1:2] = jnp.sum(dh, axis=0, keepdims=True)
    scaled = dh * gain[...]
    dy = dx_i[...] + inverse * (
        scaled
        - jnp.mean(scaled, axis=-1, keepdims=True)
        - n * jnp.mean(scaled * n, axis=-1, keepdims=True)
    )
    dy_o[...] = dy
    low_o[...] = dy.astype(LOW)


def log2(n):
    return n.bit_length() - 1


def make_program(n_dp, n_chi, n_clo, n_mp):
    group_bits = [("chi", 1 << k) for k in range(log2(n_chi))]
    group_bits += [("dp", 1 << k) for k in range(log2(n_dp))]
    n_groups = n_dp * n_chi
    n_pieces = 2 * n_groups
    sizes = {"dp": n_dp, "chi": n_chi, "clo": n_clo, "mp": n_mp}
    up_order = list(range(len(group_bits)))
    down_order = up_order[::-1]

    def swap(value, axis, bit):
        return lax.ppermute(value, axis, [(i, i ^ bit) for i in range(sizes[axis])])

    def relative(value):
        block = value.shape[-1] // n_groups
        me = lax.axis_index("dp") * n_chi + lax.axis_index("chi")
        parts = [
            lax.dynamic_slice_in_dim(value, (me ^ r) * block, block, value.ndim - 1)
            for r in range(n_groups)
        ]
        return jnp.concatenate(parts, axis=-1)

    def gather_weights(low_cols, high_cols):
        odd = lax.axis_index("clo") == 1
        keep = jnp.where(odd, high_cols, low_cols)
        other = swap(jnp.where(odd, low_cols, high_cols), "clo", 1)
        a = {0: jnp.where(odd, other, keep)}
        b = {0: jnp.where(odd, keep, other)}
        for ka, kb in zip(up_order, down_order):
            for have, k in ((a, ka), (b, kb)):
                fresh = {r | (1 << k): swap(have[r], *group_bits[k]) for r in list(have)}
                have.update(fresh)
        return [x for r in range(n_groups) for x in (a[r], b[r])]

    def spread(pieces):
        a, b = dict(enumerate(pieces[0::2])), dict(enumerate(pieces[1::2]))
        for ka, kb in zip(down_order, up_order):
            for have, k in ((a, ka), (b, kb)):
                for r in [r for r in have if r & (1 << k)]:
                    moved = swap(have.pop(r), *group_bits[k])
                    to = r ^ (1 << k)
                    have[to] = (have[to].astype(F32) + moved.astype(F32)).astype(LOW)
        odd = lax.axis_index("clo") == 1
        keep = jnp.where(odd, b[0], a[0])
        other = swap(jnp.where(odd, a[0], b[0]), "clo", 1)
        return jnp.where(odd, other, keep), jnp.where(odd, keep, other)

    def token_gather(own):
        half = [own] + [swap(own, "mp", r) for r in range(1, n_mp)]
        return half + [swap(part, "clo", 1) for part in half]

    def token_reduce(own_half, send_half):
        rows, width = own_half.shape
        sub = rows // n_mp
        moved = swap(send_half, "clo", 1)
        outs = [shape((sub, width), F32)] + [shape((sub, width), LOW)] * (n_mp - 1)
        parts = call(middle, 0, [own_half, moved], outs, [], rows * width)
        return [parts[0]] + [swap(parts[r], "mp", r) for r in range(1, n_mp)]

    def own_tokens(value):
        seqs, block, width = value.shape
        sub = block * n_chi // n_mp
        per_block = block // sub
        place = lax.axis_index("mp") % per_block
        mine = lax.dynamic_slice_in_dim(value, place * sub, sub, 1)
        chi = lax.axis_index("chi")
        here = lax.dynamic_index_in_dim(mine, chi, 0, keepdims=False)
        there = swap(lax.dynamic_index_in_dim(mine, 1 - chi, 0, keepdims=False), "chi", 1)
        return jnp.where(lax.axis_index("mp") // per_block == chi, here, there)

    def tokens_out(own, block):
        sub, width = own.shape
        per_block = block // sub
        chi, mp = lax.axis_index("chi"), lax.axis_index("mp")
        parts = jnp.stack([own] + [swap(own, "mp", r) for r in range(1, n_mp)])
        parts = parts.reshape(n_chi, per_block, sub, width)
        parts = jnp.where(mp % per_block == 1, jnp.flip(parts, 1), parts)
        parts = parts.reshape(n_chi, block, width)
        here = (mp // per_block) == chi
        mine = jnp.where(here, parts[0], parts[1])
        moved = swap(jnp.where(here, parts[1], parts[0]), "chi", 1)
        return jnp.where(chi == 0, jnp.stack([mine, moved]), jnp.stack([moved, mine]))

    def on_device(
        tokens, segments, cotangent, first_gain, first_bias, qkv_weight, qkv_bias,
        out_weight, second_gain, second_bias, gate_up_weight, down_weight,
    ):
        n_seq, block, width = tokens.shape
        rows_dev = qkv_weight.shape[1]
        half_in = qkv_weight.shape[3] // 2
        half_ff = down_weight.shape[2] // 2
        heads = half_in // HEAD
        total = block * n_chi * n_clo
        half_total = total // n_clo
        sub = half_total // n_mp
        n_parts = n_clo * n_mp
        mp, clo, chi = (lax.axis_index(a) for a in ("mp", "clo", "chi"))
        attn_cols, mlp_cols = 4 * half_in, 3 * half_ff

        x_own = relative(own_tokens(tokens)).astype(F32)

        def halves(l, which):
            lo, hi = (slice(None, half_in), slice(half_in, None)), (
                slice(None, half_ff),
                slice(half_ff, None),
            )
            out = []
            for i in range(2):
                if which == 0:
                    parts = [qkv_weight[l, :, c, lo[i]] for c in range(3)]
                    parts.append(out_weight[l, :, lo[i]])
                else:
                    parts = [gate_up_weight[l, :, c, hi[i]] for c in range(2)]
                    parts.append(down_weight[l, :, hi[i]])
                out.append(jnp.concatenate(parts, axis=1))
            return out

        weights = [
            (gather_weights(*halves(l, 0)), gather_weights(*halves(l, 1))) for l in range(LAYERS)
        ]
        dx = relative(own_tokens(cotangent))
        gains = relative(jnp.stack([first_gain, first_bias, second_gain, second_bias]))
        half_bias = jnp.where(clo == 1, qkv_bias[:, :, half_in:], qkv_bias[:, :, :half_in])
        half_bias = half_bias.reshape(LAYERS, 1, 3 * half_in)

        there = swap(lax.dynamic_index_in_dim(segments, 1 - chi, 0, keepdims=False), "chi", 1)
        here = lax.dynamic_index_in_dim(segments, chi, 0, keepdims=False)
        pair = jnp.stack([jnp.where(chi == 0, here, there), jnp.where(chi == 0, there, here)])
        other = swap(pair, "clo", 1)
        whole = jnp.stack(
            [jnp.where(clo == 0, pair, other), jnp.where(clo == 0, other, pair)], axis=1
        ).reshape(total)
        core_of = jnp.arange(n_clo, dtype=jnp.int32) ^ clo
        mp_of = jnp.arange(n_mp, dtype=jnp.int32) ^ mp
        per_block = block // sub
        place = (
            (mp_of // per_block * (n_clo * block) + mp_of % per_block * sub)[None, :, None]
            + (core_of * block)[:, None, None]
            + jnp.arange(sub, dtype=jnp.int32)[None, None, :]
        ).reshape(total)
        match = place[:, None] == jnp.arange(total, dtype=jnp.int32)[None, :]
        seg = jnp.sum(jnp.where(match, whole[None, :], 0), axis=1)
        starts = jnp.sum((seg[None, :] < seg[:, None]).astype(jnp.int32), axis=1)
        freq = jnp.exp(
            jnp.arange(ROT // 2, dtype=F32) * (-2.0 * math.log(10000.0) / ROT)
        )
        angles = freq[:, None] * (place - starts).astype(F32)[None, :]
        cos_t, sin_t = jnp.cos(angles).T, jnp.sin(angles).T
        zeros = jnp.zeros((total, ROT // 2), F32)
        tail = jnp.zeros((total, HEAD - ROT), F32)
        tables = [
            jnp.tile(jnp.concatenate(parts, axis=1), (1, heads))
            for parts in (
                (cos_t, cos_t, tail + 1.0),
                (-sin_t, zeros, tail),
                (zeros, sin_t, tail),
            )
        ]
        geometry = [place[:, None], seg[:, None], place[None, :], seg[None, :]] + tables

        act = shape((total, half_in), LOW)
        reduced = [shape((half_total, width), F32), shape((half_total, width), LOW)]
        n_w = n_pieces
        sems = pltpu.SemaphoreType.DMA((n_parts + n_w,))
        h_scratch = pltpu.VMEM((total, width), LOW)

        def mm(*dims):
            return 2 * math.prod(dims)

        def norm(x, gain, offset, terms):
            outs = [shape(x.shape, F32), shape(x.shape, LOW)]
            return call(norm_forward, 0, [x, gain[None], offset[None]] + terms, outs, [], 10 * x.size)

        def norm_back(dx, y, gain, terms):
            outs = [shape(y.shape, F32), shape(y.shape, LOW), shape((2, width), F32)]
            return call(norm_backward, 0, [dx, y, gain[None]] + terms, outs, [], 20 * y.size)

        def grads(a_parts, b_parts, da, db, cols):
            outs = [shape((width // n_w, cols), LOW)] * n_w
            return call(
                functools.partial(weight_grads, n_parts, n_w),
                2 * n_parts,
                a_parts + b_parts + [da, db],
                outs,
                [h_scratch, h_scratch, pltpu.SemaphoreType.DMA((2 * n_parts,))],
                mm(total, width, cols),
            )

        saved = []
        terms = []
        for l in range(LAYERS):
            w_attn, w_mlp = weights[l]
            x_own, h = norm(x_own, gains[0, l], gains[1, l], terms)
            h1 = token_gather(h)
            q, k, v, o, own, send = call(
                functools.partial(attn_forward, n_parts, n_w, heads),
                n_parts + n_w,
                h1 + w_attn + [half_bias[l]] + geometry,
                [act] * 4 + reduced,
                [
                    h_scratch,
                    pltpu.VMEM((width, attn_cols), LOW),
                    pltpu.VMEM((total, 3 * half_in), F32),
                    sems,
                ],
                mm(total, width, attn_cols) + 2 * mm(heads, total, total, 2 * half_in),
            )
            y_own, h = norm(x_own, gains[2, l], gains[3, l], token_reduce(own, send))
            h2 = token_gather(h)
            gu, z, own, send = call(
                functools.partial(mlp_forward, n_parts, n_w),
                n_parts + n_w,
                h2 + w_mlp,
                [shape((total, 2 * half_ff), F32), shape((total, half_ff), LOW)] + reduced,
                [h_scratch, pltpu.VMEM((width, mlp_cols), LOW), sems],
                mm(total, width, mlp_cols),
            )
            saved.append((x_own, h1, q, k, v, o, y_own, h2, gu, z))
            x_own, terms = y_own, token_reduce(own, send)
        for t in terms:
            x_own = x_own + t.astype(F32)
        activations = tokens_out(relative(x_own.astype(LOW)), block)

        low = dx
        dx = dx.astype(F32)
        weight_out = [None] * LAYERS
        small_out = [None] * LAYERS
        for l in reversed(range(LAYERS)):
            w_attn, w_mlp = weights[l]
            x_own, h1, q, k, v, o, y_own, h2, gu, z = saved[l]
            dm = token_gather(low)
            dp2, own, send = call(
                functools.partial(mlp_backward, n_parts, n_w),
                n_parts + n_w,
                dm + w_mlp + [gu],
                [shape((total, 2 * half_ff), LOW)] + reduced,
                [
                    h_scratch,
                    pltpu.VMEM((width, mlp_cols), LOW),
                    pltpu.VMEM((total, half_ff), F32),
                    sems,
                ],
                mm(total, width, mlp_cols),
            )
            terms = token_reduce(own, send)
            g_mlp = spread(grads(h2, dm, dp2, z, mlp_cols))
            dy, low, small_two = norm_back(dx, y_own, gains[2, l], terms)
            da = token_gather(low)
            dp1, bias_grad, own, send = call(
                functools.partial(attn_backward, n_parts, n_w, heads),
                n_parts + n_w,
                da + w_attn + [q, k, v] + geometry,
                [shape((total, 3 * half_in), LOW), shape((1, 3 * half_in), F32)] + reduced,
                [
                    h_scratch,
                    pltpu.VMEM((width, attn_cols), LOW),
                    pltpu.VMEM((total, half_in), F32),
                    sems,
                ],
                mm(total, width, attn_cols) + 5 * mm(heads, total, total, half_in),
            )
            terms = token_reduce(own, send)
            g_attn = spread(grads(h1, da, dp1, o, attn_cols))
            dx, low, small_one = norm_back(dy, x_own, gains[0, l], terms)
            weight_out[l] = (g_attn, g_mlp)
            small_out[l] = (small_one, small_two, bias_grad)
        tokens_grad = tokens_out(relative(low), block).astype(F32)

        norms = relative(
            jnp.stack([jnp.concatenate(small_out[l][:2], axis=0) for l in range(LAYERS)], axis=1)
        )
        bias = jnp.stack([small_out[l][2] for l in range(LAYERS)]).reshape(LAYERS, 3, half_in)
        for k in range(log2(n_mp)):
            norms = norms + swap(norms, "mp", 1 << k)
        norms = norms + swap(norms, "clo", 1)
        for name, bit in group_bits:
            norms = norms + swap(norms, name, bit)
            bias = bias + swap(bias, name, bit)
        bias_other = swap(bias, "clo", 1)
        bias = jnp.concatenate(
            [jnp.where(clo == 0, bias, bias_other), jnp.where(clo == 0, bias_other, bias)], axis=2
        )

        def columns(which, first, count, parts):
            layers = []
            for l in range(LAYERS):
                pieces = [
                    piece[:, first : first + count].reshape((rows_dev,) + parts + (-1,))
                    for piece in weight_out[l][which]
                ]
                layers.append(jnp.concatenate(pieces, axis=-1).astype(F32))
            return jnp.stack(layers)

        return (
            activations, tokens_grad, norms[0], norms[1],
            columns(0, 0, 3 * half_in, (3,)), bias,
            columns(0, 3 * half_in, half_in, ()), norms[2], norms[3],
            columns(1, 0, 2 * half_ff, (2,)), columns(1, 2 * half_ff, half_ff, ()),
        )

    return on_device


def solution(mesh):
    n_dp, n_ctx, n_mp = (mesh.shape[a] for a in ("dp", "ctx", "mp"))
    n_clo = 2
    n_chi = n_ctx // n_clo
    fine = Mesh(mesh.devices.reshape(n_dp, n_chi, n_clo, n_mp), ("dp", "chi", "clo", "mp"))
    rows = ("dp", "chi", "clo")
    ctx = ("chi", "clo")
    token_spec = P("dp", ctx, None)
    four, three = P(None, rows, None, "mp"), P(None, rows, "mp")
    bias_spec = P(None, None, "mp")
    return jax.shard_map(
        make_program(n_dp, n_chi, n_clo, n_mp),
        mesh=fine,
        in_specs=(
            token_spec, P("dp", ctx), token_spec, P(), P(), four, bias_spec, three, P(), P(),
            four, three,
        ),
        out_specs=(
            token_spec, token_spec, P(), P(), four, bias_spec, three, P(), P(), four, three,
        ),
        check_vma=False,
    )
```

time: 1040 us -> 1020 us (0.981)
  Pallas kernels: 0 us -> 129 us
  local copies, waits for them, and re-layouts: 138 us -> 262 us
  waiting for transfers between devices: 461 us -> 357 us
  matrix products: 79.9 us -> 0 us
  other arithmetic: 124 us -> 75.6 us
  starting transfers between devices: 221 us -> 177 us
    pallas_call x0 -> x28, Pallas kernels: none -> 129 us  [call(): pl.pallas_call(body, out_shape=tuple(outs), in_specs=[ANY] * n_any + [VME...]
    ppermute x196 -> x164, waiting for transfers between devices: 461 us -> 357 us  [swap(): return lax.ppermute(value, axis, [(i, i ^ bit) for i in range(sizes[axis])])]
    dot_general x36 -> x0, matrix products: 79.9 us -> none  [the longest x24 69.6 us: dot(): return lax.dot_general(a, b, (dims, ((), ())), preferred_element_type=F32)]
    unnamed x380 -> x536, local copies, waits for them, and re-layouts: 43.6 us -> 111 us
    ppermute x0 -> x28, local copies, waits for them, and re-layouts: none -> 66.3 us  [swap(): return lax.ppermute(value, axis, [(i, i ^ bit) for i in range(sizes[axis])])]
    ppermute x196 -> x164, starting transfers between devices: 221 us -> 177 us  [swap(): return lax.ppermute(value, axis, [(i, i ^ bit) for i in range(sizes[axis])])]
    reshape x14 -> x0, local copies, waits for them, and re-layouts: 20.8 us -> none  [the longest x8 19 us: joined(): piece.reshape((rows_dev,) + parts + (-1,))]
    reduce_sum x16 -> x0, other arithmetic: 20.8 us -> none  [the longest x4 12.2 us: normalize(): center = values - jnp.mean(values, axis=-1, keepdims=True)]
  transfers between devices with their start and end apart: 196 -> 164, of which waited for: 71 -> 47; matrix products, arithmetic and copies ran while one was open for 25% -> 24% of each run, Pallas kernels for 0% -> 12%
where the time goes in v2:
time: 1020 us; the launch traced here: 1000 us
  waiting for transfers between devices  357 us (35%)
  local copies, waits for them, and re-layouts  262 us (26%)
  starting transfers between devices  177 us (17%)
  Pallas kernels  129 us (13%)
  other arithmetic  75.6 us (7%)
    ppermute x164, waiting for transfers between devices, swap(): return lax.ppermute(value, axis, [(i, i ^ bit) for i in range(sizes[axis])])  357 us
    ppermute x164, starting transfers between devices, swap(): return lax.ppermute(value, axis, [(i, i ^ bit) for i in range(sizes[axis])])  177 us
    pallas_call x28, Pallas kernels, call(): pl.pallas_call(body, out_shape=tuple(outs), in_specs=[ANY] * n_any + [VME...  129 us
    unnamed x536, local copies, waits for them, and re-layouts  111 us
    ppermute x28, local copies, waits for them, and re-layouts, swap(): return lax.ppermute(value, axis, [(i, i ^ bit) for i in range(sizes[axis])])  66.3 us
  transfers between devices with their start and end apart: 164, of which 47 were waited for; matrix products, arithmetic and copies ran while one was open for 24% of the time, Pallas kernels for 12%

profile of v2, /device:TPU:0, one launch (start us, length us, event | category | flops | bytes accessed | tf_op | source)
XLA Modules:
  0.0 1003.6 jit_solution(2616423602461658019)
XLA Ops:
  1.5 2.9 collective-permute-start.15
  12.2 9.5 fusion.18
  34.2 4.2 collective-permute-start.3
  45.7 11.0 %collective-permute-start.1 = (bf16[64,2048]{1,0:T(8,128)(2,1)S(1)}, bf16[64,2048]{1,0:T(8,128)(2,1)}, u32[]{:S(2)}, u32[]{:S(2)}) collective-permute-start(bf16[64,2048]{1,0:T(8,128)(2,1)S(1)} %get-tuple-element.129.refs_0_), channel_id=1, source_target_pairs={{0,1},{1,0},{2,3},{3,2},{4,5},{5,4},{6,7},{7,6},{8,9},{9,8},{10,11... | collective-permute-start | bytes 786440 | tf_op jit(solution)/shard_map/ppermute | solution.py:314
  56.7 4.7 collective-permute-done.2.refs_2_
  77.9 4.9 collective-permute-done.10.refs_11_
  85.1 8.9 collective-permute-done.14.refs_15_
  105.9 9.3 shard_map.204
  126.5 19.9 %collective-permute-done.32 = bf16[256,2112]{0,1:T(8,128)(2,1)} collective-permute-done((bf16[256,2112]{0,1:T(8,128)(2,1)}, bf16[256,2112]{0,1:T(8,128)(2,1)}, u32[]{:S(2)}, u32[]{:S(2)}) %collective-permute-start.32) | collective-permute-done | bytes 1081376 | tf_op jit(solution)/shard_map/ppermute | solution.py:314
  146.8 13.7 %collective-permute-done.19.refs_2_ = bf16[64,2048]{1,0:T(8,128)(2,1)S(1)} collective-permute-done((bf16[64,2048]{1,0:T(8,128)(2,1)S(1)}, bf16[64,2048]{1,0:T(8,128)(2,1)S(1)}, u32[]{:S(2)}, u32[]{:S(2)}) %collective-permute-start.19) | collective-permute-done | bytes 262176 | tf_op jit(solution)/shard_map/ppermute | solution.py:314
  161.8 8.9 collective-permute-done.20.refs_3_
  176.1 7.0 collective-permute-done.23.refs_3_
  183.1 14.7 %collective-permute-done.22.refs_2_ = bf16[64,2048]{1,0:T(8,128)(2,1)S(1)} collective-permute-done((bf16[64,2048]{1,0:T(8,128)(2,1)}, bf16[64,2048]{1,0:T(8,128)(2,1)S(1)}, u32[]{:S(2)}, u32[]{:S(2)}) %collective-permute-start.22) | collective-permute-done | bytes 262176 | tf_op jit(solution)/shard_map/ppermute | solution.py:314
  201.6 3.4 concatenate.185
  205.0 3.4 concatenate.184
  230.0 8.5 shard_map.207
  253.3 6.6 collective-permute-done.50.refs_13_
  263.0 7.4 collective-permute-done.37.refs_2_
  277.9 4.1 collective-permute-start.40
  287.6 7.9 collective-permute-done.52.refs_15_
  296.1 4.4 collective-permute-done.40.refs_2_
  318.2 9.5 shard_map.210
  334.0 6.8 collective-permute-done.82.refs_3_.refs_11_
  345.2 3.6 collective-permute-done.54.refs_1_
  351.5 10.6 %collective-permute-done.55.refs_2_ = bf16[64,2048]{1,0:T(8,128)(2,1)S(1)} collective-permute-done((bf16[64,2048]{1,0:T(8,128)(2,1)S(1)}, bf16[64,2048]{1,0:T(8,128)(2,1)S(1)}, u32[]{:S(2)}, u32[]{:S(2)}) %collective-permute-start.55) | collective-permute-done | bytes 262176 | tf_op jit(solution)/shard_map/ppermute | solution.py:314
  364.8 6.5 collective-permute-done.56.refs_3_
  371.3 3.6 collective-permute-start.81
  376.8 8.9 collective-permute-done.81.refs_2_.refs_10_
  390.9 6.9 collective-permute-done.59.refs_3_
  397.8 10.7 %collective-permute-done.58.refs_2_ = bf16[64,2048]{1,0:T(8,128)(2,1)} collective-permute-done((bf16[64,2048]{1,0:T(8,128)(2,1)}, bf16[64,2048]{1,0:T(8,128)(2,1)}, u32[]{:S(2)}, u32[]{:S(2)}) %collective-permute-start.58) | collective-permute-done | bytes 262176 | tf_op jit(solution)/shard_map/ppermute | solution.py:314
  429.2 8.8 shard_map.213
  438.1 10.9 %shard_map.215 = (bf16[512,1408]{1,0:T(8,128)(2,1)}, f32[256,2048]{1,0:T(8,128)}, bf16[256,2048]{1,0:T(8,128)(2,1)S(1)}) custom-call(bf16[64,2048]{1,0:T(8,128)(2,1)} %get-tuple-element.344.refs_0_.refs_8_, bf16[64,2048]{1,0:T(8,128)(2,1)} %collective-permute-done.80.refs_1_.refs_9_, bf16[64,2048]{1,0:T(8,128)(2,1)S(1)} %copy-done.158, ...), custom_call_target="tpu_custom_call" | custom-call | flops 4429185024 | bytes 18219008 | tf_op jit(solution)/shard_map/pallas_call | solution.py:47
  453.5 3.2 collective-permute-start.89
  457.9 9.1 collective-permute-done.88.refs_1_
  467.0 8.1 collective-permute-done.89.refs_2_
  480.3 4.4 collective-permute-start.92
  486.8 16.7 %collective-permute-done.92.refs_2_.refs_10_ = bf16[64,2048]{1,0:T(8,128)(2,1)} collective-permute-done((bf16[64,2048]{1,0:T(8,128)(2,1)}, bf16[64,2048]{1,0:T(8,128)(2,1)}, u32[]{:S(2)}, u32[]{:S(2)}) %collective-permute-start.92) | collective-permute-done | bytes 262176 | tf_op jit(solution)/shard_map/ppermute | solution.py:314
  504.1 9.7 shard_map.230
  532.2 11.1 %shard_map.218 = (bf16[512,768]{1,0:T(8,128)(2,1)S(1)}, f32[1,768]{1,0:T(1,128)S(1)}, f32[256,2048]{1,0:T(8,128)}, bf16[256,2048]{1,0:T(8,128)(2,1)}) custom-call(bf16[64,2048]{1,0:T(8,128)(2,1)} %get-tuple-element.168.refs_0_.refs_8_, bf16[64,2048]{1,0:T(8,128)(2,1)} %collective-permute-done.91.refs_1_.refs_9_, ...), custom_call_target="tpu_custom_call" | custom-call | flops 4831838208 | bytes 12594176 | tf_op jit(solution)/shard_map/pallas_call | solution.py:47
  579.3 17.5 %collective-permute-done.157 = bf16[256,2112]{0,1:T(8,128)(2,1)} collective-permute-done((bf16[256,2112]{0,1:T(8,128)(2,1)}, bf16[256,2112]{0,1:T(8,128)(2,1)}, u32[]{:S(2)}, u32[]{:S(2)}) %collective-permute-start.157) | collective-permute-done | bytes 1081376 | tf_op jit(solution)/shard_map/ppermute | solution.py:314
  606.8 5.6 collective-permute-done.101.refs_3_
  627.1 8.0 collective-permute-start.103
  637.0 14.6 %collective-permute-done.103.refs_2_.refs_10_ = bf16[64,2048]{1,0:T(8,128)(2,1)} collective-permute-done((bf16[64,2048]{1,0:T(8,128)(2,1)}, bf16[64,2048]{1,0:T(8,128)(2,1)}, u32[]{:S(2)}, u32[]{:S(2)}) %collective-permute-start.103) | collective-permute-done | bytes 262176 | tf_op jit(solution)/shard_map/ppermute | solution.py:314
  653.0 4.7 shard_map.228
  676.0 12.6 %shard_map.221 = (bf16[512,1408]{1,0:T(8,128)(2,1)}, f32[256,2048]{1,0:T(8,128)}, bf16[256,2048]{1,0:T(8,128)(2,1)}) custom-call(bf16[64,2048]{1,0:T(8,128)(2,1)} %get-tuple-element.179.refs_0_.refs_8_, bf16[64,2048]{1,0:T(8,128)(2,1)} %collective-permute-done.102.refs_1_.refs_9_, bf16[64,2048]{1,0:T(8,128)(2,1)} %collective-permute-done.103.refs_2_.refs_10_, ...), custom_call_target="tpu_custom_call" | custom-call | flops 4429185024 | bytes 18219008 | tf_op jit(solution)/shard_map/pallas_call | solution.py:47
  700.1 9.9 shard_map.229
  731.9 10.2 %collective-permute-done.142 = bf16[256,1024]{1,0:T(8,128)(2,1)} collective-permute-done((bf16[256,1024]{1,0:T(8,128)(2,1)}, bf16[256,1024]{1,0:T(8,128)(2,1)}, u32[]{:S(2)}, u32[]{:S(2)}) %collective-permute-start.142) | collective-permute-done | bytes 524320 | tf_op jit(solution)/shard_map/ppermute | solution.py:314
  755.5 9.3 collective-permute-done.154
  775.7 4.2 collective-permute-done.115.refs_3_.refs_11_
  780.0 13.1 %collective-permute-done.114.refs_2_.refs_10_ = bf16[64,2048]{1,0:T(8,128)(2,1)} collective-permute-done((bf16[64,2048]{1,0:T(8,128)(2,1)}, bf16[64,2048]{1,0:T(8,128)(2,1)}, u32[]{:S(2)}, u32[]{:S(2)}) %collective-permute-start.114) | collective-permute-done | bytes 262176 | tf_op jit(solution)/shard_map/ppermute | solution.py:314
  807.0 11.3 %shard_map.224 = (bf16[512,768]{1,0:T(8,128)(2,1)S(1)}, f32[1,768]{1,0:T(1,128)S(1)}, f32[256,2048]{1,0:T(8,128)}, bf16[256,2048]{1,0:T(8,128)(2,1)}) custom-call(bf16[64,2048]{1,0:T(8,128)(2,1)} %get-tuple-element.188.refs_0_.refs_8_, bf16[64,2048]{1,0:T(8,128)(2,1)} %collective-permute-done.113.refs_1_.refs_9_, ...), custom_call_target="tpu_custom_call" | custom-call | flops 4831838208 | bytes 12594176 | tf_op jit(solution)/shard_map/pallas_call | solution.py:47
  821.7 27.6 %collective-permute-done.147 = f32[2,3,256]{2,1,0:T(4,128)S(1)} collective-permute-done((f32[2,3,256]{2,1,0:T(4,128)S(1)}, f32[2,3,256]{2,1,0:T(4,128)S(1)}, u32[]{:S(2)}, u32[]{:S(2)}) %collective-permute-start.147) | collective-permute-done | bytes 6176 | tf_op jit(solution)/shard_map/ppermute | solution.py:314
  850.5 5.2 shard_map.227
  878.9 3.7 collective-permute-done.137
  885.7 4.2 broadcast_select_fusion.7
  894.8 9.6 collective-permute-done.135
  905.9 3.1 broadcast_select_fusion.23
  909.1 5.8 collective-permute-done.122.refs_2_
  916.4 5.1 collective-permute-start.128
  930.4 3.8 broadcast_select_fusion.1
  939.8 4.0 maximum_convert_fusion
  943.9 6.1 collective-permute-done.129
  954.3 9.6 copy.292
  981.3 16.3 %collective-permute-done.78 = bf16[128,2048]{1,0:T(8,128)(2,1)} collective-permute-done((bf16[128,2048]{1,0:T(8,128)(2,1)}, bf16[128,2048]{1,0:T(8,128)(2,1)}, u32[]{:S(2)}, u32[]{:S(2)}) %collective-permute-start.78) | collective-permute-done | bytes 524320 | tf_op jit(solution)/shard_map/ppermute | solution.py:314
  (1010 shorter events, 461.0 us)
Async XLA Ops:
  1.5 28.7 %collective-permute-start.15 = (s32[128]{0:T(128)S(1)}, s32[128]{0:T(128)S(1)}, u32[]{:S(2)}, u32[]{:S(2)}) collective-permute-start(s32[128]{0:T(128)S(1)} %fusion.13), channel_id=1, source_target_pairs={{0,8},{8,0},{1,9},{9,1},{2,10},{10,2},{3,11},{11,3},{4,12},{12,4},... | collective-permute-start | bytes 1544 | tf_op jit(solution)/shard_map/ppermute | solution.py:314
  6.1 26.4 %collective-permute-start = (bf16[64,2048]{1,0:T(8,128)(2,1)}, bf16[64,2048]{1,0:T(8,128)(2,1)}, u32[]{:S(2)}, u32[]{:S(2)}) collective-permute-start(bf16[64,2048]{1,0:T(8,128)(2,1)} %dynamic-slice_bitcast_fusion.1), channel_id=1, source_target_pairs={{0,8},{8,0},{1,9},{9,1},{2,10},{10,2},{3,11},{11,3},{4,12},{12,4},... | collective-permute-start | bytes 786440 | tf_op jit(solution)/shard_map/ppermute | solution.py:314
  10.0 28.4 %collective-permute-start.8 = (bf16[256,1024]{1,0:T(8,128)(2,1)}, bf16[256,1024]{1,0:T(8,128)(2,1)}, u32[]{:S(2)}, u32[]{:S(2)}) collective-permute-start(bf16[256,1024]{1,0:T(8,128)(2,1)} %broadcast_select_fusion.31), channel_id=1, source_target_pairs={{0,4},{4,0},{1,5},{5,1},{2,6},{6,2},{3,7},{7,3},{8,12},{12,8},{9,1... | collective-permute-start | bytes 1572872 | tf_op jit(solution)/shard_map/ppermute | solution.py:314
  28.6 32.8 %collective-permute-start.28 = (bf16[256,2112]{0,1:T(8,128)(2,1)}, bf16[256,2112]{0,1:T(8,128)(2,1)}, u32[]{:S(2)}, u32[]{:S(2)}) collective-permute-start(bf16[256,2112]{0,1:T(8,128)(2,1)} %copy.195), channel_id=1, source_target_pairs={{0,4},{4,0},{1,5},{5,1},{2,6},{6,2},{3,7},{7,3},{8,12},{12,8},{9,1... | collective-permute-start | bytes 3244040 | tf_op jit(solution)/shard_map/ppermute | solution.py:314
  40.8 31.4 %collective-permute-start.12 = (bf16[256,1024]{1,0:T(8,128)(2,1)}, bf16[256,1024]{1,0:T(8,128)(2,1)}, u32[]{:S(2)}, u32[]{:S(2)}) collective-permute-start(bf16[256,1024]{1,0:T(8,128)(2,1)} %get-tuple-element.324.refs_9_), channel_id=1, source_target_pairs={{0,16},{16,0},{1,17},{17,1},{2,18},{18,2},{3,19},{19,3},{4,20},{20... | collective-permute-start | bytes 1572872 | tf_op jit(solution)/shard_map/ppermute | solution.py:314
  42.3 30.3 %collective-permute-start.9 = (bf16[256,1024]{1,0:T(8,128)(2,1)}, bf16[256,1024]{1,0:T(8,128)(2,1)}, u32[]{:S(2)}, u32[]{:S(2)}) collective-permute-start(bf16[256,1024]{1,0:T(8,128)(2,1)} %get-tuple-element.325.refs_8_), channel_id=1, source_target_pairs={{0,8},{8,0},{1,9},{9,1},{2,10},{10,2},{3,11},{11,3},{4,12},{12,4},... | collective-permute-start | bytes 1572872 | tf_op jit(solution)/shard_map/ppermute | solution.py:314
  76.4 45.5 %collective-permute-start.29 = (bf16[256,2112]{0,1:T(8,128)(2,1)}, bf16[256,2112]{0,1:T(8,128)(2,1)}, u32[]{:S(2)}, u32[]{:S(2)}) collective-permute-start(bf16[256,2112]{0,1:T(8,128)(2,1)} %copy.198), channel_id=1, source_target_pairs={{0,8},{8,0},{1,9},{9,1},{2,10},{10,2},{3,11},{11,3},{4,12},{12,4},... | collective-permute-start | bytes 3244040 | tf_op jit(solution)/shard_map/ppermute | solution.py:314
  119.4 27.0 %collective-permute-start.32 = (bf16[256,2112]{0,1:T(8,128)(2,1)}, bf16[256,2112]{0,1:T(8,128)(2,1)}, u32[]{:S(2)}, u32[]{:S(2)}) collective-permute-start(bf16[256,2112]{0,1:T(8,128)(2,1)} %copy.199), channel_id=1, source_target_pairs={{0,16},{16,0},{1,17},{17,1},{2,18},{18,2},{3,19},{19,3},{4,20},{20... | collective-permute-start | bytes 3244040 | tf_op jit(solution)/shard_map/ppermute | solution.py:314
  120.9 52.1 %collective-permute-start.31 = (bf16[256,2112]{0,1:T(8,128)(2,1)}, bf16[256,2112]{0,1:T(8,128)(2,1)S(1)}, u32[]{:S(2)}, u32[]{:S(2)}) collective-permute-start(bf16[256,2112]{0,1:T(8,128)(2,1)} %copy.198), channel_id=1, source_target_pairs={{0,16},{16,0},{1,17},{17,1},{2,18},{18,2},{3,19},{19,3},{4,20},{20... | collective-permute-start | bytes 3244040 | tf_op jit(solution)/shard_map/ppermute | solution.py:314
  121.4 53.9 %collective-permute-start.30 = (bf16[256,2112]{0,1:T(8,128)(2,1)}, bf16[256,2112]{0,1:T(8,128)(2,1)S(1)}, u32[]{:S(2)}, u32[]{:S(2)}) collective-permute-start(bf16[256,2112]{0,1:T(8,128)(2,1)} %copy.199), channel_id=1, source_target_pairs={{0,8},{8,0},{1,9},{9,1},{2,10},{10,2},{3,11},{11,3},{4,12},{12,4},... | collective-permute-start | bytes 3244040 | tf_op jit(solution)/shard_map/ppermute | solution.py:314
  121.9 76.4 %collective-permute-start.33 = (bf16[256,2112]{0,1:T(8,128)(2,1)}, bf16[256,2112]{0,1:T(8,128)(2,1)S(1)}, u32[]{:S(2)}, u32[]{:S(2)}) collective-permute-start(bf16[256,2112]{0,1:T(8,128)(2,1)} %collective-permute-done.29), channel_id=1, source_target_pairs={{0,16},{16,0},{1,17},{17,1},{2,18},{18,2},{3,19},{19,3},{4,20},{20... | collective-permute-start | bytes 3244040 | tf_op jit(solution)/shard_map/ppermute | solution.py:314
  146.4 76.1 %collective-permute-start.34 = (bf16[256,2112]{0,1:T(8,128)(2,1)}, bf16[256,2112]{0,1:T(8,128)(2,1)}, u32[]{:S(2)}, u32[]{:S(2)}) collective-permute-start(bf16[256,2112]{0,1:T(8,128)(2,1)} %collective-permute-done.32), channel_id=1, source_target_pairs={{0,8},{8,0},{1,9},{9,1},{2,10},{10,2},{3,11},{11,3},{4,12},{12,4},... | collective-permute-start | bytes 3244040 | tf_op jit(solution)/shard_map/ppermute | solution.py:314
  183.1 42.1 %collective-permute-start.24 = (bf16[64,2048]{1,0:T(8,128)(2,1)}, bf16[64,2048]{1,0:T(8,128)(2,1)}, u32[]{:S(2)}, u32[]{:S(2)}) collective-permute-start(bf16[64,2048]{1,0:T(8,128)(2,1)} %get-tuple-element.137.refs_0_), channel_id=1, source_target_pairs={{0,4},{4,0},{1,5},{5,1},{2,6},{6,2},{3,7},{7,3},{8,12},{12,8},{9,1... | collective-permute-start | bytes 786440 | tf_op jit(solution)/shard_map/ppermute | solution.py:314
  197.8 27.4 %collective-permute-start.27 = (bf16[64,2048]{1,0:T(8,128)(2,1)S(1)}, bf16[64,2048]{1,0:T(8,128)(2,1)}, u32[]{:S(2)}, u32[]{:S(2)}) collective-permute-start(bf16[64,2048]{1,0:T(8,128)(2,1)S(1)} %collective-permute-done.23.refs_3_), channel_id=1, source_target_pairs={{0,4},{4,0},{1,5},{5,1},{2,6},{6,2},{3,7},{7,3},{8,12},{12,8},{9,1... | collective-permute-start | bytes 786440 | tf_op jit(solution)/shard_map/ppermute | solution.py:314
  197.8 27.4 %collective-permute-start.26 = (bf16[64,2048]{1,0:T(8,128)(2,1)S(1)}, bf16[64,2048]{1,0:T(8,128)(2,1)}, u32[]{:S(2)}, u32[]{:S(2)}) collective-permute-start(bf16[64,2048]{1,0:T(8,128)(2,1)S(1)} %collective-permute-done.22.refs_2_), channel_id=1, source_target_pairs={{0,4},{4,0},{1,5},{5,1},{2,6},{6,2},{3,7},{7,3},{8,12},{12,8},{9,1... | collective-permute-start | bytes 786440 | tf_op jit(solution)/shard_map/ppermute | solution.py:314
  198.3 26.9 %collective-permute-start.25 = (bf16[64,2048]{1,0:T(8,128)(2,1)S(1)}, bf16[64,2048]{1,0:T(8,128)(2,1)}, u32[]{:S(2)}, u32[]{:S(2)}) collective-permute-start(bf16[64,2048]{1,0:T(8,128)(2,1)S(1)} %collective-permute-done.21.refs_1_), channel_id=1, source_target_pairs={{0,4},{4,0},{1,5},{5,1},{2,6},{6,2},{3,7},{7,3},{8,12},{12,8},{9,1... | collective-permute-start | bytes 786440 | tf_op jit(solution)/shard_map/ppermute | solution.py:314
  243.1 38.9 %collective-permute-start.64 = (bf16[256,2112]{0,1:T(8,128)(2,1)}, bf16[256,2112]{0,1:T(8,128)(2,1)}, u32[]{:S(2)}, u32[]{:S(2)}) collective-permute-start(bf16[256,2112]{0,1:T(8,128)(2,1)} %copy.217), channel_id=1, source_target_pairs={{0,4},{4,0},{1,5},{5,1},{2,6},{6,2},{3,7},{7,3},{8,12},{12,8},{9,1... | collective-permute-start | bytes 3244040 | tf_op jit(solution)/shard_map/ppermute | solution.py:314
  308.2 34.9 %collective-permute-start.65 = (bf16[256,2112]{0,1:T(8,128)(2,1)}, bf16[256,2112]{0,1:T(8,128)(2,1)S(1)}, u32[]{:S(2)}, u32[]{:S(2)}) collective-permute-start(bf16[256,2112]{0,1:T(8,128)(2,1)} %copy.220), channel_id=1, source_target_pairs={{0,8},{8,0},{1,9},{9,1},{2,10},{10,2},{3,11},{11,3},{4,12},{12,4},... | collective-permute-start | bytes 3244040 | tf_op jit(solution)/shard_map/ppermute | solution.py:314
  309.6 35.0 %collective-permute-start.68 = (bf16[256,2112]{0,1:T(8,128)(2,1)}, bf16[256,2112]{0,1:T(8,128)(2,1)S(1)}, u32[]{:S(2)}, u32[]{:S(2)}) collective-permute-start(bf16[256,2112]{0,1:T(8,128)(2,1)} %copy.221), channel_id=1, source_target_pairs={{0,16},{16,0},{1,17},{17,1},{2,18},{18,2},{3,19},{19,3},{4,20},{20... | collective-permute-start | bytes 3244040 | tf_op jit(solution)/shard_map/ppermute | solution.py:314
  331.8 56.0 %collective-permute-start.67 = (bf16[256,2112]{0,1:T(8,128)(2,1)S(1)}, bf16[256,2112]{0,1:T(8,128)(2,1)S(1)}, u32[]{:S(2)}, u32[]{:S(2)}) collective-permute-start(bf16[256,2112]{0,1:T(8,128)(2,1)S(1)} %copy-done.240), channel_id=1, source_target_pairs={{0,16},{16,0},{1,17},{17,1},{2,18},{18,2},{3,19},{19,3},{4,20},{20... | collective-permute-start | bytes 3244040 | tf_op jit(solution)/shard_map/ppermute | solution.py:314
  333.3 54.5 %collective-permute-start.66 = (bf16[256,2112]{0,1:T(8,128)(2,1)S(1)}, bf16[256,2112]{0,1:T(8,128)(2,1)S(1)}, u32[]{:S(2)}, u32[]{:S(2)}) collective-permute-start(bf16[256,2112]{0,1:T(8,128)(2,1)S(1)} %copy-done.239), channel_id=1, source_target_pairs={{0,8},{8,0},{1,9},{9,1},{2,10},{10,2},{3,11},{11,3},{4,12},{12,4},... | collective-permute-start | bytes 3244040 | tf_op jit(solution)/shard_map/ppermute | solution.py:314
  343.1 47.6 %collective-permute-start.69 = (bf16[256,2112]{0,1:T(8,128)(2,1)S(1)}, bf16[256,2112]{0,1:T(8,128)(2,1)S(1)}, u32[]{:S(2)}, u32[]{:S(2)}) collective-permute-start(bf16[256,2112]{0,1:T(8,128)(2,1)S(1)} %collective-permute-done.65), channel_id=1, source_target_pairs={{0,16},{16,0},{1,17},{17,1},{2,18},{18,2},{3,19},{19,3},{4,20},{20... | collective-permute-start | bytes 3244040 | tf_op jit(solution)/shard_map/ppermute | solution.py:314
  344.6 46.2 %collective-permute-start.70 = (bf16[256,2112]{0,1:T(8,128)(2,1)S(1)}, bf16[256,2112]{0,1:T(8,128)(2,1)S(1)}, u32[]{:S(2)}, u32[]{:S(2)}) collective-permute-start(bf16[256,2112]{0,1:T(8,128)(2,1)S(1)} %collective-permute-done.68), channel_id=1, source_target_pairs={{0,8},{8,0},{1,9},{9,1},{2,10},{10,2},{3,11},{11,3},{4,12},{12,4},... | collective-permute-start | bytes 3244040 | tf_op jit(solution)/shard_map/ppermute | solution.py:314
  390.8 32.4 %collective-permute-start.80 = (bf16[64,2048]{1,0:T(8,128)(2,1)}, bf16[64,2048]{1,0:T(8,128)(2,1)}, u32[]{:S(2)}, u32[]{:S(2)}) collective-permute-start(bf16[64,2048]{1,0:T(8,128)(2,1)} %get-tuple-element.344.refs_0_.refs_8_), channel_id=1, source_target_pairs={{0,1},{1,0},{2,3},{3,2},{4,5},{5,4},{6,7},{7,6},{8,9},{9,8},{10,11... | collective-permute-start | bytes 786440 | tf_op jit(solution)/shard_map/ppermute | solution.py:314
  390.9 32.3 %collective-permute-start.60 = (bf16[64,2048]{1,0:T(8,128)(2,1)}, bf16[64,2048]{1,0:T(8,128)(2,1)}, u32[]{:S(2)}, u32[]{:S(2)}) collective-permute-start(bf16[64,2048]{1,0:T(8,128)(2,1)} %get-tuple-element.153.refs_0_), channel_id=1, source_target_pairs={{0,4},{4,0},{1,5},{5,1},{2,6},{6,2},{3,7},{7,3},{8,12},{12,8},{9,1... | collective-permute-start | bytes 786440 | tf_op jit(solution)/shard_map/ppermute | solution.py:314
  397.8 25.9 %collective-permute-start.63 = (bf16[64,2048]{1,0:T(8,128)(2,1)}, bf16[64,2048]{1,0:T(8,128)(2,1)}, u32[]{:S(2)}, u32[]{:S(2)}) collective-permute-start(bf16[64,2048]{1,0:T(8,128)(2,1)} %collective-permute-done.59.refs_3_), channel_id=1, source_target_pairs={{0,4},{4,0},{1,5},{5,1},{2,6},{6,2},{3,7},{7,3},{8,12},{12,8},{9,1... | collective-permute-start | bytes 786440 | tf_op jit(solution)/shard_map/ppermute | solution.py:314
  484.7 69.5 %collective-permute-start.71 = (bf16[256,2048]{1,0:T(8,128)(2,1)}, bf16[256,2048]{1,0:T(8,128)(2,1)}, u32[]{:S(2)}, u32[]{:S(2)}) collective-permute-start(bf16[256,2048]{1,0:T(8,128)(2,1)} %get-tuple-element.155), channel_id=1, source_target_pairs={{0,4},{4,0},{1,5},{5,1},{2,6},{6,2},{3,7},{7,3},{8,12},{12,8},{9,1... | collective-permute-start | bytes 3145736 | tf_op jit(solution)/shard_map/ppermute | solution.py:314
  484.8 35.5 %collective-permute-start.94 = (bf16[64,2048]{1,0:T(8,128)(2,1)}, bf16[64,2048]{1,0:T(8,128)(2,1)}, u32[]{:S(2)}, u32[]{:S(2)}) collective-permute-start(bf16[64,2048]{1,0:T(8,128)(2,1)} %get-tuple-element.168.refs_0_.refs_8_), channel_id=1, source_target_pairs={{0,4},{4,0},{1,5},{5,1},{2,6},{6,2},{3,7},{7,3},{8,12},{12,8},{9,1... | collective-permute-start | bytes 786440 | tf_op jit(solution)/shard_map/ppermute | solution.py:314
  486.8 34.9 %collective-permute-start.97 = (bf16[64,2048]{1,0:T(8,128)(2,1)}, bf16[64,2048]{1,0:T(8,128)(2,1)}, u32[]{:S(2)}, u32[]{:S(2)}) collective-permute-start(bf16[64,2048]{1,0:T(8,128)(2,1)} %collective-permute-done.93.refs_3_.refs_11_), channel_id=1, source_target_pairs={{0,4},{4,0},{1,5},{5,1},{2,6},{6,2},{3,7},{7,3},{8,12},{12,8},{9,1... | collective-permute-start | bytes 786440 | tf_op jit(solution)/shard_map/ppermute | solution.py:314
  520.3 38.7 %collective-permute-start.161 = (bf16[256,2112]{0,1:T(8,128)(2,1)}, bf16[256,2112]{0,1:T(8,128)(2,1)}, u32[]{:S(2)}, u32[]{:S(2)}) collective-permute-start(bf16[256,2112]{0,1:T(8,128)(2,1)} %copy.281), channel_id=1, source_target_pairs={{0,8},{8,0},{1,9},{9,1},{2,10},{10,2},{3,11},{11,3},{4,12},{12,4},... | collective-permute-start | bytes 3244040 | tf_op jit(solution)/shard_map/ppermute | solution.py:314
  547.0 27.0 %collective-permute-start.158 = (bf16[256,2112]{0,1:T(8,128)(2,1)}, bf16[256,2112]{0,1:T(8,128)(2,1)}, u32[]{:S(2)}, u32[]{:S(2)}) collective-permute-start(bf16[256,2112]{0,1:T(8,128)(2,1)} %copy.275), channel_id=1, source_target_pairs={{0,16},{16,0},{1,17},{17,1},{2,18},{18,2},{3,19},{19,3},{4,20},{20... | collective-permute-start | bytes 3244040 | tf_op jit(solution)/shard_map/ppermute | solution.py:314
  550.4 26.3 %collective-permute-start.160 = (bf16[256,2112]{0,1:T(8,128)(2,1)}, bf16[256,2112]{0,1:T(8,128)(2,1)}, u32[]{:S(2)}, u32[]{:S(2)}) collective-permute-start(bf16[256,2112]{0,1:T(8,128)(2,1)} %copy.279), channel_id=1, source_target_pairs={{0,8},{8,0},{1,9},{9,1},{2,10},{10,2},{3,11},{11,3},{4,12},{12,4},... | collective-permute-start | bytes 3244040 | tf_op jit(solution)/shard_map/ppermute | solution.py:314
  554.3 42.5 %collective-permute-start.157 = (bf16[256,2112]{0,1:T(8,128)(2,1)}, bf16[256,2112]{0,1:T(8,128)(2,1)}, u32[]{:S(2)}, u32[]{:S(2)}) collective-permute-start(bf16[256,2112]{0,1:T(8,128)(2,1)} %copy.273), channel_id=1, source_target_pairs={{0,16},{16,0},{1,17},{17,1},{2,18},{18,2},{3,19},{19,3},{4,20},{20... | collective-permute-start | bytes 3244040 | tf_op jit(solution)/shard_map/ppermute | solution.py:314
  566.7 32.5 %collective-permute-start.99 = (bf16[64,2048]{1,0:T(8,128)(2,1)}, bf16[64,2048]{1,0:T(8,128)(2,1)S(1)}, u32[]{:S(2)}, u32[]{:S(2)}) collective-permute-start(bf16[64,2048]{1,0:T(8,128)(2,1)} %get-tuple-element.175), channel_id=1, source_target_pairs={{0,1},{1,0},{2,3},{3,2},{4,5},{5,4},{6,7},{7,6},{8,9},{9,8},{10,11... | collective-permute-start | bytes 786440 | tf_op jit(solution)/shard_map/ppermute | solution.py:314
  566.7 33.5 %collective-permute-start.100 = (bf16[64,2048]{1,0:T(8,128)(2,1)S(1)}, bf16[64,2048]{1,0:T(8,128)(2,1)S(1)}, u32[]{:S(2)}, u32[]{:S(2)}) collective-permute-start(bf16[64,2048]{1,0:T(8,128)(2,1)S(1)} %get-tuple-element.176), channel_id=1, source_target_pairs={{0,2},{1,3},{2,0},{3,1},{4,6},{5,7},{6,4},{7,5},{8,10},{9,11},{10,... | collective-permute-start | bytes 786440 | tf_op jit(solution)/shard_map/ppermute | solution.py:314
  574.0 50.7 %collective-permute-start.72 = (bf16[64,2048]{1,0:T(8,128)(2,1)}, bf16[64,2048]{1,0:T(8,128)(2,1)}, u32[]{:S(2)}, u32[]{:S(2)}) collective-permute-start(bf16[64,2048]{1,0:T(8,128)(2,1)} %get-tuple-element.157), channel_id=1, source_target_pairs={{0,1},{1,0},{2,3},{3,2},{4,5},{5,4},{6,7},{7,6},{8,9},{9,8},{10,11... | collective-permute-start | bytes 786440 | tf_op jit(solution)/shard_map/ppermute | solution.py:314
  576.7 50.4 %collective-permute-start.73 = (bf16[64,2048]{1,0:T(8,128)(2,1)}, bf16[64,2048]{1,0:T(8,128)(2,1)}, u32[]{:S(2)}, u32[]{:S(2)}) collective-permute-start(bf16[64,2048]{1,0:T(8,128)(2,1)} %get-tuple-element.158), channel_id=1, source_target_pairs={{0,2},{1,3},{2,0},{3,1},{4,6},{5,7},{6,4},{7,5},{8,10},{9,11},{10,... | collective-permute-start | bytes 786440 | tf_op jit(solution)/shard_map/ppermute | solution.py:314
  596.7 38.3 %collective-permute-start.74 = (bf16[64,2048]{1,0:T(8,128)(2,1)}, bf16[64,2048]{1,0:T(8,128)(2,1)}, u32[]{:S(2)}, u32[]{:S(2)}) collective-permute-start(bf16[64,2048]{1,0:T(8,128)(2,1)} %get-tuple-element.159), channel_id=1, source_target_pairs={{0,3},{1,2},{2,1},{3,0},{4,7},{5,6},{6,5},{7,4},{8,11},{9,10},{10,... | collective-permute-start | bytes 786440 | tf_op jit(solution)/shard_map/ppermute | solution.py:314
  599.2 37.3 %collective-permute-start.162 = (bf16[256,2112]{0,1:T(8,128)(2,1)}, bf16[256,2112]{0,1:T(8,128)(2,1)}, u32[]{:S(2)}, u32[]{:S(2)}) collective-permute-start(bf16[256,2112]{0,1:T(8,128)(2,1)} %copy.283), channel_id=1, source_target_pairs={{0,16},{16,0},{1,17},{17,1},{2,18},{18,2},{3,19},{19,3},{4,20},{20... | collective-permute-start | bytes 3244040 | tf_op jit(solution)/shard_map/ppermute | solution.py:314
  613.1 52.6 %collective-permute-start.159 = (bf16[256,2112]{0,1:T(8,128)(2,1)}, bf16[256,2112]{0,1:T(8,128)(2,1)}, u32[]{:S(2)}, u32[]{:S(2)}) collective-permute-start(bf16[256,2112]{0,1:T(8,128)(2,1)} %copy.277), channel_id=1, source_target_pairs={{0,8},{8,0},{1,9},{9,1},{2,10},{10,2},{3,11},{11,3},{4,12},{12,4},... | collective-permute-start | bytes 3244040 | tf_op jit(solution)/shard_map/ppermute | solution.py:314
  636.5 31.7 %collective-permute-start.105 = (bf16[64,2048]{1,0:T(8,128)(2,1)}, bf16[64,2048]{1,0:T(8,128)(2,1)}, u32[]{:S(2)}, u32[]{:S(2)}) collective-permute-start(bf16[64,2048]{1,0:T(8,128)(2,1)} %get-tuple-element.179.refs_0_.refs_8_), channel_id=1, source_target_pairs={{0,4},{4,0},{1,5},{5,1},{2,6},{6,2},{3,7},{7,3},{8,12},{12,8},{9,1... | collective-permute-start | bytes 786440 | tf_op jit(solution)/shard_map/ppermute | solution.py:314
  636.5 33.5 %collective-permute-start.108 = (bf16[64,2048]{1,0:T(8,128)(2,1)}, bf16[64,2048]{1,0:T(8,128)(2,1)}, u32[]{:S(2)}, u32[]{:S(2)}) collective-permute-start(bf16[64,2048]{1,0:T(8,128)(2,1)} %collective-permute-done.104.refs_3_.refs_11_), channel_id=1, source_target_pairs={{0,4},{4,0},{1,5},{5,1},{2,6},{6,2},{3,7},{7,3},{8,12},{12,8},{9,1... | collective-permute-start | bytes 786440 | tf_op jit(solution)/shard_map/ppermute | solution.py:314
  665.7 34.3 %collective-permute-start.76 = (bf16[64,2048]{1,0:T(8,128)(2,1)}, bf16[64,2048]{1,0:T(8,128)(2,1)}, u32[]{:S(2)}, u32[]{:S(2)}) collective-permute-start(bf16[64,2048]{1,0:T(8,128)(2,1)} %get-tuple-element.351), channel_id=1, source_target_pairs={{0,2},{1,3},{2,0},{3,1},{4,6},{5,7},{6,4},{7,5},{8,10},{9,11},{10,... | collective-permute-start | bytes 786440 | tf_op jit(solution)/shard_map/ppermute | solution.py:314
  668.2 47.6 %collective-permute-start.75 = (bf16[64,2048]{1,0:T(8,128)(2,1)}, bf16[64,2048]{1,0:T(8,128)(2,1)}, u32[]{:S(2)}, u32[]{:S(2)}) collective-permute-start(bf16[64,2048]{1,0:T(8,128)(2,1)} %get-tuple-element.351), channel_id=1, source_target_pairs={{0,1},{1,0},{2,3},{3,2},{4,5},{5,4},{6,7},{7,6},{8,9},{9,8},{10,11... | collective-permute-start | bytes 786440 | tf_op jit(solution)/shard_map/ppermute | solution.py:314
  671.6 25.4 %collective-permute-start.144 = (bf16[256,1024]{1,0:T(8,128)(2,1)}, bf16[256,1024]{1,0:T(8,128)(2,1)}, u32[]{:S(2)}, u32[]{:S(2)}) collective-permute-start(bf16[256,1024]{1,0:T(8,128)(2,1)} %copy-done.128), channel_id=1, source_target_pairs={{0,8},{8,0},{1,9},{9,1},{2,10},{10,2},{3,11},{11,3},{4,12},{12,4},... | collective-permute-start | bytes 1572872 | tf_op jit(solution)/shard_map/ppermute | solution.py:314
  688.6 30.3 %collective-permute-start.109 = (bf16[256,2048]{1,0:T(8,128)(2,1)}, bf16[256,2048]{1,0:T(8,128)(2,1)S(1)}, u32[]{:S(2)}, u32[]{:S(2)}) collective-permute-start(bf16[256,2048]{1,0:T(8,128)(2,1)} %get-tuple-element.182), channel_id=1, source_target_pairs={{0,4},{4,0},{1,5},{5,1},{2,6},{6,2},{3,7},{7,3},{8,12},{12,8},{9,1... | collective-permute-start | bytes 3145736 | tf_op jit(solution)/shard_map/ppermute | solution.py:314
  700.1 44.0 %collective-permute-start.163 = (bf16[256,2112]{0,1:T(8,128)(2,1)}, bf16[256,2112]{0,1:T(8,128)(2,1)}, u32[]{:S(2)}, u32[]{:S(2)}) collective-permute-start(bf16[256,2112]{0,1:T(8,128)(2,1)} %copy.285), channel_id=1, source_target_pairs={{0,4},{4,0},{1,5},{5,1},{2,6},{6,2},{3,7},{7,3},{8,12},{12,8},{9,1... | collective-permute-start | bytes 3244040 | tf_op jit(solution)/shard_map/ppermute | solution.py:314
  716.8 25.3 %collective-permute-start.142 = (bf16[256,1024]{1,0:T(8,128)(2,1)}, bf16[256,1024]{1,0:T(8,128)(2,1)}, u32[]{:S(2)}, u32[]{:S(2)}) collective-permute-start(bf16[256,1024]{1,0:T(8,128)(2,1)} %add_convert_fusion.16), channel_id=1, source_target_pairs={{0,8},{8,0},{1,9},{9,1},{2,10},{10,2},{3,11},{11,3},{4,12},{12,4},... | collective-permute-start | bytes 1572872 | tf_op jit(solution)/shard_map/ppermute | solution.py:314
  718.9 46.0 %collective-permute-start.154 = (bf16[256,2112]{0,1:T(8,128)(2,1)}, bf16[256,2112]{0,1:T(8,128)(2,1)}, u32[]{:S(2)}, u32[]{:S(2)}) collective-permute-start(bf16[256,2112]{0,1:T(8,128)(2,1)} %copy.264), channel_id=1, source_target_pairs={{0,8},{8,0},{1,9},{9,1},{2,10},{10,2},{3,11},{11,3},{4,12},{12,4},... | collective-permute-start | bytes 3244040 | tf_op jit(solution)/shard_map/ppermute | solution.py:314
  730.8 42.4 %collective-permute-start.151 = (bf16[256,2112]{0,1:T(8,128)(2,1)}, bf16[256,2112]{0,1:T(8,128)(2,1)}, u32[]{:S(2)}, u32[]{:S(2)}) collective-permute-start(bf16[256,2112]{0,1:T(8,128)(2,1)} %copy.258), channel_id=1, source_target_pairs={{0,16},{16,0},{1,17},{17,1},{2,18},{18,2},{3,19},{19,3},{4,20},{20... | collective-permute-start | bytes 3244040 | tf_op jit(solution)/shard_map/ppermute | solution.py:314
  764.8 54.4 %collective-permute-start.146 = (bf16[256,1024]{1,0:T(8,128)(2,1)}, bf16[256,1024]{1,0:T(8,128)(2,1)}, u32[]{:S(2)}, u32[]{:S(2)}) collective-permute-start(bf16[256,1024]{1,0:T(8,128)(2,1)} %get-tuple-element.287), channel_id=1, source_target_pairs={{0,4},{4,0},{1,5},{5,1},{2,6},{6,2},{3,7},{7,3},{8,12},{12,8},{9,1... | collective-permute-start | bytes 1572872 | tf_op jit(solution)/shard_map/ppermute | solution.py:314
  800.0 59.1 %collective-permute-start.153 = (bf16[256,2112]{0,1:T(8,128)(2,1)}, bf16[256,2112]{0,1:T(8,128)(2,1)}, u32[]{:S(2)}, u32[]{:S(2)}) collective-permute-start(bf16[256,2112]{0,1:T(8,128)(2,1)} %copy.262), channel_id=1, source_target_pairs={{0,8},{8,0},{1,9},{9,1},{2,10},{10,2},{3,11},{11,3},{4,12},{12,4},... | collective-permute-start | bytes 3244040 | tf_op jit(solution)/shard_map/ppermute | solution.py:314
  800.9 63.2 %collective-permute-start.150 = (bf16[256,2112]{0,1:T(8,128)(2,1)}, bf16[256,2112]{0,1:T(8,128)(2,1)}, u32[]{:S(2)}, u32[]{:S(2)}) collective-permute-start(bf16[256,2112]{0,1:T(8,128)(2,1)} %copy.256), channel_id=1, source_target_pairs={{0,16},{16,0},{1,17},{17,1},{2,18},{18,2},{3,19},{19,3},{4,20},{20... | collective-permute-start | bytes 3244040 | tf_op jit(solution)/shard_map/ppermute | solution.py:314
  802.5 67.1 %collective-permute-start.155 = (bf16[256,2112]{0,1:T(8,128)(2,1)}, bf16[256,2112]{0,1:T(8,128)(2,1)}, u32[]{:S(2)}, u32[]{:S(2)}) collective-permute-start(bf16[256,2112]{0,1:T(8,128)(2,1)} %copy.266), channel_id=1, source_target_pairs={{0,16},{16,0},{1,17},{17,1},{2,18},{18,2},{3,19},{19,3},{4,20},{20... | collective-permute-start | bytes 3244040 | tf_op jit(solution)/shard_map/ppermute | solution.py:314
  803.0 69.6 %collective-permute-start.152 = (bf16[256,2112]{0,1:T(8,128)(2,1)}, bf16[256,2112]{0,1:T(8,128)(2,1)}, u32[]{:S(2)}, u32[]{:S(2)}) collective-permute-start(bf16[256,2112]{0,1:T(8,128)(2,1)} %copy.260), channel_id=1, source_target_pairs={{0,8},{8,0},{1,9},{9,1},{2,10},{10,2},{3,11},{11,3},{4,12},{12,4},... | collective-permute-start | bytes 3244040 | tf_op jit(solution)/shard_map/ppermute | solution.py:314
  819.2 30.1 %collective-permute-start.147 = (f32[2,3,256]{2,1,0:T(4,128)S(1)}, f32[2,3,256]{2,1,0:T(4,128)S(1)}, u32[]{:S(2)}, u32[]{:S(2)}) collective-permute-start(f32[2,3,256]{2,1,0:T(4,128)S(1)} %constant_dynamic-update-slice_fusion), channel_id=1, source_target_pairs={{0,8},{8,0},{1,9},{9,1},{2,10},{10,2},{3,11},{11,3},{4,12},{12,4},... | collective-permute-start | bytes 18440 | tf_op jit(solution)/shard_map/ppermute | solution.py:314
  866.5 26.2 %collective-permute-start.133 = (bf16[256,1024]{1,0:T(8,128)(2,1)}, bf16[256,1024]{1,0:T(8,128)(2,1)}, u32[]{:S(2)}, u32[]{:S(2)}) collective-permute-start(bf16[256,1024]{1,0:T(8,128)(2,1)} %get-tuple-element.206), channel_id=1, source_target_pairs={{0,16},{16,0},{1,17},{17,1},{2,18},{18,2},{3,19},{19,3},{4,20},{20... | collective-permute-start | bytes 1572872 | tf_op jit(solution)/shard_map/ppermute | solution.py:314
  877.5 26.9 %collective-permute-start.135 = (bf16[256,1024]{1,0:T(8,128)(2,1)}, bf16[256,1024]{1,0:T(8,128)(2,1)}, u32[]{:S(2)}, u32[]{:S(2)}) collective-permute-start(bf16[256,1024]{1,0:T(8,128)(2,1)} %add_convert_fusion.22), channel_id=1, source_target_pairs={{0,8},{8,0},{1,9},{9,1},{2,10},{10,2},{3,11},{11,3},{4,12},{12,4},... | collective-permute-start | bytes 1572872 | tf_op jit(solution)/shard_map/ppermute | solution.py:314
  892.5 34.3 %collective-permute-start.156 = (bf16[256,2112]{0,1:T(8,128)(2,1)}, bf16[256,2112]{0,1:T(8,128)(2,1)}, u32[]{:S(2)}, u32[]{:S(2)}) collective-permute-start(bf16[256,2112]{0,1:T(8,128)(2,1)} %copy.268), channel_id=1, source_target_pairs={{0,4},{4,0},{1,5},{5,1},{2,6},{6,2},{3,7},{7,3},{8,12},{12,8},{9,1... | collective-permute-start | bytes 3244040 | tf_op jit(solution)/shard_map/ppermute | solution.py:314
  909.0 57.2 %collective-permute-start.139 = (bf16[256,1024]{1,0:T(8,128)(2,1)}, bf16[256,1024]{1,0:T(8,128)(2,1)}, u32[]{:S(2)}, u32[]{:S(2)}) collective-permute-start(bf16[256,1024]{1,0:T(8,128)(2,1)} %get-tuple-element.284), channel_id=1, source_target_pairs={{0,4},{4,0},{1,5},{5,1},{2,6},{6,2},{3,7},{7,3},{8,12},{12,8},{9,1... | collective-permute-start | bytes 1572872 | tf_op jit(solution)/shard_map/ppermute | solution.py:314
  922.4 46.3 %collective-permute-start.125 = (bf16[64,2048]{1,0:T(8,128)(2,1)}, bf16[64,2048]{1,0:T(8,128)(2,1)}, u32[]{:S(2)}, u32[]{:S(2)}) collective-permute-start(bf16[64,2048]{1,0:T(8,128)(2,1)} %get-tuple-element.339), channel_id=1, source_target_pairs={{0,2},{1,3},{2,0},{3,1},{4,6},{5,7},{6,4},{7,5},{8,10},{9,11},{10,... | collective-permute-start | bytes 786440 | tf_op jit(solution)/shard_map/ppermute | solution.py:314
  922.4 46.2 %collective-permute-start.124 = (bf16[64,2048]{1,0:T(8,128)(2,1)}, bf16[64,2048]{1,0:T(8,128)(2,1)}, u32[]{:S(2)}, u32[]{:S(2)}) collective-permute-start(bf16[64,2048]{1,0:T(8,128)(2,1)} %get-tuple-element.339), channel_id=1, source_target_pairs={{0,1},{1,0},{2,3},{3,2},{4,5},{5,4},{6,7},{7,6},{8,9},{9,8},{10,11... | collective-permute-start | bytes 786440 | tf_op jit(solution)/shard_map/ppermute | solution.py:314
  924.4 44.3 %collective-permute-start.126 = (bf16[64,2048]{1,0:T(8,128)(2,1)}, bf16[64,2048]{1,0:T(8,128)(2,1)}, u32[]{:S(2)}, u32[]{:S(2)}) collective-permute-start(bf16[64,2048]{1,0:T(8,128)(2,1)} %get-tuple-element.339), channel_id=1, source_target_pairs={{0,3},{1,2},{2,1},{3,0},{4,7},{5,6},{6,5},{7,4},{8,11},{9,10},{10,... | collective-permute-start | bytes 786440 | tf_op jit(solution)/shard_map/ppermute | solution.py:314
  972.7 27.7 %collective-permute-start.127 = (bf16[128,2048]{1,0:T(8,128)(2,1)}, bf16[128,2048]{1,0:T(8,128)(2,1)}, u32[]{:S(2)}, u32[]{:S(2)}) collective-permute-start(bf16[128,2048]{1,0:T(8,128)(2,1)} %bitcast.72), channel_id=1, source_target_pairs={{0,8},{8,0},{1,9},{9,1},{2,10},{10,2},{3,11},{11,3},{4,12},{12,4},... | collective-permute-start | bytes 1572872 | tf_op jit(solution)/shard_map/ppermute | solution.py:314
  (361 other events, 3806.6 us)

commit v3 on v2

--- a/solution.py
+++ b/solution.py
@@ -17,7 +17,7 @@
 LOW = jnp.bfloat16
 F32 = jnp.float32
 VMEM_LIMIT = 44 * 1024 * 1024
-ANY = pl.BlockSpec(memory_space=pl.ANY)
+HBM = pl.BlockSpec(memory_space=pltpu.HBM)
 VMEM = pl.BlockSpec(memory_space=pltpu.VMEM)
 
 
@@ -41,14 +41,14 @@
     return jax.ShapeDtypeStruct(dims, kind)
 
 
-def call(body, n_any, args, outs, scratch, flops):
+def call(body, n_hbm, args, outs, scratch, flops, hbm_outs=0):
     moved = sum(a.size * a.dtype.itemsize for a in args)
     moved += sum(math.prod(o.shape) * jnp.dtype(o.dtype).itemsize for o in outs)
     return pl.pallas_call(
         body,
         out_shape=tuple(outs),
-        in_specs=[ANY] * n_any + [VMEM] * (len(args) - n_any),
-        out_specs=tuple([VMEM] * len(outs)),
+        in_specs=[HBM] * n_hbm + [VMEM] * (len(args) - n_hbm),
+        out_specs=tuple([HBM] * hbm_outs + [VMEM] * (len(outs) - hbm_outs)),
         scratch_shapes=scratch,
         compiler_params=pltpu.CompilerParams(vmem_limit_bytes=VMEM_LIMIT),
         cost_estimate=pl.CostEstimate(flops=flops, bytes_accessed=moved, transcendentals=0),
@@ -66,6 +66,17 @@
     return copies
 
 
+def weights_into(pieces, whole, sems, first):
+    me = lax.axis_index("clo")
+    copies = []
+    for i, piece in enumerate(pieces):
+        rows = piece.shape[0]
+        at = (i // 2 * 2) * rows + (me ^ (i % 2)) * rows
+        to = whole.at[pl.ds(pl.multiple_of(at, rows), rows)]
+        copies.append(pltpu.make_async_copy(piece, to, sems.at[first + i]))
+    return copies
+
+
 def start_all(copies):
     for c in copies:
         c.start()
@@ -76,15 +87,19 @@
         c.wait()
 
 
-def rolled(value, cos_t, sa, sb, sign):
-    width = value.shape[1]
-    ahead = pltpu.roll(value, width - ROT // 2, 1)
-    behind = pltpu.roll(value, ROT // 2, 1)
-    return value * cos_t + sign * (ahead * sa + behind * sb)
-
-
-def allowed_of(pc, sc, pr, sr):
-    return (sc == sr) & (pr <= pc)
+def rolled(value, tables, sign):
+    cos_t, ahead_t, behind_t = tables[0], tables[1], tables[2]
+    slabs = []
+    for at in range(0, value.shape[1], 128):
+        x = value[:, at : at + 128]
+        ahead = pltpu.roll(x, 128 - ROT // 2, 1)
+        behind = pltpu.roll(x, ROT // 2, 1)
+        slabs.append(x * cos_t + sign * (ahead * ahead_t + behind * behind_t))
+    return jnp.concatenate(slabs, axis=1).astype(LOW)
+
+
+def allowed_of(column, row):
+    return (column[:, 0:1] == row[0:1]) & (row[1:2] <= column[:, 1:2])
 
 
 def put_halves(tile, cols, own_ref, send_ref):
@@ -100,28 +115,41 @@
     return e / jnp.sum(e, axis=-1, keepdims=True)
 
 
+def load(pairs, sems, first):
+    return [
+        pltpu.make_async_copy(src, dst, sems.at[first + i]) for i, (src, dst) in enumerate(pairs)
+    ]
+
+
+def block_rows(w_s, n_w, w_copies=None):
+    block = w_s.shape[0] // (n_w // 2)
+    for r in range(n_w // 2):
+        if w_copies is not None:
+            wait_all(w_copies[2 * r : 2 * r + 2])
+        yield r, slice(r * block, (r + 1) * block)
+
+
 def attn_forward(n_h, n_w, heads, *refs):
     h_parts, w_parts, refs = refs[:n_h], refs[n_h : n_h + n_w], refs[n_h + n_w :]
-    bias, pc, sc, pr, sr, cos_t, sa, sb = refs[:8]
-    q_o, k_o, v_o, o_o, own_o, send_o, h_s, w_s, acc, sems = refs[8:]
+    tables, column, row, bias = refs[:4]
+    q_o, k_o, v_o, o_o, own_o, send_o, h_s, w_s, acc, tab, col, sems = refs[4:]
     width = heads * HEAD
     copies = into_rows(h_parts, h_s, sems, 0)
-    w_copies = into_rows(w_parts, w_s, sems, n_h)
-    start_all(copies + w_copies)
+    w_copies = weights_into(w_parts, w_s, sems, n_h)
+    extra = load([(tables, tab), (column, col)], sems, n_h + n_w)
+    start_all(copies + w_copies + extra)
     wait_all(copies)
-    block = w_s.shape[0] // (n_w // 2)
-    for r in range(n_w // 2):
-        wait_all(w_copies[2 * r : 2 * r + 2])
-        rows = slice(r * block, (r + 1) * block)
+    for r, rows in block_rows(w_s, n_w, w_copies):
         for c in range(3):
             cols = slice(c * width, (c + 1) * width)
             part = nn(h_s[:, rows], w_s[rows, cols])
             acc[:, cols] = part + (bias[:, cols] if r == 0 else acc[:, cols])
-    q_o[...] = rolled(acc[:, :width], cos_t[...], sa[...], sb[...], 1.0).astype(LOW)
-    k_o[...] = rolled(acc[:, width : 2 * width], cos_t[...], sa[...], sb[...], 1.0).astype(LOW)
+    wait_all(extra)
+    q_o[...] = rolled(acc[:, :width], tab, 1.0)
+    k_o[...] = rolled(acc[:, width : 2 * width], tab, 1.0)
     v_o[...] = acc[:, 2 * width :].astype(LOW)
     lane = lax.broadcasted_iota(jnp.int32, (1, width), 1) // HEAD
-    allowed = allowed_of(pc[...], sc[...], pr[...], sr[...])
+    allowed = allowed_of(col, row)
     k, v, q = k_o[...], v_o[...], q_o[...]
     zero = jnp.zeros((), LOW)
     o = None
@@ -132,30 +160,32 @@
         o = part if o is None else o + part
     o_o[...] = o.astype(LOW)
     o = o_o[...]
-    for r in range(n_w // 2):
-        rows = slice(r * block, (r + 1) * block)
+    for r, rows in block_rows(w_s, n_w):
         put_halves(nt(o, w_s[rows, 3 * width :]), rows, own_o, send_o)
 
 
 def attn_backward(n_h, n_w, heads, *refs):
     d_parts, w_parts, refs = refs[:n_h], refs[n_h : n_h + n_w], refs[n_h + n_w :]
-    q_i, k_i, v_i, pc, sc, pr, sr, cos_t, sa, sb = refs[:10]
-    dp_o, bias_o, own_o, send_o, d_s, w_s, acc, sems = refs[10:]
+    q_i, k_i, v_i, tables, column, row = refs[:6]
+    dp_o, bias_o, own_o, send_o, d_s, w_s, acc, qkv, tab, col, sems = refs[6:]
     width = heads * HEAD
     copies = into_rows(d_parts, d_s, sems, 0)
-    w_copies = into_rows(w_parts, w_s, sems, n_h)
-    start_all(copies + w_copies)
+    w_copies = weights_into(w_parts, w_s, sems, n_h)
+    extra = load(
+        [(q_i, qkv.at[0]), (k_i, qkv.at[1]), (v_i, qkv.at[2]), (tables, tab), (column, col)],
+        sems,
+        n_h + n_w,
+    )
+    start_all(copies + w_copies + extra)
     wait_all(copies)
-    block = w_s.shape[0] // (n_w // 2)
-    for r in range(n_w // 2):
-        wait_all(w_copies[2 * r : 2 * r + 2])
-        rows = slice(r * block, (r + 1) * block)
+    for r, rows in block_rows(w_s, n_w, w_copies):
         part = nn(d_s[:, rows], w_s[rows, 3 * width :])
         acc[...] = part if r == 0 else acc[...] + part
     do = acc[...].astype(LOW)
-    q, k, v = q_i[...], k_i[...], v_i[...]
+    wait_all(extra)
+    q, k, v = qkv[0], qkv[1], qkv[2]
     lane = lax.broadcasted_iota(jnp.int32, (1, width), 1) // HEAD
-    allowed = allowed_of(pc[...], sc[...], pr[...], sr[...])
+    allowed = allowed_of(col, row)
     zero = jnp.zeros((), LOW)
     scale = 1.0 / math.sqrt(HEAD)
     dq = dk = dv = None
@@ -172,19 +202,13 @@
         dq, dk, dv = (
             (dq_h, dk_h, dv_h) if h == 0 else (dq + dq_h, dk + dk_h, dv + dv_h)
         )
-    dp_o[:, :width] = rolled(dq * scale, cos_t[...], sa[...], sb[...], -1.0).astype(LOW)
-    dp_o[:, width : 2 * width] = rolled(
-        dk * scale, cos_t[...], sa[...], sb[...], -1.0
-    ).astype(LOW)
+    dp_o[:, :width] = rolled(dq * scale, tab, -1.0)
+    dp_o[:, width : 2 * width] = rolled(dk * scale, tab, -1.0)
     dp_o[:, 2 * width :] = dv.astype(LOW)
-    bias_o[...] = jnp.sum(dp_o[...].astype(F32), axis=0, keepdims=True)
-    for r in range(n_w // 2):
-        rows = slice(r * block, (r + 1) * block)
-        put_halves(nt(dp_o[...], w_s[rows, : 3 * width]), rows, own_o, send_o)
-
-
-def to_front(value, units):
-    return value[:, units : 2 * units]
+    dp = dp_o[...]
+    bias_o[...] = jnp.sum(dp.astype(F32), axis=0, keepdims=True)
+    for r, rows in block_rows(w_s, n_w):
+        put_halves(nt(dp, w_s[rows, : 3 * width]), rows, own_o, send_o)
 
 
 def mlp_forward(n_h, n_w, *refs):
@@ -192,68 +216,82 @@
     gu_o, z_o, own_o, send_o, h_s, w_s, sems = refs
     units = z_o.shape[1]
     copies = into_rows(h_parts, h_s, sems, 0)
-    w_copies = into_rows(w_parts, w_s, sems, n_h)
+    w_copies = weights_into(w_parts, w_s, sems, n_h)
     start_all(copies + w_copies)
     wait_all(copies)
-    block = w_s.shape[0] // (n_w // 2)
-    for r in range(n_w // 2):
-        wait_all(w_copies[2 * r : 2 * r + 2])
-        rows = slice(r * block, (r + 1) * block)
+    for r, rows in block_rows(w_s, n_w, w_copies):
         part = nn(h_s[:, rows], w_s[rows, : 2 * units])
         gu_o[...] = part if r == 0 else gu_o[...] + part
     g = gu_o[:, :units]
-    u = to_front(gu_o, units)
+    u = gu_o[:, units:]
     z_o[...] = (g * u / (1.0 + jnp.exp(-g))).astype(LOW)
     z = z_o[...]
-    for r in range(n_w // 2):
-        rows = slice(r * block, (r + 1) * block)
-        put_halves(nt(z, w_s[rows, 2 * units :]), rows, own_o, send_o)
+    for r, rows in block_rows(w_s, n_w):
+        put_halves(nt(z, w_s[rows, 2 * units : 3 * units]), rows, own_o, send_o)
 
 
 def mlp_backward(n_h, n_w, *refs):
     d_parts, w_parts, refs = refs[:n_h], refs[n_h : n_h + n_w], refs[n_h + n_w :]
-    gu_i, dp_o, own_o, send_o, d_s, w_s, acc, sems = refs
+    gu_i, dp_o, own_o, send_o, d_s, w_s, acc, gu, sems = refs
     units = acc.shape[1]
     copies = into_rows(d_parts, d_s, sems, 0)
-    w_copies = into_rows(w_parts, w_s, sems, n_h)
-    start_all(copies + w_copies)
+    w_copies = weights_into(w_parts, w_s, sems, n_h)
+    extra = load([(gu_i, gu)], sems, n_h + n_w)
+    start_all(copies + w_copies + extra)
     wait_all(copies)
-    block = w_s.shape[0] // (n_w // 2)
-    for r in range(n_w // 2):
-        wait_all(w_copies[2 * r : 2 * r + 2])
-        rows = slice(r * block, (r + 1) * block)
-        part = nn(d_s[:, rows], w_s[rows, 2 * units :])
+    for r, rows in block_rows(w_s, n_w, w_copies):
+        part = nn(d_s[:, rows], w_s[rows, 2 * units : 3 * units])
         acc[...] = part if r == 0 else acc[...] + part
-    g = gu_i[:, :units]
-    u = to_front(gu_i, units)
+    wait_all(extra)
+    g = gu[:, :units]
+    u = gu[:, units:]
     sig = 1.0 / (1.0 + jnp.exp(-g))
     dz = acc[...]
     dp_o[:, :units] = (dz * u * sig * (1.0 + g * (1.0 - sig))).astype(LOW)
     dp_o[:, units:] = (dz * g * sig).astype(LOW)
     dp = dp_o[...]
-    for r in range(n_w // 2):
-        rows = slice(r * block, (r + 1) * block)
+    for r, rows in block_rows(w_s, n_w):
         put_halves(nt(dp, w_s[rows, : 2 * units]), rows, own_o, send_o)
 
 
 def weight_grads(n_h, n_w, *refs):
     a_parts, b_parts, refs = refs[:n_h], refs[n_h : 2 * n_h], refs[2 * n_h :]
-    da, db = refs[:2]
-    outs, (a_s, b_s, sems) = refs[2 : 2 + n_w], refs[2 + n_w :]
+    da_i, db_i = refs[:2]
+    outs, (a_s, b_s, da_s, db_s, sems) = refs[2 : 2 + n_w], refs[2 + n_w :]
     copies = into_rows(a_parts, a_s, sems, 0) + into_rows(b_parts, b_s, sems, n_h)
+    copies += load([(da_i, da_s), (db_i, db_s)], sems, 2 * n_h)
     start_all(copies)
     wait_all(copies)
     block = a_s.shape[1] // (n_w // 2)
     half = block // 2
-    split = da.shape[1]
+    split, end = da_s.shape[1], da_s.shape[1] + db_s.shape[1]
+    swapped = lax.axis_index("clo") == 1
     for r in range(n_w // 2):
         cols = slice(r * block, (r + 1) * block)
-        first = tn(a_s[:, cols], da[...]).astype(LOW)
-        second = tn(b_s[:, cols], db[...]).astype(LOW)
+        first = tn(a_s[:, cols], da_s[...]).astype(LOW)
+        second = tn(b_s[:, cols], db_s[...]).astype(LOW)
         for i in range(2):
-            rows = slice(i * half, (i + 1) * half)
-            outs[2 * r + i][:, :split] = first[rows]
-            outs[2 * r + i][:, split:] = second[rows]
+            here, there = slice(i * half, (i + 1) * half), slice((1 - i) * half, (2 - i) * half)
+            out = outs[2 * r + i]
+            out[:, :split] = jnp.where(swapped, first[there], first[here])
+            out[:, split:end] = jnp.where(swapped, second[there], second[here])
+            if end < out.shape[1]:
+                out[:, end:] = jnp.zeros((half, out.shape[1] - end), LOW)
+
+
+def cut_columns(*refs):
+    qkv, out, keep, send, sems = refs
+    width = keep.shape[1] // 4
+    me = lax.axis_index("clo")
+    copies = []
+    for to, core in ((keep, me), (send, 1 - me)):
+        cols = pl.ds(pl.multiple_of(core * width, 128), width)
+        for c in range(4):
+            src = out.at[:, cols] if c == 3 else qkv.at[c, :, cols]
+            dst = to.at[:, pl.ds(c * width, width)]
+            copies.append(pltpu.make_async_copy(src, dst, sems.at[len(copies)]))
+    start_all(copies)
+    wait_all(copies)
 
 
 def middle(own_i, moved_i, own_o, *sends):
@@ -322,12 +360,8 @@
         ]
         return jnp.concatenate(parts, axis=-1)
 
-    def gather_weights(low_cols, high_cols):
-        odd = lax.axis_index("clo") == 1
-        keep = jnp.where(odd, high_cols, low_cols)
-        other = swap(jnp.where(odd, low_cols, high_cols), "clo", 1)
-        a = {0: jnp.where(odd, other, keep)}
-        b = {0: jnp.where(odd, keep, other)}
+    def gather_weights(keep, send):
+        a, b = {0: keep}, {0: swap(send, "clo", 1)}
         for ka, kb in zip(up_order, down_order):
             for have, k in ((a, ka), (b, kb)):
                 fresh = {r | (1 << k): swap(have[r], *group_bits[k]) for r in list(have)}
@@ -342,10 +376,7 @@
                     moved = swap(have.pop(r), *group_bits[k])
                     to = r ^ (1 << k)
                     have[to] = (have[to].astype(F32) + moved.astype(F32)).astype(LOW)
-        odd = lax.axis_index("clo") == 1
-        keep = jnp.where(odd, b[0], a[0])
-        other = swap(jnp.where(odd, a[0], b[0]), "clo", 1)
-        return jnp.where(odd, other, keep), jnp.where(odd, keep, other)
+        return a[0], swap(b[0], "clo", 1)
 
     def token_gather(own):
         half = [own] + [swap(own, "mp", r) for r in range(1, n_mp)]
@@ -397,29 +428,36 @@
         sub = half_total // n_mp
         n_parts = n_clo * n_mp
         mp, clo, chi = (lax.axis_index(a) for a in ("mp", "clo", "chi"))
-        attn_cols, mlp_cols = 4 * half_in, 3 * half_ff
-
         x_own = relative(own_tokens(tokens)).astype(F32)
 
-        def halves(l, which):
-            lo, hi = (slice(None, half_in), slice(half_in, None)), (
-                slice(None, half_ff),
-                slice(half_ff, None),
+        pad = -(3 * half_ff) % 128
+        attn_cols, mlp_cols = 4 * half_in, 3 * half_ff + pad
+
+        def attn_columns(l):
+            view = jnp.transpose(qkv_weight[l], (1, 0, 2))
+            outs = [shape((rows_dev, attn_cols), LOW)] * 2
+            return call(
+                cut_columns, 2, [view, out_weight[l]], outs,
+                [pltpu.SemaphoreType.DMA((8,))], 0, hbm_outs=2,
             )
-            out = []
-            for i in range(2):
-                if which == 0:
-                    parts = [qkv_weight[l, :, c, lo[i]] for c in range(3)]
-                    parts.append(out_weight[l, :, lo[i]])
-                else:
-                    parts = [gate_up_weight[l, :, c, hi[i]] for c in range(2)]
-                    parts.append(down_weight[l, :, hi[i]])
-                out.append(jnp.concatenate(parts, axis=1))
-            return out
-
-        weights = [
-            (gather_weights(*halves(l, 0)), gather_weights(*halves(l, 1))) for l in range(LAYERS)
-        ]
+
+        def mlp_columns(l):
+            gu, down = jnp.transpose(gate_up_weight[l], (1, 0, 2)), down_weight[l]
+            low = [gu[0, :, :half_ff], gu[1, :, :half_ff], down[:, :half_ff]]
+            high = [gu[0, :, half_ff:], gu[1, :, half_ff:], down[:, half_ff:]]
+            fill = [jnp.zeros((rows_dev, pad), LOW)] if pad else []
+            low, high = jnp.concatenate(low + fill, axis=1), jnp.concatenate(high + fill, axis=1)
+            return jnp.where(clo == 1, high, low), jnp.where(clo == 1, low, high)
+
+        weights = [[None, None] for l in range(LAYERS)]
+        ready = None
+        for l in range(LAYERS):
+            for i, columns_of in enumerate((attn_columns, mlp_columns)):
+                keep, send = columns_of(l)
+                if ready is not None:
+                    keep, send, _ = lax.optimization_barrier((keep, send, ready))
+                weights[l][i] = gather_weights(keep, send)
+                ready = weights[l][i][2]
         dx = relative(own_tokens(cotangent))
         gains = relative(jnp.stack([first_gain, first_bias, second_gain, second_bias]))
         half_bias = jnp.where(clo == 1, qkv_bias[:, :, half_in:], qkv_bias[:, :, :half_in])
@@ -450,20 +488,28 @@
         cos_t, sin_t = jnp.cos(angles).T, jnp.sin(angles).T
         zeros = jnp.zeros((total, ROT // 2), F32)
         tail = jnp.zeros((total, HEAD - ROT), F32)
-        tables = [
-            jnp.tile(jnp.concatenate(parts, axis=1), (1, heads))
-            for parts in (
-                (cos_t, cos_t, tail + 1.0),
-                (-sin_t, zeros, tail),
-                (zeros, sin_t, tail),
-            )
+        per_slab = 128 // HEAD
+        tables = jnp.stack(
+            [
+                jnp.tile(jnp.concatenate(parts, axis=1), (1, per_slab))
+                for parts in (
+                    (cos_t, cos_t, tail + 1.0),
+                    (-sin_t, zeros, tail),
+                    (zeros, sin_t, tail),
+                )
+            ]
+        )
+        row = jnp.stack([seg, place])
+        geometry = [tables, row.T, row]
+        geometry_scratch = [
+            pltpu.VMEM((3, total, 128), F32),
+            pltpu.VMEM((total, 2), jnp.int32),
         ]
-        geometry = [place[:, None], seg[:, None], place[None, :], seg[None, :]] + tables
 
         act = shape((total, half_in), LOW)
         reduced = [shape((half_total, width), F32), shape((half_total, width), LOW)]
         n_w = n_pieces
-        sems = pltpu.SemaphoreType.DMA((n_parts + n_w,))
+        sems = pltpu.SemaphoreType.DMA((n_parts + n_w + 5,))
         h_scratch = pltpu.VMEM((total, width), LOW)
 
         def mm(*dims):
@@ -481,10 +527,16 @@
             outs = [shape((width // n_w, cols), LOW)] * n_w
             return call(
                 functools.partial(weight_grads, n_parts, n_w),
-                2 * n_parts,
+                2 * n_parts + 2,
                 a_parts + b_parts + [da, db],
                 outs,
-                [h_scratch, h_scratch, pltpu.SemaphoreType.DMA((2 * n_parts,))],
+                [
+                    h_scratch,
+                    h_scratch,
+                    pltpu.VMEM(da.shape, LOW),
+                    pltpu.VMEM(db.shape, LOW),
+                    pltpu.SemaphoreType.DMA((2 * n_parts + 2,)),
+                ],
                 mm(total, width, cols),
             )
 
@@ -496,15 +548,16 @@
             h1 = token_gather(h)
             q, k, v, o, own, send = call(
                 functools.partial(attn_forward, n_parts, n_w, heads),
-                n_parts + n_w,
-                h1 + w_attn + [half_bias[l]] + geometry,
+                n_parts + n_w + 2,
+                h1 + w_attn + geometry + [half_bias[l]],
                 [act] * 4 + reduced,
                 [
                     h_scratch,
                     pltpu.VMEM((width, attn_cols), LOW),
                     pltpu.VMEM((total, 3 * half_in), F32),
-                    sems,
-                ],
+                ]
+                + geometry_scratch
+                + [sems],
                 mm(total, width, attn_cols) + 2 * mm(heads, total, total, 2 * half_in),
             )
             y_own, h = norm(x_own, gains[2, l], gains[3, l], token_reduce(own, send))
@@ -533,13 +586,14 @@
             dm = token_gather(low)
             dp2, own, send = call(
                 functools.partial(mlp_backward, n_parts, n_w),
-                n_parts + n_w,
+                n_parts + n_w + 1,
                 dm + w_mlp + [gu],
                 [shape((total, 2 * half_ff), LOW)] + reduced,
                 [
                     h_scratch,
                     pltpu.VMEM((width, mlp_cols), LOW),
                     pltpu.VMEM((total, half_ff), F32),
+                    pltpu.VMEM(gu.shape, F32),
                     sems,
                 ],
                 mm(total, width, mlp_cols),
@@ -550,15 +604,17 @@
             da = token_gather(low)
             dp1, bias_grad, own, send = call(
                 functools.partial(attn_backward, n_parts, n_w, heads),
-                n_parts + n_w,
+                n_parts + n_w + 5,
                 da + w_attn + [q, k, v] + geometry,
                 [shape((total, 3 * half_in), LOW), shape((1, 3 * half_in), F32)] + reduced,
                 [
                     h_scratch,
                     pltpu.VMEM((width, attn_cols), LOW),
                     pltpu.VMEM((total, half_in), F32),
-                    sems,
-                ],
+                    pltpu.VMEM((3, total, half_in), LOW),
+                ]
+                + geometry_scratch
+                + [sems],
                 mm(total, width, attn_cols) + 5 * mm(heads, total, total, half_in),
             )
             terms = token_reduce(own, send)
@@ -586,11 +642,13 @@
         def columns(which, first, count, parts):
             layers = []
             for l in range(LAYERS):
-                pieces = [
+                mine, others = (
                     piece[:, first : first + count].reshape((rows_dev,) + parts + (-1,))
                     for piece in weight_out[l][which]
-                ]
-                layers.append(jnp.concatenate(pieces, axis=-1).astype(F32))
+                )
+                low = jnp.where(clo == 0, mine, others)
+                high = jnp.where(clo == 0, others, mine)
+                layers.append(jnp.concatenate([low, high], axis=-1).astype(F32))
             return jnp.stack(layers)
 
         return (

time: 1020 us -> 879 us (0.86)
  local copies, waits for them, and re-layouts: 262 us -> 101 us
  waiting for transfers between devices: 357 us -> 434 us
  other arithmetic: 75.6 us -> 54.8 us
  Pallas kernels: 129 us -> 114 us
  starting transfers between devices: 177 us -> 165 us
    ppermute x164, waiting for transfers between devices: 357 us -> 434 us  [swap(): return lax.ppermute(value, axis, [(i, i ^ bit) for i in range(sizes[axis])])]
    ppermute x28 -> x0, local copies, waits for them, and re-layouts: 66.3 us -> none  [swap(): return lax.ppermute(value, axis, [(i, i ^ bit) for i in range(sizes[axis])])]
    unnamed x536 -> x522, local copies, waits for them, and re-layouts: 111 us -> 62.8 us
    select_n x15 -> x4, other arithmetic: 32.6 us -> 4.48 us  [the longest x2 2.98 us: mlp_columns(): return (jnp.where(clo == 1, high, low), jnp.where(clo == 1, low, high))]
    pallas_call x8 -> x0, local copies, waits for them, and re-layouts: 18.3 us -> none  [call(): pl.pallas_call(body, out_shape=tuple(outs), in_specs=[ANY] * n_any + [VME...]
    pallas_call x28 -> x30, Pallas kernels: 129 us -> 114 us  [call(): pl.pallas_call(body, out_shape=tuple(outs), in_specs=[HBM] * n_hbm + [VME...]
    slice x17 -> x3, local copies, waits for them, and re-layouts: 17.3 us -> 4.84 us  [the longest x1 2.88 us: mlp_columns(): gu, down = (jnp.transpose(gate_up_weight[l], (1, 0, 2)), down_weight[l])]
    ppermute x164, starting transfers between devices: 177 us -> 165 us  [swap(): return lax.ppermute(value, axis, [(i, i ^ bit) for i in range(sizes[axis])])]
  transfers between devices with their start and end apart: 164 -> 164, of which waited for: 47 -> 56; matrix products, arithmetic and copies ran while one was open for 24% -> 12% of each run, Pallas kernels for 12% -> 11%
where the time goes in v3:
time: 879 us; the launch traced here: 872 us
  waiting for transfers between devices  434 us (49%)
  starting transfers between devices  165 us (19%)
  Pallas kernels  114 us (13%)
  local copies, waits for them, and re-layouts  101 us (11%)
  other arithmetic  54.8 us (6%)
    ppermute x164, waiting for transfers between devices, swap(): return lax.ppermute(value, axis, [(i, i ^ bit) for i in range(sizes[axis])])  434 us
    ppermute x164, starting transfers between devices, swap(): return lax.ppermute(value, axis, [(i, i ^ bit) for i in range(sizes[axis])])  165 us
    pallas_call x30, Pallas kernels, call(): pl.pallas_call(body, out_shape=tuple(outs), in_specs=[HBM] * n_hbm + [VME...  114 us
    unnamed x522, local copies, waits for them, and re-layouts  62.8 us
    convert_element_type x16, other arithmetic, spread(): have[to] = (have[to].astype(F32) + moved.astype(F32)).astype(LOW)  20 us
  transfers between devices with their start and end apart: 164, of which 56 were waited for; matrix products, arithmetic and copies ran while one was open for 12% of the time, Pallas kernels for 11%

profile of v3, /device:TPU:0, one launch (start us, length us, event | category | flops | bytes accessed | tf_op | source)
XLA Modules:
  0.0 872.2 jit_solution(13146892676266935836)
XLA Ops:
  31.3 3.7 collective-permute-start.3
  38.3 4.1 collective-permute-done.3.refs_3_
  42.4 10.9 %collective-permute-start.1 = (bf16[64,2048]{1,0:T(8,128)(2,1)S(1)}, bf16[64,2048]{1,0:T(8,128)(2,1)}, u32[]{:S(2)}, u32[]{:S(2)}) collective-permute-start(bf16[64,2048]{1,0:T(8,128)(2,1)S(1)} %get-tuple-element.139.refs_0_), channel_id=1, source_target_pairs={{0,1},{1,0},{2,3},{3,2},{4,5},{5,4},{6,7},{7,6},{8,9},{9,8},{10,11... | collective-permute-start | bytes 786440 | tf_op jit(solution)/shard_map/ppermute | solution.py:352
  54.0 3.7 collective-permute-done.2.refs_2_
  59.8 3.5 collective-permute-done.1.refs_1_
  79.2 11.2 %collective-permute-done.14.refs_15_ = bf16[256,1024]{1,0:T(8,128)(2,1)} collective-permute-done((bf16[256,1024]{1,0:T(8,128)(2,1)}, bf16[256,1024]{1,0:T(8,128)(2,1)}, u32[]{:S(2)}, u32[]{:S(2)}) %collective-permute-start.14) | collective-permute-done | bytes 524320 | tf_op jit(solution)/shard_map/ppermute | solution.py:352
  92.4 9.3 %shard_map.205 = (bf16[512,256]{1,0:T(8,128)(2,1)S(1)}, bf16[512,256]{1,0:T(8,128)(2,1)S(1)}, bf16[512,256]{1,0:T(8,128)(2,1)S(1)}, bf16[512,256]{1,0:T(8,128)(2...) custom-call(bf16[64,2048]{1,0:T(8,128)(2,1)S(1)} %copy-done.77, ...), custom_call_target="tpu_custom_call" | custom-call | flops 4294967296 | bytes 11283456 | tf_op jit(solution)/shard_map/pallas_call | solution.py:47
  104.5 9.7 %collective-permute-done.29.refs_10_ = bf16[256,2176]{1,0:T(8,128)(2,1)S(1)} collective-permute-done((bf16[256,2176]{1,0:T(8,128)(2,1)S(1)}, bf16[256,2176]{1,0:T(8,128)(2,1)S(1)}, u32[]{:S(2)}, u32[]{:S(2)}) %collective-permute-start.29) | collective-permute-done | bytes 1114144 | tf_op jit(solution)/shard_map/ppermute | solution.py:352
  117.6 11.8 %collective-permute-done.32.refs_13_ = bf16[256,2176]{1,0:T(8,128)(2,1)S(1)} collective-permute-done((bf16[256,2176]{1,0:T(8,128)(2,1)}, bf16[256,2176]{1,0:T(8,128)(2,1)S(1)}, u32[]{:S(2)}, u32[]{:S(2)}) %collective-permute-start.32) | collective-permute-done | bytes 1114144 | tf_op jit(solution)/shard_map/ppermute | solution.py:352
  130.4 13.0 %collective-permute-done.19.refs_2_ = bf16[64,2048]{1,0:T(8,128)(2,1)S(1)} collective-permute-done((bf16[64,2048]{1,0:T(8,128)(2,1)S(1)}, bf16[64,2048]{1,0:T(8,128)(2,1)S(1)}, u32[]{:S(2)}, u32[]{:S(2)}) %collective-permute-start.19) | collective-permute-done | bytes 262176 | tf_op jit(solution)/shard_map/ppermute | solution.py:352
  145.0 8.6 collective-permute-done.20.refs_3_
  158.4 18.3 %collective-permute-done.33.refs_14_ = bf16[256,2176]{1,0:T(8,128)(2,1)S(1)} collective-permute-done((bf16[256,2176]{1,0:T(8,128)(2,1)S(1)}, bf16[256,2176]{1,0:T(8,128)(2,1)S(1)}, u32[]{:S(2)}, u32[]{:S(2)}) %collective-permute-start.33) | collective-permute-done | bytes 1114144 | tf_op jit(solution)/shard_map/ppermute | solution.py:352
  183.0 8.7 shard_map.208
  199.1 3.5 concatenate.168
  209.7 7.4 collective-permute-done.47.refs_10_
  221.8 7.0 collective-permute-done.37.refs_2_
  229.8 3.7 collective-permute-done.49.refs_12_
  236.3 7.7 collective-permute-done.51.refs_14_
  245.9 12.0 %collective-permute-done.40.refs_2_ = bf16[64,2048]{1,0:T(8,128)(2,1)S(1)} collective-permute-done((bf16[64,2048]{1,0:T(8,128)(2,1)S(1)}, bf16[64,2048]{1,0:T(8,128)(2,1)S(1)}, u32[]{:S(2)}, u32[]{:S(2)}) %collective-permute-start.40) | collective-permute-done | bytes 262176 | tf_op jit(solution)/shard_map/ppermute | solution.py:352
  261.4 9.3 %shard_map.212 = (bf16[512,256]{1,0:T(8,128)(2,1)S(1)}, bf16[512,256]{1,0:T(8,128)(2,1)S(1)}, bf16[512,256]{1,0:T(8,128)(2,1)S(1)}, bf16[512,256]{1,0:T(8,128)(2...) custom-call(bf16[64,2048]{1,0:T(8,128)(2,1)S(1)} %get-tuple-element.159.refs_0_, ...), custom_call_target="tpu_custom_call" | custom-call | flops 4294967296 | bytes 11283456 | tf_op jit(solution)/shard_map/pallas_call | solution.py:47
  275.4 8.7 collective-permute-done.82.refs_3_.refs_11_
  287.4 9.7 %collective-permute-done.81.refs_2_.refs_10_ = bf16[64,2048]{1,0:T(8,128)(2,1)S(1)} collective-permute-done((bf16[64,2048]{1,0:T(8,128)(2,1)S(1)}, bf16[64,2048]{1,0:T(8,128)(2,1)S(1)}, u32[]{:S(2)}, u32[]{:S(2)}) %collective-permute-start.81) | collective-permute-done | bytes 262176 | tf_op jit(solution)/shard_map/ppermute | solution.py:352
  300.6 7.1 collective-permute-done.54.refs_1_
  309.3 4.3 collective-permute-done.55.refs_2_
  314.1 7.8 collective-permute-done.56.refs_3_
  334.4 5.1 collective-permute-done.59.refs_3_
  339.6 12.2 %collective-permute-done.58.refs_2_ = bf16[64,2048]{1,0:T(8,128)(2,1)S(1)} collective-permute-done((bf16[64,2048]{1,0:T(8,128)(2,1)S(1)}, bf16[64,2048]{1,0:T(8,128)(2,1)S(1)}, u32[]{:S(2)}, u32[]{:S(2)}) %collective-permute-start.58) | collective-permute-done | bytes 262176 | tf_op jit(solution)/shard_map/ppermute | solution.py:352
  353.7 8.5 shard_map.215
  364.8 9.3 %shard_map.217 = (bf16[512,1408]{1,0:T(8,128)(2,1)}, f32[256,2048]{1,0:T(8,128)}, bf16[256,2048]{1,0:T(8,128)(2,1)S(1)}) custom-call(bf16[64,2048]{1,0:T(8,128)(2,1)S(1)} %get-tuple-element.337.refs_0_.refs_8_, bf16[64,2048]{1,0:T(8,128)(2,1)S(1)} %collective-permute-done.80.refs_1_.refs_9_, bf16[64,2048]{1,0:T(8,128)(2,1)S(1)} %collective-permute-done.81.refs_2_.refs_10_, ...), custom_call_target="tpu_custom_call" | custom-call | flops 4563402752 | bytes 18481152 | tf_op jit(solution)/shard_map/pallas_call | solution.py:47
  390.0 6.5 collective-permute-done.88.refs_1_
  404.1 8.5 shard_map.232
  413.6 15.5 %collective-permute-done.89.refs_2_ = bf16[64,2048]{1,0:T(8,128)(2,1)S(1)} collective-permute-done((bf16[64,2048]{1,0:T(8,128)(2,1)}, bf16[64,2048]{1,0:T(8,128)(2,1)S(1)}, u32[]{:S(2)}, u32[]{:S(2)}) %collective-permute-start.89) | collective-permute-done | bytes 262176 | tf_op jit(solution)/shard_map/ppermute | solution.py:352
  432.9 3.4 collective-permute-start.92
  436.9 5.5 collective-permute-done.93.refs_3_.refs_11_
  442.5 16.2 %collective-permute-done.92.refs_2_.refs_10_ = bf16[64,2048]{1,0:T(8,128)(2,1)S(1)} collective-permute-done((bf16[64,2048]{1,0:T(8,128)(2,1)S(1)}, bf16[64,2048]{1,0:T(8,128)(2,1)S(1)}, u32[]{:S(2)}, u32[]{:S(2)}) %collective-permute-start.92) | collective-permute-done | bytes 262176 | tf_op jit(solution)/shard_map/ppermute | solution.py:352
  460.1 3.3 collective-permute-start.161
  463.6 10.7 %shard_map.220 = (bf16[512,768]{1,0:T(8,128)(2,1)S(1)}, f32[1,768]{1,0:T(1,128)S(1)}, f32[256,2048]{1,0:T(8,128)}, bf16[256,2048]{1,0:T(8,128)(2,1)S(1)}) custom-call(bf16[64,2048]{1,0:T(8,128)(2,1)S(1)} %get-tuple-element.188.refs_0_.refs_8_, bf16[64,2048]{1,0:T(8,128)(2,1)S(1)} %collective-permute-done.91.refs_1_.refs_9_, ...), custom_call_target="tpu_custom_call" | custom-call | flops 4831838208 | bytes 11807744 | tf_op jit(solution)/shard_map/pallas_call | solution.py:47
  475.9 13.1 %collective-permute-done.161 = bf16[256,2176]{1,0:T(8,128)(2,1)S(1)} collective-permute-done((bf16[256,2176]{1,0:T(8,128)(2,1)}, bf16[256,2176]{1,0:T(8,128)(2,1)S(1)}, u32[]{:S(2)}, u32[]{:S(2)}) %collective-permute-start.161) | collective-permute-done | bytes 1114144 | tf_op jit(solution)/shard_map/ppermute | solution.py:352
  491.7 5.9 collective-permute-done.75
  497.6 3.6 collective-permute-done.77
  538.4 26.9 %collective-permute-done.141 = bf16[256,1024]{1,0:T(8,128)(2,1)S(1)} collective-permute-done((bf16[256,1024]{1,0:T(8,128)(2,1)S(1)}, bf16[256,1024]{1,0:T(8,128)(2,1)S(1)}, u32[]{:S(2)}, u32[]{:S(2)}) %collective-permute-start.141) | collective-permute-done | bytes 524320 | tf_op jit(solution)/shard_map/ppermute | solution.py:352
  566.3 3.4 collective-permute-start.102
  570.0 6.4 collective-permute-done.104.refs_3_.refs_11_
  576.4 7.8 collective-permute-done.103.refs_2_.refs_10_
  587.9 9.7 %shard_map.223 = (bf16[512,1408]{1,0:T(8,128)(2,1)}, f32[256,2048]{1,0:T(8,128)}, bf16[256,2048]{1,0:T(8,128)(2,1)S(1)}) custom-call(bf16[64,2048]{1,0:T(8,128)(2,1)S(1)} %get-tuple-element.199.refs_0_.refs_8_, bf16[64,2048]{1,0:T(8,128)(2,1)S(1)} %collective-permute-done.102.refs_1_.refs_9_, bf16[64,2048]{1,0:T(8,128)(2,1)S(1)} %collective-permute-done.103.refs_2_.refs_10_, ...), custom_call_target="tpu_custom_call" | custom-call | flops 4563402752 | bytes 18481152 | tf_op jit(solution)/shard_map/pallas_call | solution.py:47
  602.4 9.0 %collective-permute-done.145 = bf16[256,1024]{1,0:T(8,128)(2,1)S(1)} collective-permute-done((bf16[256,1024]{1,0:T(8,128)(2,1)S(1)}, bf16[256,1024]{1,0:T(8,128)(2,1)S(1)}, u32[]{:S(2)}, u32[]{:S(2)}) %collective-permute-start.145) | collective-permute-done | bytes 524320 | tf_op jit(solution)/shard_map/ppermute | solution.py:352
  618.4 7.6 collective-permute-done.110.refs_1_
  626.0 8.4 collective-permute-done.111.refs_2_
  637.4 5.8 collective-permute-start.114
  643.3 8.3 shard_map.231
  654.0 8.1 collective-permute-done.114.refs_2_.refs_10_
  668.3 10.7 %shard_map.226 = (bf16[512,768]{1,0:T(8,128)(2,1)S(1)}, f32[1,768]{1,0:T(1,128)S(1)}, f32[256,2048]{1,0:T(8,128)}, bf16[256,2048]{1,0:T(8,128)(2,1)S(1)}) custom-call(bf16[64,2048]{1,0:T(8,128)(2,1)S(1)} %get-tuple-element.208.refs_0_.refs_8_, bf16[64,2048]{1,0:T(8,128)(2,1)S(1)} %collective-permute-done.113.refs_1_.refs_9_, ...), custom_call_target="tpu_custom_call" | custom-call | flops 4831838208 | bytes 11807744 | tf_op jit(solution)/shard_map/pallas_call | solution.py:47
  684.9 33.0 %collective-permute-done.147 = f32[2,3,256]{2,1,0:T(4,128)S(1)} collective-permute-done((f32[2,3,256]{2,1,0:T(4,128)S(1)}, f32[2,3,256]{2,1,0:T(4,128)S(1)}, u32[]{:S(2)}, u32[]{:S(2)}) %collective-permute-start.147) | collective-permute-done | bytes 6176 | tf_op jit(solution)/shard_map/ppermute | solution.py:352
  722.0 3.7 shard_map.229
  728.4 12.1 %collective-permute-done.152 = bf16[256,2176]{1,0:T(8,128)(2,1)S(1)} collective-permute-done((bf16[256,2176]{1,0:T(8,128)(2,1)S(1)}, bf16[256,2176]{1,0:T(8,128)(2,1)S(1)}, u32[]{:S(2)}, u32[]{:S(2)}) %collective-permute-start.152) | collective-permute-done | bytes 1114144 | tf_op jit(solution)/shard_map/ppermute | solution.py:352
  743.7 9.6 %collective-permute-done.137 = bf16[256,1024]{1,0:T(8,128)(2,1)S(1)} collective-permute-done((bf16[256,1024]{1,0:T(8,128)(2,1)S(1)}, bf16[256,1024]{1,0:T(8,128)(2,1)S(1)}, u32[]{:S(2)}, u32[]{:S(2)}) %collective-permute-start.137) | collective-permute-done | bytes 524320 | tf_op jit(solution)/shard_map/ppermute | solution.py:352
  758.2 12.8 %collective-permute-done.134 = bf16[256,1024]{1,0:T(8,128)(2,1)S(1)} collective-permute-done((bf16[256,1024]{1,0:T(8,128)(2,1)S(1)}, bf16[256,1024]{1,0:T(8,128)(2,1)S(1)}, u32[]{:S(2)}, u32[]{:S(2)}) %collective-permute-start.134) | collective-permute-done | bytes 524320 | tf_op jit(solution)/shard_map/ppermute | solution.py:352
  773.3 5.5 collective-permute-done.138
  785.8 7.0 collective-permute-done.122.refs_2_
  794.3 5.8 collective-permute-start.128
  818.5 3.7 maximum_convert_fusion
  825.6 9.6 %copy.76 = f32[2,256,2,1408]{3,2,1,0:T(2,128)} copy(f32[2,256,2,1408]{1,3,2,0:T(8,128)} %maximum_convert_fusion) | data formatting | bytes 11534336
  848.2 3.5 copy.74
  853.1 13.8 %collective-permute-done.78 = bf16[128,2048]{1,0:T(8,128)(2,1)} collective-permute-done((bf16[128,2048]{1,0:T(8,128)(2,1)}, bf16[128,2048]{1,0:T(8,128)(2,1)}, u32[]{:S(2)}, u32[]{:S(2)}) %collective-permute-start.78) | collective-permute-done | bytes 524320 | tf_op jit(solution)/shard_map/ppermute | solution.py:352
  (943 shorter events, 303.1 us)
Async XLA Ops:
  1.3 27.8 %collective-permute-start.15 = (s32[128]{0:T(128)S(1)}, s32[128]{0:T(128)S(1)}, u32[]{:S(2)}, u32[]{:S(2)}) collective-permute-start(s32[128]{0:T(128)S(1)} %fusion.13), channel_id=1, source_target_pairs={{0,8},{8,0},{1,9},{9,1},{2,10},{10,2},{3,11},{11,3},{4,12},{12,4},... | collective-permute-start | bytes 1544 | tf_op jit(solution)/shard_map/ppermute | solution.py:352
  8.4 29.1 %collective-permute-start.8 = (bf16[256,1024]{1,0:T(8,128)(2,1)}, bf16[256,1024]{1,0:T(8,128)(2,1)}, u32[]{:S(2)}, u32[]{:S(2)}) collective-permute-start(bf16[256,1024]{1,0:T(8,128)(2,1)} %get-tuple-element.141), channel_id=1, source_target_pairs={{0,4},{4,0},{1,5},{5,1},{2,6},{6,2},{3,7},{7,3},{8,12},{12,8},{9,1... | collective-permute-start | bytes 1572872 | tf_op jit(solution)/shard_map/ppermute | solution.py:352
  8.5 49.9 %collective-permute-start.9 = (bf16[256,1024]{1,0:T(8,128)(2,1)S(1)}, bf16[256,1024]{1,0:T(8,128)(2,1)}, u32[]{:S(2)}, u32[]{:S(2)}) collective-permute-start(bf16[256,1024]{1,0:T(8,128)(2,1)S(1)} %get-tuple-element.140.refs_8_), channel_id=1, source_target_pairs={{0,8},{8,0},{1,9},{9,1},{2,10},{10,2},{3,11},{11,3},{4,12},{12,4},... | collective-permute-start | bytes 1572872 | tf_op jit(solution)/shard_map/ppermute | solution.py:352
  36.0 27.3 %collective-permute-start.11 = (bf16[256,1024]{1,0:T(8,128)(2,1)S(1)}, bf16[256,1024]{1,0:T(8,128)(2,1)S(1)}, u32[]{:S(2)}, u32[]{:S(2)}) collective-permute-start(bf16[256,1024]{1,0:T(8,128)(2,1)S(1)} %get-tuple-element.140.refs_8_), channel_id=1, source_target_pairs={{0,16},{16,0},{1,17},{17,1},{2,18},{18,2},{3,19},{19,3},{4,20},{20... | collective-permute-start | bytes 1572872 | tf_op jit(solution)/shard_map/ppermute | solution.py:352
  37.5 28.8 %collective-permute-start.12 = (bf16[256,1024]{1,0:T(8,128)(2,1)}, bf16[256,1024]{1,0:T(8,128)(2,1)}, u32[]{:S(2)}, u32[]{:S(2)}) collective-permute-start(bf16[256,1024]{1,0:T(8,128)(2,1)} %collective-permute-done.8.refs_9_), channel_id=1, source_target_pairs={{0,16},{16,0},{1,17},{17,1},{2,18},{18,2},{3,19},{19,3},{4,20},{20... | collective-permute-start | bytes 1572872 | tf_op jit(solution)/shard_map/ppermute | solution.py:352
  63.3 38.4 %collective-permute-start.28 = (bf16[256,2176]{1,0:T(8,128)(2,1)}, bf16[256,2176]{1,0:T(8,128)(2,1)}, u32[]{:S(2)}, u32[]{:S(2)}) collective-permute-start(bf16[256,2176]{1,0:T(8,128)(2,1)} %get-tuple-element.151), channel_id=1, source_target_pairs={{0,4},{4,0},{1,5},{5,1},{2,6},{6,2},{3,7},{7,3},{8,12},{12,8},{9,1... | collective-permute-start | bytes 3342344 | tf_op jit(solution)/shard_map/ppermute | solution.py:352
  66.3 24.1 %collective-permute-start.14 = (bf16[256,1024]{1,0:T(8,128)(2,1)}, bf16[256,1024]{1,0:T(8,128)(2,1)}, u32[]{:S(2)}, u32[]{:S(2)}) collective-permute-start(bf16[256,1024]{1,0:T(8,128)(2,1)} %collective-permute-done.12.refs_13_), channel_id=1, source_target_pairs={{0,8},{8,0},{1,9},{9,1},{2,10},{10,2},{3,11},{11,3},{4,12},{12,4},... | collective-permute-start | bytes 1572872 | tf_op jit(solution)/shard_map/ppermute | solution.py:352
  76.9 37.3 %collective-permute-start.29 = (bf16[256,2176]{1,0:T(8,128)(2,1)S(1)}, bf16[256,2176]{1,0:T(8,128)(2,1)S(1)}, u32[]{:S(2)}, u32[]{:S(2)}) collective-permute-start(bf16[256,2176]{1,0:T(8,128)(2,1)S(1)} %get-tuple-element.150.refs_8_), channel_id=1, source_target_pairs={{0,8},{8,0},{1,9},{9,1},{2,10},{10,2},{3,11},{11,3},{4,12},{12,4},... | collective-permute-start | bytes 3342344 | tf_op jit(solution)/shard_map/ppermute | solution.py:352
  101.8 27.6 %collective-permute-start.32 = (bf16[256,2176]{1,0:T(8,128)(2,1)}, bf16[256,2176]{1,0:T(8,128)(2,1)S(1)}, u32[]{:S(2)}, u32[]{:S(2)}) collective-permute-start(bf16[256,2176]{1,0:T(8,128)(2,1)} %collective-permute-done.28.refs_9_), channel_id=1, source_target_pairs={{0,16},{16,0},{1,17},{17,1},{2,18},{18,2},{3,19},{19,3},{4,20},{20... | collective-permute-start | bytes 3342344 | tf_op jit(solution)/shard_map/ppermute | solution.py:352
  103.4 52.2 %collective-permute-start.31 = (bf16[256,2176]{1,0:T(8,128)(2,1)S(1)}, bf16[256,2176]{1,0:T(8,128)(2,1)S(1)}, u32[]{:S(2)}, u32[]{:S(2)}) collective-permute-start(bf16[256,2176]{1,0:T(8,128)(2,1)S(1)} %get-tuple-element.150.refs_8_), channel_id=1, source_target_pairs={{0,16},{16,0},{1,17},{17,1},{2,18},{18,2},{3,19},{19,3},{4,20},{20... | collective-permute-start | bytes 3342344 | tf_op jit(solution)/shard_map/ppermute | solution.py:352
  103.9 54.0 %collective-permute-start.30 = (bf16[256,2176]{1,0:T(8,128)(2,1)}, bf16[256,2176]{1,0:T(8,128)(2,1)S(1)}, u32[]{:S(2)}, u32[]{:S(2)}) collective-permute-start(bf16[256,2176]{1,0:T(8,128)(2,1)} %collective-permute-done.28.refs_9_), channel_id=1, source_target_pairs={{0,8},{8,0},{1,9},{9,1},{2,10},{10,2},{3,11},{11,3},{4,12},{12,4},... | collective-permute-start | bytes 3342344 | tf_op jit(solution)/shard_map/ppermute | solution.py:352
  114.2 62.5 %collective-permute-start.33 = (bf16[256,2176]{1,0:T(8,128)(2,1)S(1)}, bf16[256,2176]{1,0:T(8,128)(2,1)S(1)}, u32[]{:S(2)}, u32[]{:S(2)}) collective-permute-start(bf16[256,2176]{1,0:T(8,128)(2,1)S(1)} %collective-permute-done.29.refs_10_), channel_id=1, source_target_pairs={{0,16},{16,0},{1,17},{17,1},{2,18},{18,2},{3,19},{19,3},{4,20},{20... | collective-permute-start | bytes 3342344 | tf_op jit(solution)/shard_map/ppermute | solution.py:352
  129.5 52.5 %collective-permute-start.34 = (bf16[256,2176]{1,0:T(8,128)(2,1)S(1)}, bf16[256,2176]{1,0:T(8,128)(2,1)S(1)}, u32[]{:S(2)}, u32[]{:S(2)}) collective-permute-start(bf16[256,2176]{1,0:T(8,128)(2,1)S(1)} %collective-permute-done.32.refs_13_), channel_id=1, source_target_pairs={{0,8},{8,0},{1,9},{9,1},{2,10},{10,2},{3,11},{11,3},{4,12},{12,4},... | collective-permute-start | bytes 3342344 | tf_op jit(solution)/shard_map/ppermute | solution.py:352
  155.6 24.4 %collective-permute-start.22 = (bf16[64,2048]{1,0:T(8,128)(2,1)S(1)}, bf16[64,2048]{1,0:T(8,128)(2,1)S(1)}, u32[]{:S(2)}, u32[]{:S(2)}) collective-permute-start(bf16[64,2048]{1,0:T(8,128)(2,1)S(1)} %get-tuple-element.149.refs_0_), channel_id=1, source_target_pairs={{0,2},{1,3},{2,0},{3,1},{4,6},{5,7},{6,4},{7,5},{8,10},{9,11},{10,... | collective-permute-start | bytes 786440 | tf_op jit(solution)/shard_map/ppermute | solution.py:352
  217.1 41.5 %collective-permute-start.64 = (bf16[256,2176]{1,0:T(8,128)(2,1)S(1)}, bf16[256,2176]{1,0:T(8,128)(2,1)S(1)}, u32[]{:S(2)}, u32[]{:S(2)}) collective-permute-start(bf16[256,2176]{1,0:T(8,128)(2,1)S(1)} %get-tuple-element.173), channel_id=1, source_target_pairs={{0,4},{4,0},{1,5},{5,1},{2,6},{6,2},{3,7},{7,3},{8,12},{12,8},{9,1... | collective-permute-start | bytes 3342344 | tf_op jit(solution)/shard_map/ppermute | solution.py:352
  260.3 36.8 %collective-permute-start.65 = (bf16[256,2176]{1,0:T(8,128)(2,1)S(1)}, bf16[256,2176]{1,0:T(8,128)(2,1)S(1)}, u32[]{:S(2)}, u32[]{:S(2)}) collective-permute-start(bf16[256,2176]{1,0:T(8,128)(2,1)S(1)} %get-tuple-element.172.refs_8_), channel_id=1, source_target_pairs={{0,8},{8,0},{1,9},{9,1},{2,10},{10,2},{3,11},{11,3},{4,12},{12,4},... | collective-permute-start | bytes 3342344 | tf_op jit(solution)/shard_map/ppermute | solution.py:352
  260.7 38.0 %collective-permute-start.68 = (bf16[256,2176]{1,0:T(8,128)(2,1)S(1)}, bf16[256,2176]{1,0:T(8,128)(2,1)S(1)}, u32[]{:S(2)}, u32[]{:S(2)}) collective-permute-start(bf16[256,2176]{1,0:T(8,128)(2,1)S(1)} %collective-permute-done.64.refs_9_), channel_id=1, source_target_pairs={{0,16},{16,0},{1,17},{17,1},{2,18},{18,2},{3,19},{19,3},{4,20},{20... | collective-permute-start | bytes 3342344 | tf_op jit(solution)/shard_map/ppermute | solution.py:352
  284.2 46.6 %collective-permute-start.67 = (bf16[256,2176]{1,0:T(8,128)(2,1)S(1)}, bf16[256,2176]{1,0:T(8,128)(2,1)S(1)}, u32[]{:S(2)}, u32[]{:S(2)}) collective-permute-start(bf16[256,2176]{1,0:T(8,128)(2,1)S(1)} %get-tuple-element.172.refs_8_), channel_id=1, source_target_pairs={{0,16},{16,0},{1,17},{17,1},{2,18},{18,2},{3,19},{19,3},{4,20},{20... | collective-permute-start | bytes 3342344 | tf_op jit(solution)/shard_map/ppermute | solution.py:352
  285.6 46.4 %collective-permute-start.66 = (bf16[256,2176]{1,0:T(8,128)(2,1)S(1)}, bf16[256,2176]{1,0:T(8,128)(2,1)S(1)}, u32[]{:S(2)}, u32[]{:S(2)}) collective-permute-start(bf16[256,2176]{1,0:T(8,128)(2,1)S(1)} %collective-permute-done.64.refs_9_), channel_id=1, source_target_pairs={{0,8},{8,0},{1,9},{9,1},{2,10},{10,2},{3,11},{11,3},{4,12},{12,4},... | collective-permute-start | bytes 3342344 | tf_op jit(solution)/shard_map/ppermute | solution.py:352
  297.1 37.3 %collective-permute-start.69 = (bf16[256,2176]{1,0:T(8,128)(2,1)S(1)}, bf16[256,2176]{1,0:T(8,128)(2,1)S(1)}, u32[]{:S(2)}, u32[]{:S(2)}) collective-permute-start(bf16[256,2176]{1,0:T(8,128)(2,1)S(1)} %collective-permute-done.65.refs_10_), channel_id=1, source_target_pairs={{0,16},{16,0},{1,17},{17,1},{2,18},{18,2},{3,19},{19,3},{4,20},{20... | collective-permute-start | bytes 3342344 | tf_op jit(solution)/shard_map/ppermute | solution.py:352
  307.8 44.5 %collective-permute-start.70 = (bf16[256,2176]{1,0:T(8,128)(2,1)S(1)}, bf16[256,2176]{1,0:T(8,128)(2,1)S(1)}, u32[]{:S(2)}, u32[]{:S(2)}) collective-permute-start(bf16[256,2176]{1,0:T(8,128)(2,1)S(1)} %collective-permute-done.68.refs_13_), channel_id=1, source_target_pairs={{0,8},{8,0},{1,9},{9,1},{2,10},{10,2},{3,11},{11,3},{4,12},{12,4},... | collective-permute-start | bytes 3342344 | tf_op jit(solution)/shard_map/ppermute | solution.py:352
  383.2 48.1 %collective-permute-start.72 = (bf16[64,2048]{1,0:T(8,128)(2,1)S(1)}, bf16[64,2048]{1,0:T(8,128)(2,1)S(1)}, u32[]{:S(2)}, u32[]{:S(2)}) collective-permute-start(bf16[64,2048]{1,0:T(8,128)(2,1)S(1)} %get-tuple-element.177), channel_id=1, source_target_pairs={{0,1},{1,0},{2,3},{3,2},{4,5},{5,4},{6,7},{7,6},{8,9},{9,8},{10,11... | collective-permute-start | bytes 786440 | tf_op jit(solution)/shard_map/ppermute | solution.py:352
  385.3 47.6 %collective-permute-start.73 = (bf16[64,2048]{1,0:T(8,128)(2,1)S(1)}, bf16[64,2048]{1,0:T(8,128)(2,1)S(1)}, u32[]{:S(2)}, u32[]{:S(2)}) collective-permute-start(bf16[64,2048]{1,0:T(8,128)(2,1)S(1)} %get-tuple-element.178), channel_id=1, source_target_pairs={{0,2},{1,3},{2,0},{3,1},{4,6},{5,7},{6,4},{7,5},{8,10},{9,11},{10,... | collective-permute-start | bytes 786440 | tf_op jit(solution)/shard_map/ppermute | solution.py:352
  386.6 49.8 %collective-permute-start.74 = (bf16[64,2048]{1,0:T(8,128)(2,1)S(1)}, bf16[64,2048]{1,0:T(8,128)(2,1)S(1)}, u32[]{:S(2)}, u32[]{:S(2)}) collective-permute-start(bf16[64,2048]{1,0:T(8,128)(2,1)S(1)} %get-tuple-element.179), channel_id=1, source_target_pairs={{0,3},{1,2},{2,1},{3,0},{4,7},{5,6},{6,5},{7,4},{8,11},{9,10},{10,... | collective-permute-start | bytes 786440 | tf_op jit(solution)/shard_map/ppermute | solution.py:352
  388.0 41.2 %collective-permute-start.89 = (bf16[64,2048]{1,0:T(8,128)(2,1)}, bf16[64,2048]{1,0:T(8,128)(2,1)S(1)}, u32[]{:S(2)}, u32[]{:S(2)}) collective-permute-start(bf16[64,2048]{1,0:T(8,128)(2,1)} %copy-done.189), channel_id=1, source_target_pairs={{0,2},{1,3},{2,0},{3,1},{4,6},{5,7},{6,4},{7,5},{8,10},{9,11},{10,... | collective-permute-start | bytes 786440 | tf_op jit(solution)/shard_map/ppermute | solution.py:352
  396.5 34.0 %collective-permute-start.90 = (bf16[64,2048]{1,0:T(8,128)(2,1)}, bf16[64,2048]{1,0:T(8,128)(2,1)S(1)}, u32[]{:S(2)}, u32[]{:S(2)}) collective-permute-start(bf16[64,2048]{1,0:T(8,128)(2,1)} %copy-done.188), channel_id=1, source_target_pairs={{0,3},{1,2},{2,1},{3,0},{4,7},{5,6},{6,5},{7,4},{8,11},{9,10},{10,... | collective-permute-start | bytes 786440 | tf_op jit(solution)/shard_map/ppermute | solution.py:352
  429.1 45.3 %collective-permute-start.158 = (bf16[256,2176]{1,0:T(8,128)(2,1)}, bf16[256,2176]{1,0:T(8,128)(2,1)S(1)}, u32[]{:S(2)}, u32[]{:S(2)}) collective-permute-start(bf16[256,2176]{1,0:T(8,128)(2,1)} %get-tuple-element.260), channel_id=1, source_target_pairs={{0,16},{16,0},{1,17},{17,1},{2,18},{18,2},{3,19},{19,3},{4,20},{20... | collective-permute-start | bytes 3342344 | tf_op jit(solution)/shard_map/ppermute | solution.py:352
  431.3 28.1 %collective-permute-start.94 = (bf16[64,2048]{1,0:T(8,128)(2,1)S(1)}, bf16[64,2048]{1,0:T(8,128)(2,1)S(1)}, u32[]{:S(2)}, u32[]{:S(2)}) collective-permute-start(bf16[64,2048]{1,0:T(8,128)(2,1)S(1)} %get-tuple-element.188.refs_0_.refs_8_), channel_id=1, source_target_pairs={{0,4},{4,0},{1,5},{5,1},{2,6},{6,2},{3,7},{7,3},{8,12},{12,8},{9,1... | collective-permute-start | bytes 786440 | tf_op jit(solution)/shard_map/ppermute | solution.py:352
  432.9 25.8 %collective-permute-start.92 = (bf16[64,2048]{1,0:T(8,128)(2,1)S(1)}, bf16[64,2048]{1,0:T(8,128)(2,1)S(1)}, u32[]{:S(2)}, u32[]{:S(2)}) collective-permute-start(bf16[64,2048]{1,0:T(8,128)(2,1)S(1)} %get-tuple-element.188.refs_0_.refs_8_), channel_id=1, source_target_pairs={{0,2},{1,3},{2,0},{3,1},{4,6},{5,7},{6,4},{7,5},{8,10},{9,11},{10,... | collective-permute-start | bytes 786440 | tf_op jit(solution)/shard_map/ppermute | solution.py:352
  459.4 75.6 %collective-permute-start.157 = (bf16[256,2176]{1,0:T(8,128)(2,1)}, bf16[256,2176]{1,0:T(8,128)(2,1)}, u32[]{:S(2)}, u32[]{:S(2)}) collective-permute-start(bf16[256,2176]{1,0:T(8,128)(2,1)} %get-tuple-element.258), channel_id=1, source_target_pairs={{0,16},{16,0},{1,17},{17,1},{2,18},{18,2},{3,19},{19,3},{4,20},{20... | collective-permute-start | bytes 3342344 | tf_op jit(solution)/shard_map/ppermute | solution.py:352
  460.1 28.9 %collective-permute-start.161 = (bf16[256,2176]{1,0:T(8,128)(2,1)}, bf16[256,2176]{1,0:T(8,128)(2,1)S(1)}, u32[]{:S(2)}, u32[]{:S(2)}) collective-permute-start(bf16[256,2176]{1,0:T(8,128)(2,1)} %get-tuple-element.264), channel_id=1, source_target_pairs={{0,8},{8,0},{1,9},{9,1},{2,10},{10,2},{3,11},{11,3},{4,12},{12,4},... | collective-permute-start | bytes 3342344 | tf_op jit(solution)/shard_map/ppermute | solution.py:352
  463.4 25.6 %collective-permute-start.76 = (bf16[64,2048]{1,0:T(8,128)(2,1)S(1)}, bf16[64,2048]{1,0:T(8,128)(2,1)S(1)}, u32[]{:S(2)}, u32[]{:S(2)}) collective-permute-start(bf16[64,2048]{1,0:T(8,128)(2,1)S(1)} %get-tuple-element.344), channel_id=1, source_target_pairs={{0,2},{1,3},{2,0},{3,1},{4,6},{5,7},{6,4},{7,5},{8,10},{9,11},{10,... | collective-permute-start | bytes 786440 | tf_op jit(solution)/shard_map/ppermute | solution.py:352
  474.3 27.1 %collective-permute-start.98 = (bf16[256,2048]{1,0:T(8,128)(2,1)S(1)}, bf16[256,2048]{1,0:T(8,128)(2,1)S(1)}, u32[]{:S(2)}, u32[]{:S(2)}) collective-permute-start(bf16[256,2048]{1,0:T(8,128)(2,1)S(1)} %get-tuple-element.193), channel_id=1, source_target_pairs={{0,4},{4,0},{1,5},{5,1},{2,6},{6,2},{3,7},{7,3},{8,12},{12,8},{9,1... | collective-permute-start | bytes 3145736 | tf_op jit(solution)/shard_map/ppermute | solution.py:352
  475.8 59.5 %collective-permute-start.159 = (bf16[256,2176]{1,0:T(8,128)(2,1)}, bf16[256,2176]{1,0:T(8,128)(2,1)}, u32[]{:S(2)}, u32[]{:S(2)}) collective-permute-start(bf16[256,2176]{1,0:T(8,128)(2,1)} %add_convert_fusion.4), channel_id=1, source_target_pairs={{0,8},{8,0},{1,9},{9,1},{2,10},{10,2},{3,11},{11,3},{4,12},{12,4},... | collective-permute-start | bytes 3342344 | tf_op jit(solution)/shard_map/ppermute | solution.py:352
  502.5 26.8 %collective-permute-start.99 = (bf16[64,2048]{1,0:T(8,128)(2,1)}, bf16[64,2048]{1,0:T(8,128)(2,1)}, u32[]{:S(2)}, u32[]{:S(2)}) collective-permute-start(bf16[64,2048]{1,0:T(8,128)(2,1)} %get-tuple-element.195), channel_id=1, source_target_pairs={{0,1},{1,0},{2,3},{3,2},{4,5},{5,4},{6,7},{7,6},{8,9},{9,8},{10,11... | collective-permute-start | bytes 786440 | tf_op jit(solution)/shard_map/ppermute | solution.py:352
  504.1 27.0 %collective-permute-start.100 = (bf16[64,2048]{1,0:T(8,128)(2,1)}, bf16[64,2048]{1,0:T(8,128)(2,1)}, u32[]{:S(2)}, u32[]{:S(2)}) collective-permute-start(bf16[64,2048]{1,0:T(8,128)(2,1)} %get-tuple-element.196), channel_id=1, source_target_pairs={{0,2},{1,3},{2,0},{3,1},{4,6},{5,7},{6,4},{7,5},{8,10},{9,11},{10,... | collective-permute-start | bytes 786440 | tf_op jit(solution)/shard_map/ppermute | solution.py:352
  505.1 27.1 %collective-permute-start.101 = (bf16[64,2048]{1,0:T(8,128)(2,1)}, bf16[64,2048]{1,0:T(8,128)(2,1)}, u32[]{:S(2)}, u32[]{:S(2)}) collective-permute-start(bf16[64,2048]{1,0:T(8,128)(2,1)} %get-tuple-element.197), channel_id=1, source_target_pairs={{0,3},{1,2},{2,1},{3,0},{4,7},{5,6},{6,5},{7,4},{8,11},{9,10},{10,... | collective-permute-start | bytes 786440 | tf_op jit(solution)/shard_map/ppermute | solution.py:352
  529.2 68.4 %collective-permute-start.160 = (bf16[256,2176]{1,0:T(8,128)(2,1)S(1)}, bf16[256,2176]{1,0:T(8,128)(2,1)}, u32[]{:S(2)}, u32[]{:S(2)}) collective-permute-start(bf16[256,2176]{1,0:T(8,128)(2,1)S(1)} %copy-done.51), channel_id=1, source_target_pairs={{0,8},{8,0},{1,9},{9,1},{2,10},{10,2},{3,11},{11,3},{4,12},{12,4},... | collective-permute-start | bytes 3342344 | tf_op jit(solution)/shard_map/ppermute | solution.py:352
  531.1 67.8 %collective-permute-start.162 = (bf16[256,2176]{1,0:T(8,128)(2,1)S(1)}, bf16[256,2176]{1,0:T(8,128)(2,1)}, u32[]{:S(2)}, u32[]{:S(2)}) collective-permute-start(bf16[256,2176]{1,0:T(8,128)(2,1)S(1)} %copy-done.235), channel_id=1, source_target_pairs={{0,16},{16,0},{1,17},{17,1},{2,18},{18,2},{3,19},{19,3},{4,20},{20... | collective-permute-start | bytes 3342344 | tf_op jit(solution)/shard_map/ppermute | solution.py:352
  532.2 33.2 %collective-permute-start.141 = (bf16[256,1024]{1,0:T(8,128)(2,1)S(1)}, bf16[256,1024]{1,0:T(8,128)(2,1)S(1)}, u32[]{:S(2)}, u32[]{:S(2)}) collective-permute-start(bf16[256,1024]{1,0:T(8,128)(2,1)S(1)} %get-tuple-element.238), channel_id=1, source_target_pairs={{0,16},{16,0},{1,17},{17,1},{2,18},{18,2},{3,19},{19,3},{4,20},{20... | collective-permute-start | bytes 1572872 | tf_op jit(solution)/shard_map/ppermute | solution.py:352
  534.9 31.4 %collective-permute-start.144 = (bf16[256,1024]{1,0:T(8,128)(2,1)S(1)}, bf16[256,1024]{1,0:T(8,128)(2,1)S(1)}, u32[]{:S(2)}, u32[]{:S(2)}) collective-permute-start(bf16[256,1024]{1,0:T(8,128)(2,1)S(1)} %get-tuple-element.242), channel_id=1, source_target_pairs={{0,8},{8,0},{1,9},{9,1},{2,10},{10,2},{3,11},{11,3},{4,12},{12,4},... | collective-permute-start | bytes 1572872 | tf_op jit(solution)/shard_map/ppermute | solution.py:352
  535.3 31.1 %collective-permute-start.105 = (bf16[64,2048]{1,0:T(8,128)(2,1)S(1)}, bf16[64,2048]{1,0:T(8,128)(2,1)S(1)}, u32[]{:S(2)}, u32[]{:S(2)}) collective-permute-start(bf16[64,2048]{1,0:T(8,128)(2,1)S(1)} %get-tuple-element.199.refs_0_.refs_8_), channel_id=1, source_target_pairs={{0,4},{4,0},{1,5},{5,1},{2,6},{6,2},{3,7},{7,3},{8,12},{12,8},{9,1... | collective-permute-start | bytes 786440 | tf_op jit(solution)/shard_map/ppermute | solution.py:352
  584.9 28.1 %collective-permute-start.140 = (bf16[256,1024]{1,0:T(8,128)(2,1)S(1)}, bf16[256,1024]{1,0:T(8,128)(2,1)S(1)}, u32[]{:S(2)}, u32[]{:S(2)}) collective-permute-start(bf16[256,1024]{1,0:T(8,128)(2,1)S(1)} %get-tuple-element.236), channel_id=1, source_target_pairs={{0,16},{16,0},{1,17},{17,1},{2,18},{18,2},{3,19},{19,3},{4,20},{20... | collective-permute-start | bytes 1572872 | tf_op jit(solution)/shard_map/ppermute | solution.py:352
  587.5 27.5 %collective-permute-start.142 = (bf16[256,1024]{1,0:T(8,128)(2,1)S(1)}, bf16[256,1024]{1,0:T(8,128)(2,1)S(1)}, u32[]{:S(2)}, u32[]{:S(2)}) collective-permute-start(bf16[256,1024]{1,0:T(8,128)(2,1)S(1)} %add_convert_fusion.16), channel_id=1, source_target_pairs={{0,8},{8,0},{1,9},{9,1},{2,10},{10,2},{3,11},{11,3},{4,12},{12,4},... | collective-permute-start | bytes 1572872 | tf_op jit(solution)/shard_map/ppermute | solution.py:352
  601.9 50.8 %collective-permute-start.163 = (bf16[256,2176]{1,0:T(8,128)(2,1)}, bf16[256,2176]{1,0:T(8,128)(2,1)S(1)}, u32[]{:S(2)}, u32[]{:S(2)}) collective-permute-start(bf16[256,2176]{1,0:T(8,128)(2,1)} %add_convert_fusion), channel_id=1, source_target_pairs={{0,4},{4,0},{1,5},{5,1},{2,6},{6,2},{3,7},{7,3},{8,12},{12,8},{9,1... | collective-permute-start | bytes 3342344 | tf_op jit(solution)/shard_map/ppermute | solution.py:352
  612.7 40.8 %collective-permute-start.146 = (bf16[256,1024]{1,0:T(8,128)(2,1)S(1)}, bf16[256,1024]{1,0:T(8,128)(2,1)S(1)}, u32[]{:S(2)}, u32[]{:S(2)}) collective-permute-start(bf16[256,1024]{1,0:T(8,128)(2,1)S(1)} %add_convert_fusion.12), channel_id=1, source_target_pairs={{0,4},{4,0},{1,5},{5,1},{2,6},{6,2},{3,7},{7,3},{8,12},{12,8},{9,1... | collective-permute-start | bytes 1572872 | tf_op jit(solution)/shard_map/ppermute | solution.py:352
  637.4 24.8 %collective-permute-start.114 = (bf16[64,2048]{1,0:T(8,128)(2,1)S(1)}, bf16[64,2048]{1,0:T(8,128)(2,1)S(1)}, u32[]{:S(2)}, u32[]{:S(2)}) collective-permute-start(bf16[64,2048]{1,0:T(8,128)(2,1)S(1)} %get-tuple-element.208.refs_0_.refs_8_), channel_id=1, source_target_pairs={{0,2},{1,3},{2,0},{3,1},{4,6},{5,7},{6,4},{7,5},{8,10},{9,11},{10,... | collective-permute-start | bytes 786440 | tf_op jit(solution)/shard_map/ppermute | solution.py:352
  652.7 29.9 %collective-permute-start.151 = (bf16[256,2176]{1,0:T(8,128)(2,1)}, bf16[256,2176]{1,0:T(8,128)(2,1)}, u32[]{:S(2)}, u32[]{:S(2)}) collective-permute-start(bf16[256,2176]{1,0:T(8,128)(2,1)} %get-tuple-element.250), channel_id=1, source_target_pairs={{0,16},{16,0},{1,17},{17,1},{2,18},{18,2},{3,19},{19,3},{4,20},{20... | collective-permute-start | bytes 3342344 | tf_op jit(solution)/shard_map/ppermute | solution.py:352
  665.4 62.3 %collective-permute-start.150 = (bf16[256,2176]{1,0:T(8,128)(2,1)}, bf16[256,2176]{1,0:T(8,128)(2,1)}, u32[]{:S(2)}, u32[]{:S(2)}) collective-permute-start(bf16[256,2176]{1,0:T(8,128)(2,1)} %get-tuple-element.248), channel_id=1, source_target_pairs={{0,16},{16,0},{1,17},{17,1},{2,18},{18,2},{3,19},{19,3},{4,20},{20... | collective-permute-start | bytes 3342344 | tf_op jit(solution)/shard_map/ppermute | solution.py:352
  666.1 88.9 %collective-permute-start.153 = (bf16[256,2176]{1,0:T(8,128)(2,1)}, bf16[256,2176]{1,0:T(8,128)(2,1)}, u32[]{:S(2)}, u32[]{:S(2)}) collective-permute-start(bf16[256,2176]{1,0:T(8,128)(2,1)} %get-tuple-element.252), channel_id=1, source_target_pairs={{0,8},{8,0},{1,9},{9,1},{2,10},{10,2},{3,11},{11,3},{4,12},{12,4},... | collective-permute-start | bytes 3342344 | tf_op jit(solution)/shard_map/ppermute | solution.py:352
  667.6 51.5 %collective-permute-start.154 = (bf16[256,2176]{1,0:T(8,128)(2,1)}, bf16[256,2176]{1,0:T(8,128)(2,1)}, u32[]{:S(2)}, u32[]{:S(2)}) collective-permute-start(bf16[256,2176]{1,0:T(8,128)(2,1)} %get-tuple-element.254), channel_id=1, source_target_pairs={{0,8},{8,0},{1,9},{9,1},{2,10},{10,2},{3,11},{11,3},{4,12},{12,4},... | collective-permute-start | bytes 3342344 | tf_op jit(solution)/shard_map/ppermute | solution.py:352
  681.0 36.8 %collective-permute-start.147 = (f32[2,3,256]{2,1,0:T(4,128)S(1)}, f32[2,3,256]{2,1,0:T(4,128)S(1)}, u32[]{:S(2)}, u32[]{:S(2)}) collective-permute-start(f32[2,3,256]{2,1,0:T(4,128)S(1)} %constant_dynamic-update-slice_fusion), channel_id=1, source_target_pairs={{0,8},{8,0},{1,9},{9,1},{2,10},{10,2},{3,11},{11,3},{4,12},{12,4},... | collective-permute-start | bytes 18440 | tf_op jit(solution)/shard_map/ppermute | solution.py:352
  684.2 56.3 %collective-permute-start.152 = (bf16[256,2176]{1,0:T(8,128)(2,1)S(1)}, bf16[256,2176]{1,0:T(8,128)(2,1)S(1)}, u32[]{:S(2)}, u32[]{:S(2)}) collective-permute-start(bf16[256,2176]{1,0:T(8,128)(2,1)S(1)} %add_convert_fusion.10), channel_id=1, source_target_pairs={{0,8},{8,0},{1,9},{9,1},{2,10},{10,2},{3,11},{11,3},{4,12},{12,4},... | collective-permute-start | bytes 3342344 | tf_op jit(solution)/shard_map/ppermute | solution.py:352
  720.9 34.2 %collective-permute-start.155 = (bf16[256,2176]{1,0:T(8,128)(2,1)S(1)}, bf16[256,2176]{1,0:T(8,128)(2,1)S(1)}, u32[]{:S(2)}, u32[]{:S(2)}) collective-permute-start(bf16[256,2176]{1,0:T(8,128)(2,1)S(1)} %add_convert_fusion.7), channel_id=1, source_target_pairs={{0,16},{16,0},{1,17},{17,1},{2,18},{18,2},{3,19},{19,3},{4,20},{20... | collective-permute-start | bytes 3342344 | tf_op jit(solution)/shard_map/ppermute | solution.py:352
  725.7 74.5 %collective-permute-start.133 = (bf16[256,1024]{1,0:T(8,128)(2,1)S(1)}, bf16[256,1024]{1,0:T(8,128)(2,1)S(1)}, u32[]{:S(2)}, u32[]{:S(2)}) collective-permute-start(bf16[256,1024]{1,0:T(8,128)(2,1)S(1)} %get-tuple-element.226), channel_id=1, source_target_pairs={{0,16},{16,0},{1,17},{17,1},{2,18},{18,2},{3,19},{19,3},{4,20},{20... | collective-permute-start | bytes 1572872 | tf_op jit(solution)/shard_map/ppermute | solution.py:352
  727.7 43.3 %collective-permute-start.134 = (bf16[256,1024]{1,0:T(8,128)(2,1)S(1)}, bf16[256,1024]{1,0:T(8,128)(2,1)S(1)}, u32[]{:S(2)}, u32[]{:S(2)}) collective-permute-start(bf16[256,1024]{1,0:T(8,128)(2,1)S(1)} %get-tuple-element.228), channel_id=1, source_target_pairs={{0,16},{16,0},{1,17},{17,1},{2,18},{18,2},{3,19},{19,3},{4,20},{20... | collective-permute-start | bytes 1572872 | tf_op jit(solution)/shard_map/ppermute | solution.py:352
  755.1 23.7 %collective-permute-start.138 = (bf16[256,1024]{1,0:T(8,128)(2,1)S(1)}, bf16[256,1024]{1,0:T(8,128)(2,1)S(1)}, u32[]{:S(2)}, u32[]{:S(2)}) collective-permute-start(bf16[256,1024]{1,0:T(8,128)(2,1)S(1)} %add_convert_fusion.19), channel_id=1, source_target_pairs={{0,16},{16,0},{1,17},{17,1},{2,18},{18,2},{3,19},{19,3},{4,20},{20... | collective-permute-start | bytes 1572872 | tf_op jit(solution)/shard_map/ppermute | solution.py:352
  770.9 42.1 %collective-permute-start.156 = (bf16[256,2176]{1,0:T(8,128)(2,1)S(1)}, bf16[256,2176]{1,0:T(8,128)(2,1)S(1)}, u32[]{:S(2)}, u32[]{:S(2)}) collective-permute-start(bf16[256,2176]{1,0:T(8,128)(2,1)S(1)} %add_convert_fusion.6), channel_id=1, source_target_pairs={{0,4},{4,0},{1,5},{5,1},{2,6},{6,2},{3,7},{7,3},{8,12},{12,8},{9,1... | collective-permute-start | bytes 3342344 | tf_op jit(solution)/shard_map/ppermute | solution.py:352
  792.8 43.4 %collective-permute-start.139 = (bf16[256,1024]{1,0:T(8,128)(2,1)}, bf16[256,1024]{1,0:T(8,128)(2,1)}, u32[]{:S(2)}, u32[]{:S(2)}) collective-permute-start(bf16[256,1024]{1,0:T(8,128)(2,1)} %add_convert_fusion.18), channel_id=1, source_target_pairs={{0,4},{4,0},{1,5},{5,1},{2,6},{6,2},{3,7},{7,3},{8,12},{12,8},{9,1... | collective-permute-start | bytes 1572872 | tf_op jit(solution)/shard_map/ppermute | solution.py:352
  808.6 29.5 %collective-permute-start.125 = (bf16[64,2048]{1,0:T(8,128)(2,1)}, bf16[64,2048]{1,0:T(8,128)(2,1)}, u32[]{:S(2)}, u32[]{:S(2)}) collective-permute-start(bf16[64,2048]{1,0:T(8,128)(2,1)} %get-tuple-element.332), channel_id=1, source_target_pairs={{0,2},{1,3},{2,0},{3,1},{4,6},{5,7},{6,4},{7,5},{8,10},{9,11},{10,... | collective-permute-start | bytes 786440 | tf_op jit(solution)/shard_map/ppermute | solution.py:352
  810.6 27.6 %collective-permute-start.124 = (bf16[64,2048]{1,0:T(8,128)(2,1)}, bf16[64,2048]{1,0:T(8,128)(2,1)}, u32[]{:S(2)}, u32[]{:S(2)}) collective-permute-start(bf16[64,2048]{1,0:T(8,128)(2,1)} %get-tuple-element.332), channel_id=1, source_target_pairs={{0,1},{1,0},{2,3},{3,2},{4,5},{5,4},{6,7},{7,6},{8,9},{9,8},{10,11... | collective-permute-start | bytes 786440 | tf_op jit(solution)/shard_map/ppermute | solution.py:352
  810.7 27.5 %collective-permute-start.126 = (bf16[64,2048]{1,0:T(8,128)(2,1)}, bf16[64,2048]{1,0:T(8,128)(2,1)}, u32[]{:S(2)}, u32[]{:S(2)}) collective-permute-start(bf16[64,2048]{1,0:T(8,128)(2,1)} %get-tuple-element.332), channel_id=1, source_target_pairs={{0,3},{1,2},{2,1},{3,0},{4,7},{5,6},{6,5},{7,4},{8,11},{9,10},{10,... | collective-permute-start | bytes 786440 | tf_op jit(solution)/shard_map/ppermute | solution.py:352
  842.1 27.1 %collective-permute-start.127 = (bf16[128,2048]{1,0:T(8,128)(2,1)}, bf16[128,2048]{1,0:T(8,128)(2,1)}, u32[]{:S(2)}, u32[]{:S(2)}) collective-permute-start(bf16[128,2048]{1,0:T(8,128)(2,1)} %bitcast.66), channel_id=1, source_target_pairs={{0,8},{8,0},{1,9},{9,1},{2,10},{10,2},{3,11},{11,3},{4,12},{12,4},... | collective-permute-start | bytes 1572872 | tf_op jit(solution)/shard_map/ppermute | solution.py:352
  842.7 24.1 %collective-permute-start.78 = (bf16[128,2048]{1,0:T(8,128)(2,1)}, bf16[128,2048]{1,0:T(8,128)(2,1)}, u32[]{:S(2)}, u32[]{:S(2)}) collective-permute-start(bf16[128,2048]{1,0:T(8,128)(2,1)} %bitcast.56), channel_id=1, source_target_pairs={{0,8},{8,0},{1,9},{9,1},{2,10},{10,2},{3,11},{11,3},{4,12},{12,4},... | collective-permute-start | bytes 1572872 | tf_op jit(solution)/shard_map/ppermute | solution.py:352
  (357 other events, 5810.0 us)

commit v4 on v3

v4 whole, which is shorter than its diff:
```python
import functools
import math

import jax
import jax.numpy as jnp
from jax import lax
from jax.experimental import pallas as pl
from jax.experimental.layout import Layout, with_layout_constraint
from jax.experimental.pallas import tpu as pltpu
from jax.sharding import Mesh
from jax.sharding import PartitionSpec as P

HEAD = 64
ROT = 16
LAYERS = 2
NORM_EPS = 1e-05
MASK_FILL = -1e30
LOW = jnp.bfloat16
F32 = jnp.float32
MIB = 1024 * 1024
BLOCK = 512
HBM = pl.BlockSpec(memory_space=pltpu.HBM)
ANY = pl.BlockSpec(memory_space=pl.ANY)
VMEM = pl.BlockSpec(memory_space=pltpu.VMEM)


def dot(a, b, dims):
    return lax.dot_general(a, b, (dims, ((), ())), preferred_element_type=F32)


def nn(a, b):
    return dot(a, b, ((1,), (0,)))


def nt(a, b):
    return dot(a, b, ((1,), (1,)))


def tn(a, b):
    return dot(a, b, ((0,), (0,)))


def shape(dims, kind):
    return jax.ShapeDtypeStruct(dims, kind)


def call(body, n_hbm, args, outs, scratch, flops, hbm_outs=0, n_any=0, limit=32):
    moved = sum(a.size * a.dtype.itemsize for a in args)
    moved += sum(math.prod(o.shape) * jnp.dtype(o.dtype).itemsize for o in outs)
    return pl.pallas_call(
        body,
        out_shape=tuple(outs),
        in_specs=[ANY] * n_any + [HBM] * (n_hbm - n_any) + [VMEM] * (len(args) - n_hbm),
        out_specs=tuple([HBM] * hbm_outs + [VMEM] * (len(outs) - hbm_outs)),
        scratch_shapes=scratch,
        compiler_params=pltpu.CompilerParams(vmem_limit_bytes=limit * MIB),
        cost_estimate=pl.CostEstimate(flops=flops, bytes_accessed=moved, transcendentals=0),
    )(*args)


def into_rows(pieces, whole, sems, first):
    copies, row = [], 0
    for i, piece in enumerate(pieces):
        rows = piece.shape[0]
        copies.append(
            pltpu.make_async_copy(piece, whole.at[pl.ds(row, rows)], sems.at[first + i])
        )
        row += rows
    return copies


def weights_into(weights, whole, sems, first):
    rows, width = whole.shape
    cols = pl.ds(pl.multiple_of(lax.axis_index("clo") * width, 128), width)
    copies = []
    for at in range(0, rows, BLOCK):
        src, dst = weights.at[pl.ds(at, BLOCK), cols], whole.at[pl.ds(at, BLOCK)]
        copies.append(pltpu.make_async_copy(src, dst, sems.at[first + len(copies)]))
    return copies


def start_all(copies):
    for c in copies:
        c.start()


def wait_all(copies):
    for c in copies:
        c.wait()


def rolled(value, tables, sign):
    cos_t, ahead_t, behind_t = tables[0], tables[1], tables[2]
    slabs = []
    for at in range(0, value.shape[1], 128):
        x = value[:, at : at + 128]
        ahead = pltpu.roll(x, 128 - ROT // 2, 1)
        behind = pltpu.roll(x, ROT // 2, 1)
        slabs.append(x * cos_t + sign * (ahead * ahead_t + behind * behind_t))
    return jnp.concatenate(slabs, axis=1).astype(LOW)


def allowed_of(column, row):
    return (column[:, 0:1] == row[0:1]) & (row[1:2] <= column[:, 1:2])


def put_halves(tile, cols, own_ref, send_ref):
    half = own_ref.shape[0]
    own_ref[:, cols] = tile[:half]
    send_ref[:, cols] = tile[half:].astype(LOW)


def softmax_of(q_h, k, allowed, scale):
    s = jnp.where(allowed, nt(q_h, k) * scale, MASK_FILL)
    top = jnp.max(s, axis=-1, keepdims=True)
    e = jnp.exp(s - top)
    return e / jnp.sum(e, axis=-1, keepdims=True)


def load(pairs, sems, first):
    return [
        pltpu.make_async_copy(src, dst, sems.at[first + i]) for i, (src, dst) in enumerate(pairs)
    ]


def block_rows(w_s, w_copies=None):
    for i, at in enumerate(range(0, w_s.shape[0], BLOCK)):
        if w_copies is not None:
            w_copies[i].wait()
        yield i, slice(at, at + BLOCK)


def attn_forward(n_h, heads, *refs):
    h_parts, weights, refs = refs[:n_h], refs[n_h], refs[n_h + 1 :]
    tables, column, row, bias = refs[:4]
    full_o, q_o, k_o, v_o, o_o, own_o, send_o, h_s, w_s, acc, tab, col, sems = refs[4:]
    width = heads * HEAD
    copies = into_rows(h_parts, h_s, sems, 0)
    w_copies = weights_into(weights, w_s, sems, n_h)
    extra = load([(tables, tab), (column, col)], sems, n_h + len(w_copies))
    start_all(copies + w_copies + extra)
    wait_all(copies)
    whole = pltpu.make_async_copy(h_s, full_o, sems.at[0])
    whole.start()
    for r, rows in block_rows(w_s, w_copies):
        for c in range(3):
            cols = slice(c * width, (c + 1) * width)
            part = nn(h_s[:, rows], w_s[rows, cols])
            acc[:, cols] = part + (bias[:, cols] if r == 0 else acc[:, cols])
    wait_all(extra)
    q_o[...] = rolled(acc[:, :width], tab, 1.0)
    k_o[...] = rolled(acc[:, width : 2 * width], tab, 1.0)
    v_o[...] = acc[:, 2 * width :].astype(LOW)
    lane = lax.broadcasted_iota(jnp.int32, (1, width), 1) // HEAD
    allowed = allowed_of(col, row)
    k, v, q = k_o[...], v_o[...], q_o[...]
    zero = jnp.zeros((), LOW)
    o = None
    for h in range(heads):
        mine = lane == h
        w = softmax_of(jnp.where(mine, q, zero), k, allowed, 1.0 / math.sqrt(HEAD))
        part = nn(w.astype(LOW), jnp.where(mine, v, zero))
        o = part if o is None else o + part
    o_o[...] = o.astype(LOW)
    o = o_o[...]
    for r, rows in block_rows(w_s):
        put_halves(nt(o, w_s[rows, 3 * width :]), rows, own_o, send_o)
    whole.wait()


def attn_backward(n_h, heads, *refs):
    d_parts, weights, refs = refs[:n_h], refs[n_h], refs[n_h + 1 :]
    q_i, k_i, v_i, tables, column, row = refs[:6]
    full_o, dp_o, bias_o, own_o, send_o, d_s, w_s, acc, qkv, tab, col, sems = refs[6:]
    width = heads * HEAD
    copies = into_rows(d_parts, d_s, sems, 0)
    w_copies = weights_into(weights, w_s, sems, n_h)
    extra = load(
        [(q_i, qkv.at[0]), (k_i, qkv.at[1]), (v_i, qkv.at[2]), (tables, tab), (column, col)],
        sems,
        n_h + len(w_copies),
    )
    start_all(copies + w_copies + extra)
    wait_all(copies)
    whole = pltpu.make_async_copy(d_s, full_o, sems.at[0])
    whole.start()
    for r, rows in block_rows(w_s, w_copies):
        part = nn(d_s[:, rows], w_s[rows, 3 * width :])
        acc[...] = part if r == 0 else acc[...] + part
    do = acc[...].astype(LOW)
    wait_all(extra)
    q, k, v = qkv[0], qkv[1], qkv[2]
    lane = lax.broadcasted_iota(jnp.int32, (1, width), 1) // HEAD
    allowed = allowed_of(col, row)
    zero = jnp.zeros((), LOW)
    scale = 1.0 / math.sqrt(HEAD)
    dq = dk = dv = None
    for h in range(heads):
        mine = lane == h
        q_h = jnp.where(mine, q, zero)
        do_h = jnp.where(mine, do, zero)
        w = softmax_of(q_h, k, allowed, scale)
        dw = nt(do_h, v)
        ds = (w * (dw - jnp.sum(w * dw, axis=-1, keepdims=True))).astype(LOW)
        dv_h = tn(w.astype(LOW), do_h)
        dq_h = nn(ds, jnp.where(mine, k, zero))
        dk_h = tn(ds, q_h)
        dq, dk, dv = (
            (dq_h, dk_h, dv_h) if h == 0 else (dq + dq_h, dk + dk_h, dv + dv_h)
        )
    dp_o[:, :width] = rolled(dq * scale, tab, -1.0)
    dp_o[:, width : 2 * width] = rolled(dk * scale, tab, -1.0)
    dp_o[:, 2 * width :] = dv.astype(LOW)
    dp = dp_o[...]
    bias_o[...] = jnp.sum(dp.astype(F32), axis=0, keepdims=True)
    for r, rows in block_rows(w_s):
        put_halves(nt(dp, w_s[rows, : 3 * width]), rows, own_o, send_o)
    whole.wait()


def mlp_forward(n_h, *refs):
    h_parts, weights, refs = refs[:n_h], refs[n_h], refs[n_h + 1 :]
    full_o, gu_o, z_o, own_o, send_o, h_s, w_s, sems = refs
    units = z_o.shape[1]
    copies = into_rows(h_parts, h_s, sems, 0)
    w_copies = weights_into(weights, w_s, sems, n_h)
    start_all(copies + w_copies)
    wait_all(copies)
    whole = pltpu.make_async_copy(h_s, full_o, sems.at[0])
    whole.start()
    for r, rows in block_rows(w_s, w_copies):
        part = nn(h_s[:, rows], w_s[rows, : 2 * units])
        gu_o[...] = part if r == 0 else gu_o[...] + part
    g = gu_o[:, :units]
    u = gu_o[:, units:]
    z_o[...] = (g * u / (1.0 + jnp.exp(-g))).astype(LOW)
    z = z_o[...]
    for r, rows in block_rows(w_s):
        put_halves(nt(z, w_s[rows, 2 * units : 3 * units]), rows, own_o, send_o)
    whole.wait()


def mlp_backward(n_h, *refs):
    d_parts, weights, refs = refs[:n_h], refs[n_h], refs[n_h + 1 :]
    gu_i, full_o, dp_o, own_o, send_o, d_s, w_s, acc, gu, sems = refs
    units = acc.shape[1]
    copies = into_rows(d_parts, d_s, sems, 0)
    w_copies = weights_into(weights, w_s, sems, n_h)
    extra = load([(gu_i, gu)], sems, n_h + len(w_copies))
    start_all(copies + w_copies + extra)
    wait_all(copies)
    whole = pltpu.make_async_copy(d_s, full_o, sems.at[0])
    whole.start()
    for r, rows in block_rows(w_s, w_copies):
        part = nn(d_s[:, rows], w_s[rows, 2 * units : 3 * units])
        acc[...] = part if r == 0 else acc[...] + part
    wait_all(extra)
    g = gu[:, :units]
    u = gu[:, units:]
    sig = 1.0 / (1.0 + jnp.exp(-g))
    dz = acc[...]
    dp_o[:, :units] = (dz * u * sig * (1.0 + g * (1.0 - sig))).astype(LOW)
    dp_o[:, units:] = (dz * g * sig).astype(LOW)
    dp = dp_o[...]
    for r, rows in block_rows(w_s):
        put_halves(nt(dp, w_s[rows, : 2 * units]), rows, own_o, send_o)
    whole.wait()


def load_grads(args, a_s, b_s, da_s, db_s, sems):
    copies = load(list(zip(args, (a_s, b_s, da_s, db_s))), sems, 0)
    start_all(copies)
    wait_all(copies)


def weight_grads(*refs):
    out, a_s, b_s, da_s, db_s, slots, sems, out_sems = refs[4:]
    load_grads(refs[:4], a_s, b_s, da_s, db_s, sems)
    split, end = da_s.shape[1], da_s.shape[1] + db_s.shape[1]
    sent = []
    for i, at in enumerate(range(0, a_s.shape[1], BLOCK)):
        cols = slice(at, at + BLOCK)
        slot = slots.at[i % 2]
        if i >= 2:
            sent[i - 2].wait()
        slot[:, :split] = tn(a_s[:, cols], da_s[...]).astype(LOW)
        slot[:, split:end] = tn(b_s[:, cols], db_s[...]).astype(LOW)
        if end < slot.shape[1]:
            slot[:, end:] = jnp.zeros((BLOCK, slot.shape[1] - end), LOW)
        sent.append(pltpu.make_async_copy(slot, out.at[pl.ds(at, BLOCK)], out_sems.at[i]))
        sent[i].start()
    wait_all(sent[-2:])


def weight_pieces(n_groups, n_chi, *refs):
    outs, (a_s, b_s, da_s, db_s, sems) = refs[4:-5], refs[-5:]
    load_grads(refs[:4], a_s, b_s, da_s, db_s, sems)
    block = a_s.shape[1] // n_groups
    half = block // 2
    split, end = da_s.shape[1], da_s.shape[1] + db_s.shape[1]
    swapped = lax.axis_index("clo") == 1
    group = lax.axis_index("dp") * n_chi + lax.axis_index("chi")
    for r in range(n_groups):
        cols = pl.ds(pl.multiple_of((group ^ r) * block, 128), block)
        first = tn(a_s[:, cols], da_s[...]).astype(LOW)
        second = tn(b_s[:, cols], db_s[...]).astype(LOW)
        for i in range(2):
            here, there = slice(i * half, (i + 1) * half), slice((1 - i) * half, (2 - i) * half)
            out = outs[2 * r + i]
            out[:, :split] = jnp.where(swapped, first[there], first[here])
            out[:, split:end] = jnp.where(swapped, second[there], second[here])
            if end < out.shape[1]:
                out[:, end:] = jnp.zeros((half, out.shape[1] - end), LOW)


def order_columns(*refs):
    qkv, out, both, sems = refs
    width = both.shape[1] // 8
    copies = []
    for core in range(2):
        cols = pl.ds(core * width, width)
        for c in range(4):
            src = out.at[:, cols] if c == 3 else qkv.at[c, :, cols]
            dst = both.at[:, pl.ds((4 * core + c) * width, width)]
            copies.append(pltpu.make_async_copy(src, dst, sems.at[len(copies)]))
    start_all(copies)
    wait_all(copies)


def middle(own_i, moved_i, own_o, *sends):
    rows = own_o.shape[0]
    own_o[...] = own_i[:rows] + moved_i[:rows].astype(F32)
    for r, send in enumerate(sends):
        at = slice((r + 1) * rows, (r + 2) * rows)
        send[...] = (own_i[at] + moved_i[at].astype(F32)).astype(LOW)


def norm_of(value):
    center = value - jnp.mean(value, axis=-1, keepdims=True)
    inverse = lax.rsqrt(jnp.mean(center * center, axis=-1, keepdims=True) + NORM_EPS)
    return center * inverse, inverse


def norm_forward(x_i, gain, offset, *refs):
    terms, (x_o, h_o) = refs[:-2], refs[-2:]
    x = x_i[...]
    for t in terms:
        x = x + t[...].astype(F32)
    x_o[...] = x
    h_o[...] = (norm_of(x)[0] * gain[...] + offset[...]).astype(LOW)


def norm_backward(dx_i, y_i, gain, *refs):
    terms, (dy_o, low_o, small_o) = refs[:-3], refs[-3:]
    dh = terms[0][...]
    for t in terms[1:]:
        dh = dh + t[...].astype(F32)
    n, inverse = norm_of(y_i[...])
    small_o[0:1] = jnp.sum(dh * n, axis=0, keepdims=True)
    small_o[1:2] = jnp.sum(dh, axis=0, keepdims=True)
    scaled = dh * gain[...]
    dy = dx_i[...] + inverse * (
        scaled
        - jnp.mean(scaled, axis=-1, keepdims=True)
        - n * jnp.mean(scaled * n, axis=-1, keepdims=True)
    )
    dy_o[...] = dy
    low_o[...] = dy.astype(LOW)


def after(value, event):
    return lax.optimization_barrier((value, event))[0]


def log2(n):
    return n.bit_length() - 1


def reverse_bits(r, bits):
    return sum(((r >> k) & 1) << (bits - 1 - k) for k in range(bits))


def make_program(n_dp, n_chi, n_clo, n_mp):
    group_bits = [("chi", 1 << k) for k in range(log2(n_chi))]
    group_bits += [("dp", 1 << k) for k in range(log2(n_dp))]
    n_groups = n_dp * n_chi
    sizes = {"dp": n_dp, "chi": n_chi, "clo": n_clo, "mp": n_mp}
    up_order = list(range(len(group_bits)))
    down_order = up_order[::-1]

    def swap(value, axis, bit):
        return lax.ppermute(value, axis, [(i, i ^ bit) for i in range(sizes[axis])])

    def spread(pieces):
        a, b = dict(enumerate(pieces[0::2])), dict(enumerate(pieces[1::2]))
        for ka, kb in zip(down_order, up_order):
            for have, k in ((a, ka), (b, kb)):
                for r in [r for r in have if r & (1 << k)]:
                    moved = swap(have.pop(r), *group_bits[k])
                    to = r ^ (1 << k)
                    have[to] = (have[to].astype(F32) + moved.astype(F32)).astype(LOW)
        return a[0], swap(b[0], "clo", 1)

    def mp_gather(own):
        parts = [own]
        for k in reversed(range(log2(n_mp))):
            parts = parts + [swap(part, "mp", 1 << k) for part in parts]
        return [parts[reverse_bits(r, log2(n_mp))] for r in range(n_mp)]

    def token_gather(own):
        half = mp_gather(own)
        return half + [swap(part, "clo", 1) for part in half]

    def token_reduce(own_half, send_half, beside=None, before=None):
        rows, width = own_half.shape
        sub = rows // n_mp
        moved = swap(send_half, "clo", 1)
        if before is not None:
            (own_half, moved), before = lax.optimization_barrier(((own_half, moved), before))
        outs = [shape((sub, width), F32)] + [shape((sub, width), LOW)] * (n_mp - 1)
        parts = call(middle, 0, [own_half, moved], outs, [], rows * width)
        terms = [parts[0]] + [swap(parts[r], "mp", r) for r in range(1, n_mp)]
        result = None
        if beside is not None:
            work, args = beside
            terms, result = lax.optimization_barrier((terms, work(*after(args, parts[0]))))
        return terms, result, before

    def own_tokens(value):
        seqs, block, width = value.shape
        sub = block * n_chi // n_mp
        per_block = block // sub
        place = lax.axis_index("mp") % per_block
        mine = lax.dynamic_slice_in_dim(value, place * sub, sub, 1)
        chi = lax.axis_index("chi")
        here = lax.dynamic_index_in_dim(mine, chi, 0, keepdims=False)
        there = swap(lax.dynamic_index_in_dim(mine, 1 - chi, 0, keepdims=False), "chi", 1)
        return jnp.where(lax.axis_index("mp") // per_block == chi, here, there)

    def to_blocks(held, block):
        chi = lax.axis_index("chi")
        mine = lax.dynamic_slice_in_dim(held, chi * block, block, 0)
        moved = swap(lax.dynamic_slice_in_dim(held, (1 - chi) * block, block, 0), "chi", 1)
        return jnp.where(chi == 0, jnp.stack([mine, moved]), jnp.stack([moved, mine]))

    def by_place(parts):
        sub, width = parts[0].shape
        mp = lax.axis_index("mp")
        parts = jnp.stack(parts)
        for k in range(log2(n_mp)):
            pairs = parts.reshape(n_mp >> (k + 1), 2, 1 << k, sub, width)
            pairs = jnp.where((mp >> k) % 2 == 1, jnp.flip(pairs, 1), pairs)
            parts = pairs.reshape(n_mp, sub, width)
        return parts.reshape(n_mp * sub, width)

    def on_device(
        tokens, segments, cotangent, first_gain, first_bias, qkv_weight, qkv_bias,
        out_weight, second_gain, second_bias, gate_up_weight, down_weight,
    ):
        n_seq, block, width = tokens.shape
        rows_dev = qkv_weight.shape[1]
        half_in = qkv_weight.shape[3] // 2
        half_ff = down_weight.shape[2] // 2
        heads = half_in // HEAD
        total = block * n_chi * n_clo
        half_total = total // n_clo
        sub = half_total // n_mp
        n_parts = n_clo * n_mp
        mp, clo, chi = (lax.axis_index(a) for a in ("mp", "clo", "chi"))
        x_own = own_tokens(tokens).astype(F32)

        pad = -(3 * half_ff) % 128
        attn_cols, mlp_cols = 4 * half_in, 3 * half_ff + pad

        def attn_columns(l):
            view = jnp.transpose(qkv_weight[l], (1, 0, 2))
            outs = [shape((rows_dev, 2 * attn_cols), LOW)]
            args = [view, out_weight[l]]
            sems = [pltpu.SemaphoreType.DMA((8,))]
            return call(order_columns, 2, args, outs, sems, 0, hbm_outs=1)

        def mlp_columns(l):
            gu, down = jnp.transpose(gate_up_weight[l], (1, 0, 2)), down_weight[l]
            fill = jnp.zeros((rows_dev, pad), LOW)
            parts = []
            for cols in (slice(None, half_ff), slice(half_ff, None)):
                parts += [gu[0, :, cols], gu[1, :, cols], down[:, cols], fill]
            return jnp.concatenate(parts, axis=1)

        def gather_weights(own):
            return lax.all_gather(own, ("dp", "chi", "clo"), axis=0, tiled=True)

        weights = []
        for l in range(LAYERS):
            attn = [gather_weights(attn_columns(l)[0])]
            weights.append([attn, gather_weights(mlp_columns(l))])
        dx = own_tokens(cotangent)
        gains = jnp.stack([first_gain, first_bias, second_gain, second_bias])
        half_bias = jnp.where(clo == 1, qkv_bias[:, :, half_in:], qkv_bias[:, :, :half_in])
        half_bias = half_bias.reshape(LAYERS, 1, 3 * half_in)

        there = swap(lax.dynamic_index_in_dim(segments, 1 - chi, 0, keepdims=False), "chi", 1)
        here = lax.dynamic_index_in_dim(segments, chi, 0, keepdims=False)
        pair = jnp.stack([jnp.where(chi == 0, here, there), jnp.where(chi == 0, there, here)])
        other = swap(pair, "clo", 1)
        whole = jnp.stack(
            [jnp.where(clo == 0, pair, other), jnp.where(clo == 0, other, pair)], axis=1
        ).reshape(total)
        core_of = jnp.arange(n_clo, dtype=jnp.int32) ^ clo
        mp_of = jnp.arange(n_mp, dtype=jnp.int32) ^ mp
        per_block = block // sub
        place = (
            (mp_of // per_block * (n_clo * block) + mp_of % per_block * sub)[None, :, None]
            + (core_of * block)[:, None, None]
            + jnp.arange(sub, dtype=jnp.int32)[None, None, :]
        ).reshape(total)
        match = place[:, None] == jnp.arange(total, dtype=jnp.int32)[None, :]
        seg = jnp.sum(jnp.where(match, whole[None, :], 0), axis=1)
        starts = jnp.sum((seg[None, :] < seg[:, None]).astype(jnp.int32), axis=1)
        freq = jnp.exp(
            jnp.arange(ROT // 2, dtype=F32) * (-2.0 * math.log(10000.0) / ROT)
        )
        angles = freq[:, None] * (place - starts).astype(F32)[None, :]
        cos_t, sin_t = jnp.cos(angles).T, jnp.sin(angles).T
        zeros = jnp.zeros((total, ROT // 2), F32)
        tail = jnp.zeros((total, HEAD - ROT), F32)
        per_slab = 128 // HEAD
        tables = jnp.stack(
            [
                jnp.tile(jnp.concatenate(parts, axis=1), (1, per_slab))
                for parts in (
                    (cos_t, cos_t, tail + 1.0),
                    (-sin_t, zeros, tail),
                    (zeros, sin_t, tail),
                )
            ]
        )
        row = jnp.stack([seg, place])
        geometry = [tables, row.T, row]
        geometry_scratch = [
            pltpu.VMEM((3, total, 128), F32),
            pltpu.VMEM((total, 2), jnp.int32),
        ]

        act = shape((total, half_in), LOW)
        reduced = [shape((half_total, width), F32), shape((half_total, width), LOW)]
        sems = pltpu.SemaphoreType.DMA((n_parts + width // BLOCK + 5,))
        h_scratch = pltpu.VMEM((total, width), LOW)

        def mm(*dims):
            return 2 * math.prod(dims)

        def norm(x, gain, offset, terms):
            outs = [shape(x.shape, F32), shape(x.shape, LOW)]
            return call(norm_forward, 0, [x, gain[None], offset[None]] + terms, outs, [], 10 * x.size)

        def norm_back(dx, y, gain, terms):
            outs = [shape(y.shape, F32), shape(y.shape, LOW), shape((2, width), F32)]
            return call(norm_backward, 0, [dx, y, gain[None]] + terms, outs, [], 20 * y.size)

        def grads(a, b, da, db, cols, pieces):
            scratch = [pltpu.VMEM(x.shape, LOW) for x in (a, b, da, db)]
            sems = pltpu.SemaphoreType.DMA((4,))
            if pieces:
                body = functools.partial(weight_pieces, n_groups, n_chi)
                outs = [shape((rows_dev, cols), LOW)] * (2 * n_groups)
                scratch += [sems]
            else:
                body = weight_grads
                outs = [shape((width, cols), LOW)]
                scratch += [pltpu.VMEM((2, BLOCK, cols), LOW), sems]
                scratch += [pltpu.SemaphoreType.DMA((width // BLOCK,))]
            return call(
                body, 4, [a, b, da, db], outs, scratch, mm(total, width, cols),
                hbm_outs=0 if pieces else 1, limit=60,
            )

        def scatter(partial):
            return lax.psum_scatter(partial[0], ("dp", "chi"), scatter_dimension=0, tiled=True)

        def pick(block_sum):
            mine = lax.dynamic_slice_in_dim(block_sum, clo * rows_dev, rows_dev, 0)
            others = lax.dynamic_slice_in_dim(block_sum, (1 - clo) * rows_dev, rows_dev, 0)
            return mine, swap(others, "clo", 1)

        def columns(pieces, first, count, parts):
            mine, others = (
                piece[:, first : first + count].reshape((rows_dev,) + parts + (-1,))
                for piece in pieces
            )
            low = jnp.where(clo == 0, mine, others)
            high = jnp.where(clo == 0, others, mine)
            return jnp.concatenate([low, high], axis=-1).astype(F32)

        def above_zeros(x):
            layout = Layout(major_to_minor=tuple(range(x.ndim + 1)))
            return with_layout_constraint(jnp.stack([jnp.zeros_like(x), x]), layout)

        def attn_out(pieces):
            return (
                columns(pieces, 0, 3 * half_in, (3,)),
                columns(pieces, 3 * half_in, half_in, ()),
            )

        def mlp_out(pieces):
            return (
                columns(pieces, 0, 2 * half_ff, (2,)),
                columns(pieces, 2 * half_ff, half_ff, ()),
            )

        whole = shape((total, width), LOW)
        saved = []
        terms = []
        for l in range(LAYERS):
            w_attn, w_mlp = weights[l]
            x_own, h = norm(x_own, gains[0, l], gains[1, l], terms)
            h1 = token_gather(h)
            h1, q, k, v, o, own, send = call(
                functools.partial(attn_forward, n_parts, heads),
                n_parts + 3,
                h1 + w_attn + geometry + [half_bias[l]],
                [whole] + [act] * 4 + reduced,
                [
                    h_scratch,
                    pltpu.VMEM((width, attn_cols), LOW),
                    pltpu.VMEM((total, 3 * half_in), F32),
                ]
                + geometry_scratch
                + [sems],
                mm(total, width, attn_cols) + 2 * mm(heads, total, total, 2 * half_in),
                n_any=n_parts,
                hbm_outs=1,
                limit=56,
            )
            y_own, h = norm(x_own, gains[2, l], gains[3, l], token_reduce(own, send)[0])
            h2 = token_gather(h)
            h2, gu, z, own, send = call(
                functools.partial(mlp_forward, n_parts),
                n_parts + 1,
                h2 + [w_mlp],
                [whole, shape((total, 2 * half_ff), F32), shape((total, half_ff), LOW)] + reduced,
                [h_scratch, pltpu.VMEM((width, mlp_cols), LOW), sems],
                mm(total, width, mlp_cols),
                n_any=n_parts,
                hbm_outs=1,
            )
            saved.append((x_own, h1, q, k, v, o, y_own, h2, gu, z))
            x_own, terms = y_own, token_reduce(own, send)[0]

        low = dx
        dx = dx.astype(F32)
        small_out = [None] * LAYERS
        done = None
        for l in reversed(range(LAYERS)):
            w_attn, w_mlp = weights[l]
            x_own, h1, q, k, v, o, y_own, h2, gu, z = saved[l]
            parts = token_gather(low)
            dm, dp2, own, send = call(
                functools.partial(mlp_backward, n_parts),
                n_parts + 2,
                parts + [w_mlp, gu],
                [whole, shape((total, 2 * half_ff), LOW)] + reduced,
                [
                    h_scratch,
                    pltpu.VMEM((width, mlp_cols), LOW),
                    pltpu.VMEM((total, half_ff), F32),
                    pltpu.VMEM(gu.shape, F32),
                    sems,
                ],
                mm(total, width, mlp_cols),
                n_any=n_parts,
                hbm_outs=1,
            )
            work = functools.partial(grads, cols=mlp_cols, pieces=False)
            if done is None:
                terms, g_mlp, last = token_reduce(own, send, (work, (h2, dm, dp2, z)), terms)
                x_last = y_own
                for t in last:
                    x_last = x_last + t.astype(F32)
                x_last = mp_gather(x_last.astype(LOW))
            else:
                terms, g_mlp, _ = token_reduce(own, send, (work, (h2, dm, dp2, z)))
            g_mlp = scatter(g_mlp)
            dy, low, small_two = norm_back(dx, y_own, gains[2, l], terms)
            parts = token_gather(low)
            if done is not None:
                late, early = done
                early = [above_zeros(x) for x in mlp_out(pick(early))]
                parts, early = lax.optimization_barrier((parts, early))
            da, dp1, bias_grad, own, send = call(
                functools.partial(attn_backward, n_parts, heads),
                n_parts + 6,
                parts + w_attn + [q, k, v] + geometry,
                [whole, shape((total, 3 * half_in), LOW), shape((1, 3 * half_in), F32)] + reduced,
                [
                    h_scratch,
                    pltpu.VMEM((width, attn_cols), LOW),
                    pltpu.VMEM((total, half_in), F32),
                    pltpu.VMEM((3, total, half_in), LOW),
                ]
                + geometry_scratch
                + [sems],
                mm(total, width, attn_cols) + 5 * mm(heads, total, total, half_in),
                n_any=n_parts,
                hbm_outs=1,
                limit=56,
            )
            work = functools.partial(grads, cols=attn_cols, pieces=False)
            if done is None:
                terms, g_attn, x_last = token_reduce(own, send, (work, (h1, da, dp1, o)), x_last)
                activations = to_blocks(by_place(x_last), block)
                done = (scatter(g_attn), g_mlp)
            else:
                terms, g_attn, _ = token_reduce(own, send, (work, (h1, da, dp1, o)))
                late = [above_zeros(x) for x in attn_out(pick(late))]
                terms, late = lax.optimization_barrier((terms, late))
            dx, low, small_one = norm_back(dy, x_own, gains[0, l], terms)
            small_out[l] = (small_one, small_two, bias_grad)
        parts = mp_gather(low)
        tokens_grad = to_blocks(by_place(parts), block).astype(F32)
        g_mlp, small_out = after((g_mlp, small_out), parts[n_mp // 2])
        g_attn, mlp_last = pick(scatter(g_attn)), mlp_out(pick(g_mlp))
        parts = zip(late + early, attn_out(g_attn) + tuple(mlp_last))
        weight_out = [stack.at[0].set(part) for stack, part in parts]

        norms = jnp.stack(
            [jnp.concatenate(small_out[l][:2], axis=0) for l in range(LAYERS)], axis=1
        )
        bias = jnp.stack([small_out[l][2] for l in range(LAYERS)]).reshape(LAYERS, 3, half_in)
        for k in range(log2(n_mp)):
            norms = norms + swap(norms, "mp", 1 << k)
        norms = norms + swap(norms, "clo", 1)
        for name, bit in group_bits:
            norms = norms + swap(norms, name, bit)
            bias = bias + swap(bias, name, bit)
        bias_other = swap(bias, "clo", 1)
        bias = jnp.concatenate(
            [jnp.where(clo == 0, bias, bias_other), jnp.where(clo == 0, bias_other, bias)], axis=2
        )

        return (
            activations, tokens_grad, norms[0], norms[1],
            weight_out[0], bias, weight_out[1], norms[2], norms[3], weight_out[2], weight_out[3],
        )

    return on_device


def solution(mesh):
    n_dp, n_ctx, n_mp = (mesh.shape[a] for a in ("dp", "ctx", "mp"))
    n_clo = 2
    n_chi = n_ctx // n_clo
    fine = Mesh(mesh.devices.reshape(n_dp, n_chi, n_clo, n_mp), ("dp", "chi", "clo", "mp"))
    rows = ("dp", "chi", "clo")
    ctx = ("chi", "clo")
    token_spec = P("dp", ctx, None)
    four, three = P(None, rows, None, "mp"), P(None, rows, "mp")
    bias_spec = P(None, None, "mp")
    return jax.shard_map(
        make_program(n_dp, n_chi, n_clo, n_mp),
        mesh=fine,
        in_specs=(
            token_spec, P("dp", ctx), token_spec, P(), P(), four, bias_spec, three, P(), P(),
            four, three,
        ),
        out_specs=(
            token_spec, token_spec, P(), P(), four, bias_spec, three, P(), P(), four, three,
        ),
        check_vma=False,
    )
```

time: 879 us -> 761 us (0.87)
  waiting for transfers between devices: 434 us -> 358 us
  starting transfers between devices: 165 us -> 110 us
  Pallas kernels: 114 us -> 133 us
  other arithmetic: 54.8 us -> 40.7 us
  between operations: 4.21 us -> 15.8 us
    ppermute x164 -> x112, waiting for transfers between devices: 434 us -> 324 us  [swap(): return lax.ppermute(value, axis, [(i, i ^ bit) for i in range(sizes[axis])])]
    ppermute x164 -> x112, starting transfers between devices: 165 us -> 109 us  [swap(): return lax.ppermute(value, axis, [(i, i ^ bit) for i in range(sizes[axis])])]
    all_gather x0 -> x4, waiting for transfers between devices: none -> 33.5 us  [gather_weights(): return lax.all_gather(own, ('dp', 'chi', 'clo'), axis=0, tiled=True)]
    convert_element_type x19 -> x4, other arithmetic: 22.9 us -> 2.74 us  [the longest x1 1.51 us: on_device(): tokens_grad = to_blocks(by_place(parts), block).astype(F32)]
    pallas_call x30, Pallas kernels: 114 us -> 133 us  [call(): pl.pallas_call(body, out_shape=tuple(outs), in_specs=[ANY] * n_any + [HBM...]
    unnamed x522 -> x223, local copies, waits for them, and re-layouts: 62.8 us -> 54.2 us
  transfers between devices with their start and end apart: 164 -> 120, of which waited for: 56 -> 54; matrix products, arithmetic and copies ran while one was open for 12% -> 11% of each run, Pallas kernels for 11% -> 17%
where the time goes in v4:
time: 761 us; the launch traced here: 756 us
  waiting for transfers between devices  358 us (47%)
  Pallas kernels  133 us (17%)
  starting transfers between devices  110 us (14%)
  local copies, waits for them, and re-layouts  98.6 us (13%)
  other arithmetic  40.7 us (5%)
  between operations  15.8 us (2%)
    ppermute x112, waiting for transfers between devices, swap(): return lax.ppermute(value, axis, [(i, i ^ bit) for i in range(sizes[axis])])  324 us
    pallas_call x30, Pallas kernels, call(): pl.pallas_call(body, out_shape=tuple(outs), in_specs=[ANY] * n_any + [HBM...  133 us
    ppermute x112, starting transfers between devices, swap(): return lax.ppermute(value, axis, [(i, i ^ bit) for i in range(sizes[axis])])  109 us
    unnamed x223, local copies, waits for them, and re-layouts  54.2 us
    all_gather x4, waiting for transfers between devices, gather_weights(): return lax.all_gather(own, ('dp', 'chi', 'clo'), axis=0, tiled=True)  33.5 us
  transfers between devices with their start and end apart: 120, of which 54 were waited for; matrix products, arithmetic and copies ran while one was open for 11% of the time, Pallas kernels for 17%

profile of v4, /device:TPU:0, one launch (start us, length us, event | category | flops | bytes accessed | tf_op | source)
XLA Modules:
  0.0 755.8 jit_solution(6671989365099723301)
XLA Ops:
  10.0 3.7 fusion.30
  17.1 5.0 concatenate.140
  24.6 4.2 concatenate.141
  35.3 5.3 collective-permute-done.1
  45.6 9.1 %collective-permute-done.3.refs_2_ = bf16[64,2048]{1,0:T(8,128)(2,1)S(1)} collective-permute-done((bf16[64,2048]{1,0:T(8,128)(2,1)S(1)}, bf16[64,2048]{1,0:T(8,128)(2,1)S(1)}, u32[]{:S(2)}, u32[]{:S(2)}) %collective-permute-start.3) | collective-permute-done | bytes 262176 | tf_op jit(solution)/shard_map/ppermute | solution.py:392
  55.7 6.3 collective-permute-done.4.refs_3_
  67.6 11.5 %shard_map.205 = (bf16[512,2048]{1,0:T(8,128)(2,1)}, bf16[512,256]{1,0:T(8,128)(2,1)}, bf16[512,256]{1,0:T(8,128)(2,1)}, bf16[512,256]{1,0:T(8,128)(2,1)}, bf16[...) custom-call(bf16[64,2048]{1,0:T(8,128)(2,1)} %copy-done.60, bf16[64,2048]{1,0:T(8,128)(2,1)} %copy-done.96, ...), custom_call_target="tpu_custom_call" | custom-call | flops 4294967296 | bytes 17574912 | tf_op jit(solution)/shard_map/pallas_call | solution.py:50
  88.4 9.1 %collective-permute-done.12.refs_1_ = bf16[64,2048]{1,0:T(8,128)(2,1)S(1)} collective-permute-done((bf16[64,2048]{1,0:T(8,128)(2,1)S(1)}, bf16[64,2048]{1,0:T(8,128)(2,1)S(1)}, u32[]{:S(2)}, u32[]{:S(2)}) %collective-permute-start.12) | collective-permute-done | bytes 262176 | tf_op jit(solution)/shard_map/ppermute | solution.py:392
  97.5 9.4 %collective-permute-done.13.refs_2_ = bf16[64,2048]{1,0:T(8,128)(2,1)S(1)} collective-permute-done((bf16[64,2048]{1,0:T(8,128)(2,1)S(1)}, bf16[64,2048]{1,0:T(8,128)(2,1)S(1)}, u32[]{:S(2)}, u32[]{:S(2)}) %collective-permute-start.13) | collective-permute-done | bytes 262176 | tf_op jit(solution)/shard_map/ppermute | solution.py:392
  108.0 6.1 collective-permute-start.16
  114.2 11.3 %collective-permute-done.16.refs_2_ = bf16[64,2048]{1,0:T(8,128)(2,1)S(1)} collective-permute-done((bf16[64,2048]{1,0:T(8,128)(2,1)S(1)}, bf16[64,2048]{1,0:T(8,128)(2,1)S(1)}, u32[]{:S(2)}, u32[]{:S(2)}) %collective-permute-start.16) | collective-permute-done | bytes 262176 | tf_op jit(solution)/shard_map/ppermute | solution.py:392
  128.1 4.3 collective-permute-done.17.refs_3_
  136.0 28.4 %all-gather.7.cloned.1.call-done.refs_8_ = bf16[2048,4352]{1,0:T(8,128)(2,1)} async-done(((bf16[256,4352]{1,0:T(8,128)(2,1)}), bf16[2048,4352]{1,0:T(8,128)(2,1)}) %all-gather.7.cloned.1.call-update) | async-done | bytes 17825808 | tf_op jit(solution)/shard_map/all_gather | solution.py:491
  172.0 7.7 %shard_map.208 = (bf16[512,2048]{1,0:T(8,128)(2,1)S(1)}, f32[512,1408]{1,0:T(8,128)S(1)}, bf16[512,704]{1,0:T(8,128)(2,1)S(1)}, f32[256,2048]{1,0:T(8,128)S(1)}, bf16[256,2048]{1,0:T(8,128)(2,1)S(1)}) custom-call(bf16[64,2048]{1,0:T(8,128)(2,1)S(1)} %copy-done.31, bf16[64,2048]{1,0:T(8,128)(2,1)S(1)} %copy-done.41, bf16[64,2048]{1,0:T(8,128)(2,1)S(1)} %copy-done.37, ...), custom_call_target="tpu_custom_call" | custom-call | flops 4563402752 | bytes 28770304 | tf_op jit(solution)/shard_map/pallas_call | solution.py:50
  188.4 9.1 %collective-permute-done.23.refs_1_ = bf16[64,2048]{1,0:T(8,128)(2,1)S(1)} collective-permute-done((bf16[64,2048]{1,0:T(8,128)(2,1)S(1)}, bf16[64,2048]{1,0:T(8,128)(2,1)S(1)}, u32[]{:S(2)}, u32[]{:S(2)}) %collective-permute-start.23) | collective-permute-done | bytes 262176 | tf_op jit(solution)/shard_map/ppermute | solution.py:392
  197.4 9.2 %collective-permute-done.24.refs_2_ = bf16[64,2048]{1,0:T(8,128)(2,1)S(1)} collective-permute-done((bf16[64,2048]{1,0:T(8,128)(2,1)S(1)}, bf16[64,2048]{1,0:T(8,128)(2,1)S(1)}, u32[]{:S(2)}, u32[]{:S(2)}) %collective-permute-start.24) | collective-permute-done | bytes 262176 | tf_op jit(solution)/shard_map/ppermute | solution.py:392
  208.5 6.1 collective-permute-start.27
  214.7 11.8 %collective-permute-done.27.refs_2_ = bf16[64,2048]{1,0:T(8,128)(2,1)} collective-permute-done((bf16[64,2048]{1,0:T(8,128)(2,1)}, bf16[64,2048]{1,0:T(8,128)(2,1)}, u32[]{:S(2)}, u32[]{:S(2)}) %collective-permute-start.27) | collective-permute-done | bytes 262176 | tf_op jit(solution)/shard_map/ppermute | solution.py:392
  227.0 6.7 collective-permute-done.28.refs_3_
  235.6 11.4 %shard_map.212 = (bf16[512,2048]{1,0:T(8,128)(2,1)}, bf16[512,256]{1,0:T(8,128)(2,1)}, bf16[512,256]{1,0:T(8,128)(2,1)}, bf16[512,256]{1,0:T(8,128)(2,1)}, bf16[...) custom-call(bf16[64,2048]{1,0:T(8,128)(2,1)} %get-tuple-element.240.refs_0_, ...), custom_call_target="tpu_custom_call" | custom-call | flops 4294967296 | bytes 17574912 | tf_op jit(solution)/shard_map/pallas_call | solution.py:50
  257.8 7.1 collective-permute-done.34.refs_1_
  264.9 8.8 %collective-permute-done.35.refs_2_ = bf16[64,2048]{1,0:T(8,128)(2,1)S(1)} collective-permute-done((bf16[64,2048]{1,0:T(8,128)(2,1)S(1)}, bf16[64,2048]{1,0:T(8,128)(2,1)S(1)}, u32[]{:S(2)}, u32[]{:S(2)}) %collective-permute-start.35) | collective-permute-done | bytes 262176 | tf_op jit(solution)/shard_map/ppermute | solution.py:392
  274.8 5.5 collective-permute-start.45
  283.9 15.0 %collective-permute-done.45.refs_2_ = bf16[64,2048]{1,0:T(8,128)(2,1)S(1)} collective-permute-done((bf16[64,2048]{1,0:T(8,128)(2,1)S(1)}, bf16[64,2048]{1,0:T(8,128)(2,1)S(1)}, u32[]{:S(2)}, u32[]{:S(2)}) %collective-permute-start.45) | collective-permute-done | bytes 262176 | tf_op jit(solution)/shard_map/ppermute | solution.py:392
  299.1 3.9 collective-permute-done.38.refs_2_
  305.8 4.9 collective-permute-done.46.refs_3_
  310.7 4.6 collective-permute-done.39.refs_3_
  326.8 7.4 shard_map.215
  336.7 9.2 %shard_map.216 = (bf16[512,2048]{1,0:T(8,128)(2,1)S(1)}, bf16[512,1408]{1,0:T(8,128)(2,1)S(1)}, f32[256,2048]{1,0:T(8,128)S(1)}, bf16[256,2048]{1,0:T(8,128)(2,1)S(1)}) custom-call(bf16[64,2048]{1,0:T(8,128)(2,1)} %get-tuple-element.421.refs_0_, bf16[64,2048]{1,0:T(8,128)(2,1)} %collective-permute-done.37.refs_1_, ...), custom_call_target="tpu_custom_call" | custom-call | flops 4563402752 | bytes 29491200 | tf_op jit(solution)/shard_map/pallas_call | solution.py:50
  350.8 9.1 %collective-permute-done.53 = bf16[64,2048]{1,0:T(8,128)(2,1)S(1)} collective-permute-done((bf16[64,2048]{1,0:T(8,128)(2,1)S(1)}, bf16[64,2048]{1,0:T(8,128)(2,1)S(1)}, u32[]{:S(2)}, u32[]{:S(2)}) %collective-permute-start.53) | collective-permute-done | bytes 262176 | tf_op jit(solution)/shard_map/ppermute | solution.py:392
  359.9 8.9 %collective-permute-done.54 = bf16[64,2048]{1,0:T(8,128)(2,1)S(1)} collective-permute-done((bf16[64,2048]{1,0:T(8,128)(2,1)S(1)}, bf16[64,2048]{1,0:T(8,128)(2,1)S(1)}, u32[]{:S(2)}, u32[]{:S(2)}) %collective-permute-start.54) | collective-permute-done | bytes 262176 | tf_op jit(solution)/shard_map/ppermute | solution.py:392
  370.8 5.2 collective-permute-start.56
  378.4 10.4 %shard_map.219 = bf16[2048,2176]{1,0:T(8,128)(2,1)} custom-call(bf16[512,2048]{1,0:T(8,128)(2,1)} %copy-done.53, bf16[512,2048]{1,0:T(8,128)(2,1)} %copy-done.54, bf16[512,1408]{1,0:T(8,128)(2,1)} %copy-done.56, bf16[512,704]{1,0:T(8,128)(2,1)} %copy-done.59), custom_call_target="tpu_custom_call" | custom-call | flops 4563402752 | bytes 15269888 | tf_op jit(solution)/shard_map/pallas_call | solution.py:50
  388.8 8.8 %collective-permute-done.57.refs_2_ = bf16[64,2048]{1,0:T(8,128)(2,1)} collective-permute-done((bf16[64,2048]{1,0:T(8,128)(2,1)}, bf16[64,2048]{1,0:T(8,128)(2,1)}, u32[]{:S(2)}, u32[]{:S(2)}) %collective-permute-start.57) | collective-permute-done | bytes 262176 | tf_op jit(solution)/shard_map/ppermute | solution.py:392
  403.8 5.0 collective-permute-start.60
  408.7 10.1 %collective-permute-done.60.refs_2_ = bf16[64,2048]{1,0:T(8,128)(2,1)S(1)} collective-permute-done((bf16[64,2048]{1,0:T(8,128)(2,1)S(1)}, bf16[64,2048]{1,0:T(8,128)(2,1)S(1)}, u32[]{:S(2)}, u32[]{:S(2)}) %collective-permute-start.60) | collective-permute-done | bytes 262176 | tf_op jit(solution)/shard_map/ppermute | solution.py:392
  419.5 6.3 collective-permute-done.61.refs_3_
  428.1 13.8 %shard_map.221 = (bf16[512,2048]{1,0:T(8,128)(2,1)}, bf16[512,768]{1,0:T(8,128)(2,1)}, f32[1,768]{1,0:T(1,128)}, f32[256,2048]{1,0:T(8,128)}, bf16[256,2048]{1,0:T(8,128)(2,1)}) custom-call(bf16[64,2048]{1,0:T(8,128)(2,1)} %copy-done.61, bf16[64,2048]{1,0:T(8,128)(2,1)} %copy-done.102, bf16[64,2048]{1,0:T(8,128)(2,1)} %copy-done.101, ...), custom_call_target="tpu_custom_call" | custom-call | flops 4831838208 | bytes 18099200 | tf_op jit(solution)/shard_map/pallas_call | solution.py:50
  444.1 13.2 %collective-permute-done.68 = bf16[64,2048]{1,0:T(8,128)(2,1)S(1)} collective-permute-done((bf16[64,2048]{1,0:T(8,128)(2,1)S(1)}, bf16[64,2048]{1,0:T(8,128)(2,1)S(1)}, u32[]{:S(2)}, u32[]{:S(2)}) %collective-permute-start.68) | collective-permute-done | bytes 262176 | tf_op jit(solution)/shard_map/ppermute | solution.py:392
  457.3 8.2 %collective-permute-done.69 = bf16[64,2048]{1,0:T(8,128)(2,1)S(1)} collective-permute-done((bf16[64,2048]{1,0:T(8,128)(2,1)S(1)}, bf16[64,2048]{1,0:T(8,128)(2,1)S(1)}, u32[]{:S(2)}, u32[]{:S(2)}) %collective-permute-start.69) | collective-permute-done | bytes 262176 | tf_op jit(solution)/shard_map/ppermute | solution.py:392
  471.8 6.9 shard_map.223
  479.1 10.0 %collective-permute-done.72.refs_2_ = bf16[64,2048]{1,0:T(8,128)(2,1)} collective-permute-done((bf16[64,2048]{1,0:T(8,128)(2,1)}, bf16[64,2048]{1,0:T(8,128)(2,1)}, u32[]{:S(2)}, u32[]{:S(2)}) %collective-permute-start.72) | collective-permute-done | bytes 262176 | tf_op jit(solution)/shard_map/ppermute | solution.py:392
  494.9 4.4 collective-permute-start.75
  499.6 10.1 %collective-permute-done.75.refs_2_ = bf16[64,2048]{1,0:T(8,128)(2,1)S(1)} collective-permute-done((bf16[64,2048]{1,0:T(8,128)(2,1)S(1)}, bf16[64,2048]{1,0:T(8,128)(2,1)S(1)}, u32[]{:S(2)}, u32[]{:S(2)}) %collective-permute-start.75) | collective-permute-done | bytes 262176 | tf_op jit(solution)/shard_map/ppermute | solution.py:392
  510.5 5.6 collective-permute-done.76.refs_3_
  517.6 8.7 %shard_map.225 = (bf16[512,2048]{1,0:T(8,128)(2,1)S(1)}, bf16[512,1408]{1,0:T(8,128)(2,1)S(1)}, f32[256,2048]{1,0:T(8,128)S(1)}, bf16[256,2048]{1,0:T(8,128)(2,1)S(1)}) custom-call(bf16[64,2048]{1,0:T(8,128)(2,1)S(1)} %get-tuple-element.310.refs_0_, bf16[64,2048]{1,0:T(8,128)(2,1)S(1)} %collective-permute-done.74.refs_1_, ...), custom_call_target="tpu_custom_call" | custom-call | flops 4563402752 | bytes 29491200 | tf_op jit(solution)/shard_map/pallas_call | solution.py:50
  532.1 3.4 collective-permute-start.83
  535.5 10.5 %shard_map.227 = bf16[2048,2176]{1,0:T(8,128)(2,1)} custom-call(bf16[512,2048]{1,0:T(8,128)(2,1)} %copy-done.52, bf16[512,2048]{1,0:T(8,128)(2,1)} %copy-done.55, bf16[512,1408]{1,0:T(8,128)(2,1)} %copy-done.57, bf16[512,704]{1,0:T(8,128)(2,1)} %copy-done.58), custom_call_target="tpu_custom_call" | custom-call | flops 4563402752 | bytes 15269888 | tf_op jit(solution)/shard_map/pallas_call | solution.py:50
  546.0 7.9 %collective-permute-done.83.refs_2_ = bf16[64,2048]{1,0:T(8,128)(2,1)S(1)} collective-permute-done((bf16[64,2048]{1,0:T(8,128)(2,1)S(1)}, bf16[64,2048]{1,0:T(8,128)(2,1)S(1)}, u32[]{:S(2)}, u32[]{:S(2)}) %collective-permute-start.83) | collective-permute-done | bytes 262176 | tf_op jit(solution)/shard_map/ppermute | solution.py:392
  557.7 6.4 collective-permute-start.86
  564.1 13.0 %collective-permute-done.86.refs_2_ = bf16[64,2048]{1,0:T(8,128)(2,1)} collective-permute-done((bf16[64,2048]{1,0:T(8,128)(2,1)}, bf16[64,2048]{1,0:T(8,128)(2,1)}, u32[]{:S(2)}, u32[]{:S(2)}) %collective-permute-start.86) | collective-permute-done | bytes 262176 | tf_op jit(solution)/shard_map/ppermute | solution.py:392
  577.6 7.9 %collective-permute-done.87.refs_3_ = bf16[64,2048]{1,0:T(8,128)(2,1)} collective-permute-done((bf16[64,2048]{1,0:T(8,128)(2,1)}, bf16[64,2048]{1,0:T(8,128)(2,1)}, u32[]{:S(2)}, u32[]{:S(2)}) %collective-permute-start.87) | collective-permute-done | bytes 262176 | tf_op jit(solution)/shard_map/ppermute | solution.py:392
  593.0 5.1 fusion.5
  600.1 13.6 %shard_map.229 = (bf16[512,2048]{1,0:T(8,128)(2,1)}, bf16[512,768]{1,0:T(8,128)(2,1)}, f32[1,768]{1,0:T(1,128)}, f32[256,2048]{1,0:T(8,128)}, bf16[256,2048]{1,0:T(8,128)(2,1)}) custom-call(bf16[64,2048]{1,0:T(8,128)(2,1)} %get-tuple-element.333.refs_0_, bf16[64,2048]{1,0:T(8,128)(2,1)} %collective-permute-done.85.refs_1_, ...), custom_call_target="tpu_custom_call" | custom-call | flops 4831838208 | bytes 18099200 | tf_op jit(solution)/shard_map/pallas_call | solution.py:50
  626.1 7.4 shard_map.231
  633.5 8.1 %collective-permute-done.95.refs_2_ = bf16[64,2048]{1,0:T(8,128)(2,1)S(1)} collective-permute-done((bf16[64,2048]{1,0:T(8,128)(2,1)}, bf16[64,2048]{1,0:T(8,128)(2,1)S(1)}, u32[]{:S(2)}, u32[]{:S(2)}) %collective-permute-start.95) | collective-permute-done | bytes 262176 | tf_op jit(solution)/shard_map/ppermute | solution.py:392
  659.2 5.5 collective-permute-start.99
  664.8 12.3 %collective-permute-done.99 = bf16[64,2048]{1,0:T(8,128)(2,1)S(1)} collective-permute-done((bf16[64,2048]{1,0:T(8,128)(2,1)S(1)}, bf16[64,2048]{1,0:T(8,128)(2,1)S(1)}, u32[]{:S(2)}, u32[]{:S(2)}) %collective-permute-start.99) | collective-permute-done | bytes 262176 | tf_op jit(solution)/shard_map/ppermute | solution.py:392
  679.4 5.6 collective-permute-done.100
  693.4 3.3 collective-permute-done.103
  696.8 11.5 %collective-permute-done.101 = bf16[128,2048]{1,0:T(8,128)(2,1)S(1)} collective-permute-done((bf16[128,2048]{1,0:T(8,128)(2,1)S(1)}, bf16[128,2048]{1,0:T(8,128)(2,1)S(1)}, u32[]{:S(2)}, u32[]{:S(2)}) %collective-permute-start.101) | collective-permute-done | bytes 524320 | tf_op jit(solution)/shard_map/ppermute | solution.py:392
  715.3 3.6 collective-permute-done.106
  734.7 3.4 convert_dynamic-update-slice_fusion
  741.9 4.9 copy.86
  (554 shorter events, 219.7 us)
Async XLA Ops:
  7.2 60.4 %all-gather.5.cloned.1.call-start = ((), (), s32[]{:S(2)}) async-start(), calls=%async_computation.4 | async-start | bytes 9437184 | tf_op jit(solution)/shard_map/all_gather | solution.py:491
  9.9 154.5 %all-gather.7.cloned.1.call-start = ((), (), s32[]{:S(2)}) async-start(), calls=%async_computation.5 | async-start | bytes 20054016 | tf_op jit(solution)/shard_map/all_gather | solution.py:491
  22.1 211.6 %all-gather.9.cloned.1.call-start = ((), (), s32[]{:S(2)}) async-start(), calls=%async_computation.6 | async-start | bytes 9437184 | tf_op jit(solution)/shard_map/all_gather | solution.py:491
  23.2 297.8 %all-gather.11.cloned.1.call-start = ((), (), s32[]{:S(2)}) async-start(), calls=%async_computation.7 | async-start | bytes 20054016 | tf_op jit(solution)/shard_map/all_gather | solution.py:491
  28.9 525.1 %reduce-scatter.5.cloned.1.call-start = ((), (), s32[]{:S(2)}) async-start(), calls=%async_computation.8 | async-start | bytes 11141120 | tf_op jit(solution)/shard_map/reduce_scatter | solution.py:579
  41.0 13.7 %collective-permute-start.3 = (bf16[64,2048]{1,0:T(8,128)(2,1)S(1)}, bf16[64,2048]{1,0:T(8,128)(2,1)S(1)}, u32[]{:S(2)}, u32[]{:S(2)}) collective-permute-start(bf16[64,2048]{1,0:T(8,128)(2,1)S(1)} %get-tuple-element.224.refs_0_), channel_id=1, source_target_pairs={{0,2},{1,3},{2,0},{3,1},{4,6},{5,7},{6,4},{7,5},{8,10},{9,11},{10,... | collective-permute-start | bytes 786440 | tf_op jit(solution)/shard_map/ppermute | solution.py:392
  83.9 13.6 %collective-permute-start.12 = (bf16[64,2048]{1,0:T(8,128)(2,1)S(1)}, bf16[64,2048]{1,0:T(8,128)(2,1)S(1)}, u32[]{:S(2)}, u32[]{:S(2)}) collective-permute-start(bf16[64,2048]{1,0:T(8,128)(2,1)S(1)} %get-tuple-element.228), channel_id=1, source_target_pairs={{0,1},{1,0},{2,3},{3,2},{4,5},{5,4},{6,7},{7,6},{8,9},{9,8},{10,11... | collective-permute-start | bytes 786440 | tf_op jit(solution)/shard_map/ppermute | solution.py:392
  85.5 21.3 %collective-permute-start.13 = (bf16[64,2048]{1,0:T(8,128)(2,1)S(1)}, bf16[64,2048]{1,0:T(8,128)(2,1)S(1)}, u32[]{:S(2)}, u32[]{:S(2)}) collective-permute-start(bf16[64,2048]{1,0:T(8,128)(2,1)S(1)} %get-tuple-element.229), channel_id=1, source_target_pairs={{0,2},{1,3},{2,0},{3,1},{4,6},{5,7},{6,4},{7,5},{8,10},{9,11},{10,... | collective-permute-start | bytes 786440 | tf_op jit(solution)/shard_map/ppermute | solution.py:392
  87.9 18.9 %collective-permute-start.14 = (bf16[64,2048]{1,0:T(8,128)(2,1)S(1)}, bf16[64,2048]{1,0:T(8,128)(2,1)S(1)}, u32[]{:S(2)}, u32[]{:S(2)}) collective-permute-start(bf16[64,2048]{1,0:T(8,128)(2,1)S(1)} %get-tuple-element.230), channel_id=1, source_target_pairs={{0,3},{1,2},{2,1},{3,0},{4,7},{5,6},{6,5},{7,4},{8,11},{9,10},{10,... | collective-permute-start | bytes 786440 | tf_op jit(solution)/shard_map/ppermute | solution.py:392
  108.0 17.5 %collective-permute-start.16 = (bf16[64,2048]{1,0:T(8,128)(2,1)S(1)}, bf16[64,2048]{1,0:T(8,128)(2,1)S(1)}, u32[]{:S(2)}, u32[]{:S(2)}) collective-permute-start(bf16[64,2048]{1,0:T(8,128)(2,1)S(1)} %get-tuple-element.232.refs_0_), channel_id=1, source_target_pairs={{0,2},{1,3},{2,0},{3,1},{4,6},{5,7},{6,4},{7,5},{8,10},{9,11},{10,... | collective-permute-start | bytes 786440 | tf_op jit(solution)/shard_map/ppermute | solution.py:392
  114.1 13.3 %collective-permute-start.15 = (bf16[64,2048]{1,0:T(8,128)(2,1)S(1)}, bf16[64,2048]{1,0:T(8,128)(2,1)S(1)}, u32[]{:S(2)}, u32[]{:S(2)}) collective-permute-start(bf16[64,2048]{1,0:T(8,128)(2,1)S(1)} %get-tuple-element.232.refs_0_), channel_id=1, source_target_pairs={{0,1},{1,0},{2,3},{3,2},{4,5},{5,4},{6,7},{7,6},{8,9},{9,8},{10,11... | collective-permute-start | bytes 786440 | tf_op jit(solution)/shard_map/ppermute | solution.py:392
  183.9 13.5 %collective-permute-start.23 = (bf16[64,2048]{1,0:T(8,128)(2,1)S(1)}, bf16[64,2048]{1,0:T(8,128)(2,1)S(1)}, u32[]{:S(2)}, u32[]{:S(2)}) collective-permute-start(bf16[64,2048]{1,0:T(8,128)(2,1)S(1)} %get-tuple-element.236), channel_id=1, source_target_pairs={{0,1},{1,0},{2,3},{3,2},{4,5},{5,4},{6,7},{7,6},{8,9},{9,8},{10,11... | collective-permute-start | bytes 786440 | tf_op jit(solution)/shard_map/ppermute | solution.py:392
  185.3 21.4 %collective-permute-start.24 = (bf16[64,2048]{1,0:T(8,128)(2,1)S(1)}, bf16[64,2048]{1,0:T(8,128)(2,1)S(1)}, u32[]{:S(2)}, u32[]{:S(2)}) collective-permute-start(bf16[64,2048]{1,0:T(8,128)(2,1)S(1)} %get-tuple-element.237), channel_id=1, source_target_pairs={{0,2},{1,3},{2,0},{3,1},{4,6},{5,7},{6,4},{7,5},{8,10},{9,11},{10,... | collective-permute-start | bytes 786440 | tf_op jit(solution)/shard_map/ppermute | solution.py:392
  187.7 18.9 %collective-permute-start.25 = (bf16[64,2048]{1,0:T(8,128)(2,1)S(1)}, bf16[64,2048]{1,0:T(8,128)(2,1)S(1)}, u32[]{:S(2)}, u32[]{:S(2)}) collective-permute-start(bf16[64,2048]{1,0:T(8,128)(2,1)S(1)} %get-tuple-element.238), channel_id=1, source_target_pairs={{0,3},{1,2},{2,1},{3,0},{4,7},{5,6},{6,5},{7,4},{8,11},{9,10},{10,... | collective-permute-start | bytes 786440 | tf_op jit(solution)/shard_map/ppermute | solution.py:392
  208.5 17.9 %collective-permute-start.27 = (bf16[64,2048]{1,0:T(8,128)(2,1)}, bf16[64,2048]{1,0:T(8,128)(2,1)}, u32[]{:S(2)}, u32[]{:S(2)}) collective-permute-start(bf16[64,2048]{1,0:T(8,128)(2,1)} %get-tuple-element.240.refs_0_), channel_id=1, source_target_pairs={{0,2},{1,3},{2,0},{3,1},{4,6},{5,7},{6,4},{7,5},{8,10},{9,11},{10,... | collective-permute-start | bytes 786440 | tf_op jit(solution)/shard_map/ppermute | solution.py:392
  251.7 13.1 %collective-permute-start.34 = (bf16[64,2048]{1,0:T(8,128)(2,1)S(1)}, bf16[64,2048]{1,0:T(8,128)(2,1)S(1)}, u32[]{:S(2)}, u32[]{:S(2)}) collective-permute-start(bf16[64,2048]{1,0:T(8,128)(2,1)S(1)} %get-tuple-element.244), channel_id=1, source_target_pairs={{0,1},{1,0},{2,3},{3,2},{4,5},{5,4},{6,7},{7,6},{8,9},{9,8},{10,11... | collective-permute-start | bytes 786440 | tf_op jit(solution)/shard_map/ppermute | solution.py:392
  252.3 21.3 %collective-permute-start.35 = (bf16[64,2048]{1,0:T(8,128)(2,1)S(1)}, bf16[64,2048]{1,0:T(8,128)(2,1)S(1)}, u32[]{:S(2)}, u32[]{:S(2)}) collective-permute-start(bf16[64,2048]{1,0:T(8,128)(2,1)S(1)} %get-tuple-element.245), channel_id=1, source_target_pairs={{0,2},{1,3},{2,0},{3,1},{4,6},{5,7},{6,4},{7,5},{8,10},{9,11},{10,... | collective-permute-start | bytes 786440 | tf_op jit(solution)/shard_map/ppermute | solution.py:392
  254.2 19.5 %collective-permute-start.36 = (bf16[64,2048]{1,0:T(8,128)(2,1)S(1)}, bf16[64,2048]{1,0:T(8,128)(2,1)S(1)}, u32[]{:S(2)}, u32[]{:S(2)}) collective-permute-start(bf16[64,2048]{1,0:T(8,128)(2,1)S(1)} %get-tuple-element.246), channel_id=1, source_target_pairs={{0,3},{1,2},{2,1},{3,0},{4,7},{5,6},{6,5},{7,4},{8,11},{9,10},{10,... | collective-permute-start | bytes 786440 | tf_op jit(solution)/shard_map/ppermute | solution.py:392
  256.3 24.1 %collective-permute-start = (bf16[64,2048]{1,0:T(8,128)(2,1)S(1)}, bf16[64,2048]{1,0:T(8,128)(2,1)S(1)}, u32[]{:S(2)}, u32[]{:S(2)}) collective-permute-start(bf16[64,2048]{1,0:T(8,128)(2,1)S(1)} %dynamic-slice_bitcast_fusion.3), channel_id=1, source_target_pairs={{0,8},{8,0},{1,9},{9,1},{2,10},{10,2},{3,11},{11,3},{4,12},{12,4},... | collective-permute-start | bytes 786440 | tf_op jit(solution)/shard_map/ppermute | solution.py:392
  274.8 24.1 %collective-permute-start.45 = (bf16[64,2048]{1,0:T(8,128)(2,1)S(1)}, bf16[64,2048]{1,0:T(8,128)(2,1)S(1)}, u32[]{:S(2)}, u32[]{:S(2)}) collective-permute-start(bf16[64,2048]{1,0:T(8,128)(2,1)S(1)} %get-tuple-element.248.refs_0_), channel_id=1, source_target_pairs={{0,2},{1,3},{2,0},{3,1},{4,6},{5,7},{6,4},{7,5},{8,10},{9,11},{10,... | collective-permute-start | bytes 786440 | tf_op jit(solution)/shard_map/ppermute | solution.py:392
  281.3 21.7 %collective-permute-start.38 = (bf16[64,2048]{1,0:T(8,128)(2,1)}, bf16[64,2048]{1,0:T(8,128)(2,1)}, u32[]{:S(2)}, u32[]{:S(2)}) collective-permute-start(bf16[64,2048]{1,0:T(8,128)(2,1)} %get-tuple-element.421.refs_0_), channel_id=1, source_target_pairs={{0,2},{1,3},{2,0},{3,1},{4,6},{5,7},{6,4},{7,5},{8,10},{9,11},{10,... | collective-permute-start | bytes 786440 | tf_op jit(solution)/shard_map/ppermute | solution.py:392
  281.4 21.7 %collective-permute-start.44 = (bf16[64,2048]{1,0:T(8,128)(2,1)S(1)}, bf16[64,2048]{1,0:T(8,128)(2,1)S(1)}, u32[]{:S(2)}, u32[]{:S(2)}) collective-permute-start(bf16[64,2048]{1,0:T(8,128)(2,1)S(1)} %get-tuple-element.248.refs_0_), channel_id=1, source_target_pairs={{0,1},{1,0},{2,3},{3,2},{4,5},{5,4},{6,7},{7,6},{8,9},{9,8},{10,11... | collective-permute-start | bytes 786440 | tf_op jit(solution)/shard_map/ppermute | solution.py:392
  283.9 21.2 %collective-permute-start.37 = (bf16[64,2048]{1,0:T(8,128)(2,1)}, bf16[64,2048]{1,0:T(8,128)(2,1)}, u32[]{:S(2)}, u32[]{:S(2)}) collective-permute-start(bf16[64,2048]{1,0:T(8,128)(2,1)} %get-tuple-element.421.refs_0_), channel_id=1, source_target_pairs={{0,1},{1,0},{2,3},{3,2},{4,5},{5,4},{6,7},{7,6},{8,9},{9,8},{10,11... | collective-permute-start | bytes 786440 | tf_op jit(solution)/shard_map/ppermute | solution.py:392
  303.0 13.5 %collective-permute-start.48 = (bf16[64,2048]{1,0:T(8,128)(2,1)S(1)}, bf16[64,2048]{1,0:T(8,128)(2,1)S(1)}, u32[]{:S(2)}, u32[]{:S(2)}) collective-permute-start(bf16[64,2048]{1,0:T(8,128)(2,1)S(1)} %collective-permute-done.44.refs_1_), channel_id=1, source_target_pairs={{0,4},{4,0},{1,5},{5,1},{2,6},{6,2},{3,7},{7,3},{8,12},{12,8},{9,1... | collective-permute-start | bytes 786440 | tf_op jit(solution)/shard_map/ppermute | solution.py:392
  315.3 21.3 %collective-permute-start.40 = (bf16[64,2048]{1,0:T(8,128)(2,1)}, bf16[64,2048]{1,0:T(8,128)(2,1)}, u32[]{:S(2)}, u32[]{:S(2)}) collective-permute-start(bf16[64,2048]{1,0:T(8,128)(2,1)} %get-tuple-element.421.refs_0_), channel_id=1, source_target_pairs={{0,4},{4,0},{1,5},{5,1},{2,6},{6,2},{3,7},{7,3},{8,12},{12,8},{9,1... | collective-permute-start | bytes 786440 | tf_op jit(solution)/shard_map/ppermute | solution.py:392
  316.0 20.6 %collective-permute-start.42 = (bf16[64,2048]{1,0:T(8,128)(2,1)}, bf16[64,2048]{1,0:T(8,128)(2,1)}, u32[]{:S(2)}, u32[]{:S(2)}) collective-permute-start(bf16[64,2048]{1,0:T(8,128)(2,1)} %collective-permute-done.38.refs_2_), channel_id=1, source_target_pairs={{0,4},{4,0},{1,5},{5,1},{2,6},{6,2},{3,7},{7,3},{8,12},{12,8},{9,1... | collective-permute-start | bytes 786440 | tf_op jit(solution)/shard_map/ppermute | solution.py:392
  317.2 19.4 %collective-permute-start.41 = (bf16[64,2048]{1,0:T(8,128)(2,1)}, bf16[64,2048]{1,0:T(8,128)(2,1)}, u32[]{:S(2)}, u32[]{:S(2)}) collective-permute-start(bf16[64,2048]{1,0:T(8,128)(2,1)} %collective-permute-done.37.refs_1_), channel_id=1, source_target_pairs={{0,4},{4,0},{1,5},{5,1},{2,6},{6,2},{3,7},{7,3},{8,12},{12,8},{9,1... | collective-permute-start | bytes 786440 | tf_op jit(solution)/shard_map/ppermute | solution.py:392
  318.0 18.7 %collective-permute-start.43 = (bf16[64,2048]{1,0:T(8,128)(2,1)}, bf16[64,2048]{1,0:T(8,128)(2,1)}, u32[]{:S(2)}, u32[]{:S(2)}) collective-permute-start(bf16[64,2048]{1,0:T(8,128)(2,1)} %collective-permute-done.39.refs_3_), channel_id=1, source_target_pairs={{0,4},{4,0},{1,5},{5,1},{2,6},{6,2},{3,7},{7,3},{8,12},{12,8},{9,1... | collective-permute-start | bytes 786440 | tf_op jit(solution)/shard_map/ppermute | solution.py:392
  346.3 13.6 %collective-permute-start.53 = (bf16[64,2048]{1,0:T(8,128)(2,1)S(1)}, bf16[64,2048]{1,0:T(8,128)(2,1)S(1)}, u32[]{:S(2)}, u32[]{:S(2)}) collective-permute-start(bf16[64,2048]{1,0:T(8,128)(2,1)S(1)} %get-tuple-element.255), channel_id=1, source_target_pairs={{0,1},{1,0},{2,3},{3,2},{4,5},{5,4},{6,7},{7,6},{8,9},{9,8},{10,11... | collective-permute-start | bytes 786440 | tf_op jit(solution)/shard_map/ppermute | solution.py:392
  347.5 21.3 %collective-permute-start.54 = (bf16[64,2048]{1,0:T(8,128)(2,1)S(1)}, bf16[64,2048]{1,0:T(8,128)(2,1)S(1)}, u32[]{:S(2)}, u32[]{:S(2)}) collective-permute-start(bf16[64,2048]{1,0:T(8,128)(2,1)S(1)} %get-tuple-element.256), channel_id=1, source_target_pairs={{0,2},{1,3},{2,0},{3,1},{4,6},{5,7},{6,4},{7,5},{8,10},{9,11},{10,... | collective-permute-start | bytes 786440 | tf_op jit(solution)/shard_map/ppermute | solution.py:392
  349.9 18.9 %collective-permute-start.55 = (bf16[64,2048]{1,0:T(8,128)(2,1)S(1)}, bf16[64,2048]{1,0:T(8,128)(2,1)S(1)}, u32[]{:S(2)}, u32[]{:S(2)}) collective-permute-start(bf16[64,2048]{1,0:T(8,128)(2,1)S(1)} %get-tuple-element.257), channel_id=1, source_target_pairs={{0,3},{1,2},{2,1},{3,0},{4,7},{5,6},{6,5},{7,4},{8,11},{9,10},{10,... | collective-permute-start | bytes 786440 | tf_op jit(solution)/shard_map/ppermute | solution.py:392
  370.8 18.0 %collective-permute-start.56 = (bf16[64,2048]{1,0:T(8,128)(2,1)}, bf16[64,2048]{1,0:T(8,128)(2,1)}, u32[]{:S(2)}, u32[]{:S(2)}) collective-permute-start(bf16[64,2048]{1,0:T(8,128)(2,1)} %get-tuple-element.261), channel_id=1, source_target_pairs={{0,1},{1,0},{2,3},{3,2},{4,5},{5,4},{6,7},{7,6},{8,9},{9,8},{10,11... | collective-permute-start | bytes 786440 | tf_op jit(solution)/shard_map/ppermute | solution.py:392
  376.0 21.7 %collective-permute-start.57 = (bf16[64,2048]{1,0:T(8,128)(2,1)}, bf16[64,2048]{1,0:T(8,128)(2,1)}, u32[]{:S(2)}, u32[]{:S(2)}) collective-permute-start(bf16[64,2048]{1,0:T(8,128)(2,1)} %get-tuple-element.262), channel_id=1, source_target_pairs={{0,2},{1,3},{2,0},{3,1},{4,6},{5,7},{6,4},{7,5},{8,10},{9,11},{10,... | collective-permute-start | bytes 786440 | tf_op jit(solution)/shard_map/ppermute | solution.py:392
  377.0 20.7 %collective-permute-start.58 = (bf16[64,2048]{1,0:T(8,128)(2,1)}, bf16[64,2048]{1,0:T(8,128)(2,1)}, u32[]{:S(2)}, u32[]{:S(2)}) collective-permute-start(bf16[64,2048]{1,0:T(8,128)(2,1)} %get-tuple-element.263), channel_id=1, source_target_pairs={{0,3},{1,2},{2,1},{3,0},{4,7},{5,6},{6,5},{7,4},{8,11},{9,10},{10,... | collective-permute-start | bytes 786440 | tf_op jit(solution)/shard_map/ppermute | solution.py:392
  397.7 246.0 %reduce-scatter.7.cloned.1.call-start = ((), (), s32[]{:S(2)}) async-start(), calls=%async_computation.9 | async-start | bytes 5242880 | tf_op jit(solution)/shard_map/reduce_scatter | solution.py:579
  403.8 15.1 %collective-permute-start.60 = (bf16[64,2048]{1,0:T(8,128)(2,1)S(1)}, bf16[64,2048]{1,0:T(8,128)(2,1)S(1)}, u32[]{:S(2)}, u32[]{:S(2)}) collective-permute-start(bf16[64,2048]{1,0:T(8,128)(2,1)S(1)} %get-tuple-element.276.refs_0_), channel_id=1, source_target_pairs={{0,2},{1,3},{2,0},{3,1},{4,6},{5,7},{6,4},{7,5},{8,10},{9,11},{10,... | collective-permute-start | bytes 786440 | tf_op jit(solution)/shard_map/ppermute | solution.py:392
  441.9 23.6 %collective-permute-start.66 = (bf16[256,2048]{1,0:T(8,128)(2,1)}, bf16[256,2048]{1,0:T(8,128)(2,1)S(1)}, u32[]{:S(2)}, u32[]{:S(2)}) collective-permute-start(bf16[256,2048]{1,0:T(8,128)(2,1)} %get-tuple-element.281), channel_id=1, source_target_pairs={{0,4},{4,0},{1,5},{5,1},{2,6},{6,2},{3,7},{7,3},{8,12},{12,8},{9,1... | collective-permute-start | bytes 3145736 | tf_op jit(solution)/shard_map/ppermute | solution.py:392
  442.4 14.8 %collective-permute-start.68 = (bf16[64,2048]{1,0:T(8,128)(2,1)S(1)}, bf16[64,2048]{1,0:T(8,128)(2,1)S(1)}, u32[]{:S(2)}, u32[]{:S(2)}) collective-permute-start(bf16[64,2048]{1,0:T(8,128)(2,1)S(1)} %add_convert_fusion), channel_id=1, source_target_pairs={{0,2},{1,3},{2,0},{3,1},{4,6},{5,7},{6,4},{7,5},{8,10},{9,11},{10,... | collective-permute-start | bytes 786440 | tf_op jit(solution)/shard_map/ppermute | solution.py:392
  442.9 14.3 %collective-permute-start.67 = (bf16[64,2048]{1,0:T(8,128)(2,1)S(1)}, bf16[64,2048]{1,0:T(8,128)(2,1)S(1)}, u32[]{:S(2)}, u32[]{:S(2)}) collective-permute-start(bf16[64,2048]{1,0:T(8,128)(2,1)S(1)} %add_convert_fusion), channel_id=1, source_target_pairs={{0,1},{1,0},{2,3},{3,2},{4,5},{5,4},{6,7},{7,6},{8,9},{9,8},{10,11... | collective-permute-start | bytes 786440 | tf_op jit(solution)/shard_map/ppermute | solution.py:392
  467.6 21.4 %collective-permute-start.72 = (bf16[64,2048]{1,0:T(8,128)(2,1)}, bf16[64,2048]{1,0:T(8,128)(2,1)}, u32[]{:S(2)}, u32[]{:S(2)}) collective-permute-start(bf16[64,2048]{1,0:T(8,128)(2,1)} %get-tuple-element.295), channel_id=1, source_target_pairs={{0,2},{1,3},{2,0},{3,1},{4,6},{5,7},{6,4},{7,5},{8,10},{9,11},{10,... | collective-permute-start | bytes 786440 | tf_op jit(solution)/shard_map/ppermute | solution.py:392
  468.5 20.5 %collective-permute-start.73 = (bf16[64,2048]{1,0:T(8,128)(2,1)}, bf16[64,2048]{1,0:T(8,128)(2,1)}, u32[]{:S(2)}, u32[]{:S(2)}) collective-permute-start(bf16[64,2048]{1,0:T(8,128)(2,1)} %get-tuple-element.296), channel_id=1, source_target_pairs={{0,3},{1,2},{2,1},{3,0},{4,7},{5,6},{6,5},{7,4},{8,11},{9,10},{10,... | collective-permute-start | bytes 786440 | tf_op jit(solution)/shard_map/ppermute | solution.py:392
  489.1 196.6 %reduce-scatter.9.cloned.1.call-start = ((), (), s32[]{:S(2)}) async-start(), calls=%async_computation.10 | async-start | bytes 11141120 | tf_op jit(solution)/shard_map/reduce_scatter | solution.py:579
  494.9 14.8 %collective-permute-start.75 = (bf16[64,2048]{1,0:T(8,128)(2,1)S(1)}, bf16[64,2048]{1,0:T(8,128)(2,1)S(1)}, u32[]{:S(2)}, u32[]{:S(2)}) collective-permute-start(bf16[64,2048]{1,0:T(8,128)(2,1)S(1)} %get-tuple-element.310.refs_0_), channel_id=1, source_target_pairs={{0,2},{1,3},{2,0},{3,1},{4,6},{5,7},{6,4},{7,5},{8,10},{9,11},{10,... | collective-permute-start | bytes 786440 | tf_op jit(solution)/shard_map/ppermute | solution.py:392
  530.5 15.5 %collective-permute-start.82 = (bf16[64,2048]{1,0:T(8,128)(2,1)S(1)}, bf16[64,2048]{1,0:T(8,128)(2,1)S(1)}, u32[]{:S(2)}, u32[]{:S(2)}) collective-permute-start(bf16[64,2048]{1,0:T(8,128)(2,1)S(1)} %get-tuple-element.315), channel_id=1, source_target_pairs={{0,1},{1,0},{2,3},{3,2},{4,5},{5,4},{6,7},{7,6},{8,9},{9,8},{10,11... | collective-permute-start | bytes 786440 | tf_op jit(solution)/shard_map/ppermute | solution.py:392
  532.1 21.8 %collective-permute-start.83 = (bf16[64,2048]{1,0:T(8,128)(2,1)S(1)}, bf16[64,2048]{1,0:T(8,128)(2,1)S(1)}, u32[]{:S(2)}, u32[]{:S(2)}) collective-permute-start(bf16[64,2048]{1,0:T(8,128)(2,1)S(1)} %get-tuple-element.316), channel_id=1, source_target_pairs={{0,2},{1,3},{2,0},{3,1},{4,6},{5,7},{6,4},{7,5},{8,10},{9,11},{10,... | collective-permute-start | bytes 786440 | tf_op jit(solution)/shard_map/ppermute | solution.py:392
  535.5 18.4 %collective-permute-start.84 = (bf16[64,2048]{1,0:T(8,128)(2,1)S(1)}, bf16[64,2048]{1,0:T(8,128)(2,1)S(1)}, u32[]{:S(2)}, u32[]{:S(2)}) collective-permute-start(bf16[64,2048]{1,0:T(8,128)(2,1)S(1)} %get-tuple-element.317), channel_id=1, source_target_pairs={{0,3},{1,2},{2,1},{3,0},{4,7},{5,6},{6,5},{7,4},{8,11},{9,10},{10,... | collective-permute-start | bytes 786440 | tf_op jit(solution)/shard_map/ppermute | solution.py:392
  553.9 169.9 %reduce-scatter.11.cloned.1.call-start = ((), (), s32[]{:S(2)}) async-start(), calls=%async_computation.11 | async-start | bytes 5242880 | tf_op jit(solution)/shard_map/reduce_scatter | solution.py:579
  556.4 29.1 %collective-permute-start.92 = (bf16[256,2176]{1,0:T(8,128)(2,1)}, bf16[256,2176]{1,0:T(8,128)(2,1)}, u32[]{:S(2)}, u32[]{:S(2)}) collective-permute-start(bf16[256,2176]{1,0:T(8,128)(2,1)} %constant_dynamic-slice_fusion.4), channel_id=1, source_target_pairs={{0,4},{4,0},{1,5},{5,1},{2,6},{6,2},{3,7},{7,3},{8,12},{12,8},{9,1... | collective-permute-start | bytes 3342344 | tf_op jit(solution)/shard_map/ppermute | solution.py:392
  557.7 19.4 %collective-permute-start.86 = (bf16[64,2048]{1,0:T(8,128)(2,1)}, bf16[64,2048]{1,0:T(8,128)(2,1)}, u32[]{:S(2)}, u32[]{:S(2)}) collective-permute-start(bf16[64,2048]{1,0:T(8,128)(2,1)} %get-tuple-element.333.refs_0_), channel_id=1, source_target_pairs={{0,2},{1,3},{2,0},{3,1},{4,6},{5,7},{6,4},{7,5},{8,10},{9,11},{10,... | collective-permute-start | bytes 786440 | tf_op jit(solution)/shard_map/ppermute | solution.py:392
  564.1 13.5 %collective-permute-start.85 = (bf16[64,2048]{1,0:T(8,128)(2,1)}, bf16[64,2048]{1,0:T(8,128)(2,1)}, u32[]{:S(2)}, u32[]{:S(2)}) collective-permute-start(bf16[64,2048]{1,0:T(8,128)(2,1)} %get-tuple-element.333.refs_0_), channel_id=1, source_target_pairs={{0,1},{1,0},{2,3},{3,2},{4,5},{5,4},{6,7},{7,6},{8,9},{9,8},{10,11... | collective-permute-start | bytes 786440 | tf_op jit(solution)/shard_map/ppermute | solution.py:392
  577.1 22.9 %collective-permute-start.88 = (bf16[64,2048]{1,0:T(8,128)(2,1)}, bf16[64,2048]{1,0:T(8,128)(2,1)}, u32[]{:S(2)}, u32[]{:S(2)}) collective-permute-start(bf16[64,2048]{1,0:T(8,128)(2,1)} %get-tuple-element.333.refs_0_), channel_id=1, source_target_pairs={{0,4},{4,0},{1,5},{5,1},{2,6},{6,2},{3,7},{7,3},{8,12},{12,8},{9,1... | collective-permute-start | bytes 786440 | tf_op jit(solution)/shard_map/ppermute | solution.py:392
  577.1 22.9 %collective-permute-start.90 = (bf16[64,2048]{1,0:T(8,128)(2,1)}, bf16[64,2048]{1,0:T(8,128)(2,1)}, u32[]{:S(2)}, u32[]{:S(2)}) collective-permute-start(bf16[64,2048]{1,0:T(8,128)(2,1)} %collective-permute-done.86.refs_2_), channel_id=1, source_target_pairs={{0,4},{4,0},{1,5},{5,1},{2,6},{6,2},{3,7},{7,3},{8,12},{12,8},{9,1... | collective-permute-start | bytes 786440 | tf_op jit(solution)/shard_map/ppermute | solution.py:392
  577.6 22.4 %collective-permute-start.89 = (bf16[64,2048]{1,0:T(8,128)(2,1)}, bf16[64,2048]{1,0:T(8,128)(2,1)}, u32[]{:S(2)}, u32[]{:S(2)}) collective-permute-start(bf16[64,2048]{1,0:T(8,128)(2,1)} %collective-permute-done.85.refs_1_), channel_id=1, source_target_pairs={{0,4},{4,0},{1,5},{5,1},{2,6},{6,2},{3,7},{7,3},{8,12},{12,8},{9,1... | collective-permute-start | bytes 786440 | tf_op jit(solution)/shard_map/ppermute | solution.py:392
  585.5 14.6 %collective-permute-start.91 = (bf16[64,2048]{1,0:T(8,128)(2,1)}, bf16[64,2048]{1,0:T(8,128)(2,1)}, u32[]{:S(2)}, u32[]{:S(2)}) collective-permute-start(bf16[64,2048]{1,0:T(8,128)(2,1)} %collective-permute-done.87.refs_3_), channel_id=1, source_target_pairs={{0,4},{4,0},{1,5},{5,1},{2,6},{6,2},{3,7},{7,3},{8,12},{12,8},{9,1... | collective-permute-start | bytes 786440 | tf_op jit(solution)/shard_map/ppermute | solution.py:392
  619.6 13.9 %collective-permute-start.94 = (bf16[64,2048]{1,0:T(8,128)(2,1)}, bf16[64,2048]{1,0:T(8,128)(2,1)S(1)}, u32[]{:S(2)}, u32[]{:S(2)}) collective-permute-start(bf16[64,2048]{1,0:T(8,128)(2,1)} %get-tuple-element.347), channel_id=1, source_target_pairs={{0,1},{1,0},{2,3},{3,2},{4,5},{5,4},{6,7},{7,6},{8,9},{9,8},{10,11... | collective-permute-start | bytes 786440 | tf_op jit(solution)/shard_map/ppermute | solution.py:392
  620.1 21.5 %collective-permute-start.95 = (bf16[64,2048]{1,0:T(8,128)(2,1)}, bf16[64,2048]{1,0:T(8,128)(2,1)S(1)}, u32[]{:S(2)}, u32[]{:S(2)}) collective-permute-start(bf16[64,2048]{1,0:T(8,128)(2,1)} %get-tuple-element.348), channel_id=1, source_target_pairs={{0,2},{1,3},{2,0},{3,1},{4,6},{5,7},{6,4},{7,5},{8,10},{9,11},{10,... | collective-permute-start | bytes 786440 | tf_op jit(solution)/shard_map/ppermute | solution.py:392
  621.8 19.8 %collective-permute-start.96 = (bf16[64,2048]{1,0:T(8,128)(2,1)}, bf16[64,2048]{1,0:T(8,128)(2,1)S(1)}, u32[]{:S(2)}, u32[]{:S(2)}) collective-permute-start(bf16[64,2048]{1,0:T(8,128)(2,1)} %get-tuple-element.349), channel_id=1, source_target_pairs={{0,3},{1,2},{2,1},{3,0},{4,7},{5,6},{6,5},{7,4},{8,11},{9,10},{10,... | collective-permute-start | bytes 786440 | tf_op jit(solution)/shard_map/ppermute | solution.py:392
  646.2 30.9 %collective-permute-start.70 = (bf16[128,2048]{1,0:T(8,128)(2,1)}, bf16[128,2048]{1,0:T(8,128)(2,1)}, u32[]{:S(2)}, u32[]{:S(2)}) collective-permute-start(bf16[128,2048]{1,0:T(8,128)(2,1)} %get-tuple-element.455), channel_id=1, source_target_pairs={{0,8},{8,0},{1,9},{9,1},{2,10},{10,2},{3,11},{11,3},{4,12},{12,4},... | collective-permute-start | bytes 1572872 | tf_op jit(solution)/shard_map/ppermute | solution.py:392
  659.2 17.8 %collective-permute-start.99 = (bf16[64,2048]{1,0:T(8,128)(2,1)S(1)}, bf16[64,2048]{1,0:T(8,128)(2,1)S(1)}, u32[]{:S(2)}, u32[]{:S(2)}) collective-permute-start(bf16[64,2048]{1,0:T(8,128)(2,1)S(1)} %get-tuple-element.367), channel_id=1, source_target_pairs={{0,2},{1,3},{2,0},{3,1},{4,6},{5,7},{6,4},{7,5},{8,10},{9,11},{10,... | collective-permute-start | bytes 786440 | tf_op jit(solution)/shard_map/ppermute | solution.py:392
  664.8 14.7 %collective-permute-start.98 = (bf16[64,2048]{1,0:T(8,128)(2,1)S(1)}, bf16[64,2048]{1,0:T(8,128)(2,1)S(1)}, u32[]{:S(2)}, u32[]{:S(2)}) collective-permute-start(bf16[64,2048]{1,0:T(8,128)(2,1)S(1)} %get-tuple-element.367), channel_id=1, source_target_pairs={{0,1},{1,0},{2,3},{3,2},{4,5},{5,4},{6,7},{7,6},{8,9},{9,8},{10,11... | collective-permute-start | bytes 786440 | tf_op jit(solution)/shard_map/ppermute | solution.py:392
  687.1 21.2 %collective-permute-start.101 = (bf16[128,2048]{1,0:T(8,128)(2,1)S(1)}, bf16[128,2048]{1,0:T(8,128)(2,1)S(1)}, u32[]{:S(2)}, u32[]{:S(2)}) collective-permute-start(bf16[128,2048]{1,0:T(8,128)(2,1)S(1)} %get-tuple-element.453), channel_id=1, source_target_pairs={{0,8},{8,0},{1,9},{9,1},{2,10},{10,2},{3,11},{11,3},{4,12},{12,4},... | collective-permute-start | bytes 1572872 | tf_op jit(solution)/shard_map/ppermute | solution.py:392
  692.2 29.3 %collective-permute-start.111 = (bf16[256,2176]{1,0:T(8,128)(2,1)S(1)}, bf16[256,2176]{1,0:T(8,128)(2,1)S(1)}, u32[]{:S(2)}, u32[]{:S(2)}) collective-permute-start(bf16[256,2176]{1,0:T(8,128)(2,1)S(1)} %constant_dynamic-slice_fusion), channel_id=1, source_target_pairs={{0,4},{4,0},{1,5},{5,1},{2,6},{6,2},{3,7},{7,3},{8,12},{12,8},{9,1... | collective-permute-start | bytes 3342344 | tf_op jit(solution)/shard_map/ppermute | solution.py:392
  693.4 19.0 %collective-permute-start.110 = (f32[2,3,256]{2,1,0:T(4,128)S(1)}, f32[2,3,256]{2,1,0:T(4,128)S(1)}, u32[]{:S(2)}, u32[]{:S(2)}) collective-permute-start(f32[2,3,256]{2,1,0:T(4,128)S(1)} %add.228), channel_id=1, source_target_pairs={{0,4},{4,0},{1,5},{5,1},{2,6},{6,2},{3,7},{7,3},{8,12},{12,8},{9,1... | collective-permute-start | bytes 18440 | tf_op jit(solution)/shard_map/ppermute | solution.py:392
  696.7 13.1 %collective-permute-start.104 = (f32[4,2,2048]{2,0,1:T(4,128)S(1)}, f32[4,2,2048]{2,0,1:T(4,128)S(1)}, u32[]{:S(2)}, u32[]{:S(2)}) collective-permute-start(f32[4,2,2048]{2,0,1:T(4,128)S(1)} %fusion.35), channel_id=1, source_target_pairs={{0,4},{4,0},{1,5},{5,1},{2,6},{6,2},{3,7},{7,3},{8,12},{12,8},{9,1... | collective-permute-start | bytes 196616 | tf_op jit(solution)/shard_map/ppermute | solution.py:392
  (164 other events, 1070.3 us)
Sparse Core Ops, SparseCore 0:
  10.5 57.0 all-gather.4
  70.1 94.2 all-gather.6
  166.9 54.3 all-gather.8
  223.6 97.4 all-gather.10
  397.8 92.3 reduce-scatter.4
  493.0 52.6 reduce-scatter.6
  554.0 93.7 reduce-scatter.8
  651.0 62.1 reduce-scatter.10

commit v5 on v4

--- a/solution.py
+++ b/solution.py
@@ -44,7 +44,7 @@
     return jax.ShapeDtypeStruct(dims, kind)
 
 
-def call(body, n_hbm, args, outs, scratch, flops, hbm_outs=0, n_any=0, limit=32):
+def call(body, n_hbm, args, outs, scratch, flops, hbm_outs=0, n_any=0, limit=32, aliases=None):
     moved = sum(a.size * a.dtype.itemsize for a in args)
     moved += sum(math.prod(o.shape) * jnp.dtype(o.dtype).itemsize for o in outs)
     return pl.pallas_call(
@@ -53,6 +53,7 @@
         in_specs=[ANY] * n_any + [HBM] * (n_hbm - n_any) + [VMEM] * (len(args) - n_hbm),
         out_specs=tuple([HBM] * hbm_outs + [VMEM] * (len(outs) - hbm_outs)),
         scratch_shapes=scratch,
+        input_output_aliases=aliases or {},
         compiler_params=pltpu.CompilerParams(vmem_limit_bytes=limit * MIB),
         cost_estimate=pl.CostEstimate(flops=flops, bytes_accessed=moved, transcendentals=0),
     )(*args)
@@ -292,25 +293,38 @@
     wait_all(sent[-2:])
 
 
-def weight_pieces(n_groups, n_chi, *refs):
-    outs, (a_s, b_s, da_s, db_s, sems) = refs[4:-5], refs[-5:]
-    load_grads(refs[:4], a_s, b_s, da_s, db_s, sems)
-    block = a_s.shape[1] // n_groups
-    half = block // 2
-    split, end = da_s.shape[1], da_s.shape[1] + db_s.shape[1]
-    swapped = lax.axis_index("clo") == 1
-    group = lax.axis_index("dp") * n_chi + lax.axis_index("chi")
-    for r in range(n_groups):
-        cols = pl.ds(pl.multiple_of((group ^ r) * block, 128), block)
-        first = tn(a_s[:, cols], da_s[...]).astype(LOW)
-        second = tn(b_s[:, cols], db_s[...]).astype(LOW)
-        for i in range(2):
-            here, there = slice(i * half, (i + 1) * half), slice((1 - i) * half, (2 - i) * half)
-            out = outs[2 * r + i]
-            out[:, :split] = jnp.where(swapped, first[there], first[here])
-            out[:, split:end] = jnp.where(swapped, second[there], second[here])
-            if end < out.shape[1]:
-                out[:, end:] = jnp.zeros((half, out.shape[1] - end), LOW)
+def other_rows(block_sum, out, sem):
+    rows = out.shape[0]
+    at = (1 - lax.axis_index("clo")) * rows
+    copy = pltpu.make_async_copy(
+        block_sum.at[pl.ds(pl.multiple_of(at, rows), rows)], out, sem.at[0]
+    )
+    copy.start()
+    copy.wait()
+
+
+def put_grads(layer, n_old, n_first, *refs):
+    block_sum, moved = refs[:2]
+    first_o, second_o, mine_s, moved_s, first_s, second_s, sems = refs[2 + n_old :]
+    rows = moved.shape[0]
+    me = lax.axis_index("clo")
+    own = block_sum
+    if own.shape[0] > rows:
+        own = own.at[pl.ds(pl.multiple_of(me * rows, rows), rows)]
+    copies = load([(own, mine_s), (moved, moved_s)], sems, 0)
+    start_all(copies)
+    wait_all(copies)
+    low = jnp.where(me == 0, mine_s[...], moved_s[...])
+    high = jnp.where(me == 0, moved_s[...], mine_s[...])
+    width = second_s.shape[1] // 2
+    out = load([(first_s, first_o.at[layer]), (second_s, second_o.at[layer])], sems, 2)
+    for core, part in enumerate((low, high)):
+        to = slice(core * width, (core + 1) * width)
+        for c in range(n_first):
+            first_s[c, :, to] = part[:, c * width : (c + 1) * width].astype(F32)
+        second_s[:, to] = part[:, n_first * width : (n_first + 1) * width].astype(F32)
+    start_all(out)
+    wait_all(out)
 
 
 def order_columns(*refs):
@@ -385,21 +399,9 @@
     group_bits += [("dp", 1 << k) for k in range(log2(n_dp))]
     n_groups = n_dp * n_chi
     sizes = {"dp": n_dp, "chi": n_chi, "clo": n_clo, "mp": n_mp}
-    up_order = list(range(len(group_bits)))
-    down_order = up_order[::-1]
 
     def swap(value, axis, bit):
         return lax.ppermute(value, axis, [(i, i ^ bit) for i in range(sizes[axis])])
-
-    def spread(pieces):
-        a, b = dict(enumerate(pieces[0::2])), dict(enumerate(pieces[1::2]))
-        for ka, kb in zip(down_order, up_order):
-            for have, k in ((a, ka), (b, kb)):
-                for r in [r for r in have if r & (1 << k)]:
-                    moved = swap(have.pop(r), *group_bits[k])
-                    to = r ^ (1 << k)
-                    have[to] = (have[to].astype(F32) + moved.astype(F32)).astype(LOW)
-        return a[0], swap(b[0], "clo", 1)
 
     def mp_gather(own):
         parts = [own]
@@ -437,11 +439,18 @@
         there = swap(lax.dynamic_index_in_dim(mine, 1 - chi, 0, keepdims=False), "chi", 1)
         return jnp.where(lax.axis_index("mp") // per_block == chi, here, there)
 
-    def to_blocks(held, block):
+    def chi_swap(held, block, extra=None):
         chi = lax.axis_index("chi")
         mine = lax.dynamic_slice_in_dim(held, chi * block, block, 0)
-        moved = swap(lax.dynamic_slice_in_dim(held, (1 - chi) * block, block, 0), "chi", 1)
-        return jnp.where(chi == 0, jnp.stack([mine, moved]), jnp.stack([moved, mine]))
+        sent = lax.dynamic_slice_in_dim(held, (1 - chi) * block, block, 0)
+        if extra is not None:
+            sent = jnp.concatenate([sent, extra], axis=0)
+        return mine, swap(sent, "chi", 1)
+
+    def to_blocks(mine, moved, block):
+        first = lax.axis_index("chi") == 0
+        moved = moved[:block]
+        return jnp.where(first, jnp.stack([mine, moved]), jnp.stack([moved, mine]))
 
     def by_place(parts):
         sub, width = parts[0].shape
@@ -558,55 +567,51 @@
             outs = [shape(y.shape, F32), shape(y.shape, LOW), shape((2, width), F32)]
             return call(norm_backward, 0, [dx, y, gain[None]] + terms, outs, [], 20 * y.size)
 
-        def grads(a, b, da, db, cols, pieces):
+        def grads(a, b, da, db, cols):
             scratch = [pltpu.VMEM(x.shape, LOW) for x in (a, b, da, db)]
-            sems = pltpu.SemaphoreType.DMA((4,))
-            if pieces:
-                body = functools.partial(weight_pieces, n_groups, n_chi)
-                outs = [shape((rows_dev, cols), LOW)] * (2 * n_groups)
-                scratch += [sems]
-            else:
-                body = weight_grads
-                outs = [shape((width, cols), LOW)]
-                scratch += [pltpu.VMEM((2, BLOCK, cols), LOW), sems]
-                scratch += [pltpu.SemaphoreType.DMA((width // BLOCK,))]
-            return call(
-                body, 4, [a, b, da, db], outs, scratch, mm(total, width, cols),
-                hbm_outs=0 if pieces else 1, limit=60,
-            )
+            scratch += [pltpu.VMEM((2, BLOCK, cols), LOW), pltpu.SemaphoreType.DMA((4,))]
+            scratch += [pltpu.SemaphoreType.DMA((width // BLOCK,))]
+            outs = [shape((width, cols), LOW)]
+            flops = mm(total, width, cols)
+            args = [a, b, da, db]
+            return call(weight_grads, 4, args, outs, scratch, flops, hbm_outs=1, limit=60)
 
         def scatter(partial):
             return lax.psum_scatter(partial[0], ("dp", "chi"), scatter_dimension=0, tiled=True)
 
         def pick(block_sum):
-            mine = lax.dynamic_slice_in_dim(block_sum, clo * rows_dev, rows_dev, 0)
-            others = lax.dynamic_slice_in_dim(block_sum, (1 - clo) * rows_dev, rows_dev, 0)
-            return mine, swap(others, "clo", 1)
-
-        def columns(pieces, first, count, parts):
-            mine, others = (
-                piece[:, first : first + count].reshape((rows_dev,) + parts + (-1,))
-                for piece in pieces
+            outs = [shape((rows_dev, block_sum.shape[1]), LOW)]
+            sems = [pltpu.SemaphoreType.DMA((1,))]
+            others = call(other_rows, 1, [block_sum], outs, sems, 0, hbm_outs=1)[0]
+            return block_sum, swap(others, "clo", 1)
+
+        def put(l, sums, n_first, unit, old):
+            sums, moved = sums
+            first, second = (n_first, rows_dev, 2 * unit), (rows_dev, 2 * unit)
+            piece = pltpu.VMEM(moved.shape, LOW)
+            return call(
+                functools.partial(put_grads, l, len(old), n_first),
+                2 + len(old),
+                [sums, moved] + old,
+                [shape((LAYERS,) + first, F32), shape((LAYERS,) + second, F32)],
+                [
+                    piece,
+                    piece,
+                    pltpu.VMEM(first, F32),
+                    pltpu.VMEM(second, F32),
+                    pltpu.SemaphoreType.DMA((4,)),
+                ],
+                0,
+                hbm_outs=2,
+                limit=60,
+                aliases={2: 0, 3: 1} if old else None,
             )
-            low = jnp.where(clo == 0, mine, others)
-            high = jnp.where(clo == 0, others, mine)
-            return jnp.concatenate([low, high], axis=-1).astype(F32)
-
-        def above_zeros(x):
-            layout = Layout(major_to_minor=tuple(range(x.ndim + 1)))
-            return with_layout_constraint(jnp.stack([jnp.zeros_like(x), x]), layout)
-
-        def attn_out(pieces):
-            return (
-                columns(pieces, 0, 3 * half_in, (3,)),
-                columns(pieces, 3 * half_in, half_in, ()),
-            )
-
-        def mlp_out(pieces):
-            return (
-                columns(pieces, 0, 2 * half_ff, (2,)),
-                columns(pieces, 2 * half_ff, half_ff, ()),
-            )
+
+        def put_attn(l, sums, old=()):
+            return list(put(l, sums, 3, half_in, list(old)))
+
+        def put_mlp(l, sums, old=()):
+            return list(put(l, sums, 2, half_ff, list(old)))
 
         whole = shape((total, width), LOW)
         saved = []
@@ -634,6 +639,8 @@
             )
             y_own, h = norm(x_own, gains[2, l], gains[3, l], token_reduce(own, send)[0])
             h2 = token_gather(h)
+            if l == 0:
+                h2, dm_parts = lax.optimization_barrier((h2, token_gather(dx)))
             h2, gu, z, own, send = call(
                 functools.partial(mlp_forward, n_parts),
                 n_parts + 1,
@@ -647,14 +654,15 @@
             saved.append((x_own, h1, q, k, v, o, y_own, h2, gu, z))
             x_own, terms = y_own, token_reduce(own, send)[0]
 
-        low = dx
         dx = dx.astype(F32)
         small_out = [None] * LAYERS
         done = None
         for l in reversed(range(LAYERS)):
             w_attn, w_mlp = weights[l]
             x_own, h1, q, k, v, o, y_own, h2, gu, z = saved[l]
-            parts = token_gather(low)
+            parts = dm_parts if done is None else token_gather(low)
+            if done is None:
+                gu = after(gu, terms[0])
             dm, dp2, own, send = call(
                 functools.partial(mlp_backward, n_parts),
                 n_parts + 2,
@@ -671,22 +679,22 @@
                 n_any=n_parts,
                 hbm_outs=1,
             )
-            work = functools.partial(grads, cols=mlp_cols, pieces=False)
+            work = functools.partial(grads, cols=mlp_cols)
             if done is None:
-                terms, g_mlp, last = token_reduce(own, send, (work, (h2, dm, dp2, z)), terms)
+                before = terms, work(h2, dm, dp2, z)
+                terms, _, (last, g_mlp) = token_reduce(own, send, before=before)
                 x_last = y_own
                 for t in last:
                     x_last = x_last + t.astype(F32)
-                x_last = mp_gather(x_last.astype(LOW))
+                x_last = x_last.astype(LOW)
             else:
                 terms, g_mlp, _ = token_reduce(own, send, (work, (h2, dm, dp2, z)))
             g_mlp = scatter(g_mlp)
             dy, low, small_two = norm_back(dx, y_own, gains[2, l], terms)
             parts = token_gather(low)
             if done is not None:
-                late, early = done
-                early = [above_zeros(x) for x in mlp_out(pick(early))]
-                parts, early = lax.optimization_barrier((parts, early))
+                sums = put_mlp(l + 1, pick(done[1])), put_attn(l + 1, pick(done[0]))
+                parts, (mlp_sum, attn_sum) = lax.optimization_barrier((parts, sums))
             da, dp1, bias_grad, own, send = call(
                 functools.partial(attn_backward, n_parts, heads),
                 n_parts + 6,
@@ -705,42 +713,50 @@
                 hbm_outs=1,
                 limit=56,
             )
-            work = functools.partial(grads, cols=attn_cols, pieces=False)
+            work = functools.partial(grads, cols=attn_cols)
             if done is None:
-                terms, g_attn, x_last = token_reduce(own, send, (work, (h1, da, dp1, o)), x_last)
-                activations = to_blocks(by_place(x_last), block)
+                terms, g_attn, _ = token_reduce(own, send, (work, (h1, da, dp1, o)))
                 done = (scatter(g_attn), g_mlp)
             else:
                 terms, g_attn, _ = token_reduce(own, send, (work, (h1, da, dp1, o)))
-                late = [above_zeros(x) for x in attn_out(pick(late))]
-                terms, late = lax.optimization_barrier((terms, late))
             dx, low, small_one = norm_back(dy, x_own, gains[0, l], terms)
             small_out[l] = (small_one, small_two, bias_grad)
-        parts = mp_gather(low)
-        tokens_grad = to_blocks(by_place(parts), block).astype(F32)
-        g_mlp, small_out = after((g_mlp, small_out), parts[n_mp // 2])
-        g_attn, mlp_last = pick(scatter(g_attn)), mlp_out(pick(g_mlp))
-        parts = zip(late + early, attn_out(g_attn) + tuple(mlp_last))
-        weight_out = [stack.at[0].set(part) for stack, part in parts]
-
-        norms = jnp.stack(
-            [jnp.concatenate(small_out[l][:2], axis=0) for l in range(LAYERS)], axis=1
+        norms = jnp.concatenate([part for l in range(LAYERS) for part in small_out[l][:2]], axis=0)
+        bias = jnp.concatenate([small_out[l][2] for l in range(LAYERS)], axis=1)
+        rows = -(-bias.size // width)
+        bias = jnp.pad(bias, ((0, 0), (0, rows * width - bias.size))).reshape(rows, width)
+        parts = mp_gather(jnp.concatenate([low, norms.astype(LOW)], axis=0))
+        norms = sum(part[sub:].astype(F32) for part in parts)
+        both = jnp.concatenate([norms, bias], axis=0).astype(LOW)
+        mine, moved = chi_swap(by_place([part[:sub] for part in parts]), block, both)
+        g_mlp, x_last = after((g_mlp, x_last), parts[n_mp // 2])
+        g_gu, g_down = put_mlp(0, pick(g_mlp), mlp_sum)
+        g_gu = jnp.swapaxes(g_gu, 1, 2)
+        g_gu = with_layout_constraint(g_gu, Layout(major_to_minor=(0, 1, 2, 3)))
+        x_parts = after(mp_gather(x_last), g_gu)
+        x_mine, x_moved = chi_swap(by_place(x_parts), block)
+        moved = after(moved, x_parts)
+        tokens_grad = to_blocks(mine, moved, block).astype(F32)
+        both = both.astype(F32) + moved[block:].astype(F32)
+        activations = to_blocks(x_mine, x_moved, block)
+        for name, bit in group_bits[1:]:
+            both = both + swap(both, name, bit)
+        other = swap(both, "clo", 1)
+        norms = (both + other)[: 4 * LAYERS].reshape(LAYERS, 4, width)
+        mine, others = (
+            x[4 * LAYERS :].reshape(-1)[: LAYERS * 3 * half_in].reshape(LAYERS, 3, half_in)
+            for x in (both, other)
         )
-        bias = jnp.stack([small_out[l][2] for l in range(LAYERS)]).reshape(LAYERS, 3, half_in)
-        for k in range(log2(n_mp)):
-            norms = norms + swap(norms, "mp", 1 << k)
-        norms = norms + swap(norms, "clo", 1)
-        for name, bit in group_bits:
-            norms = norms + swap(norms, name, bit)
-            bias = bias + swap(bias, name, bit)
-        bias_other = swap(bias, "clo", 1)
-        bias = jnp.concatenate(
-            [jnp.where(clo == 0, bias, bias_other), jnp.where(clo == 0, bias_other, bias)], axis=2
-        )
+        low, high = jnp.where(clo == 0, mine, others), jnp.where(clo == 0, others, mine)
+        bias = jnp.concatenate([low, high], axis=2)
+        norms = [norms[:, i] for i in range(4)]
+        g_attn = after(scatter(g_attn), (tokens_grad, activations, g_gu, norms, bias))
+        g_qkv, g_out = put_attn(0, pick(g_attn), attn_sum)
+        g_qkv = jnp.swapaxes(g_qkv, 1, 2)
 
         return (
             activations, tokens_grad, norms[0], norms[1],
-            weight_out[0], bias, weight_out[1], norms[2], norms[3], weight_out[2], weight_out[3],
+            g_qkv, bias, g_out, norms[2], norms[3], g_gu, g_down,
         )
 
     return on_device

time: 761 us -> 730 us (0.959)
  other arithmetic: 40.7 us -> 11.4 us
  waiting for transfers between devices: 358 us -> 337 us
  Pallas kernels: 133 us -> 150 us
    ppermute x112 -> x106, waiting for transfers between devices: 324 us -> 306 us  [swap(): return lax.ppermute(value, axis, [(i, i ^ bit) for i in range(sizes[axis])])]
    pallas_call x30 -> x38, Pallas kernels: 133 us -> 150 us  [call(): pl.pallas_call(body, out_shape=tuple(outs), in_specs=[ANY] * n_any + [HBM...]
    pallas_call x0 -> x1, local copies, waits for them, and re-layouts: none -> 9.8 us  [call(): pl.pallas_call(body, out_shape=tuple(outs), in_specs=[ANY] * n_any + [HBM...]
    another operation x7, other arithmetic: 10.5 us -> 0.89 us  [the longest x4 10.4 us: above_zeros(): return with_layout_constraint(jnp.stack([jnp.zeros_like(x), x]), layout)]
    unnamed x223 -> x232, local copies, waits for them, and re-layouts: 54.2 us -> 63.2 us
    select_n x8 -> x2, local copies, waits for them, and re-layouts: 8.3 us -> 0.02 us  [the longest x1 0.01 us: on_device(): jnp.where(clo == 0, mine, others)]
    select_n x6 -> x2, other arithmetic: 9.37 us -> 1.17 us  [the longest x1 1.13 us: to_blocks(): return jnp.where(first, jnp.stack([mine, moved]), jnp.stack([moved, mine]))]
    ppermute x112 -> x106, starting transfers between devices: 109 us -> 114 us  [swap(): return lax.ppermute(value, axis, [(i, i ^ bit) for i in range(sizes[axis])])]
  transfers between devices with their start and end apart: 120 -> 114, of which waited for: 54 -> 53; matrix products, arithmetic and copies ran while one was open for 11% -> 6% of each run, Pallas kernels for 17% -> 18%
where the time goes in v5:
time: 730 us; the launch traced here: 725 us
  waiting for transfers between devices  337 us (46%)
  Pallas kernels  150 us (21%)
  starting transfers between devices  115 us (16%)
  local copies, waits for them, and re-layouts  95.5 us (13%)
  between operations  16.1 us (2%)
  other arithmetic  11.4 us (2%)
    ppermute x106, waiting for transfers between devices, swap(): return lax.ppermute(value, axis, [(i, i ^ bit) for i in range(sizes[axis])])  306 us
    pallas_call x38, Pallas kernels, call(): pl.pallas_call(body, out_shape=tuple(outs), in_specs=[ANY] * n_any + [HBM...  150 us
    ppermute x106, starting transfers between devices, swap(): return lax.ppermute(value, axis, [(i, i ^ bit) for i in range(sizes[axis])])  114 us
    unnamed x232, local copies, waits for them, and re-layouts  63.2 us
    all_gather x4, waiting for transfers between devices, gather_weights(): return lax.all_gather(own, ('dp', 'chi', 'clo'), axis=0, tiled=True)  31.4 us
  transfers between devices with their start and end apart: 114, of which 53 were waited for; matrix products, arithmetic and copies ran while one was open for 6% of the time, Pallas kernels for 18%

profile of v5, /device:TPU:0, one launch (start us, length us, event | category | flops | bytes accessed | tf_op | source)
XLA Modules:
  0.0 725.2 jit_solution(11487011371578562235)
XLA Ops:
  10.0 3.7 fusion.17
  17.1 5.0 concatenate.41
  24.6 4.2 concatenate.42
  34.1 6.5 collective-permute-done.9
  46.8 10.6 %collective-permute-done.3.refs_2_ = bf16[64,2048]{1,0:T(8,128)(2,1)S(1)} collective-permute-done((bf16[64,2048]{1,0:T(8,128)(2,1)S(1)}, bf16[64,2048]{1,0:T(8,128)(2,1)S(1)}, u32[]{:S(2)}, u32[]{:S(2)}) %collective-permute-start.3) | collective-permute-done | bytes 262176 | tf_op jit(solution)/shard_map/ppermute | solution.py:404
  58.6 6.3 collective-permute-done.4.refs_3_
  68.7 11.5 %shard_map.205 = (bf16[512,2048]{1,0:T(8,128)(2,1)}, bf16[512,256]{1,0:T(8,128)(2,1)}, bf16[512,256]{1,0:T(8,128)(2,1)}, bf16[512,256]{1,0:T(8,128)(2,1)}, bf16[...) custom-call(bf16[64,2048]{1,0:T(8,128)(2,1)} %copy-done.78, bf16[64,2048]{1,0:T(8,128)(2,1)} %copy-done.99, ...), custom_call_target="tpu_custom_call" | custom-call | flops 4294967296 | bytes 17574912 | tf_op jit(solution)/shard_map/pallas_call | solution.py:50
  89.5 5.7 collective-permute-done
  97.4 3.3 collective-permute-start.23
  100.7 7.3 %collective-permute-done.13.refs_2_ = bf16[64,2048]{1,0:T(8,128)(2,1)S(1)} collective-permute-done((bf16[64,2048]{1,0:T(8,128)(2,1)S(1)}, bf16[64,2048]{1,0:T(8,128)(2,1)S(1)}, u32[]{:S(2)}, u32[]{:S(2)}) %collective-permute-start.13) | collective-permute-done | bytes 262176 | tf_op jit(solution)/shard_map/ppermute | solution.py:404
  109.2 13.0 %collective-permute-start.16 = (bf16[64,2048]{1,0:T(8,128)(2,1)S(1)}, bf16[64,2048]{1,0:T(8,128)(2,1)S(1)}, u32[]{:S(2)}, u32[]{:S(2)}) collective-permute-start(bf16[64,2048]{1,0:T(8,128)(2,1)S(1)} %get-tuple-element.193.refs_0_), channel_id=1, source_target_pairs={{0,2},{1,3},{2,0},{3,1},{4,6},{5,7},{6,4},{7,5},{8,10},{9,11},{10,... | collective-permute-start | bytes 786440 | tf_op jit(solution)/shard_map/ppermute | solution.py:404
  122.2 8.3 %collective-permute-done.23.refs_2_ = bf16[64,2048]{1,0:T(8,128)(2,1)S(1)} collective-permute-done((bf16[64,2048]{1,0:T(8,128)(2,1)S(1)}, bf16[64,2048]{1,0:T(8,128)(2,1)S(1)}, u32[]{:S(2)}, u32[]{:S(2)}) %collective-permute-start.23) | collective-permute-done | bytes 262176 | tf_op jit(solution)/shard_map/ppermute | solution.py:404
  135.6 5.6 collective-permute-done.24.refs_3_
  147.6 4.8 collective-permute-done.17.refs_3_
  156.7 13.0 %all-gather.7.cloned.1.call-done.refs_8_ = bf16[2048,4352]{1,0:T(8,128)(2,1)} async-done(((bf16[256,4352]{1,0:T(8,128)(2,1)}), bf16[2048,4352]{1,0:T(8,128)(2,1)}) %all-gather.7.cloned.1.call-update) | async-done | bytes 17825808 | tf_op jit(solution)/shard_map/all_gather | solution.py:500
  177.3 7.7 %shard_map.208 = (bf16[512,2048]{1,0:T(8,128)(2,1)S(1)}, f32[512,1408]{1,0:T(8,128)S(1)}, bf16[512,704]{1,0:T(8,128)(2,1)S(1)}, f32[256,2048]{1,0:T(8,128)S(1)}, bf16[256,2048]{1,0:T(8,128)(2,1)S(1)}) custom-call(bf16[64,2048]{1,0:T(8,128)(2,1)S(1)} %copy-done.47, bf16[64,2048]{1,0:T(8,128)(2,1)S(1)} %copy-done.51, bf16[64,2048]{1,0:T(8,128)(2,1)S(1)} %copy-done.49, ...), custom_call_target="tpu_custom_call" | custom-call | flops 4563402752 | bytes 28770304 | tf_op jit(solution)/shard_map/pallas_call | solution.py:50
  193.7 9.1 %collective-permute-done.30.refs_1_ = bf16[64,2048]{1,0:T(8,128)(2,1)S(1)} collective-permute-done((bf16[64,2048]{1,0:T(8,128)(2,1)S(1)}, bf16[64,2048]{1,0:T(8,128)(2,1)S(1)}, u32[]{:S(2)}, u32[]{:S(2)}) %collective-permute-start.30) | collective-permute-done | bytes 262176 | tf_op jit(solution)/shard_map/ppermute | solution.py:404
  202.8 9.2 %collective-permute-done.31.refs_2_ = bf16[64,2048]{1,0:T(8,128)(2,1)S(1)} collective-permute-done((bf16[64,2048]{1,0:T(8,128)(2,1)S(1)}, bf16[64,2048]{1,0:T(8,128)(2,1)S(1)}, u32[]{:S(2)}, u32[]{:S(2)}) %collective-permute-start.31) | collective-permute-done | bytes 262176 | tf_op jit(solution)/shard_map/ppermute | solution.py:404
  213.9 6.1 collective-permute-start.34
  220.0 11.8 %collective-permute-done.34.refs_2_ = bf16[64,2048]{1,0:T(8,128)(2,1)} collective-permute-done((bf16[64,2048]{1,0:T(8,128)(2,1)}, bf16[64,2048]{1,0:T(8,128)(2,1)}, u32[]{:S(2)}, u32[]{:S(2)}) %collective-permute-start.34) | collective-permute-done | bytes 262176 | tf_op jit(solution)/shard_map/ppermute | solution.py:404
  232.3 6.7 collective-permute-done.35.refs_3_
  241.0 11.4 %shard_map.212 = (bf16[512,2048]{1,0:T(8,128)(2,1)}, bf16[512,256]{1,0:T(8,128)(2,1)}, bf16[512,256]{1,0:T(8,128)(2,1)}, bf16[512,256]{1,0:T(8,128)(2,1)}, bf16[...) custom-call(bf16[64,2048]{1,0:T(8,128)(2,1)} %get-tuple-element.208.refs_0_, ...), custom_call_target="tpu_custom_call" | custom-call | flops 4294967296 | bytes 17574912 | tf_op jit(solution)/shard_map/pallas_call | solution.py:50
  261.5 8.7 %collective-permute-done.41.refs_1_ = bf16[64,2048]{1,0:T(8,128)(2,1)S(1)} collective-permute-done((bf16[64,2048]{1,0:T(8,128)(2,1)S(1)}, bf16[64,2048]{1,0:T(8,128)(2,1)S(1)}, u32[]{:S(2)}, u32[]{:S(2)}) %collective-permute-start.41) | collective-permute-done | bytes 262176 | tf_op jit(solution)/shard_map/ppermute | solution.py:404
  270.2 8.8 %collective-permute-done.42.refs_2_ = bf16[64,2048]{1,0:T(8,128)(2,1)S(1)} collective-permute-done((bf16[64,2048]{1,0:T(8,128)(2,1)S(1)}, bf16[64,2048]{1,0:T(8,128)(2,1)S(1)}, u32[]{:S(2)}, u32[]{:S(2)}) %collective-permute-start.42) | collective-permute-done | bytes 262176 | tf_op jit(solution)/shard_map/ppermute | solution.py:404
  280.8 5.5 collective-permute-start.45
  286.3 11.5 %collective-permute-done.45.refs_2_ = bf16[64,2048]{1,0:T(8,128)(2,1)} collective-permute-done((bf16[64,2048]{1,0:T(8,128)(2,1)}, bf16[64,2048]{1,0:T(8,128)(2,1)}, u32[]{:S(2)}, u32[]{:S(2)}) %collective-permute-start.45) | collective-permute-done | bytes 262176 | tf_op jit(solution)/shard_map/ppermute | solution.py:404
  298.4 6.5 collective-permute-done.46.refs_3_
  304.9 18.4 %all-gather.11.cloned.1.call-done.refs_8_ = bf16[2048,4352]{1,0:T(8,128)(2,1)} async-done(((bf16[256,4352]{1,0:T(8,128)(2,1)}), bf16[2048,4352]{1,0:T(8,128)(2,1)}) %all-gather.11.cloned.1.call-update) | async-done | bytes 17825808 | tf_op jit(solution)/shard_map/all_gather | solution.py:500
  323.3 8.0 %shard_map.215 = (bf16[512,2048]{1,0:T(8,128)(2,1)S(1)}, f32[512,1408]{1,0:T(8,128)S(1)}, bf16[512,704]{1,0:T(8,128)(2,1)S(1)}, f32[256,2048]{1,0:T(8,128)S(1)}, bf16[256,2048]{1,0:T(8,128)(2,1)S(1)}) custom-call(bf16[64,2048]{1,0:T(8,128)(2,1)} %get-tuple-element.224.refs_0_, bf16[64,2048]{1,0:T(8,128)(2,1)} %collective-permute-done.44.refs_1_, ...), custom_call_target="tpu_custom_call" | custom-call | flops 4563402752 | bytes 28770304 | tf_op jit(solution)/shard_map/pallas_call | solution.py:50
  338.1 9.6 %shard_map.217 = (bf16[512,2048]{1,0:T(8,128)(2,1)S(1)}, bf16[512,1408]{1,0:T(8,128)(2,1)S(1)}, f32[256,2048]{1,0:T(8,128)S(1)}, bf16[256,2048]{1,0:T(8,128)(2,1)}) custom-call(bf16[64,2048]{1,0:T(8,128)(2,1)S(1)} %copy-done.21, bf16[64,2048]{1,0:T(8,128)(2,1)S(1)} %copy-done.33, bf16[64,2048]{1,0:T(8,128)(2,1)S(1)} %copy-done.35, ...), custom_call_target="tpu_custom_call" | custom-call | flops 4563402752 | bytes 29491200 | tf_op jit(solution)/shard_map/pallas_call | solution.py:50
  356.1 10.4 %shard_map.218 = bf16[2048,2176]{1,0:T(8,128)(2,1)} custom-call(bf16[512,2048]{1,0:T(8,128)(2,1)} %copy-done.71, bf16[512,2048]{1,0:T(8,128)(2,1)} %copy-done.73, bf16[512,1408]{1,0:T(8,128)(2,1)} %copy-done.75, bf16[512,704]{1,0:T(8,128)(2,1)} %copy-done.77), custom_call_target="tpu_custom_call" | custom-call | flops 4563402752 | bytes 15269888 | tf_op jit(solution)/shard_map/pallas_call | solution.py:50
  366.6 8.3 %collective-permute-done.54 = bf16[64,2048]{1,0:T(8,128)(2,1)} collective-permute-done((bf16[64,2048]{1,0:T(8,128)(2,1)}, bf16[64,2048]{1,0:T(8,128)(2,1)}, u32[]{:S(2)}, u32[]{:S(2)}) %collective-permute-start.54) | collective-permute-done | bytes 262176 | tf_op jit(solution)/shard_map/ppermute | solution.py:404
  378.5 5.3 collective-permute-start.56
  386.2 7.6 %collective-permute-done.56.refs_1_ = bf16[64,2048]{1,0:T(8,128)(2,1)S(1)} collective-permute-done((bf16[64,2048]{1,0:T(8,128)(2,1)S(1)}, bf16[64,2048]{1,0:T(8,128)(2,1)S(1)}, u32[]{:S(2)}, u32[]{:S(2)}) %collective-permute-start.56) | collective-permute-done | bytes 262176 | tf_op jit(solution)/shard_map/ppermute | solution.py:404
  393.9 11.3 %collective-permute-done.57.refs_2_ = bf16[64,2048]{1,0:T(8,128)(2,1)S(1)} collective-permute-done((bf16[64,2048]{1,0:T(8,128)(2,1)S(1)}, bf16[64,2048]{1,0:T(8,128)(2,1)S(1)}, u32[]{:S(2)}, u32[]{:S(2)}) %collective-permute-start.57) | collective-permute-done | bytes 262176 | tf_op jit(solution)/shard_map/ppermute | solution.py:404
  406.7 5.0 collective-permute-start.60
  411.7 10.2 %collective-permute-done.60.refs_2_ = bf16[64,2048]{1,0:T(8,128)(2,1)S(1)} collective-permute-done((bf16[64,2048]{1,0:T(8,128)(2,1)S(1)}, bf16[64,2048]{1,0:T(8,128)(2,1)S(1)}, u32[]{:S(2)}, u32[]{:S(2)}) %collective-permute-start.60) | collective-permute-done | bytes 262176 | tf_op jit(solution)/shard_map/ppermute | solution.py:404
  422.5 6.3 collective-permute-done.61.refs_3_
  431.1 13.6 %shard_map.221 = (bf16[512,2048]{1,0:T(8,128)(2,1)}, bf16[512,768]{1,0:T(8,128)(2,1)}, f32[1,768]{1,0:T(1,128)}, f32[256,2048]{1,0:T(8,128)}, bf16[256,2048]{1,0:T(8,128)(2,1)}) custom-call(bf16[64,2048]{1,0:T(8,128)(2,1)} %copy-done.79, bf16[64,2048]{1,0:T(8,128)(2,1)} %copy-done.106, bf16[64,2048]{1,0:T(8,128)(2,1)} %copy-done.105, ...), custom_call_target="tpu_custom_call" | custom-call | flops 4831838208 | bytes 18099200 | tf_op jit(solution)/shard_map/pallas_call | solution.py:50
  455.5 7.0 shard_map.223
  463.9 9.1 %collective-permute-done.68.refs_2_ = bf16[64,2048]{1,0:T(8,128)(2,1)} collective-permute-done((bf16[64,2048]{1,0:T(8,128)(2,1)}, bf16[64,2048]{1,0:T(8,128)(2,1)}, u32[]{:S(2)}, u32[]{:S(2)}) %collective-permute-start.68) | collective-permute-done | bytes 262176 | tf_op jit(solution)/shard_map/ppermute | solution.py:404
  478.9 5.2 collective-permute-start.71
  484.3 10.9 %collective-permute-done.71.refs_2_ = bf16[64,2048]{1,0:T(8,128)(2,1)S(1)} collective-permute-done((bf16[64,2048]{1,0:T(8,128)(2,1)S(1)}, bf16[64,2048]{1,0:T(8,128)(2,1)S(1)}, u32[]{:S(2)}, u32[]{:S(2)}) %collective-permute-start.71) | collective-permute-done | bytes 262176 | tf_op jit(solution)/shard_map/ppermute | solution.py:404
  495.8 5.7 collective-permute-done.72.refs_3_
  503.1 8.7 %shard_map.225 = (bf16[512,2048]{1,0:T(8,128)(2,1)S(1)}, bf16[512,1408]{1,0:T(8,128)(2,1)S(1)}, f32[256,2048]{1,0:T(8,128)S(1)}, bf16[256,2048]{1,0:T(8,128)(2,1)S(1)}) custom-call(bf16[64,2048]{1,0:T(8,128)(2,1)S(1)} %get-tuple-element.268.refs_0_, bf16[64,2048]{1,0:T(8,128)(2,1)S(1)} %collective-permute-done.70.refs_1_, ...), custom_call_target="tpu_custom_call" | custom-call | flops 4563402752 | bytes 29491200 | tf_op jit(solution)/shard_map/pallas_call | solution.py:50
  518.0 3.4 collective-permute-start.79
  521.4 10.5 %shard_map.227 = bf16[2048,2176]{1,0:T(8,128)(2,1)} custom-call(bf16[512,2048]{1,0:T(8,128)(2,1)} %copy-done.70, bf16[512,2048]{1,0:T(8,128)(2,1)} %copy-done.72, bf16[512,1408]{1,0:T(8,128)(2,1)} %copy-done.74, bf16[512,704]{1,0:T(8,128)(2,1)} %copy-done.76), custom_call_target="tpu_custom_call" | custom-call | flops 4563402752 | bytes 15269888 | tf_op jit(solution)/shard_map/pallas_call | solution.py:50
  532.6 7.2 collective-permute-done.79.refs_2_
  545.5 5.6 collective-permute-start.82
  552.7 10.3 %collective-permute-done.82.refs_2_ = bf16[64,2048]{1,0:T(8,128)(2,1)S(1)} collective-permute-done((bf16[64,2048]{1,0:T(8,128)(2,1)}, bf16[64,2048]{1,0:T(8,128)(2,1)S(1)}, u32[]{:S(2)}, u32[]{:S(2)}) %collective-permute-start.82) | collective-permute-done | bytes 262176 | tf_op jit(solution)/shard_map/ppermute | solution.py:404
  563.0 3.3 collective-permute-done.81.refs_1_
  566.4 5.3 collective-permute-done.83.refs_3_
  575.1 4.2 shard_map.230
  580.1 13.6 %shard_map.233 = (bf16[512,2048]{1,0:T(8,128)(2,1)}, bf16[512,768]{1,0:T(8,128)(2,1)}, f32[1,768]{1,0:T(1,128)}, f32[256,2048]{1,0:T(8,128)}, bf16[256,2048]{1,0:T(8,128)(2,1)}) custom-call(bf16[64,2048]{1,0:T(8,128)(2,1)} %get-tuple-element.302.refs_0_, bf16[64,2048]{1,0:T(8,128)(2,1)} %copy-done.104, bf16[64,2048]{1,0:T(8,128)(2,1)} %copy-done.101, ...), custom_call_target="tpu_custom_call" | custom-call | flops 4831838208 | bytes 18099200 | tf_op jit(solution)/shard_map/pallas_call | solution.py:50
  604.6 7.5 %shard_map.235 = bf16[2048,1024]{1,0:T(8,128)(2,1)} custom-call(bf16[512,2048]{1,0:T(8,128)(2,1)} %get-tuple-element.323.refs_0_, bf16[512,2048]{1,0:T(8,128)(2,1)} %get-tuple-element.324.refs_1_, bf16[512,768]{1,0:T(8,128)(2,1)} %get-tuple-element.325.refs_2_, bf16[512,256]{1,0:T(8,128)(2,1)} %get-tuple-element.326.refs_3_), custom_call_target="tpu_custom_call" | custom-call | flops 2147483648 | bytes 9437184 | tf_op jit(solution)/shard_map/pallas_call | solution.py:50
  612.6 9.1 %collective-permute-done.92.refs_2_ = bf16[64,2048]{1,0:T(8,128)(2,1)S(1)} collective-permute-done((bf16[64,2048]{1,0:T(8,128)(2,1)}, bf16[64,2048]{1,0:T(8,128)(2,1)S(1)}, u32[]{:S(2)}, u32[]{:S(2)}) %collective-permute-start.92) | collective-permute-done | bytes 262176 | tf_op jit(solution)/shard_map/ppermute | solution.py:404
  626.2 5.1 collective-permute-start.94
  632.7 11.6 %collective-permute-done.94 = bf16[72,2048]{1,0:T(8,128)(2,1)S(1)} collective-permute-done((bf16[72,2048]{1,0:T(8,128)(2,1)S(1)}, bf16[72,2048]{1,0:T(8,128)(2,1)S(1)}, u32[]{:S(2)}, u32[]{:S(2)}) %collective-permute-start.94) | collective-permute-done | bytes 294944 | tf_op jit(solution)/shard_map/ppermute | solution.py:404
  645.0 7.2 collective-permute-done.101
  659.8 11.8 %collective-permute-done.96 = bf16[64,2048]{1,0:T(8,128)(2,1)S(1)} collective-permute-done((bf16[64,2048]{1,0:T(8,128)(2,1)S(1)}, bf16[64,2048]{1,0:T(8,128)(2,1)S(1)}, u32[]{:S(2)}, u32[]{:S(2)}) %collective-permute-start.96) | collective-permute-done | bytes 262176 | tf_op jit(solution)/shard_map/ppermute | solution.py:404
  672.7 4.2 shard_map.238
  676.9 9.8 %copy.85 = f32[2,2,256,1408]{3,1,2,0:T(2,128)} copy(f32[2,2,256,1408]{3,2,1,0:T(8,128)} %get-tuple-element.340) | data formatting | bytes 11534336 | tf_op jit(solution)/shard_map/pallas_call | solution.py:50
  690.4 5.3 collective-permute-done.103
  700.8 9.3 %collective-permute-done.99 = bf16[128,2048]{1,0:T(8,128)(2,1)S(1)} collective-permute-done((bf16[128,2048]{1,0:T(8,128)(2,1)S(1)}, bf16[128,2048]{1,0:T(8,128)(2,1)S(1)}, u32[]{:S(2)}, u32[]{:S(2)}) %collective-permute-start.99) | collective-permute-done | bytes 524320 | tf_op jit(solution)/shard_map/ppermute | solution.py:404
  (529 shorter events, 192.5 us)
Async XLA Ops:
  7.2 60.8 %all-gather.5.cloned.1.call-start = ((), (), s32[]{:S(2)}) async-start(), calls=%async_computation.4 | async-start | bytes 9437184 | tf_op jit(solution)/shard_map/all_gather | solution.py:500
  9.9 159.8 %all-gather.7.cloned.1.call-start = ((), (), s32[]{:S(2)}) async-start(), calls=%async_computation.5 | async-start | bytes 20054016 | tf_op jit(solution)/shard_map/all_gather | solution.py:500
  22.1 217.0 %all-gather.9.cloned.1.call-start = ((), (), s32[]{:S(2)}) async-start(), calls=%async_computation.6 | async-start | bytes 9437184 | tf_op jit(solution)/shard_map/all_gather | solution.py:500
  23.2 300.0 %all-gather.11.cloned.1.call-start = ((), (), s32[]{:S(2)}) async-start(), calls=%async_computation.7 | async-start | bytes 20054016 | tf_op jit(solution)/shard_map/all_gather | solution.py:500
  28.9 512.4 %reduce-scatter.7.cloned.1.call-start = ((), (), s32[]{:S(2)}) async-start(), calls=%async_computation.9 | async-start | bytes 11141120 | tf_op jit(solution)/shard_map/reduce_scatter | solution.py:580
  42.3 15.1 %collective-permute-start.3 = (bf16[64,2048]{1,0:T(8,128)(2,1)S(1)}, bf16[64,2048]{1,0:T(8,128)(2,1)S(1)}, u32[]{:S(2)}, u32[]{:S(2)}) collective-permute-start(bf16[64,2048]{1,0:T(8,128)(2,1)S(1)} %get-tuple-element.184.refs_0_), channel_id=1, source_target_pairs={{0,2},{1,3},{2,0},{3,1},{4,6},{5,7},{6,4},{7,5},{8,10},{9,11},{10,... | collective-permute-start | bytes 786440 | tf_op jit(solution)/shard_map/ppermute | solution.py:404
  45.3 13.2 %collective-permute-start.2 = (bf16[64,2048]{1,0:T(8,128)(2,1)S(1)}, bf16[64,2048]{1,0:T(8,128)(2,1)S(1)}, u32[]{:S(2)}, u32[]{:S(2)}) collective-permute-start(bf16[64,2048]{1,0:T(8,128)(2,1)S(1)} %get-tuple-element.184.refs_0_), channel_id=1, source_target_pairs={{0,1},{1,0},{2,3},{3,2},{4,5},{5,4},{6,7},{7,6},{8,9},{9,8},{10,11... | collective-permute-start | bytes 786440 | tf_op jit(solution)/shard_map/ppermute | solution.py:404
  80.8 14.4 %collective-permute-start = (bf16[64,2048]{1,0:T(8,128)(2,1)S(1)}, bf16[64,2048]{1,0:T(8,128)(2,1)S(1)}, u32[]{:S(2)}, u32[]{:S(2)}) collective-permute-start(bf16[64,2048]{1,0:T(8,128)(2,1)S(1)} %dynamic-slice_bitcast_fusion.3), channel_id=1, source_target_pairs={{0,8},{8,0},{1,9},{9,1},{2,10},{10,2},{3,11},{11,3},{4,12},{12,4},... | collective-permute-start | bytes 786440 | tf_op jit(solution)/shard_map/ppermute | solution.py:404
  85.0 15.7 %collective-permute-start.12 = (bf16[64,2048]{1,0:T(8,128)(2,1)S(1)}, bf16[64,2048]{1,0:T(8,128)(2,1)S(1)}, u32[]{:S(2)}, u32[]{:S(2)}) collective-permute-start(bf16[64,2048]{1,0:T(8,128)(2,1)S(1)} %get-tuple-element.188), channel_id=1, source_target_pairs={{0,1},{1,0},{2,3},{3,2},{4,5},{5,4},{6,7},{7,6},{8,9},{9,8},{10,11... | collective-permute-start | bytes 786440 | tf_op jit(solution)/shard_map/ppermute | solution.py:404
  86.3 21.6 %collective-permute-start.13 = (bf16[64,2048]{1,0:T(8,128)(2,1)S(1)}, bf16[64,2048]{1,0:T(8,128)(2,1)S(1)}, u32[]{:S(2)}, u32[]{:S(2)}) collective-permute-start(bf16[64,2048]{1,0:T(8,128)(2,1)S(1)} %get-tuple-element.189), channel_id=1, source_target_pairs={{0,2},{1,3},{2,0},{3,1},{4,6},{5,7},{6,4},{7,5},{8,10},{9,11},{10,... | collective-permute-start | bytes 786440 | tf_op jit(solution)/shard_map/ppermute | solution.py:404
  89.5 18.4 %collective-permute-start.14 = (bf16[64,2048]{1,0:T(8,128)(2,1)S(1)}, bf16[64,2048]{1,0:T(8,128)(2,1)S(1)}, u32[]{:S(2)}, u32[]{:S(2)}) collective-permute-start(bf16[64,2048]{1,0:T(8,128)(2,1)S(1)} %get-tuple-element.190), channel_id=1, source_target_pairs={{0,3},{1,2},{2,1},{3,0},{4,7},{5,6},{6,5},{7,4},{8,11},{9,10},{10,... | collective-permute-start | bytes 786440 | tf_op jit(solution)/shard_map/ppermute | solution.py:404
  96.1 34.3 %collective-permute-start.22 = (bf16[64,2048]{1,0:T(8,128)(2,1)S(1)}, bf16[64,2048]{1,0:T(8,128)(2,1)S(1)}, u32[]{:S(2)}, u32[]{:S(2)}) collective-permute-start(bf16[64,2048]{1,0:T(8,128)(2,1)S(1)} %get-tuple-element.216.refs_0_), channel_id=1, source_target_pairs={{0,1},{1,0},{2,3},{3,2},{4,5},{5,4},{6,7},{7,6},{8,9},{9,8},{10,11... | collective-permute-start | bytes 786440 | tf_op jit(solution)/shard_map/ppermute | solution.py:404
  97.4 33.1 %collective-permute-start.23 = (bf16[64,2048]{1,0:T(8,128)(2,1)S(1)}, bf16[64,2048]{1,0:T(8,128)(2,1)S(1)}, u32[]{:S(2)}, u32[]{:S(2)}) collective-permute-start(bf16[64,2048]{1,0:T(8,128)(2,1)S(1)} %get-tuple-element.216.refs_0_), channel_id=1, source_target_pairs={{0,2},{1,3},{2,0},{3,1},{4,6},{5,7},{6,4},{7,5},{8,10},{9,11},{10,... | collective-permute-start | bytes 786440 | tf_op jit(solution)/shard_map/ppermute | solution.py:404
  100.7 31.7 %collective-permute-start.25 = (bf16[64,2048]{1,0:T(8,128)(2,1)S(1)}, bf16[64,2048]{1,0:T(8,128)(2,1)S(1)}, u32[]{:S(2)}, u32[]{:S(2)}) collective-permute-start(bf16[64,2048]{1,0:T(8,128)(2,1)S(1)} %get-tuple-element.216.refs_0_), channel_id=1, source_target_pairs={{0,4},{4,0},{1,5},{5,1},{2,6},{6,2},{3,7},{7,3},{8,12},{12,8},{9,1... | collective-permute-start | bytes 786440 | tf_op jit(solution)/shard_map/ppermute | solution.py:404
  109.2 26.4 %collective-permute-start.16 = (bf16[64,2048]{1,0:T(8,128)(2,1)S(1)}, bf16[64,2048]{1,0:T(8,128)(2,1)S(1)}, u32[]{:S(2)}, u32[]{:S(2)}) collective-permute-start(bf16[64,2048]{1,0:T(8,128)(2,1)S(1)} %get-tuple-element.193.refs_0_), channel_id=1, source_target_pairs={{0,2},{1,3},{2,0},{3,1},{4,6},{5,7},{6,4},{7,5},{8,10},{9,11},{10,... | collective-permute-start | bytes 786440 | tf_op jit(solution)/shard_map/ppermute | solution.py:404
  131.2 12.7 %collective-permute-start.27 = (bf16[64,2048]{1,0:T(8,128)(2,1)S(1)}, bf16[64,2048]{1,0:T(8,128)(2,1)S(1)}, u32[]{:S(2)}, u32[]{:S(2)}) collective-permute-start(bf16[64,2048]{1,0:T(8,128)(2,1)S(1)} %collective-permute-done.23.refs_2_), channel_id=1, source_target_pairs={{0,4},{4,0},{1,5},{5,1},{2,6},{6,2},{3,7},{7,3},{8,12},{12,8},{9,1... | collective-permute-start | bytes 786440 | tf_op jit(solution)/shard_map/ppermute | solution.py:404
  133.1 13.7 %collective-permute-start.15 = (bf16[64,2048]{1,0:T(8,128)(2,1)S(1)}, bf16[64,2048]{1,0:T(8,128)(2,1)S(1)}, u32[]{:S(2)}, u32[]{:S(2)}) collective-permute-start(bf16[64,2048]{1,0:T(8,128)(2,1)S(1)} %get-tuple-element.193.refs_0_), channel_id=1, source_target_pairs={{0,1},{1,0},{2,3},{3,2},{4,5},{5,4},{6,7},{7,6},{8,9},{9,8},{10,11... | collective-permute-start | bytes 786440 | tf_op jit(solution)/shard_map/ppermute | solution.py:404
  135.6 16.7 %collective-permute-start.17 = (bf16[64,2048]{1,0:T(8,128)(2,1)S(1)}, bf16[64,2048]{1,0:T(8,128)(2,1)S(1)}, u32[]{:S(2)}, u32[]{:S(2)}) collective-permute-start(bf16[64,2048]{1,0:T(8,128)(2,1)S(1)} %collective-permute-done.16.refs_2_), channel_id=1, source_target_pairs={{0,1},{1,0},{2,3},{3,2},{4,5},{5,4},{6,7},{7,6},{8,9},{9,8},{10,11... | collective-permute-start | bytes 786440 | tf_op jit(solution)/shard_map/ppermute | solution.py:404
  189.3 13.5 %collective-permute-start.30 = (bf16[64,2048]{1,0:T(8,128)(2,1)S(1)}, bf16[64,2048]{1,0:T(8,128)(2,1)S(1)}, u32[]{:S(2)}, u32[]{:S(2)}) collective-permute-start(bf16[64,2048]{1,0:T(8,128)(2,1)S(1)} %get-tuple-element.204), channel_id=1, source_target_pairs={{0,1},{1,0},{2,3},{3,2},{4,5},{5,4},{6,7},{7,6},{8,9},{9,8},{10,11... | collective-permute-start | bytes 786440 | tf_op jit(solution)/shard_map/ppermute | solution.py:404
  190.7 21.4 %collective-permute-start.31 = (bf16[64,2048]{1,0:T(8,128)(2,1)S(1)}, bf16[64,2048]{1,0:T(8,128)(2,1)S(1)}, u32[]{:S(2)}, u32[]{:S(2)}) collective-permute-start(bf16[64,2048]{1,0:T(8,128)(2,1)S(1)} %get-tuple-element.205), channel_id=1, source_target_pairs={{0,2},{1,3},{2,0},{3,1},{4,6},{5,7},{6,4},{7,5},{8,10},{9,11},{10,... | collective-permute-start | bytes 786440 | tf_op jit(solution)/shard_map/ppermute | solution.py:404
  193.1 19.0 %collective-permute-start.32 = (bf16[64,2048]{1,0:T(8,128)(2,1)S(1)}, bf16[64,2048]{1,0:T(8,128)(2,1)S(1)}, u32[]{:S(2)}, u32[]{:S(2)}) collective-permute-start(bf16[64,2048]{1,0:T(8,128)(2,1)S(1)} %get-tuple-element.206), channel_id=1, source_target_pairs={{0,3},{1,2},{2,1},{3,0},{4,7},{5,6},{6,5},{7,4},{8,11},{9,10},{10,... | collective-permute-start | bytes 786440 | tf_op jit(solution)/shard_map/ppermute | solution.py:404
  213.9 17.9 %collective-permute-start.34 = (bf16[64,2048]{1,0:T(8,128)(2,1)}, bf16[64,2048]{1,0:T(8,128)(2,1)}, u32[]{:S(2)}, u32[]{:S(2)}) collective-permute-start(bf16[64,2048]{1,0:T(8,128)(2,1)} %get-tuple-element.208.refs_0_), channel_id=1, source_target_pairs={{0,2},{1,3},{2,0},{3,1},{4,6},{5,7},{6,4},{7,5},{8,10},{9,11},{10,... | collective-permute-start | bytes 786440 | tf_op jit(solution)/shard_map/ppermute | solution.py:404
  257.0 13.1 %collective-permute-start.41 = (bf16[64,2048]{1,0:T(8,128)(2,1)S(1)}, bf16[64,2048]{1,0:T(8,128)(2,1)S(1)}, u32[]{:S(2)}, u32[]{:S(2)}) collective-permute-start(bf16[64,2048]{1,0:T(8,128)(2,1)S(1)} %get-tuple-element.212), channel_id=1, source_target_pairs={{0,1},{1,0},{2,3},{3,2},{4,5},{5,4},{6,7},{7,6},{8,9},{9,8},{10,11... | collective-permute-start | bytes 786440 | tf_op jit(solution)/shard_map/ppermute | solution.py:404
  257.6 21.3 %collective-permute-start.42 = (bf16[64,2048]{1,0:T(8,128)(2,1)S(1)}, bf16[64,2048]{1,0:T(8,128)(2,1)S(1)}, u32[]{:S(2)}, u32[]{:S(2)}) collective-permute-start(bf16[64,2048]{1,0:T(8,128)(2,1)S(1)} %get-tuple-element.213), channel_id=1, source_target_pairs={{0,2},{1,3},{2,0},{3,1},{4,6},{5,7},{6,4},{7,5},{8,10},{9,11},{10,... | collective-permute-start | bytes 786440 | tf_op jit(solution)/shard_map/ppermute | solution.py:404
  259.5 19.4 %collective-permute-start.43 = (bf16[64,2048]{1,0:T(8,128)(2,1)S(1)}, bf16[64,2048]{1,0:T(8,128)(2,1)S(1)}, u32[]{:S(2)}, u32[]{:S(2)}) collective-permute-start(bf16[64,2048]{1,0:T(8,128)(2,1)S(1)} %get-tuple-element.214), channel_id=1, source_target_pairs={{0,3},{1,2},{2,1},{3,0},{4,7},{5,6},{6,5},{7,4},{8,11},{9,10},{10,... | collective-permute-start | bytes 786440 | tf_op jit(solution)/shard_map/ppermute | solution.py:404
  280.8 17.0 %collective-permute-start.45 = (bf16[64,2048]{1,0:T(8,128)(2,1)}, bf16[64,2048]{1,0:T(8,128)(2,1)}, u32[]{:S(2)}, u32[]{:S(2)}) collective-permute-start(bf16[64,2048]{1,0:T(8,128)(2,1)} %get-tuple-element.224.refs_0_), channel_id=1, source_target_pairs={{0,2},{1,3},{2,0},{3,1},{4,6},{5,7},{6,4},{7,5},{8,10},{9,11},{10,... | collective-permute-start | bytes 786440 | tf_op jit(solution)/shard_map/ppermute | solution.py:404
  297.9 25.4 %collective-permute-start.47 = (bf16[64,2048]{1,0:T(8,128)(2,1)}, bf16[64,2048]{1,0:T(8,128)(2,1)}, u32[]{:S(2)}, u32[]{:S(2)}) collective-permute-start(bf16[64,2048]{1,0:T(8,128)(2,1)} %get-tuple-element.224.refs_0_), channel_id=1, source_target_pairs={{0,4},{4,0},{1,5},{5,1},{2,6},{6,2},{3,7},{7,3},{8,12},{12,8},{9,1... | collective-permute-start | bytes 786440 | tf_op jit(solution)/shard_map/ppermute | solution.py:404
  297.9 25.4 %collective-permute-start.49 = (bf16[64,2048]{1,0:T(8,128)(2,1)}, bf16[64,2048]{1,0:T(8,128)(2,1)}, u32[]{:S(2)}, u32[]{:S(2)}) collective-permute-start(bf16[64,2048]{1,0:T(8,128)(2,1)} %collective-permute-done.45.refs_2_), channel_id=1, source_target_pairs={{0,4},{4,0},{1,5},{5,1},{2,6},{6,2},{3,7},{7,3},{8,12},{12,8},{9,1... | collective-permute-start | bytes 786440 | tf_op jit(solution)/shard_map/ppermute | solution.py:404
  298.4 24.9 %collective-permute-start.48 = (bf16[64,2048]{1,0:T(8,128)(2,1)}, bf16[64,2048]{1,0:T(8,128)(2,1)}, u32[]{:S(2)}, u32[]{:S(2)}) collective-permute-start(bf16[64,2048]{1,0:T(8,128)(2,1)} %collective-permute-done.44.refs_1_), channel_id=1, source_target_pairs={{0,4},{4,0},{1,5},{5,1},{2,6},{6,2},{3,7},{7,3},{8,12},{12,8},{9,1... | collective-permute-start | bytes 786440 | tf_op jit(solution)/shard_map/ppermute | solution.py:404
  304.9 18.4 %collective-permute-start.50 = (bf16[64,2048]{1,0:T(8,128)(2,1)}, bf16[64,2048]{1,0:T(8,128)(2,1)}, u32[]{:S(2)}, u32[]{:S(2)}) collective-permute-start(bf16[64,2048]{1,0:T(8,128)(2,1)} %collective-permute-done.46.refs_3_), channel_id=1, source_target_pairs={{0,4},{4,0},{1,5},{5,1},{2,6},{6,2},{3,7},{7,3},{8,12},{12,8},{9,1... | collective-permute-start | bytes 786440 | tf_op jit(solution)/shard_map/ppermute | solution.py:404
  351.5 23.4 %collective-permute-start.52 = (bf16[256,2048]{1,0:T(8,128)(2,1)}, bf16[256,2048]{1,0:T(8,128)(2,1)}, u32[]{:S(2)}, u32[]{:S(2)}) collective-permute-start(bf16[256,2048]{1,0:T(8,128)(2,1)} %get-tuple-element.231), channel_id=1, source_target_pairs={{0,4},{4,0},{1,5},{5,1},{2,6},{6,2},{3,7},{7,3},{8,12},{12,8},{9,1... | collective-permute-start | bytes 3145736 | tf_op jit(solution)/shard_map/ppermute | solution.py:404
  351.8 14.8 %collective-permute-start.53 = (bf16[64,2048]{1,0:T(8,128)(2,1)}, bf16[64,2048]{1,0:T(8,128)(2,1)}, u32[]{:S(2)}, u32[]{:S(2)}) collective-permute-start(bf16[64,2048]{1,0:T(8,128)(2,1)} %get-tuple-element.232), channel_id=1, source_target_pairs={{0,1},{1,0},{2,3},{3,2},{4,5},{5,4},{6,7},{7,6},{8,9},{9,8},{10,11... | collective-permute-start | bytes 786440 | tf_op jit(solution)/shard_map/ppermute | solution.py:404
  353.2 21.6 %collective-permute-start.54 = (bf16[64,2048]{1,0:T(8,128)(2,1)}, bf16[64,2048]{1,0:T(8,128)(2,1)}, u32[]{:S(2)}, u32[]{:S(2)}) collective-permute-start(bf16[64,2048]{1,0:T(8,128)(2,1)} %get-tuple-element.233), channel_id=1, source_target_pairs={{0,2},{1,3},{2,0},{3,1},{4,6},{5,7},{6,4},{7,5},{8,10},{9,11},{10,... | collective-permute-start | bytes 786440 | tf_op jit(solution)/shard_map/ppermute | solution.py:404
  355.7 19.2 %collective-permute-start.55 = (bf16[64,2048]{1,0:T(8,128)(2,1)}, bf16[64,2048]{1,0:T(8,128)(2,1)}, u32[]{:S(2)}, u32[]{:S(2)}) collective-permute-start(bf16[64,2048]{1,0:T(8,128)(2,1)} %get-tuple-element.234), channel_id=1, source_target_pairs={{0,3},{1,2},{2,1},{3,0},{4,7},{5,6},{6,5},{7,4},{8,11},{9,10},{10,... | collective-permute-start | bytes 786440 | tf_op jit(solution)/shard_map/ppermute | solution.py:404
  374.9 176.1 %reduce-scatter.9.cloned.1.call-start = ((), (), s32[]{:S(2)}) async-start(), calls=%async_computation.10 | async-start | bytes 5242880 | tf_op jit(solution)/shard_map/reduce_scatter | solution.py:580
  378.5 15.4 %collective-permute-start.56 = (bf16[64,2048]{1,0:T(8,128)(2,1)S(1)}, bf16[64,2048]{1,0:T(8,128)(2,1)S(1)}, u32[]{:S(2)}, u32[]{:S(2)}) collective-permute-start(bf16[64,2048]{1,0:T(8,128)(2,1)S(1)} %get-tuple-element.242), channel_id=1, source_target_pairs={{0,1},{1,0},{2,3},{3,2},{4,5},{5,4},{6,7},{7,6},{8,9},{9,8},{10,11... | collective-permute-start | bytes 786440 | tf_op jit(solution)/shard_map/ppermute | solution.py:404
  383.8 21.4 %collective-permute-start.57 = (bf16[64,2048]{1,0:T(8,128)(2,1)S(1)}, bf16[64,2048]{1,0:T(8,128)(2,1)S(1)}, u32[]{:S(2)}, u32[]{:S(2)}) collective-permute-start(bf16[64,2048]{1,0:T(8,128)(2,1)S(1)} %get-tuple-element.243), channel_id=1, source_target_pairs={{0,2},{1,3},{2,0},{3,1},{4,6},{5,7},{6,4},{7,5},{8,10},{9,11},{10,... | collective-permute-start | bytes 786440 | tf_op jit(solution)/shard_map/ppermute | solution.py:404
  384.8 20.4 %collective-permute-start.58 = (bf16[64,2048]{1,0:T(8,128)(2,1)S(1)}, bf16[64,2048]{1,0:T(8,128)(2,1)S(1)}, u32[]{:S(2)}, u32[]{:S(2)}) collective-permute-start(bf16[64,2048]{1,0:T(8,128)(2,1)S(1)} %get-tuple-element.244), channel_id=1, source_target_pairs={{0,3},{1,2},{2,1},{3,0},{4,7},{5,6},{6,5},{7,4},{8,11},{9,10},{10,... | collective-permute-start | bytes 786440 | tf_op jit(solution)/shard_map/ppermute | solution.py:404
  406.7 15.2 %collective-permute-start.60 = (bf16[64,2048]{1,0:T(8,128)(2,1)S(1)}, bf16[64,2048]{1,0:T(8,128)(2,1)S(1)}, u32[]{:S(2)}, u32[]{:S(2)}) collective-permute-start(bf16[64,2048]{1,0:T(8,128)(2,1)S(1)} %get-tuple-element.246.refs_0_), channel_id=1, source_target_pairs={{0,2},{1,3},{2,0},{3,1},{4,6},{5,7},{6,4},{7,5},{8,10},{9,11},{10,... | collective-permute-start | bytes 786440 | tf_op jit(solution)/shard_map/ppermute | solution.py:404
  451.1 12.9 %collective-permute-start.67 = (bf16[64,2048]{1,0:T(8,128)(2,1)}, bf16[64,2048]{1,0:T(8,128)(2,1)}, u32[]{:S(2)}, u32[]{:S(2)}) collective-permute-start(bf16[64,2048]{1,0:T(8,128)(2,1)} %get-tuple-element.253), channel_id=1, source_target_pairs={{0,1},{1,0},{2,3},{3,2},{4,5},{5,4},{6,7},{7,6},{8,9},{9,8},{10,11... | collective-permute-start | bytes 786440 | tf_op jit(solution)/shard_map/ppermute | solution.py:404
  451.4 21.6 %collective-permute-start.68 = (bf16[64,2048]{1,0:T(8,128)(2,1)}, bf16[64,2048]{1,0:T(8,128)(2,1)}, u32[]{:S(2)}, u32[]{:S(2)}) collective-permute-start(bf16[64,2048]{1,0:T(8,128)(2,1)} %get-tuple-element.254), channel_id=1, source_target_pairs={{0,2},{1,3},{2,0},{3,1},{4,6},{5,7},{6,4},{7,5},{8,10},{9,11},{10,... | collective-permute-start | bytes 786440 | tf_op jit(solution)/shard_map/ppermute | solution.py:404
  452.6 20.4 %collective-permute-start.69 = (bf16[64,2048]{1,0:T(8,128)(2,1)}, bf16[64,2048]{1,0:T(8,128)(2,1)}, u32[]{:S(2)}, u32[]{:S(2)}) collective-permute-start(bf16[64,2048]{1,0:T(8,128)(2,1)} %get-tuple-element.255), channel_id=1, source_target_pairs={{0,3},{1,2},{2,1},{3,0},{4,7},{5,6},{6,5},{7,4},{8,11},{9,10},{10,... | collective-permute-start | bytes 786440 | tf_op jit(solution)/shard_map/ppermute | solution.py:404
  473.1 180.1 %reduce-scatter.5.cloned.1.call-start = ((), (), s32[]{:S(2)}) async-start(), calls=%async_computation.8 | async-start | bytes 11141120 | tf_op jit(solution)/shard_map/reduce_scatter | solution.py:580
  478.9 16.3 %collective-permute-start.71 = (bf16[64,2048]{1,0:T(8,128)(2,1)S(1)}, bf16[64,2048]{1,0:T(8,128)(2,1)S(1)}, u32[]{:S(2)}, u32[]{:S(2)}) collective-permute-start(bf16[64,2048]{1,0:T(8,128)(2,1)S(1)} %get-tuple-element.268.refs_0_), channel_id=1, source_target_pairs={{0,2},{1,3},{2,0},{3,1},{4,6},{5,7},{6,4},{7,5},{8,10},{9,11},{10,... | collective-permute-start | bytes 786440 | tf_op jit(solution)/shard_map/ppermute | solution.py:404
  516.8 15.2 %collective-permute-start.78 = (bf16[64,2048]{1,0:T(8,128)(2,1)S(1)}, bf16[64,2048]{1,0:T(8,128)(2,1)S(1)}, u32[]{:S(2)}, u32[]{:S(2)}) collective-permute-start(bf16[64,2048]{1,0:T(8,128)(2,1)S(1)} %get-tuple-element.273), channel_id=1, source_target_pairs={{0,1},{1,0},{2,3},{3,2},{4,5},{5,4},{6,7},{7,6},{8,9},{9,8},{10,11... | collective-permute-start | bytes 786440 | tf_op jit(solution)/shard_map/ppermute | solution.py:404
  518.0 21.8 %collective-permute-start.79 = (bf16[64,2048]{1,0:T(8,128)(2,1)S(1)}, bf16[64,2048]{1,0:T(8,128)(2,1)S(1)}, u32[]{:S(2)}, u32[]{:S(2)}) collective-permute-start(bf16[64,2048]{1,0:T(8,128)(2,1)S(1)} %get-tuple-element.274), channel_id=1, source_target_pairs={{0,2},{1,3},{2,0},{3,1},{4,6},{5,7},{6,4},{7,5},{8,10},{9,11},{10,... | collective-permute-start | bytes 786440 | tf_op jit(solution)/shard_map/ppermute | solution.py:404
  521.4 19.1 %collective-permute-start.80 = (bf16[64,2048]{1,0:T(8,128)(2,1)S(1)}, bf16[64,2048]{1,0:T(8,128)(2,1)S(1)}, u32[]{:S(2)}, u32[]{:S(2)}) collective-permute-start(bf16[64,2048]{1,0:T(8,128)(2,1)S(1)} %get-tuple-element.275), channel_id=1, source_target_pairs={{0,3},{1,2},{2,1},{3,0},{4,7},{5,6},{6,5},{7,4},{8,11},{9,10},{10,... | collective-permute-start | bytes 786440 | tf_op jit(solution)/shard_map/ppermute | solution.py:404
  541.2 169.9 %reduce-scatter.11.cloned.1.call-start = ((), (), s32[]{:S(2)}) async-start(), calls=%async_computation.11 | async-start | bytes 5242880 | tf_op jit(solution)/shard_map/reduce_scatter | solution.py:580
  543.1 32.1 %collective-permute-start.88 = (bf16[256,2176]{1,0:T(8,128)(2,1)S(1)}, bf16[256,2176]{1,0:T(8,128)(2,1)}, u32[]{:S(2)}, u32[]{:S(2)}) collective-permute-start(bf16[256,2176]{1,0:T(8,128)(2,1)S(1)} %shard_map.229), channel_id=1, source_target_pairs={{0,4},{4,0},{1,5},{5,1},{2,6},{6,2},{3,7},{7,3},{8,12},{12,8},{9,1... | collective-permute-start | bytes 3342344 | tf_op jit(solution)/shard_map/ppermute | solution.py:404
  545.5 17.5 %collective-permute-start.82 = (bf16[64,2048]{1,0:T(8,128)(2,1)}, bf16[64,2048]{1,0:T(8,128)(2,1)S(1)}, u32[]{:S(2)}, u32[]{:S(2)}) collective-permute-start(bf16[64,2048]{1,0:T(8,128)(2,1)} %get-tuple-element.302.refs_0_), channel_id=1, source_target_pairs={{0,2},{1,3},{2,0},{3,1},{4,6},{5,7},{6,4},{7,5},{8,10},{9,11},{10,... | collective-permute-start | bytes 786440 | tf_op jit(solution)/shard_map/ppermute | solution.py:404
  552.5 19.1 %collective-permute-start.89 = (bf16[256,1024]{1,0:T(8,128)(2,1)S(1)}, bf16[256,1024]{1,0:T(8,128)(2,1)S(1)}, u32[]{:S(2)}, u32[]{:S(2)}) collective-permute-start(bf16[256,1024]{1,0:T(8,128)(2,1)S(1)} %shard_map.231), channel_id=1, source_target_pairs={{0,4},{4,0},{1,5},{5,1},{2,6},{6,2},{3,7},{7,3},{8,12},{12,8},{9,1... | collective-permute-start | bytes 1572872 | tf_op jit(solution)/shard_map/ppermute | solution.py:404
  552.6 13.7 %collective-permute-start.81 = (bf16[64,2048]{1,0:T(8,128)(2,1)}, bf16[64,2048]{1,0:T(8,128)(2,1)S(1)}, u32[]{:S(2)}, u32[]{:S(2)}) collective-permute-start(bf16[64,2048]{1,0:T(8,128)(2,1)} %get-tuple-element.302.refs_0_), channel_id=1, source_target_pairs={{0,1},{1,0},{2,3},{3,2},{4,5},{5,4},{6,7},{7,6},{8,9},{9,8},{10,11... | collective-permute-start | bytes 786440 | tf_op jit(solution)/shard_map/ppermute | solution.py:404
  563.0 16.4 %collective-permute-start.84 = (bf16[64,2048]{1,0:T(8,128)(2,1)}, bf16[64,2048]{1,0:T(8,128)(2,1)}, u32[]{:S(2)}, u32[]{:S(2)}) collective-permute-start(bf16[64,2048]{1,0:T(8,128)(2,1)} %get-tuple-element.302.refs_0_), channel_id=1, source_target_pairs={{0,4},{4,0},{1,5},{5,1},{2,6},{6,2},{3,7},{7,3},{8,12},{12,8},{9,1... | collective-permute-start | bytes 786440 | tf_op jit(solution)/shard_map/ppermute | solution.py:404
  566.4 13.0 %collective-permute-start.86 = (bf16[64,2048]{1,0:T(8,128)(2,1)S(1)}, bf16[64,2048]{1,0:T(8,128)(2,1)}, u32[]{:S(2)}, u32[]{:S(2)}) collective-permute-start(bf16[64,2048]{1,0:T(8,128)(2,1)S(1)} %collective-permute-done.82.refs_2_), channel_id=1, source_target_pairs={{0,4},{4,0},{1,5},{5,1},{2,6},{6,2},{3,7},{7,3},{8,12},{12,8},{9,1... | collective-permute-start | bytes 786440 | tf_op jit(solution)/shard_map/ppermute | solution.py:404
  600.2 12.5 %collective-permute-start.91 = (bf16[64,2048]{1,0:T(8,128)(2,1)}, bf16[64,2048]{1,0:T(8,128)(2,1)S(1)}, u32[]{:S(2)}, u32[]{:S(2)}) collective-permute-start(bf16[64,2048]{1,0:T(8,128)(2,1)} %get-tuple-element.316), channel_id=1, source_target_pairs={{0,1},{1,0},{2,3},{3,2},{4,5},{5,4},{6,7},{7,6},{8,9},{9,8},{10,11... | collective-permute-start | bytes 786440 | tf_op jit(solution)/shard_map/ppermute | solution.py:404
  600.2 21.5 %collective-permute-start.92 = (bf16[64,2048]{1,0:T(8,128)(2,1)}, bf16[64,2048]{1,0:T(8,128)(2,1)S(1)}, u32[]{:S(2)}, u32[]{:S(2)}) collective-permute-start(bf16[64,2048]{1,0:T(8,128)(2,1)} %get-tuple-element.317), channel_id=1, source_target_pairs={{0,2},{1,3},{2,0},{3,1},{4,6},{5,7},{6,4},{7,5},{8,10},{9,11},{10,... | collective-permute-start | bytes 786440 | tf_op jit(solution)/shard_map/ppermute | solution.py:404
  601.4 21.0 %collective-permute-start.93 = (bf16[64,2048]{1,0:T(8,128)(2,1)}, bf16[64,2048]{1,0:T(8,128)(2,1)}, u32[]{:S(2)}, u32[]{:S(2)}) collective-permute-start(bf16[64,2048]{1,0:T(8,128)(2,1)} %get-tuple-element.318), channel_id=1, source_target_pairs={{0,3},{1,2},{2,1},{3,0},{4,7},{5,6},{6,5},{7,4},{8,11},{9,10},{10,... | collective-permute-start | bytes 786440 | tf_op jit(solution)/shard_map/ppermute | solution.py:404
  626.2 18.2 %collective-permute-start.94 = (bf16[72,2048]{1,0:T(8,128)(2,1)S(1)}, bf16[72,2048]{1,0:T(8,128)(2,1)S(1)}, u32[]{:S(2)}, u32[]{:S(2)}) collective-permute-start(bf16[72,2048]{1,0:T(8,128)(2,1)S(1)} %concatenate.43), channel_id=1, source_target_pairs={{0,2},{1,3},{2,0},{3,1},{4,6},{5,7},{6,4},{7,5},{8,10},{9,11},{10,... | collective-permute-start | bytes 884744 | tf_op jit(solution)/shard_map/ppermute | solution.py:404
  654.9 16.8 %collective-permute-start.98 = (bf16[256,2176]{1,0:T(8,128)(2,1)S(1)}, bf16[256,2176]{1,0:T(8,128)(2,1)S(1)}, u32[]{:S(2)}, u32[]{:S(2)}) collective-permute-start(bf16[256,2176]{1,0:T(8,128)(2,1)S(1)} %shard_map.237), channel_id=1, source_target_pairs={{0,4},{4,0},{1,5},{5,1},{2,6},{6,2},{3,7},{7,3},{8,12},{12,8},{9,1... | collective-permute-start | bytes 3342344 | tf_op jit(solution)/shard_map/ppermute | solution.py:404
  656.0 30.7 %collective-permute-start.102 = (bf16[137,2048]{1,0:T(8,128)(2,1)S(1)}, bf16[137,2048]{1,0:T(8,128)(2,1)S(1)}, u32[]{:S(2)}, u32[]{:S(2)}) collective-permute-start(bf16[137,2048]{1,0:T(8,128)(2,1)S(1)} %pad_maximum_fusion.3), channel_id=1, source_target_pairs={{0,8},{8,0},{1,9},{9,1},{2,10},{10,2},{3,11},{11,3},{4,12},{12,4},... | collective-permute-start | bytes 1683464 | tf_op jit(solution)/shard_map/ppermute | solution.py:404
  656.9 14.8 %collective-permute-start.96 = (bf16[64,2048]{1,0:T(8,128)(2,1)S(1)}, bf16[64,2048]{1,0:T(8,128)(2,1)S(1)}, u32[]{:S(2)}, u32[]{:S(2)}) collective-permute-start(bf16[64,2048]{1,0:T(8,128)(2,1)S(1)} %add_convert_fusion), channel_id=1, source_target_pairs={{0,2},{1,3},{2,0},{3,1},{4,6},{5,7},{6,4},{7,5},{8,10},{9,11},{10,... | collective-permute-start | bytes 786440 | tf_op jit(solution)/shard_map/ppermute | solution.py:404
  658.0 28.7 %collective-permute-start.95 = (bf16[64,2048]{1,0:T(8,128)(2,1)S(1)}, bf16[64,2048]{1,0:T(8,128)(2,1)S(1)}, u32[]{:S(2)}, u32[]{:S(2)}) collective-permute-start(bf16[64,2048]{1,0:T(8,128)(2,1)S(1)} %add_convert_fusion), channel_id=1, source_target_pairs={{0,1},{1,0},{2,3},{3,2},{4,5},{5,4},{6,7},{7,6},{8,9},{9,8},{10,11... | collective-permute-start | bytes 786440 | tf_op jit(solution)/shard_map/ppermute | solution.py:404
  671.7 15.0 %collective-permute-start.97 = (bf16[64,2048]{1,0:T(8,128)(2,1)S(1)}, bf16[64,2048]{1,0:T(8,128)(2,1)}, u32[]{:S(2)}, u32[]{:S(2)}) collective-permute-start(bf16[64,2048]{1,0:T(8,128)(2,1)S(1)} %collective-permute-done.96), channel_id=1, source_target_pairs={{0,1},{1,0},{2,3},{3,2},{4,5},{5,4},{6,7},{7,6},{8,9},{9,8},{10,11... | collective-permute-start | bytes 786440 | tf_op jit(solution)/shard_map/ppermute | solution.py:404
  689.9 20.1 %collective-permute-start.99 = (bf16[128,2048]{1,0:T(8,128)(2,1)S(1)}, bf16[128,2048]{1,0:T(8,128)(2,1)S(1)}, u32[]{:S(2)}, u32[]{:S(2)}) collective-permute-start(bf16[128,2048]{1,0:T(8,128)(2,1)S(1)} %get-tuple-element.398), channel_id=1, source_target_pairs={{0,8},{8,0},{1,9},{9,1},{2,10},{10,2},{3,11},{11,3},{4,12},{12,4},... | collective-permute-start | bytes 1572872 | tf_op jit(solution)/shard_map/ppermute | solution.py:404
  (163 other events, 872.2 us)
Sparse Core Ops, SparseCore 0:
  10.5 57.0 all-gather.4
  70.1 99.6 all-gather.6
  172.2 54.3 all-gather.8
  228.9 94.2 all-gather.10
  375.0 93.5 reduce-scatter.6
  473.2 54.7 reduce-scatter.8
  540.7 92.9 reduce-scatter.4
  636.9 69.6 reduce-scatter.10

commit v6 on v5

--- a/solution.py
+++ b/solution.py
@@ -107,15 +107,15 @@
 
 def put_halves(tile, cols, own_ref, send_ref):
     half = own_ref.shape[0]
-    own_ref[:, cols] = tile[:half]
+    own_ref[:, cols] = tile[:half].astype(LOW)
     send_ref[:, cols] = tile[half:].astype(LOW)
 
 
 def softmax_of(q_h, k, allowed, scale):
-    s = jnp.where(allowed, nt(q_h, k) * scale, MASK_FILL)
+    s = jnp.where(allowed, nt(q_h * scale, k), MASK_FILL)
     top = jnp.max(s, axis=-1, keepdims=True)
     e = jnp.exp(s - top)
-    return e / jnp.sum(e, axis=-1, keepdims=True)
+    return e * (1.0 / jnp.sum(e, axis=-1, keepdims=True))
 
 
 def load(pairs, sems, first):
@@ -159,7 +159,7 @@
     o = None
     for h in range(heads):
         mine = lane == h
-        w = softmax_of(jnp.where(mine, q, zero), k, allowed, 1.0 / math.sqrt(HEAD))
+        w = softmax_of(jnp.where(mine, q, zero), k, allowed, LOW(1.0 / math.sqrt(HEAD)))
         part = nn(w.astype(LOW), jnp.where(mine, v, zero))
         o = part if o is None else o + part
     o_o[...] = o.astype(LOW)
@@ -200,7 +200,7 @@
         mine = lane == h
         q_h = jnp.where(mine, q, zero)
         do_h = jnp.where(mine, do, zero)
-        w = softmax_of(q_h, k, allowed, scale)
+        w = softmax_of(q_h, k, allowed, LOW(scale))
         dw = nt(do_h, v)
         ds = (w * (dw - jnp.sum(w * dw, axis=-1, keepdims=True))).astype(LOW)
         dv_h = tn(w.astype(LOW), do_h)
@@ -221,7 +221,7 @@
 
 def mlp_forward(n_h, *refs):
     h_parts, weights, refs = refs[:n_h], refs[n_h], refs[n_h + 1 :]
-    full_o, gu_o, z_o, own_o, send_o, h_s, w_s, sems = refs
+    full_o, gu_o, z_o, own_o, send_o, h_s, w_s, acc, sems = refs
     units = z_o.shape[1]
     copies = into_rows(h_parts, h_s, sems, 0)
     w_copies = weights_into(weights, w_s, sems, n_h)
@@ -231,9 +231,10 @@
     whole.start()
     for r, rows in block_rows(w_s, w_copies):
         part = nn(h_s[:, rows], w_s[rows, : 2 * units])
-        gu_o[...] = part if r == 0 else gu_o[...] + part
-    g = gu_o[:, :units]
-    u = gu_o[:, units:]
+        acc[...] = part if r == 0 else acc[...] + part
+    gu_o[...] = acc[...].astype(LOW)
+    g = acc[:, :units]
+    u = acc[:, units:]
     z_o[...] = (g * u / (1.0 + jnp.exp(-g))).astype(LOW)
     z = z_o[...]
     for r, rows in block_rows(w_s):
@@ -256,8 +257,8 @@
         part = nn(d_s[:, rows], w_s[rows, 2 * units : 3 * units])
         acc[...] = part if r == 0 else acc[...] + part
     wait_all(extra)
-    g = gu[:, :units]
-    u = gu[:, units:]
+    g = gu[:, :units].astype(F32)
+    u = gu[:, units:].astype(F32)
     sig = 1.0 / (1.0 + jnp.exp(-g))
     dz = acc[...]
     dp_o[:, :units] = (dz * u * sig * (1.0 + g * (1.0 - sig))).astype(LOW)
@@ -343,10 +344,10 @@
 
 def middle(own_i, moved_i, own_o, *sends):
     rows = own_o.shape[0]
-    own_o[...] = own_i[:rows] + moved_i[:rows].astype(F32)
+    own_o[...] = own_i[:rows].astype(F32) + moved_i[:rows].astype(F32)
     for r, send in enumerate(sends):
         at = slice((r + 1) * rows, (r + 2) * rows)
-        send[...] = (own_i[at] + moved_i[at].astype(F32)).astype(LOW)
+        send[...] = (own_i[at].astype(F32) + moved_i[at].astype(F32)).astype(LOW)
 
 
 def norm_of(value):
@@ -416,9 +417,9 @@
     def token_reduce(own_half, send_half, beside=None, before=None):
         rows, width = own_half.shape
         sub = rows // n_mp
+        if before is not None:
+            send_half, before = lax.optimization_barrier((send_half, before))
         moved = swap(send_half, "clo", 1)
-        if before is not None:
-            (own_half, moved), before = lax.optimization_barrier(((own_half, moved), before))
         outs = [shape((sub, width), F32)] + [shape((sub, width), LOW)] * (n_mp - 1)
         parts = call(middle, 0, [own_half, moved], outs, [], rows * width)
         terms = [parts[0]] + [swap(parts[r], "mp", r) for r in range(1, n_mp)]
@@ -552,7 +553,7 @@
         ]
 
         act = shape((total, half_in), LOW)
-        reduced = [shape((half_total, width), F32), shape((half_total, width), LOW)]
+        reduced = [shape((half_total, width), LOW)] * 2
         sems = pltpu.SemaphoreType.DMA((n_parts + width // BLOCK + 5,))
         h_scratch = pltpu.VMEM((total, width), LOW)
 
@@ -645,8 +646,13 @@
                 functools.partial(mlp_forward, n_parts),
                 n_parts + 1,
                 h2 + [w_mlp],
-                [whole, shape((total, 2 * half_ff), F32), shape((total, half_ff), LOW)] + reduced,
-                [h_scratch, pltpu.VMEM((width, mlp_cols), LOW), sems],
+                [whole, shape((total, 2 * half_ff), LOW), shape((total, half_ff), LOW)] + reduced,
+                [
+                    h_scratch,
+                    pltpu.VMEM((width, mlp_cols), LOW),
+                    pltpu.VMEM((total, 2 * half_ff), F32),
+                    sems,
+                ],
                 mm(total, width, mlp_cols),
                 n_any=n_parts,
                 hbm_outs=1,
@@ -672,7 +678,7 @@
                     h_scratch,
                     pltpu.VMEM((width, mlp_cols), LOW),
                     pltpu.VMEM((total, half_ff), F32),
-                    pltpu.VMEM(gu.shape, F32),
+                    pltpu.VMEM(gu.shape, LOW),
                     sems,
                 ],
                 mm(total, width, mlp_cols),
@@ -731,11 +737,12 @@
         mine, moved = chi_swap(by_place([part[:sub] for part in parts]), block, both)
         g_mlp, x_last = after((g_mlp, x_last), parts[n_mp // 2])
         g_gu, g_down = put_mlp(0, pick(g_mlp), mlp_sum)
-        g_gu = jnp.swapaxes(g_gu, 1, 2)
+        x_parts = after(mp_gather(x_last), g_gu)
+        held = by_place(x_parts)
+        x_mine, x_moved = chi_swap(held, block)
+        g_gu = jnp.swapaxes(after(g_gu, held), 1, 2)
         g_gu = with_layout_constraint(g_gu, Layout(major_to_minor=(0, 1, 2, 3)))
-        x_parts = after(mp_gather(x_last), g_gu)
-        x_mine, x_moved = chi_swap(by_place(x_parts), block)
-        moved = after(moved, x_parts)
+        moved = after(moved, g_gu)
         tokens_grad = to_blocks(mine, moved, block).astype(F32)
         both = both.astype(F32) + moved[block:].astype(F32)
         activations = to_blocks(x_mine, x_moved, block)

time: 730 us -> 714 us (0.978)
  local copies, waits for them, and re-layouts: 95.5 us -> 75.1 us
  waiting for transfers between devices: 337 us -> 349 us
    unnamed x232 -> x192, local copies, waits for them, and re-layouts: 63.2 us -> 45.7 us
    all_gather x4, waiting for transfers between devices: 31.4 us -> 45 us  [gather_weights(): return lax.all_gather(own, ('dp', 'chi', 'clo'), axis=0, tiled=True)]
    pallas_call x1 -> x0, local copies, waits for them, and re-layouts: 9.8 us -> none  [call(): pl.pallas_call(body, out_shape=tuple(outs), in_specs=[ANY] * n_any + [HBM...]
  transfers between devices with their start and end apart: 114 -> 114, of which waited for: 53 -> 55; matrix products, arithmetic and copies ran while one was open for 6% -> 6% of each run, Pallas kernels for 18% -> 19%
where the time goes in v6:
time: 714 us; the launch traced here: 710 us
  waiting for transfers between devices  349 us (49%)
  Pallas kernels  145 us (20%)
  starting transfers between devices  114 us (16%)
  local copies, waits for them, and re-layouts  75.1 us (11%)
  between operations  16.1 us (2%)
  other arithmetic  10.7 us (1%)
    ppermute x106, waiting for transfers between devices, swap(): return lax.ppermute(value, axis, [(i, i ^ bit) for i in range(sizes[axis])])  304 us
    pallas_call x38, Pallas kernels, call(): pl.pallas_call(body, out_shape=tuple(outs), in_specs=[ANY] * n_any + [HBM...  145 us
    ppermute x106, starting transfers between devices, swap(): return lax.ppermute(value, axis, [(i, i ^ bit) for i in range(sizes[axis])])  113 us
    unnamed x192, local copies, waits for them, and re-layouts  45.7 us
    all_gather x4, waiting for transfers between devices, gather_weights(): return lax.all_gather(own, ('dp', 'chi', 'clo'), axis=0, tiled=True)  45 us
  transfers between devices with their start and end apart: 114, of which 55 were waited for; matrix products, arithmetic and copies ran while one was open for 6% of the time, Pallas kernels for 19%

profile of v6, /device:TPU:0, one launch (start us, length us, event | category | flops | bytes accessed | tf_op | source)
XLA Modules:
  0.0 709.8 jit_solution(18190061758721415870)
XLA Ops:
  10.0 3.7 fusion.17
  17.1 5.0 concatenate.41
  24.6 4.2 concatenate.42
  30.1 3.0 collective-permute-start.1
  34.1 6.5 collective-permute-done.9
  46.8 10.6 %collective-permute-done.3.refs_2_ = bf16[64,2048]{1,0:T(8,128)(2,1)S(1)} collective-permute-done((bf16[64,2048]{1,0:T(8,128)(2,1)S(1)}, bf16[64,2048]{1,0:T(8,128)(2,1)S(1)}, u32[]{:S(2)}, u32[]{:S(2)}) %collective-permute-start.3) | collective-permute-done | bytes 262176 | tf_op jit(solution)/shard_map/ppermute | solution.py:405
  58.6 6.3 collective-permute-done.4.refs_3_
  68.8 11.0 %shard_map.205 = (bf16[512,2048]{1,0:T(8,128)(2,1)}, bf16[512,256]{1,0:T(8,128)(2,1)}, bf16[512,256]{1,0:T(8,128)(2,1)}, bf16[512,256]{1,0:T(8,128)(2,1)}, bf16[...) custom-call(bf16[64,2048]{1,0:T(8,128)(2,1)} %copy-done.55, ...), custom_call_target="tpu_custom_call" | custom-call | flops 4294967296 | bytes 16526336 | tf_op jit(solution)/shard_map/pallas_call | solution.py:50
  85.5 3.4 collective-permute-start.13
  88.9 5.9 collective-permute-done
  96.0 3.6 collective-permute-start.23
  99.6 7.7 %collective-permute-done.13.refs_2_ = bf16[64,2048]{1,0:T(8,128)(2,1)S(1)} collective-permute-done((bf16[64,2048]{1,0:T(8,128)(2,1)S(1)}, bf16[64,2048]{1,0:T(8,128)(2,1)S(1)}, u32[]{:S(2)}, u32[]{:S(2)}) %collective-permute-start.13) | collective-permute-done | bytes 262176 | tf_op jit(solution)/shard_map/ppermute | solution.py:405
  107.6 13.1 %collective-permute-start.16 = (bf16[64,2048]{1,0:T(8,128)(2,1)S(1)}, bf16[64,2048]{1,0:T(8,128)(2,1)S(1)}, u32[]{:S(2)}, u32[]{:S(2)}) collective-permute-start(bf16[64,2048]{1,0:T(8,128)(2,1)S(1)} %get-tuple-element.193.refs_0_), channel_id=1, source_target_pairs={{0,2},{1,3},{2,0},{3,1},{4,6},{5,7},{6,4},{7,5},{8,10},{9,11},{10,... | collective-permute-start | bytes 786440 | tf_op jit(solution)/shard_map/ppermute | solution.py:405
  120.7 9.1 %collective-permute-done.23.refs_2_ = bf16[64,2048]{1,0:T(8,128)(2,1)S(1)} collective-permute-done((bf16[64,2048]{1,0:T(8,128)(2,1)S(1)}, bf16[64,2048]{1,0:T(8,128)(2,1)S(1)}, u32[]{:S(2)}, u32[]{:S(2)}) %collective-permute-start.23) | collective-permute-done | bytes 262176 | tf_op jit(solution)/shard_map/ppermute | solution.py:405
  134.9 5.6 collective-permute-done.24.refs_3_
  146.2 5.5 collective-permute-done.17.refs_3_
  153.9 15.8 %all-gather.7.cloned.1.call-done.refs_8_ = bf16[2048,4352]{1,0:T(8,128)(2,1)} async-done(((bf16[256,4352]{1,0:T(8,128)(2,1)}), bf16[2048,4352]{1,0:T(8,128)(2,1)}) %all-gather.7.cloned.1.call-update) | async-done | bytes 17825808 | tf_op jit(solution)/shard_map/all_gather | solution.py:501
  171.7 7.3 %shard_map.208 = (bf16[512,2048]{1,0:T(8,128)(2,1)S(1)}, bf16[512,1408]{1,0:T(8,128)(2,1)S(1)}, bf16[512,704]{1,0:T(8,128)(2,1)S(1)}, bf16[256,2048]{1,0:T(8,128)(2,1)S(1)}, bf16[256,2048]{1,0:T(8,128)(2,1)S(1)}) custom-call(bf16[64,2048]{1,0:T(8,128)(2,1)S(1)} %get-tuple-element.193.refs_0_, bf16[64,2048]{1,0:T(8,128)(2,1)S(1)} %collective-permute-done.15.refs_1_, ...), custom_call_target="tpu_custom_call" | custom-call | flops 4563402752 | bytes 26279936 | tf_op jit(solution)/shard_map/pallas_call | solution.py:50
  187.7 9.1 %collective-permute-done.30.refs_1_ = bf16[64,2048]{1,0:T(8,128)(2,1)S(1)} collective-permute-done((bf16[64,2048]{1,0:T(8,128)(2,1)S(1)}, bf16[64,2048]{1,0:T(8,128)(2,1)S(1)}, u32[]{:S(2)}, u32[]{:S(2)}) %collective-permute-start.30) | collective-permute-done | bytes 262176 | tf_op jit(solution)/shard_map/ppermute | solution.py:405
  196.8 9.3 %collective-permute-done.31.refs_2_ = bf16[64,2048]{1,0:T(8,128)(2,1)S(1)} collective-permute-done((bf16[64,2048]{1,0:T(8,128)(2,1)S(1)}, bf16[64,2048]{1,0:T(8,128)(2,1)S(1)}, u32[]{:S(2)}, u32[]{:S(2)}) %collective-permute-start.31) | collective-permute-done | bytes 262176 | tf_op jit(solution)/shard_map/ppermute | solution.py:405
  206.4 6.2 collective-permute-start.34
  212.7 11.5 %collective-permute-done.34.refs_2_ = bf16[64,2048]{1,0:T(8,128)(2,1)S(1)} collective-permute-done((bf16[64,2048]{1,0:T(8,128)(2,1)S(1)}, bf16[64,2048]{1,0:T(8,128)(2,1)S(1)}, u32[]{:S(2)}, u32[]{:S(2)}) %collective-permute-start.34) | collective-permute-done | bytes 262176 | tf_op jit(solution)/shard_map/ppermute | solution.py:405
  224.7 6.4 collective-permute-done.35.refs_3_
  232.8 11.4 %shard_map.212 = (bf16[512,2048]{1,0:T(8,128)(2,1)}, bf16[512,256]{1,0:T(8,128)(2,1)}, bf16[512,256]{1,0:T(8,128)(2,1)}, bf16[512,256]{1,0:T(8,128)(2,1)}, bf16[...) custom-call(bf16[64,2048]{1,0:T(8,128)(2,1)} %copy-done.56, ...), custom_call_target="tpu_custom_call" | custom-call | flops 4294967296 | bytes 16526336 | tf_op jit(solution)/shard_map/pallas_call | solution.py:50
  249.9 3.1 collective-permute-start.43
  253.0 7.9 %collective-permute-done.41.refs_1_ = bf16[64,2048]{1,0:T(8,128)(2,1)S(1)} collective-permute-done((bf16[64,2048]{1,0:T(8,128)(2,1)S(1)}, bf16[64,2048]{1,0:T(8,128)(2,1)S(1)}, u32[]{:S(2)}, u32[]{:S(2)}) %collective-permute-start.41) | collective-permute-done | bytes 262176 | tf_op jit(solution)/shard_map/ppermute | solution.py:405
  260.9 9.1 %collective-permute-done.42.refs_2_ = bf16[64,2048]{1,0:T(8,128)(2,1)S(1)} collective-permute-done((bf16[64,2048]{1,0:T(8,128)(2,1)S(1)}, bf16[64,2048]{1,0:T(8,128)(2,1)S(1)}, u32[]{:S(2)}, u32[]{:S(2)}) %collective-permute-start.42) | collective-permute-done | bytes 262176 | tf_op jit(solution)/shard_map/ppermute | solution.py:405
  270.4 5.4 collective-permute-start.45
  275.9 11.2 %collective-permute-done.45.refs_2_ = bf16[64,2048]{1,0:T(8,128)(2,1)S(1)} collective-permute-done((bf16[64,2048]{1,0:T(8,128)(2,1)S(1)}, bf16[64,2048]{1,0:T(8,128)(2,1)S(1)}, u32[]{:S(2)}, u32[]{:S(2)}) %collective-permute-start.45) | collective-permute-done | bytes 262176 | tf_op jit(solution)/shard_map/ppermute | solution.py:405
  287.7 6.5 collective-permute-done.46.refs_3_
  294.2 29.1 %all-gather.11.cloned.1.call-done.refs_8_ = bf16[2048,4352]{1,0:T(8,128)(2,1)} async-done(((bf16[256,4352]{1,0:T(8,128)(2,1)}), bf16[2048,4352]{1,0:T(8,128)(2,1)}) %all-gather.11.cloned.1.call-update) | async-done | bytes 17825808 | tf_op jit(solution)/shard_map/all_gather | solution.py:501
  323.3 7.9 %shard_map.215 = (bf16[512,2048]{1,0:T(8,128)(2,1)S(1)}, bf16[512,1408]{1,0:T(8,128)(2,1)S(1)}, bf16[512,704]{1,0:T(8,128)(2,1)S(1)}, bf16[256,2048]{1,0:T(8,128)(2,1)S(1)}, bf16[256,2048]{1,0:T(8,128)(2,1)S(1)}) custom-call(bf16[64,2048]{1,0:T(8,128)(2,1)S(1)} %get-tuple-element.224.refs_0_, bf16[64,2048]{1,0:T(8,128)(2,1)} %collective-permute-done.44.refs_1_, ...), custom_call_target="tpu_custom_call" | custom-call | flops 4563402752 | bytes 26279936 | tf_op jit(solution)/shard_map/pallas_call | solution.py:50
  340.7 8.9 %shard_map.217 = (bf16[512,2048]{1,0:T(8,128)(2,1)S(1)}, bf16[512,1408]{1,0:T(8,128)(2,1)S(1)}, bf16[256,2048]{1,0:T(8,128)(2,1)S(1)}, bf16[256,2048]{1,0:T(8,128)(2,1)S(1)}) custom-call(bf16[64,2048]{1,0:T(8,128)(2,1)S(1)} %get-tuple-element.216.refs_0_, bf16[64,2048]{1,0:T(8,128)(2,1)S(1)} %copy-done.33, bf16[64,2048]{1,0:T(8,128)(2,1)S(1)} %copy-done.35, ...), custom_call_target="tpu_custom_call" | custom-call | flops 4563402752 | bytes 27000832 | tf_op jit(solution)/shard_map/pallas_call | solution.py:50
  354.0 10.5 %shard_map.218 = bf16[2048,2176]{1,0:T(8,128)(2,1)} custom-call(bf16[512,2048]{1,0:T(8,128)(2,1)} %copy-done.47, bf16[512,2048]{1,0:T(8,128)(2,1)} %copy-done.49, bf16[512,1408]{1,0:T(8,128)(2,1)} %copy-done.51, bf16[512,704]{1,0:T(8,128)(2,1)} %copy-done.54), custom_call_target="tpu_custom_call" | custom-call | flops 4563402752 | bytes 15269888 | tf_op jit(solution)/shard_map/pallas_call | solution.py:50
  370.1 3.3 collective-permute-start.57
  373.9 9.1 %collective-permute-done.56.refs_1_ = bf16[64,2048]{1,0:T(8,128)(2,1)S(1)} collective-permute-done((bf16[64,2048]{1,0:T(8,128)(2,1)S(1)}, bf16[64,2048]{1,0:T(8,128)(2,1)S(1)}, u32[]{:S(2)}, u32[]{:S(2)}) %collective-permute-start.56) | collective-permute-done | bytes 262176 | tf_op jit(solution)/shard_map/ppermute | solution.py:405
  382.9 8.9 %collective-permute-done.57.refs_2_ = bf16[64,2048]{1,0:T(8,128)(2,1)S(1)} collective-permute-done((bf16[64,2048]{1,0:T(8,128)(2,1)S(1)}, bf16[64,2048]{1,0:T(8,128)(2,1)S(1)}, u32[]{:S(2)}, u32[]{:S(2)}) %collective-permute-start.57) | collective-permute-done | bytes 262176 | tf_op jit(solution)/shard_map/ppermute | solution.py:405
  393.3 6.3 collective-permute-start.60
  399.6 11.6 %collective-permute-done.60.refs_2_ = bf16[64,2048]{1,0:T(8,128)(2,1)S(1)} collective-permute-done((bf16[64,2048]{1,0:T(8,128)(2,1)S(1)}, bf16[64,2048]{1,0:T(8,128)(2,1)S(1)}, u32[]{:S(2)}, u32[]{:S(2)}) %collective-permute-start.60) | collective-permute-done | bytes 262176 | tf_op jit(solution)/shard_map/ppermute | solution.py:405
  411.8 6.4 collective-permute-done.61.refs_3_
  420.5 13.0 %shard_map.221 = (bf16[512,2048]{1,0:T(8,128)(2,1)}, bf16[512,768]{1,0:T(8,128)(2,1)}, f32[1,768]{1,0:T(1,128)}, bf16[256,2048]{1,0:T(8,128)(2,1)}, bf16[256,2048]{1,0:T(8,128)(2,1)}) custom-call(bf16[64,2048]{1,0:T(8,128)(2,1)} %copy-done.57, bf16[64,2048]{1,0:T(8,128)(2,1)} %copy-done.85, bf16[64,2048]{1,0:T(8,128)(2,1)} %copy-done.84, ...), custom_call_target="tpu_custom_call" | custom-call | flops 4831838208 | bytes 17050624 | tf_op jit(solution)/shard_map/pallas_call | solution.py:50
  443.1 6.9 shard_map.223
  451.7 8.8 %collective-permute-done.68.refs_2_ = bf16[64,2048]{1,0:T(8,128)(2,1)} collective-permute-done((bf16[64,2048]{1,0:T(8,128)(2,1)}, bf16[64,2048]{1,0:T(8,128)(2,1)}, u32[]{:S(2)}, u32[]{:S(2)}) %collective-permute-start.68) | collective-permute-done | bytes 262176 | tf_op jit(solution)/shard_map/ppermute | solution.py:405
  464.4 5.4 collective-permute-start.71
  469.7 11.2 %collective-permute-done.71.refs_2_ = bf16[64,2048]{1,0:T(8,128)(2,1)S(1)} collective-permute-done((bf16[64,2048]{1,0:T(8,128)(2,1)S(1)}, bf16[64,2048]{1,0:T(8,128)(2,1)S(1)}, u32[]{:S(2)}, u32[]{:S(2)}) %collective-permute-start.71) | collective-permute-done | bytes 262176 | tf_op jit(solution)/shard_map/ppermute | solution.py:405
  481.4 6.1 collective-permute-done.72.refs_3_
  489.1 8.9 %shard_map.225 = (bf16[512,2048]{1,0:T(8,128)(2,1)S(1)}, bf16[512,1408]{1,0:T(8,128)(2,1)S(1)}, bf16[256,2048]{1,0:T(8,128)(2,1)S(1)}, bf16[256,2048]{1,0:T(8,128)(2,1)S(1)}) custom-call(bf16[64,2048]{1,0:T(8,128)(2,1)S(1)} %get-tuple-element.267.refs_0_, bf16[64,2048]{1,0:T(8,128)(2,1)S(1)} %collective-permute-done.70.refs_1_, ...), custom_call_target="tpu_custom_call" | custom-call | flops 4563402752 | bytes 27000832 | tf_op jit(solution)/shard_map/pallas_call | solution.py:50
  508.2 10.4 %shard_map.227 = bf16[2048,2176]{1,0:T(8,128)(2,1)} custom-call(bf16[512,2048]{1,0:T(8,128)(2,1)} %copy-done.46, bf16[512,2048]{1,0:T(8,128)(2,1)} %copy-done.48, bf16[512,1408]{1,0:T(8,128)(2,1)} %copy-done.50, bf16[512,704]{1,0:T(8,128)(2,1)} %copy-done.53), custom_call_target="tpu_custom_call" | custom-call | flops 4563402752 | bytes 15269888 | tf_op jit(solution)/shard_map/pallas_call | solution.py:50
  518.6 7.5 %collective-permute-done.79.refs_2_ = bf16[64,2048]{1,0:T(8,128)(2,1)S(1)} collective-permute-done((bf16[64,2048]{1,0:T(8,128)(2,1)}, bf16[64,2048]{1,0:T(8,128)(2,1)S(1)}, u32[]{:S(2)}, u32[]{:S(2)}) %collective-permute-start.79) | collective-permute-done | bytes 262176 | tf_op jit(solution)/shard_map/ppermute | solution.py:405
  532.2 5.6 collective-permute-start.82
  539.4 10.8 %collective-permute-done.82.refs_2_ = bf16[64,2048]{1,0:T(8,128)(2,1)S(1)} collective-permute-done((bf16[64,2048]{1,0:T(8,128)(2,1)}, bf16[64,2048]{1,0:T(8,128)(2,1)S(1)}, u32[]{:S(2)}, u32[]{:S(2)}) %collective-permute-start.82) | collective-permute-done | bytes 262176 | tf_op jit(solution)/shard_map/ppermute | solution.py:405
  552.9 5.3 collective-permute-done.83.refs_3_
  561.8 4.2 shard_map.230
  566.8 13.1 %shard_map.233 = (bf16[512,2048]{1,0:T(8,128)(2,1)}, bf16[512,768]{1,0:T(8,128)(2,1)}, f32[1,768]{1,0:T(1,128)}, bf16[256,2048]{1,0:T(8,128)(2,1)}, bf16[256,2048]{1,0:T(8,128)(2,1)}) custom-call(bf16[64,2048]{1,0:T(8,128)(2,1)} %get-tuple-element.301.refs_0_, bf16[64,2048]{1,0:T(8,128)(2,1)} %copy-done.80, bf16[64,2048]{1,0:T(8,128)(2,1)} %copy-done.77, ...), custom_call_target="tpu_custom_call" | custom-call | flops 4831838208 | bytes 17050624 | tf_op jit(solution)/shard_map/pallas_call | solution.py:50
  590.6 6.9 shard_map.235
  599.7 8.4 %collective-permute-done.92.refs_2_ = bf16[64,2048]{1,0:T(8,128)(2,1)S(1)} collective-permute-done((bf16[64,2048]{1,0:T(8,128)(2,1)}, bf16[64,2048]{1,0:T(8,128)(2,1)S(1)}, u32[]{:S(2)}, u32[]{:S(2)}) %collective-permute-start.92) | collective-permute-done | bytes 262176 | tf_op jit(solution)/shard_map/ppermute | solution.py:405
  611.6 5.5 collective-permute-start.94
  619.2 10.8 %collective-permute-done.94 = bf16[72,2048]{1,0:T(8,128)(2,1)S(1)} collective-permute-done((bf16[72,2048]{1,0:T(8,128)(2,1)S(1)}, bf16[72,2048]{1,0:T(8,128)(2,1)S(1)}, u32[]{:S(2)}, u32[]{:S(2)}) %collective-permute-start.94) | collective-permute-done | bytes 294944 | tf_op jit(solution)/shard_map/ppermute | solution.py:405
  631.9 6.0 collective-permute-done.101
  643.6 12.2 %collective-permute-done.96 = bf16[64,2048]{1,0:T(8,128)(2,1)S(1)} collective-permute-done((bf16[64,2048]{1,0:T(8,128)(2,1)}, bf16[64,2048]{1,0:T(8,128)(2,1)S(1)}, u32[]{:S(2)}, u32[]{:S(2)}) %collective-permute-start.96) | collective-permute-done | bytes 262176 | tf_op jit(solution)/shard_map/ppermute | solution.py:405
  659.3 4.2 shard_map.238
  666.7 7.0 copy.85
  673.7 8.1 %collective-permute-done.102 = bf16[137,2048]{1,0:T(8,128)(2,1)S(1)} collective-permute-done((bf16[137,2048]{1,0:T(8,128)(2,1)}, bf16[137,2048]{1,0:T(8,128)(2,1)S(1)}, u32[]{:S(2)}, u32[]{:S(2)}) %collective-permute-start.102) | collective-permute-done | bytes 561184 | tf_op jit(solution)/shard_map/ppermute | solution.py:405
  691.1 3.6 collective-permute-done.99
  (489 shorter events, 177.5 us)
Async XLA Ops:
  7.2 60.8 %all-gather.5.cloned.1.call-start = ((), (), s32[]{:S(2)}) async-start(), calls=%async_computation.4 | async-start | bytes 9437184 | tf_op jit(solution)/shard_map/all_gather | solution.py:501
  9.9 159.8 %all-gather.7.cloned.1.call-start = ((), (), s32[]{:S(2)}) async-start(), calls=%async_computation.5 | async-start | bytes 20054016 | tf_op jit(solution)/shard_map/all_gather | solution.py:501
  22.1 208.9 %all-gather.9.cloned.1.call-start = ((), (), s32[]{:S(2)}) async-start(), calls=%async_computation.6 | async-start | bytes 9437184 | tf_op jit(solution)/shard_map/all_gather | solution.py:501
  23.2 300.0 %all-gather.11.cloned.1.call-start = ((), (), s32[]{:S(2)}) async-start(), calls=%async_computation.7 | async-start | bytes 20054016 | tf_op jit(solution)/shard_map/all_gather | solution.py:501
  28.9 498.7 %reduce-scatter.7.cloned.1.call-start = ((), (), s32[]{:S(2)}) async-start(), calls=%async_computation.9 | async-start | bytes 11141120 | tf_op jit(solution)/shard_map/reduce_scatter | solution.py:581
  42.3 15.1 %collective-permute-start.3 = (bf16[64,2048]{1,0:T(8,128)(2,1)S(1)}, bf16[64,2048]{1,0:T(8,128)(2,1)S(1)}, u32[]{:S(2)}, u32[]{:S(2)}) collective-permute-start(bf16[64,2048]{1,0:T(8,128)(2,1)S(1)} %get-tuple-element.184.refs_0_), channel_id=1, source_target_pairs={{0,2},{1,3},{2,0},{3,1},{4,6},{5,7},{6,4},{7,5},{8,10},{9,11},{10,... | collective-permute-start | bytes 786440 | tf_op jit(solution)/shard_map/ppermute | solution.py:405
  45.3 13.2 %collective-permute-start.2 = (bf16[64,2048]{1,0:T(8,128)(2,1)S(1)}, bf16[64,2048]{1,0:T(8,128)(2,1)S(1)}, u32[]{:S(2)}, u32[]{:S(2)}) collective-permute-start(bf16[64,2048]{1,0:T(8,128)(2,1)S(1)} %get-tuple-element.184.refs_0_), channel_id=1, source_target_pairs={{0,1},{1,0},{2,3},{3,2},{4,5},{5,4},{6,7},{7,6},{8,9},{9,8},{10,11... | collective-permute-start | bytes 786440 | tf_op jit(solution)/shard_map/ppermute | solution.py:405
  80.4 14.4 %collective-permute-start = (bf16[64,2048]{1,0:T(8,128)(2,1)S(1)}, bf16[64,2048]{1,0:T(8,128)(2,1)S(1)}, u32[]{:S(2)}, u32[]{:S(2)}) collective-permute-start(bf16[64,2048]{1,0:T(8,128)(2,1)S(1)} %dynamic-slice_bitcast_fusion.3), channel_id=1, source_target_pairs={{0,8},{8,0},{1,9},{9,1},{2,10},{10,2},{3,11},{11,3},{4,12},{12,4},... | collective-permute-start | bytes 786440 | tf_op jit(solution)/shard_map/ppermute | solution.py:405
  84.3 15.3 %collective-permute-start.12 = (bf16[64,2048]{1,0:T(8,128)(2,1)S(1)}, bf16[64,2048]{1,0:T(8,128)(2,1)S(1)}, u32[]{:S(2)}, u32[]{:S(2)}) collective-permute-start(bf16[64,2048]{1,0:T(8,128)(2,1)S(1)} %get-tuple-element.188), channel_id=1, source_target_pairs={{0,1},{1,0},{2,3},{3,2},{4,5},{5,4},{6,7},{7,6},{8,9},{9,8},{10,11... | collective-permute-start | bytes 786440 | tf_op jit(solution)/shard_map/ppermute | solution.py:405
  85.5 21.8 %collective-permute-start.13 = (bf16[64,2048]{1,0:T(8,128)(2,1)S(1)}, bf16[64,2048]{1,0:T(8,128)(2,1)S(1)}, u32[]{:S(2)}, u32[]{:S(2)}) collective-permute-start(bf16[64,2048]{1,0:T(8,128)(2,1)S(1)} %get-tuple-element.189), channel_id=1, source_target_pairs={{0,2},{1,3},{2,0},{3,1},{4,6},{5,7},{6,4},{7,5},{8,10},{9,11},{10,... | collective-permute-start | bytes 786440 | tf_op jit(solution)/shard_map/ppermute | solution.py:405
  88.9 18.4 %collective-permute-start.14 = (bf16[64,2048]{1,0:T(8,128)(2,1)S(1)}, bf16[64,2048]{1,0:T(8,128)(2,1)S(1)}, u32[]{:S(2)}, u32[]{:S(2)}) collective-permute-start(bf16[64,2048]{1,0:T(8,128)(2,1)S(1)} %get-tuple-element.190), channel_id=1, source_target_pairs={{0,3},{1,2},{2,1},{3,0},{4,7},{5,6},{6,5},{7,4},{8,11},{9,10},{10,... | collective-permute-start | bytes 786440 | tf_op jit(solution)/shard_map/ppermute | solution.py:405
  94.9 34.9 %collective-permute-start.22 = (bf16[64,2048]{1,0:T(8,128)(2,1)S(1)}, bf16[64,2048]{1,0:T(8,128)(2,1)S(1)}, u32[]{:S(2)}, u32[]{:S(2)}) collective-permute-start(bf16[64,2048]{1,0:T(8,128)(2,1)S(1)} %get-tuple-element.216.refs_0_), channel_id=1, source_target_pairs={{0,1},{1,0},{2,3},{3,2},{4,5},{5,4},{6,7},{7,6},{8,9},{9,8},{10,11... | collective-permute-start | bytes 786440 | tf_op jit(solution)/shard_map/ppermute | solution.py:405
  96.0 33.8 %collective-permute-start.23 = (bf16[64,2048]{1,0:T(8,128)(2,1)S(1)}, bf16[64,2048]{1,0:T(8,128)(2,1)S(1)}, u32[]{:S(2)}, u32[]{:S(2)}) collective-permute-start(bf16[64,2048]{1,0:T(8,128)(2,1)S(1)} %get-tuple-element.216.refs_0_), channel_id=1, source_target_pairs={{0,2},{1,3},{2,0},{3,1},{4,6},{5,7},{6,4},{7,5},{8,10},{9,11},{10,... | collective-permute-start | bytes 786440 | tf_op jit(solution)/shard_map/ppermute | solution.py:405
  99.6 32.2 %collective-permute-start.25 = (bf16[64,2048]{1,0:T(8,128)(2,1)S(1)}, bf16[64,2048]{1,0:T(8,128)(2,1)S(1)}, u32[]{:S(2)}, u32[]{:S(2)}) collective-permute-start(bf16[64,2048]{1,0:T(8,128)(2,1)S(1)} %get-tuple-element.216.refs_0_), channel_id=1, source_target_pairs={{0,4},{4,0},{1,5},{5,1},{2,6},{6,2},{3,7},{7,3},{8,12},{12,8},{9,1... | collective-permute-start | bytes 786440 | tf_op jit(solution)/shard_map/ppermute | solution.py:405
  107.6 27.3 %collective-permute-start.16 = (bf16[64,2048]{1,0:T(8,128)(2,1)S(1)}, bf16[64,2048]{1,0:T(8,128)(2,1)S(1)}, u32[]{:S(2)}, u32[]{:S(2)}) collective-permute-start(bf16[64,2048]{1,0:T(8,128)(2,1)S(1)} %get-tuple-element.193.refs_0_), channel_id=1, source_target_pairs={{0,2},{1,3},{2,0},{3,1},{4,6},{5,7},{6,4},{7,5},{8,10},{9,11},{10,... | collective-permute-start | bytes 786440 | tf_op jit(solution)/shard_map/ppermute | solution.py:405
  130.5 12.0 %collective-permute-start.27 = (bf16[64,2048]{1,0:T(8,128)(2,1)S(1)}, bf16[64,2048]{1,0:T(8,128)(2,1)S(1)}, u32[]{:S(2)}, u32[]{:S(2)}) collective-permute-start(bf16[64,2048]{1,0:T(8,128)(2,1)S(1)} %collective-permute-done.23.refs_2_), channel_id=1, source_target_pairs={{0,4},{4,0},{1,5},{5,1},{2,6},{6,2},{3,7},{7,3},{8,12},{12,8},{9,1... | collective-permute-start | bytes 786440 | tf_op jit(solution)/shard_map/ppermute | solution.py:405
  132.4 13.7 %collective-permute-start.15 = (bf16[64,2048]{1,0:T(8,128)(2,1)S(1)}, bf16[64,2048]{1,0:T(8,128)(2,1)S(1)}, u32[]{:S(2)}, u32[]{:S(2)}) collective-permute-start(bf16[64,2048]{1,0:T(8,128)(2,1)S(1)} %get-tuple-element.193.refs_0_), channel_id=1, source_target_pairs={{0,1},{1,0},{2,3},{3,2},{4,5},{5,4},{6,7},{7,6},{8,9},{9,8},{10,11... | collective-permute-start | bytes 786440 | tf_op jit(solution)/shard_map/ppermute | solution.py:405
  134.9 16.7 %collective-permute-start.17 = (bf16[64,2048]{1,0:T(8,128)(2,1)S(1)}, bf16[64,2048]{1,0:T(8,128)(2,1)S(1)}, u32[]{:S(2)}, u32[]{:S(2)}) collective-permute-start(bf16[64,2048]{1,0:T(8,128)(2,1)S(1)} %collective-permute-done.16.refs_2_), channel_id=1, source_target_pairs={{0,1},{1,0},{2,3},{3,2},{4,5},{5,4},{6,7},{7,6},{8,9},{9,8},{10,11... | collective-permute-start | bytes 786440 | tf_op jit(solution)/shard_map/ppermute | solution.py:405
  183.2 13.6 %collective-permute-start.30 = (bf16[64,2048]{1,0:T(8,128)(2,1)S(1)}, bf16[64,2048]{1,0:T(8,128)(2,1)S(1)}, u32[]{:S(2)}, u32[]{:S(2)}) collective-permute-start(bf16[64,2048]{1,0:T(8,128)(2,1)S(1)} %get-tuple-element.204), channel_id=1, source_target_pairs={{0,1},{1,0},{2,3},{3,2},{4,5},{5,4},{6,7},{7,6},{8,9},{9,8},{10,11... | collective-permute-start | bytes 786440 | tf_op jit(solution)/shard_map/ppermute | solution.py:405
  184.8 21.3 %collective-permute-start.31 = (bf16[64,2048]{1,0:T(8,128)(2,1)S(1)}, bf16[64,2048]{1,0:T(8,128)(2,1)S(1)}, u32[]{:S(2)}, u32[]{:S(2)}) collective-permute-start(bf16[64,2048]{1,0:T(8,128)(2,1)S(1)} %get-tuple-element.205), channel_id=1, source_target_pairs={{0,2},{1,3},{2,0},{3,1},{4,6},{5,7},{6,4},{7,5},{8,10},{9,11},{10,... | collective-permute-start | bytes 786440 | tf_op jit(solution)/shard_map/ppermute | solution.py:405
  187.2 18.9 %collective-permute-start.32 = (bf16[64,2048]{1,0:T(8,128)(2,1)S(1)}, bf16[64,2048]{1,0:T(8,128)(2,1)S(1)}, u32[]{:S(2)}, u32[]{:S(2)}) collective-permute-start(bf16[64,2048]{1,0:T(8,128)(2,1)S(1)} %get-tuple-element.206), channel_id=1, source_target_pairs={{0,3},{1,2},{2,1},{3,0},{4,7},{5,6},{6,5},{7,4},{8,11},{9,10},{10,... | collective-permute-start | bytes 786440 | tf_op jit(solution)/shard_map/ppermute | solution.py:405
  206.4 17.7 %collective-permute-start.34 = (bf16[64,2048]{1,0:T(8,128)(2,1)S(1)}, bf16[64,2048]{1,0:T(8,128)(2,1)S(1)}, u32[]{:S(2)}, u32[]{:S(2)}) collective-permute-start(bf16[64,2048]{1,0:T(8,128)(2,1)S(1)} %get-tuple-element.208.refs_0_), channel_id=1, source_target_pairs={{0,2},{1,3},{2,0},{3,1},{4,6},{5,7},{6,4},{7,5},{8,10},{9,11},{10,... | collective-permute-start | bytes 786440 | tf_op jit(solution)/shard_map/ppermute | solution.py:405
  248.6 12.4 %collective-permute-start.41 = (bf16[64,2048]{1,0:T(8,128)(2,1)S(1)}, bf16[64,2048]{1,0:T(8,128)(2,1)S(1)}, u32[]{:S(2)}, u32[]{:S(2)}) collective-permute-start(bf16[64,2048]{1,0:T(8,128)(2,1)S(1)} %get-tuple-element.212), channel_id=1, source_target_pairs={{0,1},{1,0},{2,3},{3,2},{4,5},{5,4},{6,7},{7,6},{8,9},{9,8},{10,11... | collective-permute-start | bytes 786440 | tf_op jit(solution)/shard_map/ppermute | solution.py:405
  248.7 21.4 %collective-permute-start.42 = (bf16[64,2048]{1,0:T(8,128)(2,1)S(1)}, bf16[64,2048]{1,0:T(8,128)(2,1)S(1)}, u32[]{:S(2)}, u32[]{:S(2)}) collective-permute-start(bf16[64,2048]{1,0:T(8,128)(2,1)S(1)} %get-tuple-element.213), channel_id=1, source_target_pairs={{0,2},{1,3},{2,0},{3,1},{4,6},{5,7},{6,4},{7,5},{8,10},{9,11},{10,... | collective-permute-start | bytes 786440 | tf_op jit(solution)/shard_map/ppermute | solution.py:405
  249.9 20.1 %collective-permute-start.43 = (bf16[64,2048]{1,0:T(8,128)(2,1)S(1)}, bf16[64,2048]{1,0:T(8,128)(2,1)S(1)}, u32[]{:S(2)}, u32[]{:S(2)}) collective-permute-start(bf16[64,2048]{1,0:T(8,128)(2,1)S(1)} %get-tuple-element.214), channel_id=1, source_target_pairs={{0,3},{1,2},{2,1},{3,0},{4,7},{5,6},{6,5},{7,4},{8,11},{9,10},{10,... | collective-permute-start | bytes 786440 | tf_op jit(solution)/shard_map/ppermute | solution.py:405
  270.4 16.8 %collective-permute-start.45 = (bf16[64,2048]{1,0:T(8,128)(2,1)S(1)}, bf16[64,2048]{1,0:T(8,128)(2,1)S(1)}, u32[]{:S(2)}, u32[]{:S(2)}) collective-permute-start(bf16[64,2048]{1,0:T(8,128)(2,1)S(1)} %get-tuple-element.224.refs_0_), channel_id=1, source_target_pairs={{0,2},{1,3},{2,0},{3,1},{4,6},{5,7},{6,4},{7,5},{8,10},{9,11},{10,... | collective-permute-start | bytes 786440 | tf_op jit(solution)/shard_map/ppermute | solution.py:405
  287.2 36.1 %collective-permute-start.47 = (bf16[64,2048]{1,0:T(8,128)(2,1)S(1)}, bf16[64,2048]{1,0:T(8,128)(2,1)}, u32[]{:S(2)}, u32[]{:S(2)}) collective-permute-start(bf16[64,2048]{1,0:T(8,128)(2,1)S(1)} %get-tuple-element.224.refs_0_), channel_id=1, source_target_pairs={{0,4},{4,0},{1,5},{5,1},{2,6},{6,2},{3,7},{7,3},{8,12},{12,8},{9,1... | collective-permute-start | bytes 786440 | tf_op jit(solution)/shard_map/ppermute | solution.py:405
  287.2 36.1 %collective-permute-start.49 = (bf16[64,2048]{1,0:T(8,128)(2,1)S(1)}, bf16[64,2048]{1,0:T(8,128)(2,1)}, u32[]{:S(2)}, u32[]{:S(2)}) collective-permute-start(bf16[64,2048]{1,0:T(8,128)(2,1)S(1)} %collective-permute-done.45.refs_2_), channel_id=1, source_target_pairs={{0,4},{4,0},{1,5},{5,1},{2,6},{6,2},{3,7},{7,3},{8,12},{12,8},{9,1... | collective-permute-start | bytes 786440 | tf_op jit(solution)/shard_map/ppermute | solution.py:405
  287.7 35.6 %collective-permute-start.48 = (bf16[64,2048]{1,0:T(8,128)(2,1)}, bf16[64,2048]{1,0:T(8,128)(2,1)}, u32[]{:S(2)}, u32[]{:S(2)}) collective-permute-start(bf16[64,2048]{1,0:T(8,128)(2,1)} %collective-permute-done.44.refs_1_), channel_id=1, source_target_pairs={{0,4},{4,0},{1,5},{5,1},{2,6},{6,2},{3,7},{7,3},{8,12},{12,8},{9,1... | collective-permute-start | bytes 786440 | tf_op jit(solution)/shard_map/ppermute | solution.py:405
  294.2 29.1 %collective-permute-start.50 = (bf16[64,2048]{1,0:T(8,128)(2,1)}, bf16[64,2048]{1,0:T(8,128)(2,1)}, u32[]{:S(2)}, u32[]{:S(2)}) collective-permute-start(bf16[64,2048]{1,0:T(8,128)(2,1)} %collective-permute-done.46.refs_3_), channel_id=1, source_target_pairs={{0,4},{4,0},{1,5},{5,1},{2,6},{6,2},{3,7},{7,3},{8,12},{12,8},{9,1... | collective-permute-start | bytes 786440 | tf_op jit(solution)/shard_map/ppermute | solution.py:405
  336.3 28.2 %collective-permute-start.52 = (bf16[64,2048]{1,0:T(8,128)(2,1)}, bf16[64,2048]{1,0:T(8,128)(2,1)}, u32[]{:S(2)}, u32[]{:S(2)}) collective-permute-start(bf16[64,2048]{1,0:T(8,128)(2,1)} %get-tuple-element.232), channel_id=1, source_target_pairs={{0,1},{1,0},{2,3},{3,2},{4,5},{5,4},{6,7},{7,6},{8,9},{9,8},{10,11... | collective-permute-start | bytes 786440 | tf_op jit(solution)/shard_map/ppermute | solution.py:405
  337.8 26.7 %collective-permute-start.53 = (bf16[64,2048]{1,0:T(8,128)(2,1)}, bf16[64,2048]{1,0:T(8,128)(2,1)}, u32[]{:S(2)}, u32[]{:S(2)}) collective-permute-start(bf16[64,2048]{1,0:T(8,128)(2,1)} %get-tuple-element.233), channel_id=1, source_target_pairs={{0,2},{1,3},{2,0},{3,1},{4,6},{5,7},{6,4},{7,5},{8,10},{9,11},{10,... | collective-permute-start | bytes 786440 | tf_op jit(solution)/shard_map/ppermute | solution.py:405
  340.2 24.3 %collective-permute-start.54 = (bf16[64,2048]{1,0:T(8,128)(2,1)}, bf16[64,2048]{1,0:T(8,128)(2,1)}, u32[]{:S(2)}, u32[]{:S(2)}) collective-permute-start(bf16[64,2048]{1,0:T(8,128)(2,1)} %get-tuple-element.234), channel_id=1, source_target_pairs={{0,3},{1,2},{2,1},{3,0},{4,7},{5,6},{6,5},{7,4},{8,11},{9,10},{10,... | collective-permute-start | bytes 786440 | tf_op jit(solution)/shard_map/ppermute | solution.py:405
  364.6 173.2 %reduce-scatter.9.cloned.1.call-start = ((), (), s32[]{:S(2)}) async-start(), calls=%async_computation.10 | async-start | bytes 5242880 | tf_op jit(solution)/shard_map/reduce_scatter | solution.py:581
  369.4 13.5 %collective-permute-start.56 = (bf16[64,2048]{1,0:T(8,128)(2,1)S(1)}, bf16[64,2048]{1,0:T(8,128)(2,1)S(1)}, u32[]{:S(2)}, u32[]{:S(2)}) collective-permute-start(bf16[64,2048]{1,0:T(8,128)(2,1)S(1)} %get-tuple-element.241), channel_id=1, source_target_pairs={{0,1},{1,0},{2,3},{3,2},{4,5},{5,4},{6,7},{7,6},{8,9},{9,8},{10,11... | collective-permute-start | bytes 786440 | tf_op jit(solution)/shard_map/ppermute | solution.py:405
  370.1 21.7 %collective-permute-start.57 = (bf16[64,2048]{1,0:T(8,128)(2,1)S(1)}, bf16[64,2048]{1,0:T(8,128)(2,1)S(1)}, u32[]{:S(2)}, u32[]{:S(2)}) collective-permute-start(bf16[64,2048]{1,0:T(8,128)(2,1)S(1)} %get-tuple-element.242), channel_id=1, source_target_pairs={{0,2},{1,3},{2,0},{3,1},{4,6},{5,7},{6,4},{7,5},{8,10},{9,11},{10,... | collective-permute-start | bytes 786440 | tf_op jit(solution)/shard_map/ppermute | solution.py:405
  373.4 18.4 %collective-permute-start.58 = (bf16[64,2048]{1,0:T(8,128)(2,1)S(1)}, bf16[64,2048]{1,0:T(8,128)(2,1)S(1)}, u32[]{:S(2)}, u32[]{:S(2)}) collective-permute-start(bf16[64,2048]{1,0:T(8,128)(2,1)S(1)} %get-tuple-element.243), channel_id=1, source_target_pairs={{0,3},{1,2},{2,1},{3,0},{4,7},{5,6},{6,5},{7,4},{8,11},{9,10},{10,... | collective-permute-start | bytes 786440 | tf_op jit(solution)/shard_map/ppermute | solution.py:405
  393.3 18.0 %collective-permute-start.60 = (bf16[64,2048]{1,0:T(8,128)(2,1)S(1)}, bf16[64,2048]{1,0:T(8,128)(2,1)S(1)}, u32[]{:S(2)}, u32[]{:S(2)}) collective-permute-start(bf16[64,2048]{1,0:T(8,128)(2,1)S(1)} %get-tuple-element.245.refs_0_), channel_id=1, source_target_pairs={{0,2},{1,3},{2,0},{3,1},{4,6},{5,7},{6,4},{7,5},{8,10},{9,11},{10,... | collective-permute-start | bytes 786440 | tf_op jit(solution)/shard_map/ppermute | solution.py:405
  399.6 12.1 %collective-permute-start.59 = (bf16[64,2048]{1,0:T(8,128)(2,1)S(1)}, bf16[64,2048]{1,0:T(8,128)(2,1)S(1)}, u32[]{:S(2)}, u32[]{:S(2)}) collective-permute-start(bf16[64,2048]{1,0:T(8,128)(2,1)S(1)} %get-tuple-element.245.refs_0_), channel_id=1, source_target_pairs={{0,1},{1,0},{2,3},{3,2},{4,5},{5,4},{6,7},{7,6},{8,9},{9,8},{10,11... | collective-permute-start | bytes 786440 | tf_op jit(solution)/shard_map/ppermute | solution.py:405
  438.7 13.0 %collective-permute-start.67 = (bf16[64,2048]{1,0:T(8,128)(2,1)}, bf16[64,2048]{1,0:T(8,128)(2,1)S(1)}, u32[]{:S(2)}, u32[]{:S(2)}) collective-permute-start(bf16[64,2048]{1,0:T(8,128)(2,1)} %get-tuple-element.252), channel_id=1, source_target_pairs={{0,1},{1,0},{2,3},{3,2},{4,5},{5,4},{6,7},{7,6},{8,9},{9,8},{10,11... | collective-permute-start | bytes 786440 | tf_op jit(solution)/shard_map/ppermute | solution.py:405
  438.9 21.6 %collective-permute-start.68 = (bf16[64,2048]{1,0:T(8,128)(2,1)}, bf16[64,2048]{1,0:T(8,128)(2,1)}, u32[]{:S(2)}, u32[]{:S(2)}) collective-permute-start(bf16[64,2048]{1,0:T(8,128)(2,1)} %get-tuple-element.253), channel_id=1, source_target_pairs={{0,2},{1,3},{2,0},{3,1},{4,6},{5,7},{6,4},{7,5},{8,10},{9,11},{10,... | collective-permute-start | bytes 786440 | tf_op jit(solution)/shard_map/ppermute | solution.py:405
  440.6 19.9 %collective-permute-start.69 = (bf16[64,2048]{1,0:T(8,128)(2,1)}, bf16[64,2048]{1,0:T(8,128)(2,1)}, u32[]{:S(2)}, u32[]{:S(2)}) collective-permute-start(bf16[64,2048]{1,0:T(8,128)(2,1)} %get-tuple-element.254), channel_id=1, source_target_pairs={{0,3},{1,2},{2,1},{3,0},{4,7},{5,6},{6,5},{7,4},{8,11},{9,10},{10,... | collective-permute-start | bytes 786440 | tf_op jit(solution)/shard_map/ppermute | solution.py:405
  460.6 177.8 %reduce-scatter.5.cloned.1.call-start = ((), (), s32[]{:S(2)}) async-start(), calls=%async_computation.8 | async-start | bytes 11141120 | tf_op jit(solution)/shard_map/reduce_scatter | solution.py:581
  464.4 16.5 %collective-permute-start.71 = (bf16[64,2048]{1,0:T(8,128)(2,1)S(1)}, bf16[64,2048]{1,0:T(8,128)(2,1)S(1)}, u32[]{:S(2)}, u32[]{:S(2)}) collective-permute-start(bf16[64,2048]{1,0:T(8,128)(2,1)S(1)} %get-tuple-element.267.refs_0_), channel_id=1, source_target_pairs={{0,2},{1,3},{2,0},{3,1},{4,6},{5,7},{6,4},{7,5},{8,10},{9,11},{10,... | collective-permute-start | bytes 786440 | tf_op jit(solution)/shard_map/ppermute | solution.py:405
  503.8 14.8 %collective-permute-start.78 = (bf16[64,2048]{1,0:T(8,128)(2,1)}, bf16[64,2048]{1,0:T(8,128)(2,1)S(1)}, u32[]{:S(2)}, u32[]{:S(2)}) collective-permute-start(bf16[64,2048]{1,0:T(8,128)(2,1)} %get-tuple-element.272), channel_id=1, source_target_pairs={{0,1},{1,0},{2,3},{3,2},{4,5},{5,4},{6,7},{7,6},{8,9},{9,8},{10,11... | collective-permute-start | bytes 786440 | tf_op jit(solution)/shard_map/ppermute | solution.py:405
  504.6 21.5 %collective-permute-start.79 = (bf16[64,2048]{1,0:T(8,128)(2,1)}, bf16[64,2048]{1,0:T(8,128)(2,1)S(1)}, u32[]{:S(2)}, u32[]{:S(2)}) collective-permute-start(bf16[64,2048]{1,0:T(8,128)(2,1)} %get-tuple-element.273), channel_id=1, source_target_pairs={{0,2},{1,3},{2,0},{3,1},{4,6},{5,7},{6,4},{7,5},{8,10},{9,11},{10,... | collective-permute-start | bytes 786440 | tf_op jit(solution)/shard_map/ppermute | solution.py:405
  507.5 19.3 %collective-permute-start.80 = (bf16[64,2048]{1,0:T(8,128)(2,1)}, bf16[64,2048]{1,0:T(8,128)(2,1)S(1)}, u32[]{:S(2)}, u32[]{:S(2)}) collective-permute-start(bf16[64,2048]{1,0:T(8,128)(2,1)} %get-tuple-element.274), channel_id=1, source_target_pairs={{0,3},{1,2},{2,1},{3,0},{4,7},{5,6},{6,5},{7,4},{8,11},{9,10},{10,... | collective-permute-start | bytes 786440 | tf_op jit(solution)/shard_map/ppermute | solution.py:405
  527.6 168.3 %reduce-scatter.11.cloned.1.call-start = ((), (), s32[]{:S(2)}) async-start(), calls=%async_computation.11 | async-start | bytes 5242880 | tf_op jit(solution)/shard_map/reduce_scatter | solution.py:581
  530.3 31.5 %collective-permute-start.88 = (bf16[256,2176]{1,0:T(8,128)(2,1)}, bf16[256,2176]{1,0:T(8,128)(2,1)}, u32[]{:S(2)}, u32[]{:S(2)}) collective-permute-start(bf16[256,2176]{1,0:T(8,128)(2,1)} %shard_map.229), channel_id=1, source_target_pairs={{0,4},{4,0},{1,5},{5,1},{2,6},{6,2},{3,7},{7,3},{8,12},{12,8},{9,1... | collective-permute-start | bytes 3342344 | tf_op jit(solution)/shard_map/ppermute | solution.py:405
  532.2 18.0 %collective-permute-start.82 = (bf16[64,2048]{1,0:T(8,128)(2,1)}, bf16[64,2048]{1,0:T(8,128)(2,1)S(1)}, u32[]{:S(2)}, u32[]{:S(2)}) collective-permute-start(bf16[64,2048]{1,0:T(8,128)(2,1)} %get-tuple-element.301.refs_0_), channel_id=1, source_target_pairs={{0,2},{1,3},{2,0},{3,1},{4,6},{5,7},{6,4},{7,5},{8,10},{9,11},{10,... | collective-permute-start | bytes 786440 | tf_op jit(solution)/shard_map/ppermute | solution.py:405
  539.3 19.0 %collective-permute-start.89 = (bf16[256,1024]{1,0:T(8,128)(2,1)S(1)}, bf16[256,1024]{1,0:T(8,128)(2,1)S(1)}, u32[]{:S(2)}, u32[]{:S(2)}) collective-permute-start(bf16[256,1024]{1,0:T(8,128)(2,1)S(1)} %shard_map.231), channel_id=1, source_target_pairs={{0,4},{4,0},{1,5},{5,1},{2,6},{6,2},{3,7},{7,3},{8,12},{12,8},{9,1... | collective-permute-start | bytes 1572872 | tf_op jit(solution)/shard_map/ppermute | solution.py:405
  539.4 13.6 %collective-permute-start.81 = (bf16[64,2048]{1,0:T(8,128)(2,1)}, bf16[64,2048]{1,0:T(8,128)(2,1)S(1)}, u32[]{:S(2)}, u32[]{:S(2)}) collective-permute-start(bf16[64,2048]{1,0:T(8,128)(2,1)} %get-tuple-element.301.refs_0_), channel_id=1, source_target_pairs={{0,1},{1,0},{2,3},{3,2},{4,5},{5,4},{6,7},{7,6},{8,9},{9,8},{10,11... | collective-permute-start | bytes 786440 | tf_op jit(solution)/shard_map/ppermute | solution.py:405
  550.2 15.8 %collective-permute-start.84 = (bf16[64,2048]{1,0:T(8,128)(2,1)}, bf16[64,2048]{1,0:T(8,128)(2,1)}, u32[]{:S(2)}, u32[]{:S(2)}) collective-permute-start(bf16[64,2048]{1,0:T(8,128)(2,1)} %get-tuple-element.301.refs_0_), channel_id=1, source_target_pairs={{0,4},{4,0},{1,5},{5,1},{2,6},{6,2},{3,7},{7,3},{8,12},{12,8},{9,1... | collective-permute-start | bytes 786440 | tf_op jit(solution)/shard_map/ppermute | solution.py:405
  552.9 13.1 %collective-permute-start.86 = (bf16[64,2048]{1,0:T(8,128)(2,1)S(1)}, bf16[64,2048]{1,0:T(8,128)(2,1)}, u32[]{:S(2)}, u32[]{:S(2)}) collective-permute-start(bf16[64,2048]{1,0:T(8,128)(2,1)S(1)} %collective-permute-done.82.refs_2_), channel_id=1, source_target_pairs={{0,4},{4,0},{1,5},{5,1},{2,6},{6,2},{3,7},{7,3},{8,12},{12,8},{9,1... | collective-permute-start | bytes 786440 | tf_op jit(solution)/shard_map/ppermute | solution.py:405
  586.2 13.5 %collective-permute-start.91 = (bf16[64,2048]{1,0:T(8,128)(2,1)}, bf16[64,2048]{1,0:T(8,128)(2,1)S(1)}, u32[]{:S(2)}, u32[]{:S(2)}) collective-permute-start(bf16[64,2048]{1,0:T(8,128)(2,1)} %get-tuple-element.315), channel_id=1, source_target_pairs={{0,1},{1,0},{2,3},{3,2},{4,5},{5,4},{6,7},{7,6},{8,9},{9,8},{10,11... | collective-permute-start | bytes 786440 | tf_op jit(solution)/shard_map/ppermute | solution.py:405
  586.6 21.5 %collective-permute-start.92 = (bf16[64,2048]{1,0:T(8,128)(2,1)}, bf16[64,2048]{1,0:T(8,128)(2,1)S(1)}, u32[]{:S(2)}, u32[]{:S(2)}) collective-permute-start(bf16[64,2048]{1,0:T(8,128)(2,1)} %get-tuple-element.316), channel_id=1, source_target_pairs={{0,2},{1,3},{2,0},{3,1},{4,6},{5,7},{6,4},{7,5},{8,10},{9,11},{10,... | collective-permute-start | bytes 786440 | tf_op jit(solution)/shard_map/ppermute | solution.py:405
  588.4 19.8 %collective-permute-start.93 = (bf16[64,2048]{1,0:T(8,128)(2,1)}, bf16[64,2048]{1,0:T(8,128)(2,1)S(1)}, u32[]{:S(2)}, u32[]{:S(2)}) collective-permute-start(bf16[64,2048]{1,0:T(8,128)(2,1)} %get-tuple-element.317), channel_id=1, source_target_pairs={{0,3},{1,2},{2,1},{3,0},{4,7},{5,6},{6,5},{7,4},{8,11},{9,10},{10,... | collective-permute-start | bytes 786440 | tf_op jit(solution)/shard_map/ppermute | solution.py:405
  611.6 18.4 %collective-permute-start.94 = (bf16[72,2048]{1,0:T(8,128)(2,1)S(1)}, bf16[72,2048]{1,0:T(8,128)(2,1)S(1)}, u32[]{:S(2)}, u32[]{:S(2)}) collective-permute-start(bf16[72,2048]{1,0:T(8,128)(2,1)S(1)} %concatenate.43), channel_id=1, source_target_pairs={{0,2},{1,3},{2,0},{3,1},{4,6},{5,7},{6,4},{7,5},{8,10},{9,11},{10,... | collective-permute-start | bytes 884744 | tf_op jit(solution)/shard_map/ppermute | solution.py:405
  619.2 12.7 %collective-permute-start.100 = (bf16[72,2048]{1,0:T(8,128)(2,1)S(1)}, bf16[72,2048]{1,0:T(8,128)(2,1)S(1)}, u32[]{:S(2)}, u32[]{:S(2)}) collective-permute-start(bf16[72,2048]{1,0:T(8,128)(2,1)S(1)} %concatenate.43), channel_id=1, source_target_pairs={{0,1},{1,0},{2,3},{3,2},{4,5},{5,4},{6,7},{7,6},{8,9},{9,8},{10,11... | collective-permute-start | bytes 884744 | tf_op jit(solution)/shard_map/ppermute | solution.py:405
  640.2 18.2 %collective-permute-start.98 = (bf16[256,2176]{1,0:T(8,128)(2,1)S(1)}, bf16[256,2176]{1,0:T(8,128)(2,1)S(1)}, u32[]{:S(2)}, u32[]{:S(2)}) collective-permute-start(bf16[256,2176]{1,0:T(8,128)(2,1)S(1)} %shard_map.237), channel_id=1, source_target_pairs={{0,4},{4,0},{1,5},{5,1},{2,6},{6,2},{3,7},{7,3},{8,12},{12,8},{9,1... | collective-permute-start | bytes 3342344 | tf_op jit(solution)/shard_map/ppermute | solution.py:405
  640.5 15.3 %collective-permute-start.96 = (bf16[64,2048]{1,0:T(8,128)(2,1)}, bf16[64,2048]{1,0:T(8,128)(2,1)S(1)}, u32[]{:S(2)}, u32[]{:S(2)}) collective-permute-start(bf16[64,2048]{1,0:T(8,128)(2,1)} %add_convert_fusion), channel_id=1, source_target_pairs={{0,2},{1,3},{2,0},{3,1},{4,6},{5,7},{6,4},{7,5},{8,10},{9,11},{10,... | collective-permute-start | bytes 786440 | tf_op jit(solution)/shard_map/ppermute | solution.py:405
  641.4 22.1 %collective-permute-start.95 = (bf16[64,2048]{1,0:T(8,128)(2,1)}, bf16[64,2048]{1,0:T(8,128)(2,1)S(1)}, u32[]{:S(2)}, u32[]{:S(2)}) collective-permute-start(bf16[64,2048]{1,0:T(8,128)(2,1)} %add_convert_fusion), channel_id=1, source_target_pairs={{0,1},{1,0},{2,3},{3,2},{4,5},{5,4},{6,7},{7,6},{8,9},{9,8},{10,11... | collective-permute-start | bytes 786440 | tf_op jit(solution)/shard_map/ppermute | solution.py:405
  656.8 25.0 %collective-permute-start.102 = (bf16[137,2048]{1,0:T(8,128)(2,1)}, bf16[137,2048]{1,0:T(8,128)(2,1)S(1)}, u32[]{:S(2)}, u32[]{:S(2)}) collective-permute-start(bf16[137,2048]{1,0:T(8,128)(2,1)} %pad_maximum_fusion.3), channel_id=1, source_target_pairs={{0,8},{8,0},{1,9},{9,1},{2,10},{10,2},{3,11},{11,3},{4,12},{12,4},... | collective-permute-start | bytes 1683464 | tf_op jit(solution)/shard_map/ppermute | solution.py:405
  682.1 12.6 %collective-permute-start.99 = (bf16[128,2048]{1,0:T(8,128)(2,1)S(1)}, bf16[128,2048]{1,0:T(8,128)(2,1)S(1)}, u32[]{:S(2)}, u32[]{:S(2)}) collective-permute-start(bf16[128,2048]{1,0:T(8,128)(2,1)S(1)} %get-tuple-element.398), channel_id=1, source_target_pairs={{0,8},{8,0},{1,9},{9,1},{2,10},{10,2},{3,11},{11,3},{4,12},{12,4},... | collective-permute-start | bytes 1572872 | tf_op jit(solution)/shard_map/ppermute | solution.py:405
  (143 other events, 825.8 us)
Sparse Core Ops, SparseCore 0:
  10.5 57.0 all-gather.4
  70.1 99.6 all-gather.6
  172.2 54.7 all-gather.8
  229.3 93.9 all-gather.10
  364.7 90.7 reduce-scatter.6
  460.7 54.7 reduce-scatter.8
  527.7 92.8 reduce-scatter.4
  623.9 61.7 reduce-scatter.10

commit v7 on v6

--- a/solution.py
+++ b/solution.py
@@ -699,8 +699,7 @@
             dy, low, small_two = norm_back(dx, y_own, gains[2, l], terms)
             parts = token_gather(low)
             if done is not None:
-                sums = put_mlp(l + 1, pick(done[1])), put_attn(l + 1, pick(done[0]))
-                parts, (mlp_sum, attn_sum) = lax.optimization_barrier((parts, sums))
+                parts, picked = lax.optimization_barrier((parts, [pick(x) for x in done]))
             da, dp1, bias_grad, own, send = call(
                 functools.partial(attn_backward, n_parts, heads),
                 n_parts + 6,
@@ -720,11 +719,13 @@
                 limit=56,
             )
             work = functools.partial(grads, cols=attn_cols)
+            beside = work, (h1, da, dp1, o)
             if done is None:
-                terms, g_attn, _ = token_reduce(own, send, (work, (h1, da, dp1, o)))
+                terms, g_attn, _ = token_reduce(own, send, beside)
                 done = (scatter(g_attn), g_mlp)
             else:
-                terms, g_attn, _ = token_reduce(own, send, (work, (h1, da, dp1, o)))
+                terms, g_attn, x_parts = token_reduce(own, send, beside, mp_gather(x_last))
+                x_mine, x_moved = chi_swap(by_place(x_parts), block)
             dx, low, small_one = norm_back(dy, x_own, gains[0, l], terms)
             small_out[l] = (small_one, small_two, bias_grad)
         norms = jnp.concatenate([part for l in range(LAYERS) for part in small_out[l][:2]], axis=0)
@@ -732,15 +733,15 @@
         rows = -(-bias.size // width)
         bias = jnp.pad(bias, ((0, 0), (0, rows * width - bias.size))).reshape(rows, width)
         parts = mp_gather(jnp.concatenate([low, norms.astype(LOW)], axis=0))
+        sums = put_attn(LAYERS - 1, picked[0]), put_mlp(LAYERS - 1, picked[1])
+        parts, sums, x_moved = lax.optimization_barrier((parts, sums, x_moved))
+        attn_sum, mlp_sum = sums
         norms = sum(part[sub:].astype(F32) for part in parts)
         both = jnp.concatenate([norms, bias], axis=0).astype(LOW)
         mine, moved = chi_swap(by_place([part[:sub] for part in parts]), block, both)
-        g_mlp, x_last = after((g_mlp, x_last), parts[n_mp // 2])
+        g_mlp = after(g_mlp, parts[n_mp // 2])
         g_gu, g_down = put_mlp(0, pick(g_mlp), mlp_sum)
-        x_parts = after(mp_gather(x_last), g_gu)
-        held = by_place(x_parts)
-        x_mine, x_moved = chi_swap(held, block)
-        g_gu = jnp.swapaxes(after(g_gu, held), 1, 2)
+        g_gu = jnp.swapaxes(g_gu, 1, 2)
         g_gu = with_layout_constraint(g_gu, Layout(major_to_minor=(0, 1, 2, 3)))
         moved = after(moved, g_gu)
         tokens_grad = to_blocks(mine, moved, block).astype(F32)

time: 714 us -> 710 us (level)
    ppermute x106, waiting for transfers between devices: 304 us -> 289 us  [swap(): return lax.ppermute(value, axis, [(i, i ^ bit) for i in range(sizes[axis])])]
    reduce_scatter x4, waiting for transfers between devices: 0.04 us -> 12.8 us  [scatter(): lax.psum_scatter(partial[0], ('dp', 'chi'), scatter_dimension=0, tiled=True)]
    pallas_call x0 -> x1, local copies, waits for them, and re-layouts: none -> 9.61 us  [call(): pl.pallas_call(body, out_shape=tuple(outs), in_specs=[ANY] * n_any + [HBM...]
    unnamed x192 -> x188, local copies, waits for them, and re-layouts: 45.7 us -> 39.9 us
  transfers between devices with their start and end apart: 114 -> 114, of which waited for: 55 -> 51; matrix products, arithmetic and copies ran while one was open for 6% -> 6% of each run, Pallas kernels for 19% -> 19%
where the time goes in v7:
time: 710 us; the launch traced here: 705 us
  waiting for transfers between devices  347 us (49%)
  Pallas kernels  146 us (21%)
  starting transfers between devices  114 us (16%)
  local copies, waits for them, and re-layouts  71.9 us (10%)
  between operations  16.1 us (2%)
  other arithmetic  10.9 us (2%)
    ppermute x106, waiting for transfers between devices, swap(): return lax.ppermute(value, axis, [(i, i ^ bit) for i in range(sizes[axis])])  289 us
    pallas_call x38, Pallas kernels, call(): pl.pallas_call(body, out_shape=tuple(outs), in_specs=[ANY] * n_any + [HBM...  146 us
    ppermute x106, starting transfers between devices, swap(): return lax.ppermute(value, axis, [(i, i ^ bit) for i in range(sizes[axis])])  113 us
    all_gather x4, waiting for transfers between devices, gather_weights(): return lax.all_gather(own, ('dp', 'chi', 'clo'), axis=0, tiled=True)  45 us
    unnamed x188, local copies, waits for them, and re-layouts  39.9 us
  transfers between devices with their start and end apart: 114, of which 51 were waited for; matrix products, arithmetic and copies ran while one was open for 6% of the time, Pallas kernels for 19%

profile of v7, /device:TPU:0, one launch (start us, length us, event | category | flops | bytes accessed | tf_op | source)
XLA Modules:
  0.0 705.3 jit_solution(13718496653299555450)
XLA Ops:
  10.0 3.7 fusion.17
  17.1 5.0 concatenate.39
  24.6 4.2 concatenate.40
  30.1 3.0 collective-permute-start.1
  34.1 6.5 collective-permute-done.9
  46.8 10.6 %collective-permute-done.3.refs_2_ = bf16[64,2048]{1,0:T(8,128)(2,1)S(1)} collective-permute-done((bf16[64,2048]{1,0:T(8,128)(2,1)S(1)}, bf16[64,2048]{1,0:T(8,128)(2,1)S(1)}, u32[]{:S(2)}, u32[]{:S(2)}) %collective-permute-start.3) | collective-permute-done | bytes 262176 | tf_op jit(solution)/shard_map/ppermute | solution.py:405
  58.6 6.3 collective-permute-done.4.refs_3_
  68.8 11.0 %shard_map.205 = (bf16[512,2048]{1,0:T(8,128)(2,1)}, bf16[512,256]{1,0:T(8,128)(2,1)}, bf16[512,256]{1,0:T(8,128)(2,1)}, bf16[512,256]{1,0:T(8,128)(2,1)}, bf16[...) custom-call(bf16[64,2048]{1,0:T(8,128)(2,1)} %copy-done.49, ...), custom_call_target="tpu_custom_call" | custom-call | flops 4294967296 | bytes 16526336 | tf_op jit(solution)/shard_map/pallas_call | solution.py:50
  85.5 3.4 collective-permute-start.13
  88.9 5.9 collective-permute-done
  96.0 3.6 collective-permute-start.23
  99.6 7.7 %collective-permute-done.13.refs_2_ = bf16[64,2048]{1,0:T(8,128)(2,1)S(1)} collective-permute-done((bf16[64,2048]{1,0:T(8,128)(2,1)S(1)}, bf16[64,2048]{1,0:T(8,128)(2,1)S(1)}, u32[]{:S(2)}, u32[]{:S(2)}) %collective-permute-start.13) | collective-permute-done | bytes 262176 | tf_op jit(solution)/shard_map/ppermute | solution.py:405
  107.6 13.1 %collective-permute-start.16 = (bf16[64,2048]{1,0:T(8,128)(2,1)S(1)}, bf16[64,2048]{1,0:T(8,128)(2,1)S(1)}, u32[]{:S(2)}, u32[]{:S(2)}) collective-permute-start(bf16[64,2048]{1,0:T(8,128)(2,1)S(1)} %get-tuple-element.201.refs_0_), channel_id=1, source_target_pairs={{0,2},{1,3},{2,0},{3,1},{4,6},{5,7},{6,4},{7,5},{8,10},{9,11},{10,... | collective-permute-start | bytes 786440 | tf_op jit(solution)/shard_map/ppermute | solution.py:405
  120.7 9.0 %collective-permute-done.23.refs_2_ = bf16[64,2048]{1,0:T(8,128)(2,1)S(1)} collective-permute-done((bf16[64,2048]{1,0:T(8,128)(2,1)S(1)}, bf16[64,2048]{1,0:T(8,128)(2,1)S(1)}, u32[]{:S(2)}, u32[]{:S(2)}) %collective-permute-start.23) | collective-permute-done | bytes 262176 | tf_op jit(solution)/shard_map/ppermute | solution.py:405
  134.9 5.6 collective-permute-done.24.refs_3_
  143.2 2.9 collective-permute-done.15.refs_1_
  146.2 5.5 collective-permute-done.17.refs_3_
  153.9 15.8 %all-gather.7.cloned.1.call-done.refs_8_ = bf16[2048,4352]{1,0:T(8,128)(2,1)} async-done(((bf16[256,4352]{1,0:T(8,128)(2,1)}), bf16[2048,4352]{1,0:T(8,128)(2,1)}) %all-gather.7.cloned.1.call-update) | async-done | bytes 17825808 | tf_op jit(solution)/shard_map/all_gather | solution.py:501
  171.7 7.3 %shard_map.208 = (bf16[512,2048]{1,0:T(8,128)(2,1)S(1)}, bf16[512,1408]{1,0:T(8,128)(2,1)S(1)}, bf16[512,704]{1,0:T(8,128)(2,1)S(1)}, bf16[256,2048]{1,0:T(8,128)(2,1)S(1)}, bf16[256,2048]{1,0:T(8,128)(2,1)S(1)}) custom-call(bf16[64,2048]{1,0:T(8,128)(2,1)S(1)} %get-tuple-element.201.refs_0_, bf16[64,2048]{1,0:T(8,128)(2,1)S(1)} %collective-permute-done.15.refs_1_, ...), custom_call_target="tpu_custom_call" | custom-call | flops 4563402752 | bytes 26279936 | tf_op jit(solution)/shard_map/pallas_call | solution.py:50
  187.6 9.1 %collective-permute-done.30.refs_1_ = bf16[64,2048]{1,0:T(8,128)(2,1)S(1)} collective-permute-done((bf16[64,2048]{1,0:T(8,128)(2,1)S(1)}, bf16[64,2048]{1,0:T(8,128)(2,1)S(1)}, u32[]{:S(2)}, u32[]{:S(2)}) %collective-permute-start.30) | collective-permute-done | bytes 262176 | tf_op jit(solution)/shard_map/ppermute | solution.py:405
  196.8 9.3 %collective-permute-done.31.refs_2_ = bf16[64,2048]{1,0:T(8,128)(2,1)S(1)} collective-permute-done((bf16[64,2048]{1,0:T(8,128)(2,1)S(1)}, bf16[64,2048]{1,0:T(8,128)(2,1)S(1)}, u32[]{:S(2)}, u32[]{:S(2)}) %collective-permute-start.31) | collective-permute-done | bytes 262176 | tf_op jit(solution)/shard_map/ppermute | solution.py:405
  206.4 6.2 collective-permute-start.34
  212.7 11.5 %collective-permute-done.34.refs_2_ = bf16[64,2048]{1,0:T(8,128)(2,1)S(1)} collective-permute-done((bf16[64,2048]{1,0:T(8,128)(2,1)S(1)}, bf16[64,2048]{1,0:T(8,128)(2,1)S(1)}, u32[]{:S(2)}, u32[]{:S(2)}) %collective-permute-start.34) | collective-permute-done | bytes 262176 | tf_op jit(solution)/shard_map/ppermute | solution.py:405
  224.7 6.4 collective-permute-done.35.refs_3_
  232.8 11.4 %shard_map.212 = (bf16[512,2048]{1,0:T(8,128)(2,1)}, bf16[512,256]{1,0:T(8,128)(2,1)}, bf16[512,256]{1,0:T(8,128)(2,1)}, bf16[512,256]{1,0:T(8,128)(2,1)}, bf16[...) custom-call(bf16[64,2048]{1,0:T(8,128)(2,1)} %copy-done.50, ...), custom_call_target="tpu_custom_call" | custom-call | flops 4294967296 | bytes 16526336 | tf_op jit(solution)/shard_map/pallas_call | solution.py:50
  249.9 3.1 collective-permute-start.43
  253.0 7.9 %collective-permute-done.41.refs_1_ = bf16[64,2048]{1,0:T(8,128)(2,1)S(1)} collective-permute-done((bf16[64,2048]{1,0:T(8,128)(2,1)S(1)}, bf16[64,2048]{1,0:T(8,128)(2,1)S(1)}, u32[]{:S(2)}, u32[]{:S(2)}) %collective-permute-start.41) | collective-permute-done | bytes 262176 | tf_op jit(solution)/shard_map/ppermute | solution.py:405
  260.9 9.1 %collective-permute-done.42.refs_2_ = bf16[64,2048]{1,0:T(8,128)(2,1)S(1)} collective-permute-done((bf16[64,2048]{1,0:T(8,128)(2,1)S(1)}, bf16[64,2048]{1,0:T(8,128)(2,1)S(1)}, u32[]{:S(2)}, u32[]{:S(2)}) %collective-permute-start.42) | collective-permute-done | bytes 262176 | tf_op jit(solution)/shard_map/ppermute | solution.py:405
  270.4 5.4 collective-permute-start.45
  275.9 11.2 %collective-permute-done.45.refs_2_ = bf16[64,2048]{1,0:T(8,128)(2,1)S(1)} collective-permute-done((bf16[64,2048]{1,0:T(8,128)(2,1)S(1)}, bf16[64,2048]{1,0:T(8,128)(2,1)S(1)}, u32[]{:S(2)}, u32[]{:S(2)}) %collective-permute-start.45) | collective-permute-done | bytes 262176 | tf_op jit(solution)/shard_map/ppermute | solution.py:405
  287.7 6.5 collective-permute-done.46.refs_3_
  294.1 29.1 %all-gather.11.cloned.1.call-done.refs_8_ = bf16[2048,4352]{1,0:T(8,128)(2,1)} async-done(((bf16[256,4352]{1,0:T(8,128)(2,1)}), bf16[2048,4352]{1,0:T(8,128)(2,1)}) %all-gather.11.cloned.1.call-update) | async-done | bytes 17825808 | tf_op jit(solution)/shard_map/all_gather | solution.py:501
  323.3 7.9 %shard_map.215 = (bf16[512,2048]{1,0:T(8,128)(2,1)S(1)}, bf16[512,1408]{1,0:T(8,128)(2,1)S(1)}, bf16[512,704]{1,0:T(8,128)(2,1)S(1)}, bf16[256,2048]{1,0:T(8,128)(2,1)S(1)}, bf16[256,2048]{1,0:T(8,128)(2,1)S(1)}) custom-call(bf16[64,2048]{1,0:T(8,128)(2,1)S(1)} %get-tuple-element.232.refs_0_, bf16[64,2048]{1,0:T(8,128)(2,1)} %collective-permute-done.44.refs_1_, ...), custom_call_target="tpu_custom_call" | custom-call | flops 4563402752 | bytes 26279936 | tf_op jit(solution)/shard_map/pallas_call | solution.py:50
  340.7 8.9 %shard_map.217 = (bf16[512,2048]{1,0:T(8,128)(2,1)S(1)}, bf16[512,1408]{1,0:T(8,128)(2,1)S(1)}, bf16[256,2048]{1,0:T(8,128)(2,1)S(1)}, bf16[256,2048]{1,0:T(8,128)(2,1)S(1)}) custom-call(bf16[64,2048]{1,0:T(8,128)(2,1)S(1)} %get-tuple-element.224.refs_0_, bf16[64,2048]{1,0:T(8,128)(2,1)S(1)} %copy-done.27, bf16[64,2048]{1,0:T(8,128)(2,1)S(1)} %copy-done.29, ...), custom_call_target="tpu_custom_call" | custom-call | flops 4563402752 | bytes 27000832 | tf_op jit(solution)/shard_map/pallas_call | solution.py:50
  354.0 10.5 %shard_map.218 = bf16[2048,2176]{1,0:T(8,128)(2,1)} custom-call(bf16[512,2048]{1,0:T(8,128)(2,1)} %copy-done.41, bf16[512,2048]{1,0:T(8,128)(2,1)} %copy-done.43, bf16[512,1408]{1,0:T(8,128)(2,1)} %copy-done.45, bf16[512,704]{1,0:T(8,128)(2,1)} %copy-done.48), custom_call_target="tpu_custom_call" | custom-call | flops 4563402752 | bytes 15269888 | tf_op jit(solution)/shard_map/pallas_call | solution.py:50
  370.0 3.3 collective-permute-start.57
  373.8 9.1 %collective-permute-done.56.refs_1_ = bf16[64,2048]{1,0:T(8,128)(2,1)S(1)} collective-permute-done((bf16[64,2048]{1,0:T(8,128)(2,1)S(1)}, bf16[64,2048]{1,0:T(8,128)(2,1)S(1)}, u32[]{:S(2)}, u32[]{:S(2)}) %collective-permute-start.56) | collective-permute-done | bytes 262176 | tf_op jit(solution)/shard_map/ppermute | solution.py:405
  382.9 8.9 %collective-permute-done.57.refs_2_ = bf16[64,2048]{1,0:T(8,128)(2,1)S(1)} collective-permute-done((bf16[64,2048]{1,0:T(8,128)(2,1)S(1)}, bf16[64,2048]{1,0:T(8,128)(2,1)S(1)}, u32[]{:S(2)}, u32[]{:S(2)}) %collective-permute-start.57) | collective-permute-done | bytes 262176 | tf_op jit(solution)/shard_map/ppermute | solution.py:405
  393.2 6.3 collective-permute-start.60
  399.6 11.6 %collective-permute-done.60.refs_2_ = bf16[64,2048]{1,0:T(8,128)(2,1)S(1)} collective-permute-done((bf16[64,2048]{1,0:T(8,128)(2,1)S(1)}, bf16[64,2048]{1,0:T(8,128)(2,1)S(1)}, u32[]{:S(2)}, u32[]{:S(2)}) %collective-permute-start.60) | collective-permute-done | bytes 262176 | tf_op jit(solution)/shard_map/ppermute | solution.py:405
  411.8 6.4 collective-permute-done.61.refs_3_
  420.5 13.0 %shard_map.221 = (bf16[512,2048]{1,0:T(8,128)(2,1)}, bf16[512,768]{1,0:T(8,128)(2,1)}, f32[1,768]{1,0:T(1,128)}, bf16[256,2048]{1,0:T(8,128)(2,1)}, bf16[256,2048]{1,0:T(8,128)(2,1)}) custom-call(bf16[64,2048]{1,0:T(8,128)(2,1)} %copy-done.51, bf16[64,2048]{1,0:T(8,128)(2,1)} %copy-done.82, bf16[64,2048]{1,0:T(8,128)(2,1)} %copy-done.81, ...), custom_call_target="tpu_custom_call" | custom-call | flops 4831838208 | bytes 17050624 | tf_op jit(solution)/shard_map/pallas_call | solution.py:50
  443.0 6.9 shard_map.223
  451.7 8.8 %collective-permute-done.68.refs_2_ = bf16[64,2048]{1,0:T(8,128)(2,1)} collective-permute-done((bf16[64,2048]{1,0:T(8,128)(2,1)}, bf16[64,2048]{1,0:T(8,128)(2,1)}, u32[]{:S(2)}, u32[]{:S(2)}) %collective-permute-start.68) | collective-permute-done | bytes 262176 | tf_op jit(solution)/shard_map/ppermute | solution.py:405
  464.3 5.3 collective-permute-start.71
  469.7 11.2 %collective-permute-done.71.refs_2_ = bf16[64,2048]{1,0:T(8,128)(2,1)S(1)} collective-permute-done((bf16[64,2048]{1,0:T(8,128)(2,1)S(1)}, bf16[64,2048]{1,0:T(8,128)(2,1)S(1)}, u32[]{:S(2)}, u32[]{:S(2)}) %collective-permute-start.71) | collective-permute-done | bytes 262176 | tf_op jit(solution)/shard_map/ppermute | solution.py:405
  481.4 6.1 collective-permute-done.72.refs_3_
  489.0 8.9 %shard_map.225 = (bf16[512,2048]{1,0:T(8,128)(2,1)S(1)}, bf16[512,1408]{1,0:T(8,128)(2,1)S(1)}, bf16[256,2048]{1,0:T(8,128)(2,1)S(1)}, bf16[256,2048]{1,0:T(8,128)(2,1)S(1)}) custom-call(bf16[64,2048]{1,0:T(8,128)(2,1)S(1)} %get-tuple-element.276.refs_0_, bf16[64,2048]{1,0:T(8,128)(2,1)S(1)} %collective-permute-done.70.refs_1_, ...), custom_call_target="tpu_custom_call" | custom-call | flops 4563402752 | bytes 27000832 | tf_op jit(solution)/shard_map/pallas_call | solution.py:50
  508.1 10.4 %shard_map.227 = bf16[2048,2176]{1,0:T(8,128)(2,1)} custom-call(bf16[512,2048]{1,0:T(8,128)(2,1)} %copy-done.40, bf16[512,2048]{1,0:T(8,128)(2,1)} %copy-done.42, bf16[512,1408]{1,0:T(8,128)(2,1)} %copy-done.44, bf16[512,704]{1,0:T(8,128)(2,1)} %copy-done.47), custom_call_target="tpu_custom_call" | custom-call | flops 4563402752 | bytes 15269888 | tf_op jit(solution)/shard_map/pallas_call | solution.py:50
  518.6 7.6 %collective-permute-done.79.refs_2_ = bf16[64,2048]{1,0:T(8,128)(2,1)} collective-permute-done((bf16[64,2048]{1,0:T(8,128)(2,1)}, bf16[64,2048]{1,0:T(8,128)(2,1)}, u32[]{:S(2)}, u32[]{:S(2)}) %collective-permute-start.79) | collective-permute-done | bytes 262176 | tf_op jit(solution)/shard_map/ppermute | solution.py:405
  529.6 6.3 collective-permute-start.82
  541.4 13.2 %collective-permute-done.82.refs_2_ = bf16[64,2048]{1,0:T(8,128)(2,1)} collective-permute-done((bf16[64,2048]{1,0:T(8,128)(2,1)}, bf16[64,2048]{1,0:T(8,128)(2,1)}, u32[]{:S(2)}, u32[]{:S(2)}) %collective-permute-start.82) | collective-permute-done | bytes 262176 | tf_op jit(solution)/shard_map/ppermute | solution.py:405
  559.2 5.0 collective-permute-done.83.refs_3_
  567.1 13.1 %shard_map.231 = (bf16[512,2048]{1,0:T(8,128)(2,1)}, bf16[512,768]{1,0:T(8,128)(2,1)}, f32[1,768]{1,0:T(1,128)}, bf16[256,2048]{1,0:T(8,128)(2,1)}, bf16[256,2048]{1,0:T(8,128)(2,1)}) custom-call(bf16[64,2048]{1,0:T(8,128)(2,1)} %get-tuple-element.299.refs_0_, bf16[64,2048]{1,0:T(8,128)(2,1)} %copy-done.75, ...), custom_call_target="tpu_custom_call" | custom-call | flops 4831838208 | bytes 17050624 | tf_op jit(solution)/shard_map/pallas_call | solution.py:50
  590.2 6.9 shard_map.233
  598.9 8.3 %collective-permute-done.95.refs_2_ = bf16[64,2048]{1,0:T(8,128)(2,1)S(1)} collective-permute-done((bf16[64,2048]{1,0:T(8,128)(2,1)}, bf16[64,2048]{1,0:T(8,128)(2,1)S(1)}, u32[]{:S(2)}, u32[]{:S(2)}) %collective-permute-start.95) | collective-permute-done | bytes 262176 | tf_op jit(solution)/shard_map/ppermute | solution.py:405
  610.3 5.7 collective-permute-start.98
  617.5 11.3 %collective-permute-done.98 = bf16[72,2048]{1,0:T(8,128)(2,1)S(1)} collective-permute-done((bf16[72,2048]{1,0:T(8,128)(2,1)S(1)}, bf16[72,2048]{1,0:T(8,128)(2,1)S(1)}, u32[]{:S(2)}, u32[]{:S(2)}) %collective-permute-start.98) | collective-permute-done | bytes 294944 | tf_op jit(solution)/shard_map/ppermute | solution.py:405
  631.6 4.9 shard_map.236
  642.4 4.2 shard_map.238
  646.6 9.6 %copy.85 = f32[2,2,256,1408]{3,1,2,0:T(2,128)} copy(f32[2,2,256,1408]{3,2,1,0:T(8,128)} %get-tuple-element.362) | data formatting | bytes 11534336 | tf_op jit(solution)/shard_map/pallas_call | solution.py:50
  656.3 12.6 %collective-permute-done.101 = bf16[137,2048]{1,0:T(8,128)(2,1)S(1)} collective-permute-done((bf16[137,2048]{1,0:T(8,128)(2,1)S(1)}, bf16[137,2048]{1,0:T(8,128)(2,1)S(1)}, u32[]{:S(2)}, u32[]{:S(2)}) %collective-permute-start.101) | collective-permute-done | bytes 561184 | tf_op jit(solution)/shard_map/ppermute | solution.py:405
  669.2 4.9 collective-permute-done.103
  678.4 12.8 %reduce-scatter.11.cloned.1.call-done.block_sum.refs_0_ = bf16[512,1024]{1,0:T(8,128)(2,1)} async-done(((bf16[2048,1024]{1,0:T(8,128)(2,1)}), bf16[512,1024]{1,0:T(8,128)(2,1)}) %reduce-scatter.11.cloned.1.call-update) | async-done | bytes 1048592 | tf_op jit(solution)/shard_map/reduce_scatter | solution.py:581
  (486 shorter events, 162.6 us)
Async XLA Ops:
  7.2 60.8 %all-gather.5.cloned.1.call-start = ((), (), s32[]{:S(2)}) async-start(), calls=%async_computation.4 | async-start | bytes 9437184 | tf_op jit(solution)/shard_map/all_gather | solution.py:501
  9.9 159.8 %all-gather.7.cloned.1.call-start = ((), (), s32[]{:S(2)}) async-start(), calls=%async_computation.5 | async-start | bytes 20054016 | tf_op jit(solution)/shard_map/all_gather | solution.py:501
  22.1 208.9 %all-gather.9.cloned.1.call-start = ((), (), s32[]{:S(2)}) async-start(), calls=%async_computation.6 | async-start | bytes 9437184 | tf_op jit(solution)/shard_map/all_gather | solution.py:501
  23.2 300.0 %all-gather.11.cloned.1.call-start = ((), (), s32[]{:S(2)}) async-start(), calls=%async_computation.7 | async-start | bytes 20054016 | tf_op jit(solution)/shard_map/all_gather | solution.py:501
  28.9 507.0 %reduce-scatter.7.cloned.1.call-start = ((), (), s32[]{:S(2)}) async-start(), calls=%async_computation.9 | async-start | bytes 11141120 | tf_op jit(solution)/shard_map/reduce_scatter | solution.py:581
  42.3 15.1 %collective-permute-start.3 = (bf16[64,2048]{1,0:T(8,128)(2,1)S(1)}, bf16[64,2048]{1,0:T(8,128)(2,1)S(1)}, u32[]{:S(2)}, u32[]{:S(2)}) collective-permute-start(bf16[64,2048]{1,0:T(8,128)(2,1)S(1)} %get-tuple-element.192.refs_0_), channel_id=1, source_target_pairs={{0,2},{1,3},{2,0},{3,1},{4,6},{5,7},{6,4},{7,5},{8,10},{9,11},{10,... | collective-permute-start | bytes 786440 | tf_op jit(solution)/shard_map/ppermute | solution.py:405
  45.3 13.2 %collective-permute-start.2 = (bf16[64,2048]{1,0:T(8,128)(2,1)S(1)}, bf16[64,2048]{1,0:T(8,128)(2,1)S(1)}, u32[]{:S(2)}, u32[]{:S(2)}) collective-permute-start(bf16[64,2048]{1,0:T(8,128)(2,1)S(1)} %get-tuple-element.192.refs_0_), channel_id=1, source_target_pairs={{0,1},{1,0},{2,3},{3,2},{4,5},{5,4},{6,7},{7,6},{8,9},{9,8},{10,11... | collective-permute-start | bytes 786440 | tf_op jit(solution)/shard_map/ppermute | solution.py:405
  80.4 14.4 %collective-permute-start = (bf16[64,2048]{1,0:T(8,128)(2,1)S(1)}, bf16[64,2048]{1,0:T(8,128)(2,1)S(1)}, u32[]{:S(2)}, u32[]{:S(2)}) collective-permute-start(bf16[64,2048]{1,0:T(8,128)(2,1)S(1)} %dynamic-slice_bitcast_fusion.3), channel_id=1, source_target_pairs={{0,8},{8,0},{1,9},{9,1},{2,10},{10,2},{3,11},{11,3},{4,12},{12,4},... | collective-permute-start | bytes 786440 | tf_op jit(solution)/shard_map/ppermute | solution.py:405
  84.3 15.3 %collective-permute-start.12 = (bf16[64,2048]{1,0:T(8,128)(2,1)S(1)}, bf16[64,2048]{1,0:T(8,128)(2,1)S(1)}, u32[]{:S(2)}, u32[]{:S(2)}) collective-permute-start(bf16[64,2048]{1,0:T(8,128)(2,1)S(1)} %get-tuple-element.196), channel_id=1, source_target_pairs={{0,1},{1,0},{2,3},{3,2},{4,5},{5,4},{6,7},{7,6},{8,9},{9,8},{10,11... | collective-permute-start | bytes 786440 | tf_op jit(solution)/shard_map/ppermute | solution.py:405
  85.5 21.8 %collective-permute-start.13 = (bf16[64,2048]{1,0:T(8,128)(2,1)S(1)}, bf16[64,2048]{1,0:T(8,128)(2,1)S(1)}, u32[]{:S(2)}, u32[]{:S(2)}) collective-permute-start(bf16[64,2048]{1,0:T(8,128)(2,1)S(1)} %get-tuple-element.197), channel_id=1, source_target_pairs={{0,2},{1,3},{2,0},{3,1},{4,6},{5,7},{6,4},{7,5},{8,10},{9,11},{10,... | collective-permute-start | bytes 786440 | tf_op jit(solution)/shard_map/ppermute | solution.py:405
  88.9 18.4 %collective-permute-start.14 = (bf16[64,2048]{1,0:T(8,128)(2,1)S(1)}, bf16[64,2048]{1,0:T(8,128)(2,1)S(1)}, u32[]{:S(2)}, u32[]{:S(2)}) collective-permute-start(bf16[64,2048]{1,0:T(8,128)(2,1)S(1)} %get-tuple-element.198), channel_id=1, source_target_pairs={{0,3},{1,2},{2,1},{3,0},{4,7},{5,6},{6,5},{7,4},{8,11},{9,10},{10,... | collective-permute-start | bytes 786440 | tf_op jit(solution)/shard_map/ppermute | solution.py:405
  94.9 34.9 %collective-permute-start.22 = (bf16[64,2048]{1,0:T(8,128)(2,1)S(1)}, bf16[64,2048]{1,0:T(8,128)(2,1)S(1)}, u32[]{:S(2)}, u32[]{:S(2)}) collective-permute-start(bf16[64,2048]{1,0:T(8,128)(2,1)S(1)} %get-tuple-element.224.refs_0_), channel_id=1, source_target_pairs={{0,1},{1,0},{2,3},{3,2},{4,5},{5,4},{6,7},{7,6},{8,9},{9,8},{10,11... | collective-permute-start | bytes 786440 | tf_op jit(solution)/shard_map/ppermute | solution.py:405
  96.0 33.8 %collective-permute-start.23 = (bf16[64,2048]{1,0:T(8,128)(2,1)S(1)}, bf16[64,2048]{1,0:T(8,128)(2,1)S(1)}, u32[]{:S(2)}, u32[]{:S(2)}) collective-permute-start(bf16[64,2048]{1,0:T(8,128)(2,1)S(1)} %get-tuple-element.224.refs_0_), channel_id=1, source_target_pairs={{0,2},{1,3},{2,0},{3,1},{4,6},{5,7},{6,4},{7,5},{8,10},{9,11},{10,... | collective-permute-start | bytes 786440 | tf_op jit(solution)/shard_map/ppermute | solution.py:405
  99.6 32.1 %collective-permute-start.25 = (bf16[64,2048]{1,0:T(8,128)(2,1)S(1)}, bf16[64,2048]{1,0:T(8,128)(2,1)S(1)}, u32[]{:S(2)}, u32[]{:S(2)}) collective-permute-start(bf16[64,2048]{1,0:T(8,128)(2,1)S(1)} %get-tuple-element.224.refs_0_), channel_id=1, source_target_pairs={{0,4},{4,0},{1,5},{5,1},{2,6},{6,2},{3,7},{7,3},{8,12},{12,8},{9,1... | collective-permute-start | bytes 786440 | tf_op jit(solution)/shard_map/ppermute | solution.py:405
  107.6 27.3 %collective-permute-start.16 = (bf16[64,2048]{1,0:T(8,128)(2,1)S(1)}, bf16[64,2048]{1,0:T(8,128)(2,1)S(1)}, u32[]{:S(2)}, u32[]{:S(2)}) collective-permute-start(bf16[64,2048]{1,0:T(8,128)(2,1)S(1)} %get-tuple-element.201.refs_0_), channel_id=1, source_target_pairs={{0,2},{1,3},{2,0},{3,1},{4,6},{5,7},{6,4},{7,5},{8,10},{9,11},{10,... | collective-permute-start | bytes 786440 | tf_op jit(solution)/shard_map/ppermute | solution.py:405
  130.5 12.0 %collective-permute-start.27 = (bf16[64,2048]{1,0:T(8,128)(2,1)S(1)}, bf16[64,2048]{1,0:T(8,128)(2,1)S(1)}, u32[]{:S(2)}, u32[]{:S(2)}) collective-permute-start(bf16[64,2048]{1,0:T(8,128)(2,1)S(1)} %collective-permute-done.23.refs_2_), channel_id=1, source_target_pairs={{0,4},{4,0},{1,5},{5,1},{2,6},{6,2},{3,7},{7,3},{8,12},{12,8},{9,1... | collective-permute-start | bytes 786440 | tf_op jit(solution)/shard_map/ppermute | solution.py:405
  132.4 13.8 %collective-permute-start.15 = (bf16[64,2048]{1,0:T(8,128)(2,1)S(1)}, bf16[64,2048]{1,0:T(8,128)(2,1)S(1)}, u32[]{:S(2)}, u32[]{:S(2)}) collective-permute-start(bf16[64,2048]{1,0:T(8,128)(2,1)S(1)} %get-tuple-element.201.refs_0_), channel_id=1, source_target_pairs={{0,1},{1,0},{2,3},{3,2},{4,5},{5,4},{6,7},{7,6},{8,9},{9,8},{10,11... | collective-permute-start | bytes 786440 | tf_op jit(solution)/shard_map/ppermute | solution.py:405
  134.9 16.7 %collective-permute-start.17 = (bf16[64,2048]{1,0:T(8,128)(2,1)S(1)}, bf16[64,2048]{1,0:T(8,128)(2,1)S(1)}, u32[]{:S(2)}, u32[]{:S(2)}) collective-permute-start(bf16[64,2048]{1,0:T(8,128)(2,1)S(1)} %collective-permute-done.16.refs_2_), channel_id=1, source_target_pairs={{0,1},{1,0},{2,3},{3,2},{4,5},{5,4},{6,7},{7,6},{8,9},{9,8},{10,11... | collective-permute-start | bytes 786440 | tf_op jit(solution)/shard_map/ppermute | solution.py:405
  183.2 13.6 %collective-permute-start.30 = (bf16[64,2048]{1,0:T(8,128)(2,1)S(1)}, bf16[64,2048]{1,0:T(8,128)(2,1)S(1)}, u32[]{:S(2)}, u32[]{:S(2)}) collective-permute-start(bf16[64,2048]{1,0:T(8,128)(2,1)S(1)} %get-tuple-element.212), channel_id=1, source_target_pairs={{0,1},{1,0},{2,3},{3,2},{4,5},{5,4},{6,7},{7,6},{8,9},{9,8},{10,11... | collective-permute-start | bytes 786440 | tf_op jit(solution)/shard_map/ppermute | solution.py:405
  184.7 21.3 %collective-permute-start.31 = (bf16[64,2048]{1,0:T(8,128)(2,1)S(1)}, bf16[64,2048]{1,0:T(8,128)(2,1)S(1)}, u32[]{:S(2)}, u32[]{:S(2)}) collective-permute-start(bf16[64,2048]{1,0:T(8,128)(2,1)S(1)} %get-tuple-element.213), channel_id=1, source_target_pairs={{0,2},{1,3},{2,0},{3,1},{4,6},{5,7},{6,4},{7,5},{8,10},{9,11},{10,... | collective-permute-start | bytes 786440 | tf_op jit(solution)/shard_map/ppermute | solution.py:405
  187.1 18.9 %collective-permute-start.32 = (bf16[64,2048]{1,0:T(8,128)(2,1)S(1)}, bf16[64,2048]{1,0:T(8,128)(2,1)S(1)}, u32[]{:S(2)}, u32[]{:S(2)}) collective-permute-start(bf16[64,2048]{1,0:T(8,128)(2,1)S(1)} %get-tuple-element.214), channel_id=1, source_target_pairs={{0,3},{1,2},{2,1},{3,0},{4,7},{5,6},{6,5},{7,4},{8,11},{9,10},{10,... | collective-permute-start | bytes 786440 | tf_op jit(solution)/shard_map/ppermute | solution.py:405
  206.4 17.7 %collective-permute-start.34 = (bf16[64,2048]{1,0:T(8,128)(2,1)S(1)}, bf16[64,2048]{1,0:T(8,128)(2,1)S(1)}, u32[]{:S(2)}, u32[]{:S(2)}) collective-permute-start(bf16[64,2048]{1,0:T(8,128)(2,1)S(1)} %get-tuple-element.216.refs_0_), channel_id=1, source_target_pairs={{0,2},{1,3},{2,0},{3,1},{4,6},{5,7},{6,4},{7,5},{8,10},{9,11},{10,... | collective-permute-start | bytes 786440 | tf_op jit(solution)/shard_map/ppermute | solution.py:405
  212.7 12.0 %collective-permute-start.33 = (bf16[64,2048]{1,0:T(8,128)(2,1)S(1)}, bf16[64,2048]{1,0:T(8,128)(2,1)S(1)}, u32[]{:S(2)}, u32[]{:S(2)}) collective-permute-start(bf16[64,2048]{1,0:T(8,128)(2,1)S(1)} %get-tuple-element.216.refs_0_), channel_id=1, source_target_pairs={{0,1},{1,0},{2,3},{3,2},{4,5},{5,4},{6,7},{7,6},{8,9},{9,8},{10,11... | collective-permute-start | bytes 786440 | tf_op jit(solution)/shard_map/ppermute | solution.py:405
  248.5 12.4 %collective-permute-start.41 = (bf16[64,2048]{1,0:T(8,128)(2,1)S(1)}, bf16[64,2048]{1,0:T(8,128)(2,1)S(1)}, u32[]{:S(2)}, u32[]{:S(2)}) collective-permute-start(bf16[64,2048]{1,0:T(8,128)(2,1)S(1)} %get-tuple-element.220), channel_id=1, source_target_pairs={{0,1},{1,0},{2,3},{3,2},{4,5},{5,4},{6,7},{7,6},{8,9},{9,8},{10,11... | collective-permute-start | bytes 786440 | tf_op jit(solution)/shard_map/ppermute | solution.py:405
  248.6 21.4 %collective-permute-start.42 = (bf16[64,2048]{1,0:T(8,128)(2,1)S(1)}, bf16[64,2048]{1,0:T(8,128)(2,1)S(1)}, u32[]{:S(2)}, u32[]{:S(2)}) collective-permute-start(bf16[64,2048]{1,0:T(8,128)(2,1)S(1)} %get-tuple-element.221), channel_id=1, source_target_pairs={{0,2},{1,3},{2,0},{3,1},{4,6},{5,7},{6,4},{7,5},{8,10},{9,11},{10,... | collective-permute-start | bytes 786440 | tf_op jit(solution)/shard_map/ppermute | solution.py:405
  249.9 20.1 %collective-permute-start.43 = (bf16[64,2048]{1,0:T(8,128)(2,1)S(1)}, bf16[64,2048]{1,0:T(8,128)(2,1)S(1)}, u32[]{:S(2)}, u32[]{:S(2)}) collective-permute-start(bf16[64,2048]{1,0:T(8,128)(2,1)S(1)} %get-tuple-element.222), channel_id=1, source_target_pairs={{0,3},{1,2},{2,1},{3,0},{4,7},{5,6},{6,5},{7,4},{8,11},{9,10},{10,... | collective-permute-start | bytes 786440 | tf_op jit(solution)/shard_map/ppermute | solution.py:405
  270.4 16.8 %collective-permute-start.45 = (bf16[64,2048]{1,0:T(8,128)(2,1)S(1)}, bf16[64,2048]{1,0:T(8,128)(2,1)S(1)}, u32[]{:S(2)}, u32[]{:S(2)}) collective-permute-start(bf16[64,2048]{1,0:T(8,128)(2,1)S(1)} %get-tuple-element.232.refs_0_), channel_id=1, source_target_pairs={{0,2},{1,3},{2,0},{3,1},{4,6},{5,7},{6,4},{7,5},{8,10},{9,11},{10,... | collective-permute-start | bytes 786440 | tf_op jit(solution)/shard_map/ppermute | solution.py:405
  275.7 11.9 %collective-permute-start.44 = (bf16[64,2048]{1,0:T(8,128)(2,1)S(1)}, bf16[64,2048]{1,0:T(8,128)(2,1)}, u32[]{:S(2)}, u32[]{:S(2)}) collective-permute-start(bf16[64,2048]{1,0:T(8,128)(2,1)S(1)} %get-tuple-element.232.refs_0_), channel_id=1, source_target_pairs={{0,1},{1,0},{2,3},{3,2},{4,5},{5,4},{6,7},{7,6},{8,9},{9,8},{10,11... | collective-permute-start | bytes 786440 | tf_op jit(solution)/shard_map/ppermute | solution.py:405
  287.1 36.1 %collective-permute-start.47 = (bf16[64,2048]{1,0:T(8,128)(2,1)S(1)}, bf16[64,2048]{1,0:T(8,128)(2,1)}, u32[]{:S(2)}, u32[]{:S(2)}) collective-permute-start(bf16[64,2048]{1,0:T(8,128)(2,1)S(1)} %get-tuple-element.232.refs_0_), channel_id=1, source_target_pairs={{0,4},{4,0},{1,5},{5,1},{2,6},{6,2},{3,7},{7,3},{8,12},{12,8},{9,1... | collective-permute-start | bytes 786440 | tf_op jit(solution)/shard_map/ppermute | solution.py:405
  287.1 36.1 %collective-permute-start.49 = (bf16[64,2048]{1,0:T(8,128)(2,1)S(1)}, bf16[64,2048]{1,0:T(8,128)(2,1)}, u32[]{:S(2)}, u32[]{:S(2)}) collective-permute-start(bf16[64,2048]{1,0:T(8,128)(2,1)S(1)} %collective-permute-done.45.refs_2_), channel_id=1, source_target_pairs={{0,4},{4,0},{1,5},{5,1},{2,6},{6,2},{3,7},{7,3},{8,12},{12,8},{9,1... | collective-permute-start | bytes 786440 | tf_op jit(solution)/shard_map/ppermute | solution.py:405
  287.7 35.6 %collective-permute-start.48 = (bf16[64,2048]{1,0:T(8,128)(2,1)}, bf16[64,2048]{1,0:T(8,128)(2,1)}, u32[]{:S(2)}, u32[]{:S(2)}) collective-permute-start(bf16[64,2048]{1,0:T(8,128)(2,1)} %collective-permute-done.44.refs_1_), channel_id=1, source_target_pairs={{0,4},{4,0},{1,5},{5,1},{2,6},{6,2},{3,7},{7,3},{8,12},{12,8},{9,1... | collective-permute-start | bytes 786440 | tf_op jit(solution)/shard_map/ppermute | solution.py:405
  294.1 29.2 %collective-permute-start.50 = (bf16[64,2048]{1,0:T(8,128)(2,1)}, bf16[64,2048]{1,0:T(8,128)(2,1)}, u32[]{:S(2)}, u32[]{:S(2)}) collective-permute-start(bf16[64,2048]{1,0:T(8,128)(2,1)} %collective-permute-done.46.refs_3_), channel_id=1, source_target_pairs={{0,4},{4,0},{1,5},{5,1},{2,6},{6,2},{3,7},{7,3},{8,12},{12,8},{9,1... | collective-permute-start | bytes 786440 | tf_op jit(solution)/shard_map/ppermute | solution.py:405
  336.3 28.2 %collective-permute-start.52 = (bf16[64,2048]{1,0:T(8,128)(2,1)}, bf16[64,2048]{1,0:T(8,128)(2,1)}, u32[]{:S(2)}, u32[]{:S(2)}) collective-permute-start(bf16[64,2048]{1,0:T(8,128)(2,1)} %get-tuple-element.240), channel_id=1, source_target_pairs={{0,1},{1,0},{2,3},{3,2},{4,5},{5,4},{6,7},{7,6},{8,9},{9,8},{10,11... | collective-permute-start | bytes 786440 | tf_op jit(solution)/shard_map/ppermute | solution.py:405
  337.8 26.7 %collective-permute-start.53 = (bf16[64,2048]{1,0:T(8,128)(2,1)}, bf16[64,2048]{1,0:T(8,128)(2,1)}, u32[]{:S(2)}, u32[]{:S(2)}) collective-permute-start(bf16[64,2048]{1,0:T(8,128)(2,1)} %get-tuple-element.241), channel_id=1, source_target_pairs={{0,2},{1,3},{2,0},{3,1},{4,6},{5,7},{6,4},{7,5},{8,10},{9,11},{10,... | collective-permute-start | bytes 786440 | tf_op jit(solution)/shard_map/ppermute | solution.py:405
  340.2 24.3 %collective-permute-start.54 = (bf16[64,2048]{1,0:T(8,128)(2,1)}, bf16[64,2048]{1,0:T(8,128)(2,1)}, u32[]{:S(2)}, u32[]{:S(2)}) collective-permute-start(bf16[64,2048]{1,0:T(8,128)(2,1)} %get-tuple-element.242), channel_id=1, source_target_pairs={{0,3},{1,2},{2,1},{3,0},{4,7},{5,6},{6,5},{7,4},{8,11},{9,10},{10,... | collective-permute-start | bytes 786440 | tf_op jit(solution)/shard_map/ppermute | solution.py:405
  364.5 190.1 %reduce-scatter.5.cloned.1.call-start = ((), (), s32[]{:S(2)}) async-start(), calls=%async_computation.8 | async-start | bytes 5242880 | tf_op jit(solution)/shard_map/reduce_scatter | solution.py:581
  369.4 13.5 %collective-permute-start.56 = (bf16[64,2048]{1,0:T(8,128)(2,1)S(1)}, bf16[64,2048]{1,0:T(8,128)(2,1)S(1)}, u32[]{:S(2)}, u32[]{:S(2)}) collective-permute-start(bf16[64,2048]{1,0:T(8,128)(2,1)S(1)} %get-tuple-element.249), channel_id=1, source_target_pairs={{0,1},{1,0},{2,3},{3,2},{4,5},{5,4},{6,7},{7,6},{8,9},{9,8},{10,11... | collective-permute-start | bytes 786440 | tf_op jit(solution)/shard_map/ppermute | solution.py:405
  370.0 21.7 %collective-permute-start.57 = (bf16[64,2048]{1,0:T(8,128)(2,1)S(1)}, bf16[64,2048]{1,0:T(8,128)(2,1)S(1)}, u32[]{:S(2)}, u32[]{:S(2)}) collective-permute-start(bf16[64,2048]{1,0:T(8,128)(2,1)S(1)} %get-tuple-element.250), channel_id=1, source_target_pairs={{0,2},{1,3},{2,0},{3,1},{4,6},{5,7},{6,4},{7,5},{8,10},{9,11},{10,... | collective-permute-start | bytes 786440 | tf_op jit(solution)/shard_map/ppermute | solution.py:405
  373.4 18.4 %collective-permute-start.58 = (bf16[64,2048]{1,0:T(8,128)(2,1)S(1)}, bf16[64,2048]{1,0:T(8,128)(2,1)S(1)}, u32[]{:S(2)}, u32[]{:S(2)}) collective-permute-start(bf16[64,2048]{1,0:T(8,128)(2,1)S(1)} %get-tuple-element.251), channel_id=1, source_target_pairs={{0,3},{1,2},{2,1},{3,0},{4,7},{5,6},{6,5},{7,4},{8,11},{9,10},{10,... | collective-permute-start | bytes 786440 | tf_op jit(solution)/shard_map/ppermute | solution.py:405
  393.2 18.0 %collective-permute-start.60 = (bf16[64,2048]{1,0:T(8,128)(2,1)S(1)}, bf16[64,2048]{1,0:T(8,128)(2,1)S(1)}, u32[]{:S(2)}, u32[]{:S(2)}) collective-permute-start(bf16[64,2048]{1,0:T(8,128)(2,1)S(1)} %get-tuple-element.253.refs_0_), channel_id=1, source_target_pairs={{0,2},{1,3},{2,0},{3,1},{4,6},{5,7},{6,4},{7,5},{8,10},{9,11},{10,... | collective-permute-start | bytes 786440 | tf_op jit(solution)/shard_map/ppermute | solution.py:405
  399.6 12.1 %collective-permute-start.59 = (bf16[64,2048]{1,0:T(8,128)(2,1)S(1)}, bf16[64,2048]{1,0:T(8,128)(2,1)S(1)}, u32[]{:S(2)}, u32[]{:S(2)}) collective-permute-start(bf16[64,2048]{1,0:T(8,128)(2,1)S(1)} %get-tuple-element.253.refs_0_), channel_id=1, source_target_pairs={{0,1},{1,0},{2,3},{3,2},{4,5},{5,4},{6,7},{7,6},{8,9},{9,8},{10,11... | collective-permute-start | bytes 786440 | tf_op jit(solution)/shard_map/ppermute | solution.py:405
  438.6 13.0 %collective-permute-start.67 = (bf16[64,2048]{1,0:T(8,128)(2,1)}, bf16[64,2048]{1,0:T(8,128)(2,1)S(1)}, u32[]{:S(2)}, u32[]{:S(2)}) collective-permute-start(bf16[64,2048]{1,0:T(8,128)(2,1)} %get-tuple-element.260), channel_id=1, source_target_pairs={{0,1},{1,0},{2,3},{3,2},{4,5},{5,4},{6,7},{7,6},{8,9},{9,8},{10,11... | collective-permute-start | bytes 786440 | tf_op jit(solution)/shard_map/ppermute | solution.py:405
  438.8 21.7 %collective-permute-start.68 = (bf16[64,2048]{1,0:T(8,128)(2,1)}, bf16[64,2048]{1,0:T(8,128)(2,1)}, u32[]{:S(2)}, u32[]{:S(2)}) collective-permute-start(bf16[64,2048]{1,0:T(8,128)(2,1)} %get-tuple-element.261), channel_id=1, source_target_pairs={{0,2},{1,3},{2,0},{3,1},{4,6},{5,7},{6,4},{7,5},{8,10},{9,11},{10,... | collective-permute-start | bytes 786440 | tf_op jit(solution)/shard_map/ppermute | solution.py:405
  440.6 19.9 %collective-permute-start.69 = (bf16[64,2048]{1,0:T(8,128)(2,1)}, bf16[64,2048]{1,0:T(8,128)(2,1)}, u32[]{:S(2)}, u32[]{:S(2)}) collective-permute-start(bf16[64,2048]{1,0:T(8,128)(2,1)} %get-tuple-element.262), channel_id=1, source_target_pairs={{0,3},{1,2},{2,1},{3,0},{4,7},{5,6},{6,5},{7,4},{8,11},{9,10},{10,... | collective-permute-start | bytes 786440 | tf_op jit(solution)/shard_map/ppermute | solution.py:405
  460.5 176.8 %reduce-scatter.9.cloned.1.call-start = ((), (), s32[]{:S(2)}) async-start(), calls=%async_computation.10 | async-start | bytes 11141120 | tf_op jit(solution)/shard_map/reduce_scatter | solution.py:581
  464.3 16.5 %collective-permute-start.71 = (bf16[64,2048]{1,0:T(8,128)(2,1)S(1)}, bf16[64,2048]{1,0:T(8,128)(2,1)S(1)}, u32[]{:S(2)}, u32[]{:S(2)}) collective-permute-start(bf16[64,2048]{1,0:T(8,128)(2,1)S(1)} %get-tuple-element.276.refs_0_), channel_id=1, source_target_pairs={{0,2},{1,3},{2,0},{3,1},{4,6},{5,7},{6,4},{7,5},{8,10},{9,11},{10,... | collective-permute-start | bytes 786440 | tf_op jit(solution)/shard_map/ppermute | solution.py:405
  503.7 14.8 %collective-permute-start.78 = (bf16[64,2048]{1,0:T(8,128)(2,1)}, bf16[64,2048]{1,0:T(8,128)(2,1)S(1)}, u32[]{:S(2)}, u32[]{:S(2)}) collective-permute-start(bf16[64,2048]{1,0:T(8,128)(2,1)} %get-tuple-element.281), channel_id=1, source_target_pairs={{0,1},{1,0},{2,3},{3,2},{4,5},{5,4},{6,7},{7,6},{8,9},{9,8},{10,11... | collective-permute-start | bytes 786440 | tf_op jit(solution)/shard_map/ppermute | solution.py:405
  504.5 21.6 %collective-permute-start.79 = (bf16[64,2048]{1,0:T(8,128)(2,1)}, bf16[64,2048]{1,0:T(8,128)(2,1)}, u32[]{:S(2)}, u32[]{:S(2)}) collective-permute-start(bf16[64,2048]{1,0:T(8,128)(2,1)} %get-tuple-element.282), channel_id=1, source_target_pairs={{0,2},{1,3},{2,0},{3,1},{4,6},{5,7},{6,4},{7,5},{8,10},{9,11},{10,... | collective-permute-start | bytes 786440 | tf_op jit(solution)/shard_map/ppermute | solution.py:405
  507.5 18.7 %collective-permute-start.80 = (bf16[64,2048]{1,0:T(8,128)(2,1)}, bf16[64,2048]{1,0:T(8,128)(2,1)}, u32[]{:S(2)}, u32[]{:S(2)}) collective-permute-start(bf16[64,2048]{1,0:T(8,128)(2,1)} %get-tuple-element.283), channel_id=1, source_target_pairs={{0,3},{1,2},{2,1},{3,0},{4,7},{5,6},{6,5},{7,4},{8,11},{9,10},{10,... | collective-permute-start | bytes 786440 | tf_op jit(solution)/shard_map/ppermute | solution.py:405
  526.2 165.0 %reduce-scatter.11.cloned.1.call-start = ((), (), s32[]{:S(2)}) async-start(), calls=%async_computation.11 | async-start | bytes 5242880 | tf_op jit(solution)/shard_map/reduce_scatter | solution.py:581
  529.6 24.9 %collective-permute-start.82 = (bf16[64,2048]{1,0:T(8,128)(2,1)}, bf16[64,2048]{1,0:T(8,128)(2,1)}, u32[]{:S(2)}, u32[]{:S(2)}) collective-permute-start(bf16[64,2048]{1,0:T(8,128)(2,1)} %get-tuple-element.299.refs_0_), channel_id=1, source_target_pairs={{0,2},{1,3},{2,0},{3,1},{4,6},{5,7},{6,4},{7,5},{8,10},{9,11},{10,... | collective-permute-start | bytes 786440 | tf_op jit(solution)/shard_map/ppermute | solution.py:405
  537.8 28.6 %collective-permute-start.89 = (bf16[256,2176]{1,0:T(8,128)(2,1)S(1)}, bf16[256,2176]{1,0:T(8,128)(2,1)}, u32[]{:S(2)}, u32[]{:S(2)}) collective-permute-start(bf16[256,2176]{1,0:T(8,128)(2,1)S(1)} %shard_map.230), channel_id=1, source_target_pairs={{0,4},{4,0},{1,5},{5,1},{2,6},{6,2},{3,7},{7,3},{8,12},{12,8},{9,1... | collective-permute-start | bytes 3342344 | tf_op jit(solution)/shard_map/ppermute | solution.py:405
  539.1 19.5 %collective-permute-start.91 = (bf16[64,2048]{1,0:T(8,128)(2,1)S(1)}, bf16[64,2048]{1,0:T(8,128)(2,1)S(1)}, u32[]{:S(2)}, u32[]{:S(2)}) collective-permute-start(bf16[64,2048]{1,0:T(8,128)(2,1)S(1)} %add_convert_fusion), channel_id=1, source_target_pairs={{0,2},{1,3},{2,0},{3,1},{4,6},{5,7},{6,4},{7,5},{8,10},{9,11},{10,... | collective-permute-start | bytes 786440 | tf_op jit(solution)/shard_map/ppermute | solution.py:405
  539.3 19.3 %collective-permute-start.81 = (bf16[64,2048]{1,0:T(8,128)(2,1)}, bf16[64,2048]{1,0:T(8,128)(2,1)S(1)}, u32[]{:S(2)}, u32[]{:S(2)}) collective-permute-start(bf16[64,2048]{1,0:T(8,128)(2,1)} %get-tuple-element.299.refs_0_), channel_id=1, source_target_pairs={{0,1},{1,0},{2,3},{3,2},{4,5},{5,4},{6,7},{7,6},{8,9},{9,8},{10,11... | collective-permute-start | bytes 786440 | tf_op jit(solution)/shard_map/ppermute | solution.py:405
  541.4 17.8 %collective-permute-start.84 = (bf16[64,2048]{1,0:T(8,128)(2,1)}, bf16[64,2048]{1,0:T(8,128)(2,1)S(1)}, u32[]{:S(2)}, u32[]{:S(2)}) collective-permute-start(bf16[64,2048]{1,0:T(8,128)(2,1)} %get-tuple-element.299.refs_0_), channel_id=1, source_target_pairs={{0,4},{4,0},{1,5},{5,1},{2,6},{6,2},{3,7},{7,3},{8,12},{12,8},{9,1... | collective-permute-start | bytes 786440 | tf_op jit(solution)/shard_map/ppermute | solution.py:405
  564.2 16.1 %collective-permute-start.90 = (bf16[64,2048]{1,0:T(8,128)(2,1)S(1)}, bf16[64,2048]{1,0:T(8,128)(2,1)S(1)}, u32[]{:S(2)}, u32[]{:S(2)}) collective-permute-start(bf16[64,2048]{1,0:T(8,128)(2,1)S(1)} %add_convert_fusion), channel_id=1, source_target_pairs={{0,1},{1,0},{2,3},{3,2},{4,5},{5,4},{6,7},{7,6},{8,9},{9,8},{10,11... | collective-permute-start | bytes 786440 | tf_op jit(solution)/shard_map/ppermute | solution.py:405
  564.4 16.0 %collective-permute-start.92 = (bf16[64,2048]{1,0:T(8,128)(2,1)S(1)}, bf16[64,2048]{1,0:T(8,128)(2,1)S(1)}, u32[]{:S(2)}, u32[]{:S(2)}) collective-permute-start(bf16[64,2048]{1,0:T(8,128)(2,1)S(1)} %collective-permute-done.91), channel_id=1, source_target_pairs={{0,1},{1,0},{2,3},{3,2},{4,5},{5,4},{6,7},{7,6},{8,9},{9,8},{10,11... | collective-permute-start | bytes 786440 | tf_op jit(solution)/shard_map/ppermute | solution.py:405
  585.5 13.4 %collective-permute-start.94 = (bf16[64,2048]{1,0:T(8,128)(2,1)}, bf16[64,2048]{1,0:T(8,128)(2,1)S(1)}, u32[]{:S(2)}, u32[]{:S(2)}) collective-permute-start(bf16[64,2048]{1,0:T(8,128)(2,1)} %get-tuple-element.323), channel_id=1, source_target_pairs={{0,1},{1,0},{2,3},{3,2},{4,5},{5,4},{6,7},{7,6},{8,9},{9,8},{10,11... | collective-permute-start | bytes 786440 | tf_op jit(solution)/shard_map/ppermute | solution.py:405
  585.6 21.6 %collective-permute-start.95 = (bf16[64,2048]{1,0:T(8,128)(2,1)}, bf16[64,2048]{1,0:T(8,128)(2,1)S(1)}, u32[]{:S(2)}, u32[]{:S(2)}) collective-permute-start(bf16[64,2048]{1,0:T(8,128)(2,1)} %get-tuple-element.324), channel_id=1, source_target_pairs={{0,2},{1,3},{2,0},{3,1},{4,6},{5,7},{6,4},{7,5},{8,10},{9,11},{10,... | collective-permute-start | bytes 786440 | tf_op jit(solution)/shard_map/ppermute | solution.py:405
  587.9 19.2 %collective-permute-start.96 = (bf16[64,2048]{1,0:T(8,128)(2,1)S(1)}, bf16[64,2048]{1,0:T(8,128)(2,1)S(1)}, u32[]{:S(2)}, u32[]{:S(2)}) collective-permute-start(bf16[64,2048]{1,0:T(8,128)(2,1)S(1)} %get-tuple-element.325), channel_id=1, source_target_pairs={{0,3},{1,2},{2,1},{3,0},{4,7},{5,6},{6,5},{7,4},{8,11},{9,10},{10,... | collective-permute-start | bytes 786440 | tf_op jit(solution)/shard_map/ppermute | solution.py:405
  610.3 18.6 %collective-permute-start.98 = (bf16[72,2048]{1,0:T(8,128)(2,1)S(1)}, bf16[72,2048]{1,0:T(8,128)(2,1)S(1)}, u32[]{:S(2)}, u32[]{:S(2)}) collective-permute-start(bf16[72,2048]{1,0:T(8,128)(2,1)S(1)} %concatenate.41), channel_id=1, source_target_pairs={{0,2},{1,3},{2,0},{3,1},{4,6},{5,7},{6,4},{7,5},{8,10},{9,11},{10,... | collective-permute-start | bytes 884744 | tf_op jit(solution)/shard_map/ppermute | solution.py:405
  616.1 20.5 %collective-permute-start.100 = (bf16[128,2048]{1,0:T(8,128)(2,1)S(1)}, bf16[128,2048]{1,0:T(8,128)(2,1)S(1)}, u32[]{:S(2)}, u32[]{:S(2)}) collective-permute-start(bf16[128,2048]{1,0:T(8,128)(2,1)S(1)} %get-tuple-element.414), channel_id=1, source_target_pairs={{0,8},{8,0},{1,9},{9,1},{2,10},{10,2},{3,11},{11,3},{4,12},{12,4},... | collective-permute-start | bytes 1572872 | tf_op jit(solution)/shard_map/ppermute | solution.py:405
  617.5 19.1 %collective-permute-start.97 = (bf16[72,2048]{1,0:T(8,128)(2,1)S(1)}, bf16[72,2048]{1,0:T(8,128)(2,1)S(1)}, u32[]{:S(2)}, u32[]{:S(2)}) collective-permute-start(bf16[72,2048]{1,0:T(8,128)(2,1)S(1)} %concatenate.41), channel_id=1, source_target_pairs={{0,1},{1,0},{2,3},{3,2},{4,5},{5,4},{6,7},{7,6},{8,9},{9,8},{10,11... | collective-permute-start | bytes 884744 | tf_op jit(solution)/shard_map/ppermute | solution.py:405
  640.2 28.7 %collective-permute-start.101 = (bf16[137,2048]{1,0:T(8,128)(2,1)S(1)}, bf16[137,2048]{1,0:T(8,128)(2,1)S(1)}, u32[]{:S(2)}, u32[]{:S(2)}) collective-permute-start(bf16[137,2048]{1,0:T(8,128)(2,1)S(1)} %pad_maximum_fusion.3), channel_id=1, source_target_pairs={{0,8},{8,0},{1,9},{9,1},{2,10},{10,2},{3,11},{11,3},{4,12},{12,4},... | collective-permute-start | bytes 1683464 | tf_op jit(solution)/shard_map/ppermute | solution.py:405
  (141 other events, 838.5 us)
Sparse Core Ops, SparseCore 0:
  10.5 57.0 all-gather.4
  70.1 99.6 all-gather.6
  172.2 54.7 all-gather.8
  229.3 93.9 all-gather.10
  364.7 90.7 reduce-scatter.6
  460.6 54.7 reduce-scatter.4
  526.3 94.0 reduce-scatter.8
  623.7 67.5 reduce-scatter.10

commit v8 on v7

--- a/solution.py
+++ b/solution.py
@@ -78,6 +78,27 @@
         src, dst = weights.at[pl.ds(at, BLOCK), cols], whole.at[pl.ds(at, BLOCK)]
         copies.append(pltpu.make_async_copy(src, dst, sems.at[first + len(copies)]))
     return copies
+
+
+def shared_tile_into(weights, whole, sems, first):
+    rows, width = whole.shape
+    main = width - 128
+    core = lax.axis_index("clo")
+    own = pl.ds(pl.multiple_of(core * width, 128), main)
+    copies = []
+    for at in range(0, rows, BLOCK):
+        block = pl.ds(at, BLOCK)
+        for cols, to in ((own, pl.ds(0, main)), (pl.ds(main, 128), pl.ds(main, 128))):
+            src, dst = weights.at[block, cols], whole.at[block, to]
+            copies.append(pltpu.make_async_copy(src, dst, sems.at[first + len(copies)]))
+    return copies
+
+
+def settle_tile(whole, rows):
+    tile = whole[rows, whole.shape[1] - 128 :].astype(F32)
+    rolled_tile = pltpu.roll(tile, 64, 1)
+    tile = jnp.where(lax.axis_index("clo") == 0, tile, rolled_tile)
+    whole[rows, whole.shape[1] - 128 :] = tile.astype(LOW)
 
 
 def start_all(copies):
@@ -224,12 +245,14 @@
     full_o, gu_o, z_o, own_o, send_o, h_s, w_s, acc, sems = refs
     units = z_o.shape[1]
     copies = into_rows(h_parts, h_s, sems, 0)
-    w_copies = weights_into(weights, w_s, sems, n_h)
+    w_copies = shared_tile_into(weights, w_s, sems, n_h)
     start_all(copies + w_copies)
     wait_all(copies)
     whole = pltpu.make_async_copy(h_s, full_o, sems.at[0])
     whole.start()
-    for r, rows in block_rows(w_s, w_copies):
+    for r, rows in block_rows(w_s):
+        wait_all(w_copies[2 * r : 2 * r + 2])
+        settle_tile(w_s, rows)
         part = nn(h_s[:, rows], w_s[rows, : 2 * units])
         acc[...] = part if r == 0 else acc[...] + part
     gu_o[...] = acc[...].astype(LOW)
@@ -247,13 +270,15 @@
     gu_i, full_o, dp_o, own_o, send_o, d_s, w_s, acc, gu, sems = refs
     units = acc.shape[1]
     copies = into_rows(d_parts, d_s, sems, 0)
-    w_copies = weights_into(weights, w_s, sems, n_h)
+    w_copies = shared_tile_into(weights, w_s, sems, n_h)
     extra = load([(gu_i, gu)], sems, n_h + len(w_copies))
     start_all(copies + w_copies + extra)
     wait_all(copies)
     whole = pltpu.make_async_copy(d_s, full_o, sems.at[0])
     whole.start()
-    for r, rows in block_rows(w_s, w_copies):
+    for r, rows in block_rows(w_s):
+        wait_all(w_copies[2 * r : 2 * r + 2])
+        settle_tile(w_s, rows)
         part = nn(d_s[:, rows], w_s[rows, 2 * units : 3 * units])
         acc[...] = part if r == 0 else acc[...] + part
     wait_all(extra)
@@ -491,10 +516,10 @@
 
         def mlp_columns(l):
             gu, down = jnp.transpose(gate_up_weight[l], (1, 0, 2)), down_weight[l]
-            fill = jnp.zeros((rows_dev, pad), LOW)
-            parts = []
-            for cols in (slice(None, half_ff), slice(half_ff, None)):
-                parts += [gu[0, :, cols], gu[1, :, cols], down[:, cols], fill]
+            cut = half_ff - 64
+            parts = [gu[0, :, :half_ff], gu[1, :, :half_ff], down[:, :half_ff]]
+            parts += [down[:, half_ff + cut :], gu[0, :, half_ff:], gu[1, :, half_ff:]]
+            parts += [down[:, half_ff : half_ff + cut]]
             return jnp.concatenate(parts, axis=1)
 
         def gather_weights(own):
@@ -554,7 +579,7 @@
 
         act = shape((total, half_in), LOW)
         reduced = [shape((half_total, width), LOW)] * 2
-        sems = pltpu.SemaphoreType.DMA((n_parts + width // BLOCK + 5,))
+        sems = pltpu.SemaphoreType.DMA((n_parts + 2 * (width // BLOCK) + 5,))
         h_scratch = pltpu.VMEM((total, width), LOW)
 
         def mm(*dims):

time: 710 us -> 707 us (level)
  waiting for transfers between devices: 347 us -> 336 us
    all_gather x4, waiting for transfers between devices: 45 us -> 33.9 us  [gather_weights(): return lax.all_gather(own, ('dp', 'chi', 'clo'), axis=0, tiled=True)]
    unnamed x188 -> x210, local copies, waits for them, and re-layouts: 39.9 us -> 44.9 us
where the time goes in v8:
time: 707 us; the launch traced here: 702 us
  waiting for transfers between devices  336 us (48%)
  Pallas kernels  146 us (21%)
  starting transfers between devices  115 us (16%)
  local copies, waits for them, and re-layouts  78.1 us (11%)
  between operations  16.2 us (2%)
  other arithmetic  10.9 us (2%)
    ppermute x106, waiting for transfers between devices, swap(): return lax.ppermute(value, axis, [(i, i ^ bit) for i in range(sizes[axis])])  289 us
    pallas_call x38, Pallas kernels, call(): pl.pallas_call(body, out_shape=tuple(outs), in_specs=[ANY] * n_any + [HBM...  146 us
    ppermute x106, starting transfers between devices, swap(): return lax.ppermute(value, axis, [(i, i ^ bit) for i in range(sizes[axis])])  114 us
    unnamed x210, local copies, waits for them, and re-layouts  44.9 us
    all_gather x4, waiting for transfers between devices, gather_weights(): return lax.all_gather(own, ('dp', 'chi', 'clo'), axis=0, tiled=True)  33.9 us
  transfers between devices with their start and end apart: 114, of which 51 were waited for; matrix products, arithmetic and copies ran while one was open for 6% of the time, Pallas kernels for 19%

profile of v8, /device:TPU:0, one launch (start us, length us, event | category | flops | bytes accessed | tf_op | source)
XLA Modules:
  0.0 701.8 jit_solution(5144870168381239821)
XLA Ops:
  17.2 4.9 concatenate.39
  25.5 4.4 concatenate.40
  31.2 3.0 collective-permute-start.1
  35.2 5.4 collective-permute-done.9
  42.3 2.9 collective-permute-start.3
  47.4 10.2 %collective-permute-done.3.refs_2_ = bf16[64,2048]{1,0:T(8,128)(2,1)S(1)} collective-permute-done((bf16[64,2048]{1,0:T(8,128)(2,1)S(1)}, bf16[64,2048]{1,0:T(8,128)(2,1)S(1)}, u32[]{:S(2)}, u32[]{:S(2)}) %collective-permute-start.3) | collective-permute-done | bytes 262176 | tf_op jit(solution)/shard_map/ppermute | solution.py:430
  59.0 6.3 collective-permute-done.4.refs_3_
  69.2 11.0 %shard_map.205 = (bf16[512,2048]{1,0:T(8,128)(2,1)}, bf16[512,256]{1,0:T(8,128)(2,1)}, bf16[512,256]{1,0:T(8,128)(2,1)}, bf16[512,256]{1,0:T(8,128)(2,1)}, bf16[...) custom-call(bf16[64,2048]{1,0:T(8,128)(2,1)} %copy-done.59, ...), custom_call_target="tpu_custom_call" | custom-call | flops 4294967296 | bytes 16526336 | tf_op jit(solution)/shard_map/pallas_call | solution.py:50
  86.0 3.4 collective-permute-start.13
  89.4 6.0 collective-permute-done
  96.6 3.5 collective-permute-start.23
  100.1 7.7 %collective-permute-done.13.refs_2_ = bf16[64,2048]{1,0:T(8,128)(2,1)S(1)} collective-permute-done((bf16[64,2048]{1,0:T(8,128)(2,1)S(1)}, bf16[64,2048]{1,0:T(8,128)(2,1)S(1)}, u32[]{:S(2)}, u32[]{:S(2)}) %collective-permute-start.13) | collective-permute-done | bytes 262176 | tf_op jit(solution)/shard_map/ppermute | solution.py:430
  108.1 13.1 %collective-permute-start.16 = (bf16[64,2048]{1,0:T(8,128)(2,1)S(1)}, bf16[64,2048]{1,0:T(8,128)(2,1)S(1)}, u32[]{:S(2)}, u32[]{:S(2)}) collective-permute-start(bf16[64,2048]{1,0:T(8,128)(2,1)S(1)} %get-tuple-element.201.refs_0_), channel_id=1, source_target_pairs={{0,2},{1,3},{2,0},{3,1},{4,6},{5,7},{6,4},{7,5},{8,10},{9,11},{10,... | collective-permute-start | bytes 786440 | tf_op jit(solution)/shard_map/ppermute | solution.py:430
  121.2 9.1 %collective-permute-done.23.refs_2_ = bf16[64,2048]{1,0:T(8,128)(2,1)S(1)} collective-permute-done((bf16[64,2048]{1,0:T(8,128)(2,1)S(1)}, bf16[64,2048]{1,0:T(8,128)(2,1)S(1)}, u32[]{:S(2)}, u32[]{:S(2)}) %collective-permute-start.23) | collective-permute-done | bytes 262176 | tf_op jit(solution)/shard_map/ppermute | solution.py:430
  135.4 5.6 collective-permute-done.24.refs_3_
  143.0 3.6 collective-permute-done.15.refs_1_
  147.4 4.8 collective-permute-done.17.refs_3_
  156.5 11.1 %all-gather.7.cloned.1.call-done.refs_8_ = bf16[2048,4224]{1,0:T(8,128)(2,1)} async-done(((bf16[256,4224]{1,0:T(8,128)(2,1)}), bf16[2048,4224]{1,0:T(8,128)(2,1)}) %all-gather.7.cloned.1.call-update) | async-done | bytes 17301520 | tf_op jit(solution)/shard_map/all_gather | solution.py:526
  173.4 7.4 %shard_map.208 = (bf16[512,2048]{1,0:T(8,128)(2,1)S(1)}, bf16[512,1408]{1,0:T(8,128)(2,1)S(1)}, bf16[512,704]{1,0:T(8,128)(2,1)S(1)}, bf16[256,2048]{1,0:T(8,128)(2,1)S(1)}, bf16[256,2048]{1,0:T(8,128)(2,1)S(1)}) custom-call(bf16[64,2048]{1,0:T(8,128)(2,1)S(1)} %get-tuple-element.201.refs_0_, bf16[64,2048]{1,0:T(8,128)(2,1)S(1)} %copy-done.37, ...), custom_call_target="tpu_custom_call" | custom-call | flops 4563402752 | bytes 25755648 | tf_op jit(solution)/shard_map/pallas_call | solution.py:50
  189.5 9.1 %collective-permute-done.30.refs_1_ = bf16[64,2048]{1,0:T(8,128)(2,1)S(1)} collective-permute-done((bf16[64,2048]{1,0:T(8,128)(2,1)S(1)}, bf16[64,2048]{1,0:T(8,128)(2,1)S(1)}, u32[]{:S(2)}, u32[]{:S(2)}) %collective-permute-start.30) | collective-permute-done | bytes 262176 | tf_op jit(solution)/shard_map/ppermute | solution.py:430
  198.6 9.3 %collective-permute-done.31.refs_2_ = bf16[64,2048]{1,0:T(8,128)(2,1)S(1)} collective-permute-done((bf16[64,2048]{1,0:T(8,128)(2,1)S(1)}, bf16[64,2048]{1,0:T(8,128)(2,1)S(1)}, u32[]{:S(2)}, u32[]{:S(2)}) %collective-permute-start.31) | collective-permute-done | bytes 262176 | tf_op jit(solution)/shard_map/ppermute | solution.py:430
  208.3 6.2 collective-permute-start.34
  214.5 11.5 %collective-permute-done.34.refs_2_ = bf16[64,2048]{1,0:T(8,128)(2,1)S(1)} collective-permute-done((bf16[64,2048]{1,0:T(8,128)(2,1)S(1)}, bf16[64,2048]{1,0:T(8,128)(2,1)S(1)}, u32[]{:S(2)}, u32[]{:S(2)}) %collective-permute-start.34) | collective-permute-done | bytes 262176 | tf_op jit(solution)/shard_map/ppermute | solution.py:430
  226.5 6.4 collective-permute-done.35.refs_3_
  234.6 11.6 %shard_map.212 = (bf16[512,2048]{1,0:T(8,128)(2,1)}, bf16[512,256]{1,0:T(8,128)(2,1)}, bf16[512,256]{1,0:T(8,128)(2,1)}, bf16[512,256]{1,0:T(8,128)(2,1)}, bf16[...) custom-call(bf16[64,2048]{1,0:T(8,128)(2,1)} %copy-done.60, ...), custom_call_target="tpu_custom_call" | custom-call | flops 4294967296 | bytes 16526336 | tf_op jit(solution)/shard_map/pallas_call | solution.py:50
  255.0 8.6 %collective-permute-done.41.refs_1_ = bf16[64,2048]{1,0:T(8,128)(2,1)S(1)} collective-permute-done((bf16[64,2048]{1,0:T(8,128)(2,1)S(1)}, bf16[64,2048]{1,0:T(8,128)(2,1)S(1)}, u32[]{:S(2)}, u32[]{:S(2)}) %collective-permute-start.41) | collective-permute-done | bytes 262176 | tf_op jit(solution)/shard_map/ppermute | solution.py:430
  263.5 9.1 %collective-permute-done.42.refs_2_ = bf16[64,2048]{1,0:T(8,128)(2,1)S(1)} collective-permute-done((bf16[64,2048]{1,0:T(8,128)(2,1)S(1)}, bf16[64,2048]{1,0:T(8,128)(2,1)S(1)}, u32[]{:S(2)}, u32[]{:S(2)}) %collective-permute-start.42) | collective-permute-done | bytes 262176 | tf_op jit(solution)/shard_map/ppermute | solution.py:430
  273.0 5.2 collective-permute-start.45
  278.3 11.2 %collective-permute-done.45.refs_2_ = bf16[64,2048]{1,0:T(8,128)(2,1)S(1)} collective-permute-done((bf16[64,2048]{1,0:T(8,128)(2,1)S(1)}, bf16[64,2048]{1,0:T(8,128)(2,1)S(1)}, u32[]{:S(2)}, u32[]{:S(2)}) %collective-permute-start.45) | collective-permute-done | bytes 262176 | tf_op jit(solution)/shard_map/ppermute | solution.py:430
  290.2 6.1 collective-permute-done.46.refs_3_
  296.3 22.7 %all-gather.11.cloned.1.call-done.refs_8_ = bf16[2048,4224]{1,0:T(8,128)(2,1)} async-done(((bf16[256,4224]{1,0:T(8,128)(2,1)}), bf16[2048,4224]{1,0:T(8,128)(2,1)}) %all-gather.11.cloned.1.call-update) | async-done | bytes 17301520 | tf_op jit(solution)/shard_map/all_gather | solution.py:526
  319.0 7.7 %shard_map.215 = (bf16[512,2048]{1,0:T(8,128)(2,1)S(1)}, bf16[512,1408]{1,0:T(8,128)(2,1)S(1)}, bf16[512,704]{1,0:T(8,128)(2,1)S(1)}, bf16[256,2048]{1,0:T(8,128)(2,1)S(1)}, bf16[256,2048]{1,0:T(8,128)(2,1)S(1)}) custom-call(bf16[64,2048]{1,0:T(8,128)(2,1)S(1)} %get-tuple-element.232.refs_0_, bf16[64,2048]{1,0:T(8,128)(2,1)} %collective-permute-done.44.refs_1_, ...), custom_call_target="tpu_custom_call" | custom-call | flops 4563402752 | bytes 25755648 | tf_op jit(solution)/shard_map/pallas_call | solution.py:50
  336.3 9.0 %shard_map.217 = (bf16[512,2048]{1,0:T(8,128)(2,1)S(1)}, bf16[512,1408]{1,0:T(8,128)(2,1)S(1)}, bf16[256,2048]{1,0:T(8,128)(2,1)S(1)}, bf16[256,2048]{1,0:T(8,128)(2,1)S(1)}) custom-call(bf16[64,2048]{1,0:T(8,128)(2,1)S(1)} %get-tuple-element.224.refs_0_, bf16[64,2048]{1,0:T(8,128)(2,1)S(1)} %copy-done.23, bf16[64,2048]{1,0:T(8,128)(2,1)S(1)} %copy-done.25, ...), custom_call_target="tpu_custom_call" | custom-call | flops 4563402752 | bytes 26476544 | tf_op jit(solution)/shard_map/pallas_call | solution.py:50
  349.6 10.4 %shard_map.218 = bf16[2048,2176]{1,0:T(8,128)(2,1)} custom-call(bf16[512,2048]{1,0:T(8,128)(2,1)} %copy-done.51, bf16[512,2048]{1,0:T(8,128)(2,1)} %copy-done.53, bf16[512,1408]{1,0:T(8,128)(2,1)} %copy-done.55, bf16[512,704]{1,0:T(8,128)(2,1)} %copy-done.58), custom_call_target="tpu_custom_call" | custom-call | flops 4563402752 | bytes 15269888 | tf_op jit(solution)/shard_map/pallas_call | solution.py:50
  360.7 2.9 collective-permute-done.55.moved_i
  365.6 3.3 collective-permute-start.57
  369.4 9.1 %collective-permute-done.56.refs_1_ = bf16[64,2048]{1,0:T(8,128)(2,1)S(1)} collective-permute-done((bf16[64,2048]{1,0:T(8,128)(2,1)S(1)}, bf16[64,2048]{1,0:T(8,128)(2,1)S(1)}, u32[]{:S(2)}, u32[]{:S(2)}) %collective-permute-start.56) | collective-permute-done | bytes 262176 | tf_op jit(solution)/shard_map/ppermute | solution.py:430
  378.5 8.8 %collective-permute-done.57.refs_2_ = bf16[64,2048]{1,0:T(8,128)(2,1)S(1)} collective-permute-done((bf16[64,2048]{1,0:T(8,128)(2,1)S(1)}, bf16[64,2048]{1,0:T(8,128)(2,1)S(1)}, u32[]{:S(2)}, u32[]{:S(2)}) %collective-permute-start.57) | collective-permute-done | bytes 262176 | tf_op jit(solution)/shard_map/ppermute | solution.py:430
  388.9 6.4 collective-permute-start.60
  395.2 11.6 %collective-permute-done.60.refs_2_ = bf16[64,2048]{1,0:T(8,128)(2,1)S(1)} collective-permute-done((bf16[64,2048]{1,0:T(8,128)(2,1)S(1)}, bf16[64,2048]{1,0:T(8,128)(2,1)S(1)}, u32[]{:S(2)}, u32[]{:S(2)}) %collective-permute-start.60) | collective-permute-done | bytes 262176 | tf_op jit(solution)/shard_map/ppermute | solution.py:430
  407.4 6.4 collective-permute-done.61.refs_3_
  416.1 13.1 %shard_map.221 = (bf16[512,2048]{1,0:T(8,128)(2,1)}, bf16[512,768]{1,0:T(8,128)(2,1)}, f32[1,768]{1,0:T(1,128)}, bf16[256,2048]{1,0:T(8,128)(2,1)}, bf16[256,2048]{1,0:T(8,128)(2,1)}) custom-call(bf16[64,2048]{1,0:T(8,128)(2,1)} %copy-done.61, bf16[64,2048]{1,0:T(8,128)(2,1)} %copy-done.93, bf16[64,2048]{1,0:T(8,128)(2,1)} %copy-done.92, ...), custom_call_target="tpu_custom_call" | custom-call | flops 4831838208 | bytes 17050624 | tf_op jit(solution)/shard_map/pallas_call | solution.py:50
  438.7 6.9 shard_map.223
  447.3 8.8 %collective-permute-done.68.refs_2_ = bf16[64,2048]{1,0:T(8,128)(2,1)} collective-permute-done((bf16[64,2048]{1,0:T(8,128)(2,1)}, bf16[64,2048]{1,0:T(8,128)(2,1)}, u32[]{:S(2)}, u32[]{:S(2)}) %collective-permute-start.68) | collective-permute-done | bytes 262176 | tf_op jit(solution)/shard_map/ppermute | solution.py:430
  460.8 5.3 collective-permute-start.71
  466.1 11.2 %collective-permute-done.71.refs_2_ = bf16[64,2048]{1,0:T(8,128)(2,1)S(1)} collective-permute-done((bf16[64,2048]{1,0:T(8,128)(2,1)S(1)}, bf16[64,2048]{1,0:T(8,128)(2,1)S(1)}, u32[]{:S(2)}, u32[]{:S(2)}) %collective-permute-start.71) | collective-permute-done | bytes 262176 | tf_op jit(solution)/shard_map/ppermute | solution.py:430
  477.8 6.1 collective-permute-done.72.refs_3_
  485.5 9.1 %shard_map.225 = (bf16[512,2048]{1,0:T(8,128)(2,1)S(1)}, bf16[512,1408]{1,0:T(8,128)(2,1)S(1)}, bf16[256,2048]{1,0:T(8,128)(2,1)S(1)}, bf16[256,2048]{1,0:T(8,128)(2,1)S(1)}) custom-call(bf16[64,2048]{1,0:T(8,128)(2,1)S(1)} %get-tuple-element.276.refs_0_, bf16[64,2048]{1,0:T(8,128)(2,1)S(1)} %collective-permute-done.70.refs_1_, ...), custom_call_target="tpu_custom_call" | custom-call | flops 4563402752 | bytes 26476544 | tf_op jit(solution)/shard_map/pallas_call | solution.py:50
  504.8 10.4 %shard_map.227 = bf16[2048,2176]{1,0:T(8,128)(2,1)} custom-call(bf16[512,2048]{1,0:T(8,128)(2,1)} %copy-done.50, bf16[512,2048]{1,0:T(8,128)(2,1)} %copy-done.52, bf16[512,1408]{1,0:T(8,128)(2,1)} %copy-done.54, bf16[512,704]{1,0:T(8,128)(2,1)} %copy-done.57), custom_call_target="tpu_custom_call" | custom-call | flops 4563402752 | bytes 15269888 | tf_op jit(solution)/shard_map/pallas_call | solution.py:50
  515.2 7.6 %collective-permute-done.79.refs_2_ = bf16[64,2048]{1,0:T(8,128)(2,1)} collective-permute-done((bf16[64,2048]{1,0:T(8,128)(2,1)}, bf16[64,2048]{1,0:T(8,128)(2,1)}, u32[]{:S(2)}, u32[]{:S(2)}) %collective-permute-start.79) | collective-permute-done | bytes 262176 | tf_op jit(solution)/shard_map/ppermute | solution.py:430
  526.1 6.2 collective-permute-start.82
  537.9 13.0 %collective-permute-done.82.refs_2_ = bf16[64,2048]{1,0:T(8,128)(2,1)} collective-permute-done((bf16[64,2048]{1,0:T(8,128)(2,1)}, bf16[64,2048]{1,0:T(8,128)(2,1)}, u32[]{:S(2)}, u32[]{:S(2)}) %collective-permute-start.82) | collective-permute-done | bytes 262176 | tf_op jit(solution)/shard_map/ppermute | solution.py:430
  555.6 5.0 collective-permute-done.83.refs_3_
  563.5 13.1 %shard_map.231 = (bf16[512,2048]{1,0:T(8,128)(2,1)}, bf16[512,768]{1,0:T(8,128)(2,1)}, f32[1,768]{1,0:T(1,128)}, bf16[256,2048]{1,0:T(8,128)(2,1)}, bf16[256,2048]{1,0:T(8,128)(2,1)}) custom-call(bf16[64,2048]{1,0:T(8,128)(2,1)} %get-tuple-element.299.refs_0_, bf16[64,2048]{1,0:T(8,128)(2,1)} %copy-done.85, ...), custom_call_target="tpu_custom_call" | custom-call | flops 4831838208 | bytes 17050624 | tf_op jit(solution)/shard_map/pallas_call | solution.py:50
  586.5 6.8 shard_map.233
  595.2 8.4 %collective-permute-done.95.refs_2_ = bf16[64,2048]{1,0:T(8,128)(2,1)S(1)} collective-permute-done((bf16[64,2048]{1,0:T(8,128)(2,1)}, bf16[64,2048]{1,0:T(8,128)(2,1)S(1)}, u32[]{:S(2)}, u32[]{:S(2)}) %collective-permute-start.95) | collective-permute-done | bytes 262176 | tf_op jit(solution)/shard_map/ppermute | solution.py:430
  606.7 5.7 collective-permute-start.98
  614.0 11.3 %collective-permute-done.98 = bf16[72,2048]{1,0:T(8,128)(2,1)S(1)} collective-permute-done((bf16[72,2048]{1,0:T(8,128)(2,1)S(1)}, bf16[72,2048]{1,0:T(8,128)(2,1)S(1)}, u32[]{:S(2)}, u32[]{:S(2)}) %collective-permute-start.98) | collective-permute-done | bytes 294944 | tf_op jit(solution)/shard_map/ppermute | solution.py:430
  628.2 4.9 shard_map.236
  638.9 4.2 shard_map.238
  643.2 9.6 %copy.85 = f32[2,2,256,1408]{3,1,2,0:T(2,128)} copy(f32[2,2,256,1408]{3,2,1,0:T(8,128)} %get-tuple-element.362) | data formatting | bytes 11534336 | tf_op jit(solution)/shard_map/pallas_call | solution.py:50
  652.8 12.6 %collective-permute-done.101 = bf16[137,2048]{1,0:T(8,128)(2,1)S(1)} collective-permute-done((bf16[137,2048]{1,0:T(8,128)(2,1)S(1)}, bf16[137,2048]{1,0:T(8,128)(2,1)S(1)}, u32[]{:S(2)}, u32[]{:S(2)}) %collective-permute-start.101) | collective-permute-done | bytes 561184 | tf_op jit(solution)/shard_map/ppermute | solution.py:430
  665.7 5.0 collective-permute-done.103
  675.0 12.8 %reduce-scatter.11.cloned.1.call-done.block_sum.refs_0_ = bf16[512,1024]{1,0:T(8,128)(2,1)} async-done(((bf16[2048,1024]{1,0:T(8,128)(2,1)}), bf16[512,1024]{1,0:T(8,128)(2,1)}) %reduce-scatter.11.cloned.1.call-update) | async-done | bytes 1048592 | tf_op jit(solution)/shard_map/reduce_scatter | solution.py:606
  (512 shorter events, 172.5 us)
Async XLA Ops:
  7.2 61.3 %all-gather.5.cloned.1.call-start = ((), (), s32[]{:S(2)}) async-start(), calls=%async_computation.4 | async-start | bytes 9437184 | tf_op jit(solution)/shard_map/all_gather | solution.py:526
  9.9 157.7 %all-gather.7.cloned.1.call-start = ((), (), s32[]{:S(2)}) async-start(), calls=%async_computation.5 | async-start | bytes 19464192 | tf_op jit(solution)/shard_map/all_gather | solution.py:526
  22.2 210.7 %all-gather.9.cloned.1.call-start = ((), (), s32[]{:S(2)}) async-start(), calls=%async_computation.6 | async-start | bytes 9437184 | tf_op jit(solution)/shard_map/all_gather | solution.py:526
  23.3 295.7 %all-gather.11.cloned.1.call-start = ((), (), s32[]{:S(2)}) async-start(), calls=%async_computation.7 | async-start | bytes 19464192 | tf_op jit(solution)/shard_map/all_gather | solution.py:526
  30.0 502.3 %reduce-scatter.7.cloned.1.call-start = ((), (), s32[]{:S(2)}) async-start(), calls=%async_computation.9 | async-start | bytes 11141120 | tf_op jit(solution)/shard_map/reduce_scatter | solution.py:606
  42.3 15.3 %collective-permute-start.3 = (bf16[64,2048]{1,0:T(8,128)(2,1)S(1)}, bf16[64,2048]{1,0:T(8,128)(2,1)S(1)}, u32[]{:S(2)}, u32[]{:S(2)}) collective-permute-start(bf16[64,2048]{1,0:T(8,128)(2,1)S(1)} %get-tuple-element.192.refs_0_), channel_id=1, source_target_pairs={{0,2},{1,3},{2,0},{3,1},{4,6},{5,7},{6,4},{7,5},{8,10},{9,11},{10,... | collective-permute-start | bytes 786440 | tf_op jit(solution)/shard_map/ppermute | solution.py:430
  45.7 13.2 %collective-permute-start.2 = (bf16[64,2048]{1,0:T(8,128)(2,1)S(1)}, bf16[64,2048]{1,0:T(8,128)(2,1)S(1)}, u32[]{:S(2)}, u32[]{:S(2)}) collective-permute-start(bf16[64,2048]{1,0:T(8,128)(2,1)S(1)} %get-tuple-element.192.refs_0_), channel_id=1, source_target_pairs={{0,1},{1,0},{2,3},{3,2},{4,5},{5,4},{6,7},{7,6},{8,9},{9,8},{10,11... | collective-permute-start | bytes 786440 | tf_op jit(solution)/shard_map/ppermute | solution.py:430
  80.9 14.4 %collective-permute-start = (bf16[64,2048]{1,0:T(8,128)(2,1)S(1)}, bf16[64,2048]{1,0:T(8,128)(2,1)S(1)}, u32[]{:S(2)}, u32[]{:S(2)}) collective-permute-start(bf16[64,2048]{1,0:T(8,128)(2,1)S(1)} %dynamic-slice_bitcast_fusion.3), channel_id=1, source_target_pairs={{0,8},{8,0},{1,9},{9,1},{2,10},{10,2},{3,11},{11,3},{4,12},{12,4},... | collective-permute-start | bytes 786440 | tf_op jit(solution)/shard_map/ppermute | solution.py:430
  84.8 15.3 %collective-permute-start.12 = (bf16[64,2048]{1,0:T(8,128)(2,1)S(1)}, bf16[64,2048]{1,0:T(8,128)(2,1)S(1)}, u32[]{:S(2)}, u32[]{:S(2)}) collective-permute-start(bf16[64,2048]{1,0:T(8,128)(2,1)S(1)} %get-tuple-element.196), channel_id=1, source_target_pairs={{0,1},{1,0},{2,3},{3,2},{4,5},{5,4},{6,7},{7,6},{8,9},{9,8},{10,11... | collective-permute-start | bytes 786440 | tf_op jit(solution)/shard_map/ppermute | solution.py:430
  86.0 21.8 %collective-permute-start.13 = (bf16[64,2048]{1,0:T(8,128)(2,1)S(1)}, bf16[64,2048]{1,0:T(8,128)(2,1)S(1)}, u32[]{:S(2)}, u32[]{:S(2)}) collective-permute-start(bf16[64,2048]{1,0:T(8,128)(2,1)S(1)} %get-tuple-element.197), channel_id=1, source_target_pairs={{0,2},{1,3},{2,0},{3,1},{4,6},{5,7},{6,4},{7,5},{8,10},{9,11},{10,... | collective-permute-start | bytes 786440 | tf_op jit(solution)/shard_map/ppermute | solution.py:430
  89.4 18.4 %collective-permute-start.14 = (bf16[64,2048]{1,0:T(8,128)(2,1)S(1)}, bf16[64,2048]{1,0:T(8,128)(2,1)S(1)}, u32[]{:S(2)}, u32[]{:S(2)}) collective-permute-start(bf16[64,2048]{1,0:T(8,128)(2,1)S(1)} %get-tuple-element.198), channel_id=1, source_target_pairs={{0,3},{1,2},{2,1},{3,0},{4,7},{5,6},{6,5},{7,4},{8,11},{9,10},{10,... | collective-permute-start | bytes 786440 | tf_op jit(solution)/shard_map/ppermute | solution.py:430
  95.5 34.8 %collective-permute-start.22 = (bf16[64,2048]{1,0:T(8,128)(2,1)S(1)}, bf16[64,2048]{1,0:T(8,128)(2,1)S(1)}, u32[]{:S(2)}, u32[]{:S(2)}) collective-permute-start(bf16[64,2048]{1,0:T(8,128)(2,1)S(1)} %get-tuple-element.224.refs_0_), channel_id=1, source_target_pairs={{0,1},{1,0},{2,3},{3,2},{4,5},{5,4},{6,7},{7,6},{8,9},{9,8},{10,11... | collective-permute-start | bytes 786440 | tf_op jit(solution)/shard_map/ppermute | solution.py:430
  96.6 33.7 %collective-permute-start.23 = (bf16[64,2048]{1,0:T(8,128)(2,1)S(1)}, bf16[64,2048]{1,0:T(8,128)(2,1)S(1)}, u32[]{:S(2)}, u32[]{:S(2)}) collective-permute-start(bf16[64,2048]{1,0:T(8,128)(2,1)S(1)} %get-tuple-element.224.refs_0_), channel_id=1, source_target_pairs={{0,2},{1,3},{2,0},{3,1},{4,6},{5,7},{6,4},{7,5},{8,10},{9,11},{10,... | collective-permute-start | bytes 786440 | tf_op jit(solution)/shard_map/ppermute | solution.py:430
  100.1 30.8 %collective-permute-start.25 = (bf16[64,2048]{1,0:T(8,128)(2,1)S(1)}, bf16[64,2048]{1,0:T(8,128)(2,1)S(1)}, u32[]{:S(2)}, u32[]{:S(2)}) collective-permute-start(bf16[64,2048]{1,0:T(8,128)(2,1)S(1)} %get-tuple-element.224.refs_0_), channel_id=1, source_target_pairs={{0,4},{4,0},{1,5},{5,1},{2,6},{6,2},{3,7},{7,3},{8,12},{12,8},{9,1... | collective-permute-start | bytes 786440 | tf_op jit(solution)/shard_map/ppermute | solution.py:430
  108.1 27.3 %collective-permute-start.16 = (bf16[64,2048]{1,0:T(8,128)(2,1)S(1)}, bf16[64,2048]{1,0:T(8,128)(2,1)S(1)}, u32[]{:S(2)}, u32[]{:S(2)}) collective-permute-start(bf16[64,2048]{1,0:T(8,128)(2,1)S(1)} %get-tuple-element.201.refs_0_), channel_id=1, source_target_pairs={{0,2},{1,3},{2,0},{3,1},{4,6},{5,7},{6,4},{7,5},{8,10},{9,11},{10,... | collective-permute-start | bytes 786440 | tf_op jit(solution)/shard_map/ppermute | solution.py:430
  130.9 15.8 %collective-permute-start.15 = (bf16[64,2048]{1,0:T(8,128)(2,1)S(1)}, bf16[64,2048]{1,0:T(8,128)(2,1)S(1)}, u32[]{:S(2)}, u32[]{:S(2)}) collective-permute-start(bf16[64,2048]{1,0:T(8,128)(2,1)S(1)} %get-tuple-element.201.refs_0_), channel_id=1, source_target_pairs={{0,1},{1,0},{2,3},{3,2},{4,5},{5,4},{6,7},{7,6},{8,9},{9,8},{10,11... | collective-permute-start | bytes 786440 | tf_op jit(solution)/shard_map/ppermute | solution.py:430
  135.4 16.7 %collective-permute-start.17 = (bf16[64,2048]{1,0:T(8,128)(2,1)S(1)}, bf16[64,2048]{1,0:T(8,128)(2,1)S(1)}, u32[]{:S(2)}, u32[]{:S(2)}) collective-permute-start(bf16[64,2048]{1,0:T(8,128)(2,1)S(1)} %collective-permute-done.16.refs_2_), channel_id=1, source_target_pairs={{0,1},{1,0},{2,3},{3,2},{4,5},{5,4},{6,7},{7,6},{8,9},{9,8},{10,11... | collective-permute-start | bytes 786440 | tf_op jit(solution)/shard_map/ppermute | solution.py:430
  141.0 12.0 %collective-permute-start.28 = (bf16[64,2048]{1,0:T(8,128)(2,1)S(1)}, bf16[64,2048]{1,0:T(8,128)(2,1)S(1)}, u32[]{:S(2)}, u32[]{:S(2)}) collective-permute-start(bf16[64,2048]{1,0:T(8,128)(2,1)S(1)} %collective-permute-done.24.refs_3_), channel_id=1, source_target_pairs={{0,4},{4,0},{1,5},{5,1},{2,6},{6,2},{3,7},{7,3},{8,12},{12,8},{9,1... | collective-permute-start | bytes 786440 | tf_op jit(solution)/shard_map/ppermute | solution.py:430
  143.0 12.2 %collective-permute-start.20 = (bf16[64,2048]{1,0:T(8,128)(2,1)S(1)}, bf16[64,2048]{1,0:T(8,128)(2,1)S(1)}, u32[]{:S(2)}, u32[]{:S(2)}) collective-permute-start(bf16[64,2048]{1,0:T(8,128)(2,1)S(1)} %collective-permute-done.16.refs_2_), channel_id=1, source_target_pairs={{0,4},{4,0},{1,5},{5,1},{2,6},{6,2},{3,7},{7,3},{8,12},{12,8},{9,1... | collective-permute-start | bytes 786440 | tf_op jit(solution)/shard_map/ppermute | solution.py:430
  185.0 13.6 %collective-permute-start.30 = (bf16[64,2048]{1,0:T(8,128)(2,1)S(1)}, bf16[64,2048]{1,0:T(8,128)(2,1)S(1)}, u32[]{:S(2)}, u32[]{:S(2)}) collective-permute-start(bf16[64,2048]{1,0:T(8,128)(2,1)S(1)} %get-tuple-element.212), channel_id=1, source_target_pairs={{0,1},{1,0},{2,3},{3,2},{4,5},{5,4},{6,7},{7,6},{8,9},{9,8},{10,11... | collective-permute-start | bytes 786440 | tf_op jit(solution)/shard_map/ppermute | solution.py:430
  186.6 21.3 %collective-permute-start.31 = (bf16[64,2048]{1,0:T(8,128)(2,1)S(1)}, bf16[64,2048]{1,0:T(8,128)(2,1)S(1)}, u32[]{:S(2)}, u32[]{:S(2)}) collective-permute-start(bf16[64,2048]{1,0:T(8,128)(2,1)S(1)} %get-tuple-element.213), channel_id=1, source_target_pairs={{0,2},{1,3},{2,0},{3,1},{4,6},{5,7},{6,4},{7,5},{8,10},{9,11},{10,... | collective-permute-start | bytes 786440 | tf_op jit(solution)/shard_map/ppermute | solution.py:430
  189.0 18.9 %collective-permute-start.32 = (bf16[64,2048]{1,0:T(8,128)(2,1)S(1)}, bf16[64,2048]{1,0:T(8,128)(2,1)S(1)}, u32[]{:S(2)}, u32[]{:S(2)}) collective-permute-start(bf16[64,2048]{1,0:T(8,128)(2,1)S(1)} %get-tuple-element.214), channel_id=1, source_target_pairs={{0,3},{1,2},{2,1},{3,0},{4,7},{5,6},{6,5},{7,4},{8,11},{9,10},{10,... | collective-permute-start | bytes 786440 | tf_op jit(solution)/shard_map/ppermute | solution.py:430
  208.3 17.7 %collective-permute-start.34 = (bf16[64,2048]{1,0:T(8,128)(2,1)S(1)}, bf16[64,2048]{1,0:T(8,128)(2,1)S(1)}, u32[]{:S(2)}, u32[]{:S(2)}) collective-permute-start(bf16[64,2048]{1,0:T(8,128)(2,1)S(1)} %get-tuple-element.216.refs_0_), channel_id=1, source_target_pairs={{0,2},{1,3},{2,0},{3,1},{4,6},{5,7},{6,4},{7,5},{8,10},{9,11},{10,... | collective-permute-start | bytes 786440 | tf_op jit(solution)/shard_map/ppermute | solution.py:430
  214.5 12.0 %collective-permute-start.33 = (bf16[64,2048]{1,0:T(8,128)(2,1)S(1)}, bf16[64,2048]{1,0:T(8,128)(2,1)S(1)}, u32[]{:S(2)}, u32[]{:S(2)}) collective-permute-start(bf16[64,2048]{1,0:T(8,128)(2,1)S(1)} %get-tuple-element.216.refs_0_), channel_id=1, source_target_pairs={{0,1},{1,0},{2,3},{3,2},{4,5},{5,4},{6,7},{7,6},{8,9},{9,8},{10,11... | collective-permute-start | bytes 786440 | tf_op jit(solution)/shard_map/ppermute | solution.py:430
  250.5 13.0 %collective-permute-start.41 = (bf16[64,2048]{1,0:T(8,128)(2,1)S(1)}, bf16[64,2048]{1,0:T(8,128)(2,1)S(1)}, u32[]{:S(2)}, u32[]{:S(2)}) collective-permute-start(bf16[64,2048]{1,0:T(8,128)(2,1)S(1)} %get-tuple-element.220), channel_id=1, source_target_pairs={{0,1},{1,0},{2,3},{3,2},{4,5},{5,4},{6,7},{7,6},{8,9},{9,8},{10,11... | collective-permute-start | bytes 786440 | tf_op jit(solution)/shard_map/ppermute | solution.py:430
  251.4 21.3 %collective-permute-start.42 = (bf16[64,2048]{1,0:T(8,128)(2,1)S(1)}, bf16[64,2048]{1,0:T(8,128)(2,1)S(1)}, u32[]{:S(2)}, u32[]{:S(2)}) collective-permute-start(bf16[64,2048]{1,0:T(8,128)(2,1)S(1)} %get-tuple-element.221), channel_id=1, source_target_pairs={{0,2},{1,3},{2,0},{3,1},{4,6},{5,7},{6,4},{7,5},{8,10},{9,11},{10,... | collective-permute-start | bytes 786440 | tf_op jit(solution)/shard_map/ppermute | solution.py:430
  252.9 19.8 %collective-permute-start.43 = (bf16[64,2048]{1,0:T(8,128)(2,1)S(1)}, bf16[64,2048]{1,0:T(8,128)(2,1)S(1)}, u32[]{:S(2)}, u32[]{:S(2)}) collective-permute-start(bf16[64,2048]{1,0:T(8,128)(2,1)S(1)} %get-tuple-element.222), channel_id=1, source_target_pairs={{0,3},{1,2},{2,1},{3,0},{4,7},{5,6},{6,5},{7,4},{8,11},{9,10},{10,... | collective-permute-start | bytes 786440 | tf_op jit(solution)/shard_map/ppermute | solution.py:430
  273.0 16.4 %collective-permute-start.45 = (bf16[64,2048]{1,0:T(8,128)(2,1)S(1)}, bf16[64,2048]{1,0:T(8,128)(2,1)S(1)}, u32[]{:S(2)}, u32[]{:S(2)}) collective-permute-start(bf16[64,2048]{1,0:T(8,128)(2,1)S(1)} %get-tuple-element.232.refs_0_), channel_id=1, source_target_pairs={{0,2},{1,3},{2,0},{3,1},{4,6},{5,7},{6,4},{7,5},{8,10},{9,11},{10,... | collective-permute-start | bytes 786440 | tf_op jit(solution)/shard_map/ppermute | solution.py:430
  289.5 29.5 %collective-permute-start.47 = (bf16[64,2048]{1,0:T(8,128)(2,1)S(1)}, bf16[64,2048]{1,0:T(8,128)(2,1)}, u32[]{:S(2)}, u32[]{:S(2)}) collective-permute-start(bf16[64,2048]{1,0:T(8,128)(2,1)S(1)} %get-tuple-element.232.refs_0_), channel_id=1, source_target_pairs={{0,4},{4,0},{1,5},{5,1},{2,6},{6,2},{3,7},{7,3},{8,12},{12,8},{9,1... | collective-permute-start | bytes 786440 | tf_op jit(solution)/shard_map/ppermute | solution.py:430
  289.5 29.5 %collective-permute-start.49 = (bf16[64,2048]{1,0:T(8,128)(2,1)S(1)}, bf16[64,2048]{1,0:T(8,128)(2,1)}, u32[]{:S(2)}, u32[]{:S(2)}) collective-permute-start(bf16[64,2048]{1,0:T(8,128)(2,1)S(1)} %collective-permute-done.45.refs_2_), channel_id=1, source_target_pairs={{0,4},{4,0},{1,5},{5,1},{2,6},{6,2},{3,7},{7,3},{8,12},{12,8},{9,1... | collective-permute-start | bytes 786440 | tf_op jit(solution)/shard_map/ppermute | solution.py:430
  290.0 29.0 %collective-permute-start.48 = (bf16[64,2048]{1,0:T(8,128)(2,1)}, bf16[64,2048]{1,0:T(8,128)(2,1)}, u32[]{:S(2)}, u32[]{:S(2)}) collective-permute-start(bf16[64,2048]{1,0:T(8,128)(2,1)} %collective-permute-done.44.refs_1_), channel_id=1, source_target_pairs={{0,4},{4,0},{1,5},{5,1},{2,6},{6,2},{3,7},{7,3},{8,12},{12,8},{9,1... | collective-permute-start | bytes 786440 | tf_op jit(solution)/shard_map/ppermute | solution.py:430
  296.3 22.7 %collective-permute-start.50 = (bf16[64,2048]{1,0:T(8,128)(2,1)}, bf16[64,2048]{1,0:T(8,128)(2,1)}, u32[]{:S(2)}, u32[]{:S(2)}) collective-permute-start(bf16[64,2048]{1,0:T(8,128)(2,1)} %collective-permute-done.46.refs_3_), channel_id=1, source_target_pairs={{0,4},{4,0},{1,5},{5,1},{2,6},{6,2},{3,7},{7,3},{8,12},{12,8},{9,1... | collective-permute-start | bytes 786440 | tf_op jit(solution)/shard_map/ppermute | solution.py:430
  331.9 28.2 %collective-permute-start.52 = (bf16[64,2048]{1,0:T(8,128)(2,1)}, bf16[64,2048]{1,0:T(8,128)(2,1)}, u32[]{:S(2)}, u32[]{:S(2)}) collective-permute-start(bf16[64,2048]{1,0:T(8,128)(2,1)} %get-tuple-element.240), channel_id=1, source_target_pairs={{0,1},{1,0},{2,3},{3,2},{4,5},{5,4},{6,7},{7,6},{8,9},{9,8},{10,11... | collective-permute-start | bytes 786440 | tf_op jit(solution)/shard_map/ppermute | solution.py:430
  333.3 26.8 %collective-permute-start.53 = (bf16[64,2048]{1,0:T(8,128)(2,1)}, bf16[64,2048]{1,0:T(8,128)(2,1)}, u32[]{:S(2)}, u32[]{:S(2)}) collective-permute-start(bf16[64,2048]{1,0:T(8,128)(2,1)} %get-tuple-element.241), channel_id=1, source_target_pairs={{0,2},{1,3},{2,0},{3,1},{4,6},{5,7},{6,4},{7,5},{8,10},{9,11},{10,... | collective-permute-start | bytes 786440 | tf_op jit(solution)/shard_map/ppermute | solution.py:430
  335.8 24.3 %collective-permute-start.54 = (bf16[64,2048]{1,0:T(8,128)(2,1)}, bf16[64,2048]{1,0:T(8,128)(2,1)}, u32[]{:S(2)}, u32[]{:S(2)}) collective-permute-start(bf16[64,2048]{1,0:T(8,128)(2,1)} %get-tuple-element.242), channel_id=1, source_target_pairs={{0,3},{1,2},{2,1},{3,0},{4,7},{5,6},{6,5},{7,4},{8,11},{9,10},{10,... | collective-permute-start | bytes 786440 | tf_op jit(solution)/shard_map/ppermute | solution.py:430
  360.1 190.7 %reduce-scatter.5.cloned.1.call-start = ((), (), s32[]{:S(2)}) async-start(), calls=%async_computation.8 | async-start | bytes 5242880 | tf_op jit(solution)/shard_map/reduce_scatter | solution.py:606
  365.0 13.5 %collective-permute-start.56 = (bf16[64,2048]{1,0:T(8,128)(2,1)S(1)}, bf16[64,2048]{1,0:T(8,128)(2,1)S(1)}, u32[]{:S(2)}, u32[]{:S(2)}) collective-permute-start(bf16[64,2048]{1,0:T(8,128)(2,1)S(1)} %get-tuple-element.249), channel_id=1, source_target_pairs={{0,1},{1,0},{2,3},{3,2},{4,5},{5,4},{6,7},{7,6},{8,9},{9,8},{10,11... | collective-permute-start | bytes 786440 | tf_op jit(solution)/shard_map/ppermute | solution.py:430
  365.6 21.7 %collective-permute-start.57 = (bf16[64,2048]{1,0:T(8,128)(2,1)S(1)}, bf16[64,2048]{1,0:T(8,128)(2,1)S(1)}, u32[]{:S(2)}, u32[]{:S(2)}) collective-permute-start(bf16[64,2048]{1,0:T(8,128)(2,1)S(1)} %get-tuple-element.250), channel_id=1, source_target_pairs={{0,2},{1,3},{2,0},{3,1},{4,6},{5,7},{6,4},{7,5},{8,10},{9,11},{10,... | collective-permute-start | bytes 786440 | tf_op jit(solution)/shard_map/ppermute | solution.py:430
  368.9 18.4 %collective-permute-start.58 = (bf16[64,2048]{1,0:T(8,128)(2,1)S(1)}, bf16[64,2048]{1,0:T(8,128)(2,1)S(1)}, u32[]{:S(2)}, u32[]{:S(2)}) collective-permute-start(bf16[64,2048]{1,0:T(8,128)(2,1)S(1)} %get-tuple-element.251), channel_id=1, source_target_pairs={{0,3},{1,2},{2,1},{3,0},{4,7},{5,6},{6,5},{7,4},{8,11},{9,10},{10,... | collective-permute-start | bytes 786440 | tf_op jit(solution)/shard_map/ppermute | solution.py:430
  388.9 18.0 %collective-permute-start.60 = (bf16[64,2048]{1,0:T(8,128)(2,1)S(1)}, bf16[64,2048]{1,0:T(8,128)(2,1)S(1)}, u32[]{:S(2)}, u32[]{:S(2)}) collective-permute-start(bf16[64,2048]{1,0:T(8,128)(2,1)S(1)} %get-tuple-element.253.refs_0_), channel_id=1, source_target_pairs={{0,2},{1,3},{2,0},{3,1},{4,6},{5,7},{6,4},{7,5},{8,10},{9,11},{10,... | collective-permute-start | bytes 786440 | tf_op jit(solution)/shard_map/ppermute | solution.py:430
  395.2 12.1 %collective-permute-start.59 = (bf16[64,2048]{1,0:T(8,128)(2,1)S(1)}, bf16[64,2048]{1,0:T(8,128)(2,1)S(1)}, u32[]{:S(2)}, u32[]{:S(2)}) collective-permute-start(bf16[64,2048]{1,0:T(8,128)(2,1)S(1)} %get-tuple-element.253.refs_0_), channel_id=1, source_target_pairs={{0,1},{1,0},{2,3},{3,2},{4,5},{5,4},{6,7},{7,6},{8,9},{9,8},{10,11... | collective-permute-start | bytes 786440 | tf_op jit(solution)/shard_map/ppermute | solution.py:430
  434.3 13.0 %collective-permute-start.67 = (bf16[64,2048]{1,0:T(8,128)(2,1)}, bf16[64,2048]{1,0:T(8,128)(2,1)S(1)}, u32[]{:S(2)}, u32[]{:S(2)}) collective-permute-start(bf16[64,2048]{1,0:T(8,128)(2,1)} %get-tuple-element.260), channel_id=1, source_target_pairs={{0,1},{1,0},{2,3},{3,2},{4,5},{5,4},{6,7},{7,6},{8,9},{9,8},{10,11... | collective-permute-start | bytes 786440 | tf_op jit(solution)/shard_map/ppermute | solution.py:430
  434.5 21.7 %collective-permute-start.68 = (bf16[64,2048]{1,0:T(8,128)(2,1)}, bf16[64,2048]{1,0:T(8,128)(2,1)}, u32[]{:S(2)}, u32[]{:S(2)}) collective-permute-start(bf16[64,2048]{1,0:T(8,128)(2,1)} %get-tuple-element.261), channel_id=1, source_target_pairs={{0,2},{1,3},{2,0},{3,1},{4,6},{5,7},{6,4},{7,5},{8,10},{9,11},{10,... | collective-permute-start | bytes 786440 | tf_op jit(solution)/shard_map/ppermute | solution.py:430
  436.2 19.9 %collective-permute-start.69 = (bf16[64,2048]{1,0:T(8,128)(2,1)}, bf16[64,2048]{1,0:T(8,128)(2,1)}, u32[]{:S(2)}, u32[]{:S(2)}) collective-permute-start(bf16[64,2048]{1,0:T(8,128)(2,1)} %get-tuple-element.262), channel_id=1, source_target_pairs={{0,3},{1,2},{2,1},{3,0},{4,7},{5,6},{6,5},{7,4},{8,11},{9,10},{10,... | collective-permute-start | bytes 786440 | tf_op jit(solution)/shard_map/ppermute | solution.py:430
  456.2 177.7 %reduce-scatter.9.cloned.1.call-start = ((), (), s32[]{:S(2)}) async-start(), calls=%async_computation.10 | async-start | bytes 11141120 | tf_op jit(solution)/shard_map/reduce_scatter | solution.py:606
  460.8 16.5 %collective-permute-start.71 = (bf16[64,2048]{1,0:T(8,128)(2,1)S(1)}, bf16[64,2048]{1,0:T(8,128)(2,1)S(1)}, u32[]{:S(2)}, u32[]{:S(2)}) collective-permute-start(bf16[64,2048]{1,0:T(8,128)(2,1)S(1)} %get-tuple-element.276.refs_0_), channel_id=1, source_target_pairs={{0,2},{1,3},{2,0},{3,1},{4,6},{5,7},{6,4},{7,5},{8,10},{9,11},{10,... | collective-permute-start | bytes 786440 | tf_op jit(solution)/shard_map/ppermute | solution.py:430
  500.4 14.8 %collective-permute-start.78 = (bf16[64,2048]{1,0:T(8,128)(2,1)}, bf16[64,2048]{1,0:T(8,128)(2,1)S(1)}, u32[]{:S(2)}, u32[]{:S(2)}) collective-permute-start(bf16[64,2048]{1,0:T(8,128)(2,1)} %get-tuple-element.281), channel_id=1, source_target_pairs={{0,1},{1,0},{2,3},{3,2},{4,5},{5,4},{6,7},{7,6},{8,9},{9,8},{10,11... | collective-permute-start | bytes 786440 | tf_op jit(solution)/shard_map/ppermute | solution.py:430
  501.2 21.7 %collective-permute-start.79 = (bf16[64,2048]{1,0:T(8,128)(2,1)}, bf16[64,2048]{1,0:T(8,128)(2,1)}, u32[]{:S(2)}, u32[]{:S(2)}) collective-permute-start(bf16[64,2048]{1,0:T(8,128)(2,1)} %get-tuple-element.282), channel_id=1, source_target_pairs={{0,2},{1,3},{2,0},{3,1},{4,6},{5,7},{6,4},{7,5},{8,10},{9,11},{10,... | collective-permute-start | bytes 786440 | tf_op jit(solution)/shard_map/ppermute | solution.py:430
  504.0 18.8 %collective-permute-start.80 = (bf16[64,2048]{1,0:T(8,128)(2,1)}, bf16[64,2048]{1,0:T(8,128)(2,1)}, u32[]{:S(2)}, u32[]{:S(2)}) collective-permute-start(bf16[64,2048]{1,0:T(8,128)(2,1)} %get-tuple-element.283), channel_id=1, source_target_pairs={{0,3},{1,2},{2,1},{3,0},{4,7},{5,6},{6,5},{7,4},{8,11},{9,10},{10,... | collective-permute-start | bytes 786440 | tf_op jit(solution)/shard_map/ppermute | solution.py:430
  522.8 164.9 %reduce-scatter.11.cloned.1.call-start = ((), (), s32[]{:S(2)}) async-start(), calls=%async_computation.11 | async-start | bytes 5242880 | tf_op jit(solution)/shard_map/reduce_scatter | solution.py:606
  526.1 24.8 %collective-permute-start.82 = (bf16[64,2048]{1,0:T(8,128)(2,1)}, bf16[64,2048]{1,0:T(8,128)(2,1)}, u32[]{:S(2)}, u32[]{:S(2)}) collective-permute-start(bf16[64,2048]{1,0:T(8,128)(2,1)} %get-tuple-element.299.refs_0_), channel_id=1, source_target_pairs={{0,2},{1,3},{2,0},{3,1},{4,6},{5,7},{6,4},{7,5},{8,10},{9,11},{10,... | collective-permute-start | bytes 786440 | tf_op jit(solution)/shard_map/ppermute | solution.py:430
  534.4 28.4 %collective-permute-start.89 = (bf16[256,2176]{1,0:T(8,128)(2,1)S(1)}, bf16[256,2176]{1,0:T(8,128)(2,1)}, u32[]{:S(2)}, u32[]{:S(2)}) collective-permute-start(bf16[256,2176]{1,0:T(8,128)(2,1)S(1)} %shard_map.230), channel_id=1, source_target_pairs={{0,4},{4,0},{1,5},{5,1},{2,6},{6,2},{3,7},{7,3},{8,12},{12,8},{9,1... | collective-permute-start | bytes 3342344 | tf_op jit(solution)/shard_map/ppermute | solution.py:430
  535.7 19.2 %collective-permute-start.91 = (bf16[64,2048]{1,0:T(8,128)(2,1)S(1)}, bf16[64,2048]{1,0:T(8,128)(2,1)S(1)}, u32[]{:S(2)}, u32[]{:S(2)}) collective-permute-start(bf16[64,2048]{1,0:T(8,128)(2,1)S(1)} %add_convert_fusion), channel_id=1, source_target_pairs={{0,2},{1,3},{2,0},{3,1},{4,6},{5,7},{6,4},{7,5},{8,10},{9,11},{10,... | collective-permute-start | bytes 786440 | tf_op jit(solution)/shard_map/ppermute | solution.py:430
  535.9 19.1 %collective-permute-start.81 = (bf16[64,2048]{1,0:T(8,128)(2,1)}, bf16[64,2048]{1,0:T(8,128)(2,1)S(1)}, u32[]{:S(2)}, u32[]{:S(2)}) collective-permute-start(bf16[64,2048]{1,0:T(8,128)(2,1)} %get-tuple-element.299.refs_0_), channel_id=1, source_target_pairs={{0,1},{1,0},{2,3},{3,2},{4,5},{5,4},{6,7},{7,6},{8,9},{9,8},{10,11... | collective-permute-start | bytes 786440 | tf_op jit(solution)/shard_map/ppermute | solution.py:430
  537.9 17.6 %collective-permute-start.84 = (bf16[64,2048]{1,0:T(8,128)(2,1)}, bf16[64,2048]{1,0:T(8,128)(2,1)S(1)}, u32[]{:S(2)}, u32[]{:S(2)}) collective-permute-start(bf16[64,2048]{1,0:T(8,128)(2,1)} %get-tuple-element.299.refs_0_), channel_id=1, source_target_pairs={{0,4},{4,0},{1,5},{5,1},{2,6},{6,2},{3,7},{7,3},{8,12},{12,8},{9,1... | collective-permute-start | bytes 786440 | tf_op jit(solution)/shard_map/ppermute | solution.py:430
  560.6 16.1 %collective-permute-start.90 = (bf16[64,2048]{1,0:T(8,128)(2,1)S(1)}, bf16[64,2048]{1,0:T(8,128)(2,1)S(1)}, u32[]{:S(2)}, u32[]{:S(2)}) collective-permute-start(bf16[64,2048]{1,0:T(8,128)(2,1)S(1)} %add_convert_fusion), channel_id=1, source_target_pairs={{0,1},{1,0},{2,3},{3,2},{4,5},{5,4},{6,7},{7,6},{8,9},{9,8},{10,11... | collective-permute-start | bytes 786440 | tf_op jit(solution)/shard_map/ppermute | solution.py:430
  560.7 16.0 %collective-permute-start.92 = (bf16[64,2048]{1,0:T(8,128)(2,1)S(1)}, bf16[64,2048]{1,0:T(8,128)(2,1)S(1)}, u32[]{:S(2)}, u32[]{:S(2)}) collective-permute-start(bf16[64,2048]{1,0:T(8,128)(2,1)S(1)} %collective-permute-done.91), channel_id=1, source_target_pairs={{0,1},{1,0},{2,3},{3,2},{4,5},{5,4},{6,7},{7,6},{8,9},{9,8},{10,11... | collective-permute-start | bytes 786440 | tf_op jit(solution)/shard_map/ppermute | solution.py:430
  581.9 13.3 %collective-permute-start.94 = (bf16[64,2048]{1,0:T(8,128)(2,1)}, bf16[64,2048]{1,0:T(8,128)(2,1)S(1)}, u32[]{:S(2)}, u32[]{:S(2)}) collective-permute-start(bf16[64,2048]{1,0:T(8,128)(2,1)} %get-tuple-element.323), channel_id=1, source_target_pairs={{0,1},{1,0},{2,3},{3,2},{4,5},{5,4},{6,7},{7,6},{8,9},{9,8},{10,11... | collective-permute-start | bytes 786440 | tf_op jit(solution)/shard_map/ppermute | solution.py:430
  582.1 21.5 %collective-permute-start.95 = (bf16[64,2048]{1,0:T(8,128)(2,1)}, bf16[64,2048]{1,0:T(8,128)(2,1)S(1)}, u32[]{:S(2)}, u32[]{:S(2)}) collective-permute-start(bf16[64,2048]{1,0:T(8,128)(2,1)} %get-tuple-element.324), channel_id=1, source_target_pairs={{0,2},{1,3},{2,0},{3,1},{4,6},{5,7},{6,4},{7,5},{8,10},{9,11},{10,... | collective-permute-start | bytes 786440 | tf_op jit(solution)/shard_map/ppermute | solution.py:430
  584.4 19.3 %collective-permute-start.96 = (bf16[64,2048]{1,0:T(8,128)(2,1)S(1)}, bf16[64,2048]{1,0:T(8,128)(2,1)S(1)}, u32[]{:S(2)}, u32[]{:S(2)}) collective-permute-start(bf16[64,2048]{1,0:T(8,128)(2,1)S(1)} %get-tuple-element.325), channel_id=1, source_target_pairs={{0,3},{1,2},{2,1},{3,0},{4,7},{5,6},{6,5},{7,4},{8,11},{9,10},{10,... | collective-permute-start | bytes 786440 | tf_op jit(solution)/shard_map/ppermute | solution.py:430
  606.7 18.7 %collective-permute-start.98 = (bf16[72,2048]{1,0:T(8,128)(2,1)S(1)}, bf16[72,2048]{1,0:T(8,128)(2,1)S(1)}, u32[]{:S(2)}, u32[]{:S(2)}) collective-permute-start(bf16[72,2048]{1,0:T(8,128)(2,1)S(1)} %concatenate.41), channel_id=1, source_target_pairs={{0,2},{1,3},{2,0},{3,1},{4,6},{5,7},{6,4},{7,5},{8,10},{9,11},{10,... | collective-permute-start | bytes 884744 | tf_op jit(solution)/shard_map/ppermute | solution.py:430
  612.5 20.6 %collective-permute-start.100 = (bf16[128,2048]{1,0:T(8,128)(2,1)S(1)}, bf16[128,2048]{1,0:T(8,128)(2,1)S(1)}, u32[]{:S(2)}, u32[]{:S(2)}) collective-permute-start(bf16[128,2048]{1,0:T(8,128)(2,1)S(1)} %get-tuple-element.414), channel_id=1, source_target_pairs={{0,8},{8,0},{1,9},{9,1},{2,10},{10,2},{3,11},{11,3},{4,12},{12,4},... | collective-permute-start | bytes 1572872 | tf_op jit(solution)/shard_map/ppermute | solution.py:430
  614.0 19.1 %collective-permute-start.97 = (bf16[72,2048]{1,0:T(8,128)(2,1)S(1)}, bf16[72,2048]{1,0:T(8,128)(2,1)S(1)}, u32[]{:S(2)}, u32[]{:S(2)}) collective-permute-start(bf16[72,2048]{1,0:T(8,128)(2,1)S(1)} %concatenate.41), channel_id=1, source_target_pairs={{0,1},{1,0},{2,3},{3,2},{4,5},{5,4},{6,7},{7,6},{8,9},{9,8},{10,11... | collective-permute-start | bytes 884744 | tf_op jit(solution)/shard_map/ppermute | solution.py:430
  636.7 28.7 %collective-permute-start.101 = (bf16[137,2048]{1,0:T(8,128)(2,1)S(1)}, bf16[137,2048]{1,0:T(8,128)(2,1)S(1)}, u32[]{:S(2)}, u32[]{:S(2)}) collective-permute-start(bf16[137,2048]{1,0:T(8,128)(2,1)S(1)} %pad_maximum_fusion.3), channel_id=1, source_target_pairs={{0,8},{8,0},{1,9},{9,1},{2,10},{10,2},{3,11},{11,3},{4,12},{12,4},... | collective-permute-start | bytes 1683464 | tf_op jit(solution)/shard_map/ppermute | solution.py:430
  (152 other events, 1052.0 us)
Sparse Core Ops, SparseCore 0:
  10.5 57.0 all-gather.4
  70.1 97.5 all-gather.6
  170.1 54.3 all-gather.8
  226.9 92.0 all-gather.10
  360.3 90.7 reduce-scatter.6
  456.3 54.7 reduce-scatter.4
  523.0 93.9 reduce-scatter.8
  620.2 67.5 reduce-scatter.10

commit v9 on v8

--- a/solution.py
+++ b/solution.py
@@ -629,7 +629,7 @@
                 ],
                 0,
                 hbm_outs=2,
-                limit=60,
+                limit=60 if n_first == 2 else 32,
                 aliases={2: 0, 3: 1} if old else None,
             )
 

time: 707 us -> 698 us (0.987)
  waiting for transfers between devices: 336 us -> 323 us
    unnamed x210 -> x212, local copies, waits for them, and re-layouts: 44.9 us -> 45.3 us
  transfers between devices with their start and end apart: 114 -> 114, of which waited for: 51 -> 53; matrix products, arithmetic and copies ran while one was open for 6% -> 7% of each run, Pallas kernels for 19% -> 19%
where the time goes in v9:
time: 698 us; the launch traced here: 694 us
  waiting for transfers between devices  323 us (46%)
  Pallas kernels  145 us (21%)
  starting transfers between devices  116 us (17%)
  local copies, waits for them, and re-layouts  81.5 us (12%)
  between operations  16.2 us (2%)
  other arithmetic  12.6 us (2%)
    ppermute x106, waiting for transfers between devices, swap(): return lax.ppermute(value, axis, [(i, i ^ bit) for i in range(sizes[axis])])  282 us
    pallas_call x38, Pallas kernels, call(): pl.pallas_call(body, out_shape=tuple(outs), in_specs=[ANY] * n_any + [HBM...  145 us
    ppermute x106, starting transfers between devices, swap(): return lax.ppermute(value, axis, [(i, i ^ bit) for i in range(sizes[axis])])  115 us
    unnamed x212, local copies, waits for them, and re-layouts  45.3 us
    all_gather x4, waiting for transfers between devices, gather_weights(): return lax.all_gather(own, ('dp', 'chi', 'clo'), axis=0, tiled=True)  33.8 us
  transfers between devices with their start and end apart: 114, of which 53 were waited for; matrix products, arithmetic and copies ran while one was open for 7% of the time, Pallas kernels for 19%

profile of v9, /device:TPU:0, one launch (start us, length us, event | category | flops | bytes accessed | tf_op | source)
XLA Modules:
  0.0 693.6 jit_solution(13013798160317604610)
XLA Ops:
  17.2 4.9 concatenate.39
  25.5 4.4 concatenate.40
  31.2 3.0 collective-permute-start.1
  35.2 5.4 collective-permute-done.9
  42.3 2.9 collective-permute-start.3
  47.4 10.2 %collective-permute-done.3.refs_2_ = bf16[64,2048]{1,0:T(8,128)(2,1)S(1)} collective-permute-done((bf16[64,2048]{1,0:T(8,128)(2,1)S(1)}, bf16[64,2048]{1,0:T(8,128)(2,1)S(1)}, u32[]{:S(2)}, u32[]{:S(2)}) %collective-permute-start.3) | collective-permute-done | bytes 262176 | tf_op jit(solution)/shard_map/ppermute | solution.py:430
  59.0 6.3 collective-permute-done.4.refs_3_
  69.3 11.0 %shard_map.205 = (bf16[512,2048]{1,0:T(8,128)(2,1)}, bf16[512,256]{1,0:T(8,128)(2,1)}, bf16[512,256]{1,0:T(8,128)(2,1)}, bf16[512,256]{1,0:T(8,128)(2,1)}, bf16[...) custom-call(bf16[64,2048]{1,0:T(8,128)(2,1)} %copy-done.60, ...), custom_call_target="tpu_custom_call" | custom-call | flops 4294967296 | bytes 16526336 | tf_op jit(solution)/shard_map/pallas_call | solution.py:50
  86.1 3.4 collective-permute-start.13
  89.4 6.0 collective-permute-done
  96.7 3.5 collective-permute-start.23
  100.2 7.7 %collective-permute-done.13.refs_2_ = bf16[64,2048]{1,0:T(8,128)(2,1)S(1)} collective-permute-done((bf16[64,2048]{1,0:T(8,128)(2,1)S(1)}, bf16[64,2048]{1,0:T(8,128)(2,1)S(1)}, u32[]{:S(2)}, u32[]{:S(2)}) %collective-permute-start.13) | collective-permute-done | bytes 262176 | tf_op jit(solution)/shard_map/ppermute | solution.py:430
  108.2 13.1 %collective-permute-start.16 = (bf16[64,2048]{1,0:T(8,128)(2,1)S(1)}, bf16[64,2048]{1,0:T(8,128)(2,1)S(1)}, u32[]{:S(2)}, u32[]{:S(2)}) collective-permute-start(bf16[64,2048]{1,0:T(8,128)(2,1)S(1)} %get-tuple-element.201.refs_0_), channel_id=1, source_target_pairs={{0,2},{1,3},{2,0},{3,1},{4,6},{5,7},{6,4},{7,5},{8,10},{9,11},{10,... | collective-permute-start | bytes 786440 | tf_op jit(solution)/shard_map/ppermute | solution.py:430
  121.3 9.1 %collective-permute-done.23.refs_2_ = bf16[64,2048]{1,0:T(8,128)(2,1)S(1)} collective-permute-done((bf16[64,2048]{1,0:T(8,128)(2,1)S(1)}, bf16[64,2048]{1,0:T(8,128)(2,1)S(1)}, u32[]{:S(2)}, u32[]{:S(2)}) %collective-permute-start.23) | collective-permute-done | bytes 262176 | tf_op jit(solution)/shard_map/ppermute | solution.py:430
  135.5 5.6 collective-permute-done.24.refs_3_
  143.1 3.6 collective-permute-done.15.refs_1_
  147.5 4.8 collective-permute-done.17.refs_3_
  156.6 11.1 %all-gather.7.cloned.1.call-done.refs_8_ = bf16[2048,4224]{1,0:T(8,128)(2,1)} async-done(((bf16[256,4224]{1,0:T(8,128)(2,1)}), bf16[2048,4224]{1,0:T(8,128)(2,1)}) %all-gather.7.cloned.1.call-update) | async-done | bytes 17301520 | tf_op jit(solution)/shard_map/all_gather | solution.py:526
  173.4 7.4 %shard_map.208 = (bf16[512,2048]{1,0:T(8,128)(2,1)S(1)}, bf16[512,1408]{1,0:T(8,128)(2,1)S(1)}, bf16[512,704]{1,0:T(8,128)(2,1)S(1)}, bf16[256,2048]{1,0:T(8,128)(2,1)S(1)}, bf16[256,2048]{1,0:T(8,128)(2,1)S(1)}) custom-call(bf16[64,2048]{1,0:T(8,128)(2,1)S(1)} %get-tuple-element.201.refs_0_, bf16[64,2048]{1,0:T(8,128)(2,1)S(1)} %copy-done.38, ...), custom_call_target="tpu_custom_call" | custom-call | flops 4563402752 | bytes 25755648 | tf_op jit(solution)/shard_map/pallas_call | solution.py:50
  189.5 9.1 %collective-permute-done.30.refs_1_ = bf16[64,2048]{1,0:T(8,128)(2,1)S(1)} collective-permute-done((bf16[64,2048]{1,0:T(8,128)(2,1)S(1)}, bf16[64,2048]{1,0:T(8,128)(2,1)S(1)}, u32[]{:S(2)}, u32[]{:S(2)}) %collective-permute-start.30) | collective-permute-done | bytes 262176 | tf_op jit(solution)/shard_map/ppermute | solution.py:430
  198.6 9.3 %collective-permute-done.31.refs_2_ = bf16[64,2048]{1,0:T(8,128)(2,1)S(1)} collective-permute-done((bf16[64,2048]{1,0:T(8,128)(2,1)S(1)}, bf16[64,2048]{1,0:T(8,128)(2,1)S(1)}, u32[]{:S(2)}, u32[]{:S(2)}) %collective-permute-start.31) | collective-permute-done | bytes 262176 | tf_op jit(solution)/shard_map/ppermute | solution.py:430
  208.3 6.2 collective-permute-start.34
  214.5 11.5 %collective-permute-done.34.refs_2_ = bf16[64,2048]{1,0:T(8,128)(2,1)S(1)} collective-permute-done((bf16[64,2048]{1,0:T(8,128)(2,1)S(1)}, bf16[64,2048]{1,0:T(8,128)(2,1)S(1)}, u32[]{:S(2)}, u32[]{:S(2)}) %collective-permute-start.34) | collective-permute-done | bytes 262176 | tf_op jit(solution)/shard_map/ppermute | solution.py:430
  226.5 6.4 collective-permute-done.35.refs_3_
  234.6 11.6 %shard_map.212 = (bf16[512,2048]{1,0:T(8,128)(2,1)}, bf16[512,256]{1,0:T(8,128)(2,1)}, bf16[512,256]{1,0:T(8,128)(2,1)}, bf16[512,256]{1,0:T(8,128)(2,1)}, bf16[...) custom-call(bf16[64,2048]{1,0:T(8,128)(2,1)} %copy-done.61, ...), custom_call_target="tpu_custom_call" | custom-call | flops 4294967296 | bytes 16526336 | tf_op jit(solution)/shard_map/pallas_call | solution.py:50
  255.0 8.6 %collective-permute-done.41.refs_1_ = bf16[64,2048]{1,0:T(8,128)(2,1)S(1)} collective-permute-done((bf16[64,2048]{1,0:T(8,128)(2,1)S(1)}, bf16[64,2048]{1,0:T(8,128)(2,1)S(1)}, u32[]{:S(2)}, u32[]{:S(2)}) %collective-permute-start.41) | collective-permute-done | bytes 262176 | tf_op jit(solution)/shard_map/ppermute | solution.py:430
  263.6 9.1 %collective-permute-done.42.refs_2_ = bf16[64,2048]{1,0:T(8,128)(2,1)S(1)} collective-permute-done((bf16[64,2048]{1,0:T(8,128)(2,1)S(1)}, bf16[64,2048]{1,0:T(8,128)(2,1)S(1)}, u32[]{:S(2)}, u32[]{:S(2)}) %collective-permute-start.42) | collective-permute-done | bytes 262176 | tf_op jit(solution)/shard_map/ppermute | solution.py:430
  273.1 5.2 collective-permute-start.45
  278.3 11.2 %collective-permute-done.45.refs_2_ = bf16[64,2048]{1,0:T(8,128)(2,1)S(1)} collective-permute-done((bf16[64,2048]{1,0:T(8,128)(2,1)S(1)}, bf16[64,2048]{1,0:T(8,128)(2,1)S(1)}, u32[]{:S(2)}, u32[]{:S(2)}) %collective-permute-start.45) | collective-permute-done | bytes 262176 | tf_op jit(solution)/shard_map/ppermute | solution.py:430
  290.2 6.1 collective-permute-done.46.refs_3_
  296.3 22.7 %all-gather.11.cloned.1.call-done.refs_8_ = bf16[2048,4224]{1,0:T(8,128)(2,1)} async-done(((bf16[256,4224]{1,0:T(8,128)(2,1)}), bf16[2048,4224]{1,0:T(8,128)(2,1)}) %all-gather.11.cloned.1.call-update) | async-done | bytes 17301520 | tf_op jit(solution)/shard_map/all_gather | solution.py:526
  319.0 7.7 %shard_map.215 = (bf16[512,2048]{1,0:T(8,128)(2,1)S(1)}, bf16[512,1408]{1,0:T(8,128)(2,1)S(1)}, bf16[512,704]{1,0:T(8,128)(2,1)S(1)}, bf16[256,2048]{1,0:T(8,128)(2,1)S(1)}, bf16[256,2048]{1,0:T(8,128)(2,1)S(1)}) custom-call(bf16[64,2048]{1,0:T(8,128)(2,1)S(1)} %get-tuple-element.232.refs_0_, bf16[64,2048]{1,0:T(8,128)(2,1)} %collective-permute-done.44.refs_1_, ...), custom_call_target="tpu_custom_call" | custom-call | flops 4563402752 | bytes 25755648 | tf_op jit(solution)/shard_map/pallas_call | solution.py:50
  336.3 9.0 %shard_map.217 = (bf16[512,2048]{1,0:T(8,128)(2,1)S(1)}, bf16[512,1408]{1,0:T(8,128)(2,1)S(1)}, bf16[256,2048]{1,0:T(8,128)(2,1)S(1)}, bf16[256,2048]{1,0:T(8,128)(2,1)S(1)}) custom-call(bf16[64,2048]{1,0:T(8,128)(2,1)S(1)} %get-tuple-element.224.refs_0_, bf16[64,2048]{1,0:T(8,128)(2,1)S(1)} %copy-done.24, bf16[64,2048]{1,0:T(8,128)(2,1)S(1)} %copy-done.26, ...), custom_call_target="tpu_custom_call" | custom-call | flops 4563402752 | bytes 26476544 | tf_op jit(solution)/shard_map/pallas_call | solution.py:50
  349.6 10.5 %shard_map.218 = bf16[2048,2176]{1,0:T(8,128)(2,1)} custom-call(bf16[512,2048]{1,0:T(8,128)(2,1)} %copy-done.52, bf16[512,2048]{1,0:T(8,128)(2,1)} %copy-done.54, bf16[512,1408]{1,0:T(8,128)(2,1)} %copy-done.56, bf16[512,704]{1,0:T(8,128)(2,1)} %copy-done.59), custom_call_target="tpu_custom_call" | custom-call | flops 4563402752 | bytes 15269888 | tf_op jit(solution)/shard_map/pallas_call | solution.py:50
  360.7 2.9 collective-permute-done.55.moved_i
  365.7 3.3 collective-permute-start.57
  369.5 9.1 %collective-permute-done.56.refs_1_ = bf16[64,2048]{1,0:T(8,128)(2,1)S(1)} collective-permute-done((bf16[64,2048]{1,0:T(8,128)(2,1)S(1)}, bf16[64,2048]{1,0:T(8,128)(2,1)S(1)}, u32[]{:S(2)}, u32[]{:S(2)}) %collective-permute-start.56) | collective-permute-done | bytes 262176 | tf_op jit(solution)/shard_map/ppermute | solution.py:430
  378.5 8.9 %collective-permute-done.57.refs_2_ = bf16[64,2048]{1,0:T(8,128)(2,1)S(1)} collective-permute-done((bf16[64,2048]{1,0:T(8,128)(2,1)S(1)}, bf16[64,2048]{1,0:T(8,128)(2,1)S(1)}, u32[]{:S(2)}, u32[]{:S(2)}) %collective-permute-start.57) | collective-permute-done | bytes 262176 | tf_op jit(solution)/shard_map/ppermute | solution.py:430
  388.9 6.4 collective-permute-start.60
  395.2 11.6 %collective-permute-done.60.refs_2_ = bf16[64,2048]{1,0:T(8,128)(2,1)S(1)} collective-permute-done((bf16[64,2048]{1,0:T(8,128)(2,1)S(1)}, bf16[64,2048]{1,0:T(8,128)(2,1)S(1)}, u32[]{:S(2)}, u32[]{:S(2)}) %collective-permute-start.60) | collective-permute-done | bytes 262176 | tf_op jit(solution)/shard_map/ppermute | solution.py:430
  407.4 6.4 collective-permute-done.61.refs_3_
  416.1 13.1 %shard_map.221 = (bf16[512,2048]{1,0:T(8,128)(2,1)}, bf16[512,768]{1,0:T(8,128)(2,1)}, f32[1,768]{1,0:T(1,128)}, bf16[256,2048]{1,0:T(8,128)(2,1)}, bf16[256,2048]{1,0:T(8,128)(2,1)}) custom-call(bf16[64,2048]{1,0:T(8,128)(2,1)} %copy-done.62, bf16[64,2048]{1,0:T(8,128)(2,1)} %copy-done.94, bf16[64,2048]{1,0:T(8,128)(2,1)} %copy-done.93, ...), custom_call_target="tpu_custom_call" | custom-call | flops 4831838208 | bytes 17050624 | tf_op jit(solution)/shard_map/pallas_call | solution.py:50
  438.7 6.9 shard_map.223
  447.3 8.8 %collective-permute-done.68.refs_2_ = bf16[64,2048]{1,0:T(8,128)(2,1)} collective-permute-done((bf16[64,2048]{1,0:T(8,128)(2,1)}, bf16[64,2048]{1,0:T(8,128)(2,1)}, u32[]{:S(2)}, u32[]{:S(2)}) %collective-permute-start.68) | collective-permute-done | bytes 262176 | tf_op jit(solution)/shard_map/ppermute | solution.py:430
  461.0 5.3 collective-permute-start.71
  466.3 11.2 %collective-permute-done.71.refs_2_ = bf16[64,2048]{1,0:T(8,128)(2,1)S(1)} collective-permute-done((bf16[64,2048]{1,0:T(8,128)(2,1)S(1)}, bf16[64,2048]{1,0:T(8,128)(2,1)S(1)}, u32[]{:S(2)}, u32[]{:S(2)}) %collective-permute-start.71) | collective-permute-done | bytes 262176 | tf_op jit(solution)/shard_map/ppermute | solution.py:430
  478.0 6.1 collective-permute-done.72.refs_3_
  485.7 8.9 %shard_map.225 = (bf16[512,2048]{1,0:T(8,128)(2,1)S(1)}, bf16[512,1408]{1,0:T(8,128)(2,1)S(1)}, bf16[256,2048]{1,0:T(8,128)(2,1)S(1)}, bf16[256,2048]{1,0:T(8,128)(2,1)S(1)}) custom-call(bf16[64,2048]{1,0:T(8,128)(2,1)S(1)} %get-tuple-element.276.refs_0_, bf16[64,2048]{1,0:T(8,128)(2,1)S(1)} %collective-permute-done.70.refs_1_, ...), custom_call_target="tpu_custom_call" | custom-call | flops 4563402752 | bytes 26476544 | tf_op jit(solution)/shard_map/pallas_call | solution.py:50
  504.0 10.4 %shard_map.227 = bf16[2048,2176]{1,0:T(8,128)(2,1)} custom-call(bf16[512,2048]{1,0:T(8,128)(2,1)} %copy-done.51, bf16[512,2048]{1,0:T(8,128)(2,1)} %copy-done.53, bf16[512,1408]{1,0:T(8,128)(2,1)} %copy-done.55, bf16[512,704]{1,0:T(8,128)(2,1)} %copy-done.58), custom_call_target="tpu_custom_call" | custom-call | flops 4563402752 | bytes 15269888 | tf_op jit(solution)/shard_map/pallas_call | solution.py:50
  514.5 7.6 %collective-permute-done.79.refs_2_ = bf16[64,2048]{1,0:T(8,128)(2,1)} collective-permute-done((bf16[64,2048]{1,0:T(8,128)(2,1)}, bf16[64,2048]{1,0:T(8,128)(2,1)}, u32[]{:S(2)}, u32[]{:S(2)}) %collective-permute-start.79) | collective-permute-done | bytes 262176 | tf_op jit(solution)/shard_map/ppermute | solution.py:430
  525.5 6.2 collective-permute-start.82
  538.4 11.9 %collective-permute-done.82.refs_2_ = bf16[64,2048]{1,0:T(8,128)(2,1)S(1)} collective-permute-done((bf16[64,2048]{1,0:T(8,128)(2,1)}, bf16[64,2048]{1,0:T(8,128)(2,1)S(1)}, u32[]{:S(2)}, u32[]{:S(2)}) %collective-permute-start.82) | collective-permute-done | bytes 262176 | tf_op jit(solution)/shard_map/ppermute | solution.py:430
  555.1 5.0 collective-permute-done.83.refs_3_
  563.0 13.2 %shard_map.231 = (bf16[512,2048]{1,0:T(8,128)(2,1)}, bf16[512,768]{1,0:T(8,128)(2,1)}, f32[1,768]{1,0:T(1,128)}, bf16[256,2048]{1,0:T(8,128)(2,1)}, bf16[256,2048]{1,0:T(8,128)(2,1)}) custom-call(bf16[64,2048]{1,0:T(8,128)(2,1)} %get-tuple-element.299.refs_0_, bf16[64,2048]{1,0:T(8,128)(2,1)} %copy-done.85, bf16[64,2048]{1,0:T(8,128)(2,1)} %copy-done.81, ...), custom_call_target="tpu_custom_call" | custom-call | flops 4831838208 | bytes 17050624 | tf_op jit(solution)/shard_map/pallas_call | solution.py:50
  586.9 7.5 %shard_map.233 = bf16[2048,1024]{1,0:T(8,128)(2,1)} custom-call(bf16[512,2048]{1,0:T(8,128)(2,1)} %get-tuple-element.330.refs_0_, bf16[512,2048]{1,0:T(8,128)(2,1)} %get-tuple-element.331.refs_1_, bf16[512,768]{1,0:T(8,128)(2,1)} %get-tuple-element.332.refs_2_, bf16[512,256]{1,0:T(8,128)(2,1)} %get-tuple-element.333.refs_3_), custom_call_target="tpu_custom_call" | custom-call | flops 2147483648 | bytes 9437184 | tf_op jit(solution)/shard_map/pallas_call | solution.py:50
  595.6 8.3 %collective-permute-done.95.refs_2_ = bf16[64,2048]{1,0:T(8,128)(2,1)S(1)} collective-permute-done((bf16[64,2048]{1,0:T(8,128)(2,1)}, bf16[64,2048]{1,0:T(8,128)(2,1)S(1)}, u32[]{:S(2)}, u32[]{:S(2)}) %collective-permute-start.95) | collective-permute-done | bytes 262176 | tf_op jit(solution)/shard_map/ppermute | solution.py:430
  607.0 5.5 collective-permute-start.98
  615.2 10.0 %collective-permute-done.98 = bf16[72,2048]{1,0:T(8,128)(2,1)S(1)} collective-permute-done((bf16[72,2048]{1,0:T(8,128)(2,1)S(1)}, bf16[72,2048]{1,0:T(8,128)(2,1)S(1)}, u32[]{:S(2)}, u32[]{:S(2)}) %collective-permute-start.98) | collective-permute-done | bytes 294944 | tf_op jit(solution)/shard_map/ppermute | solution.py:430
  627.1 4.2 shard_map.236
  642.7 4.3 shard_map.238
  647.0 9.7 %copy.85 = f32[2,2,256,1408]{3,1,2,0:T(2,128)} copy(f32[2,2,256,1408]{3,2,1,0:T(8,128)} %get-tuple-element.362) | data formatting | bytes 11534336 | tf_op jit(solution)/shard_map/pallas_call | solution.py:50
  656.7 6.7 collective-permute-done.101
  665.0 5.3 collective-permute-done.103
  674.6 6.9 reduce-scatter.11.cloned.1.call-done.block_sum.refs_0_
  (514 shorter events, 178.5 us)
Async XLA Ops:
  7.2 61.3 %all-gather.5.cloned.1.call-start = ((), (), s32[]{:S(2)}) async-start(), calls=%async_computation.4 | async-start | bytes 9437184 | tf_op jit(solution)/shard_map/all_gather | solution.py:526
  9.9 157.8 %all-gather.7.cloned.1.call-start = ((), (), s32[]{:S(2)}) async-start(), calls=%async_computation.5 | async-start | bytes 19464192 | tf_op jit(solution)/shard_map/all_gather | solution.py:526
  22.2 210.7 %all-gather.9.cloned.1.call-start = ((), (), s32[]{:S(2)}) async-start(), calls=%async_computation.6 | async-start | bytes 9437184 | tf_op jit(solution)/shard_map/all_gather | solution.py:526
  23.3 295.7 %all-gather.11.cloned.1.call-start = ((), (), s32[]{:S(2)}) async-start(), calls=%async_computation.7 | async-start | bytes 19464192 | tf_op jit(solution)/shard_map/all_gather | solution.py:526
  30.0 501.7 %reduce-scatter.7.cloned.1.call-start = ((), (), s32[]{:S(2)}) async-start(), calls=%async_computation.9 | async-start | bytes 11141120 | tf_op jit(solution)/shard_map/reduce_scatter | solution.py:606
  42.3 15.3 %collective-permute-start.3 = (bf16[64,2048]{1,0:T(8,128)(2,1)S(1)}, bf16[64,2048]{1,0:T(8,128)(2,1)S(1)}, u32[]{:S(2)}, u32[]{:S(2)}) collective-permute-start(bf16[64,2048]{1,0:T(8,128)(2,1)S(1)} %get-tuple-element.192.refs_0_), channel_id=1, source_target_pairs={{0,2},{1,3},{2,0},{3,1},{4,6},{5,7},{6,4},{7,5},{8,10},{9,11},{10,... | collective-permute-start | bytes 786440 | tf_op jit(solution)/shard_map/ppermute | solution.py:430
  45.7 13.2 %collective-permute-start.2 = (bf16[64,2048]{1,0:T(8,128)(2,1)S(1)}, bf16[64,2048]{1,0:T(8,128)(2,1)S(1)}, u32[]{:S(2)}, u32[]{:S(2)}) collective-permute-start(bf16[64,2048]{1,0:T(8,128)(2,1)S(1)} %get-tuple-element.192.refs_0_), channel_id=1, source_target_pairs={{0,1},{1,0},{2,3},{3,2},{4,5},{5,4},{6,7},{7,6},{8,9},{9,8},{10,11... | collective-permute-start | bytes 786440 | tf_op jit(solution)/shard_map/ppermute | solution.py:430
  81.0 14.5 %collective-permute-start = (bf16[64,2048]{1,0:T(8,128)(2,1)S(1)}, bf16[64,2048]{1,0:T(8,128)(2,1)S(1)}, u32[]{:S(2)}, u32[]{:S(2)}) collective-permute-start(bf16[64,2048]{1,0:T(8,128)(2,1)S(1)} %dynamic-slice_bitcast_fusion.3), channel_id=1, source_target_pairs={{0,8},{8,0},{1,9},{9,1},{2,10},{10,2},{3,11},{11,3},{4,12},{12,4},... | collective-permute-start | bytes 786440 | tf_op jit(solution)/shard_map/ppermute | solution.py:430
  84.9 15.3 %collective-permute-start.12 = (bf16[64,2048]{1,0:T(8,128)(2,1)S(1)}, bf16[64,2048]{1,0:T(8,128)(2,1)S(1)}, u32[]{:S(2)}, u32[]{:S(2)}) collective-permute-start(bf16[64,2048]{1,0:T(8,128)(2,1)S(1)} %get-tuple-element.196), channel_id=1, source_target_pairs={{0,1},{1,0},{2,3},{3,2},{4,5},{5,4},{6,7},{7,6},{8,9},{9,8},{10,11... | collective-permute-start | bytes 786440 | tf_op jit(solution)/shard_map/ppermute | solution.py:430
  86.1 21.8 %collective-permute-start.13 = (bf16[64,2048]{1,0:T(8,128)(2,1)S(1)}, bf16[64,2048]{1,0:T(8,128)(2,1)S(1)}, u32[]{:S(2)}, u32[]{:S(2)}) collective-permute-start(bf16[64,2048]{1,0:T(8,128)(2,1)S(1)} %get-tuple-element.197), channel_id=1, source_target_pairs={{0,2},{1,3},{2,0},{3,1},{4,6},{5,7},{6,4},{7,5},{8,10},{9,11},{10,... | collective-permute-start | bytes 786440 | tf_op jit(solution)/shard_map/ppermute | solution.py:430
  89.4 18.4 %collective-permute-start.14 = (bf16[64,2048]{1,0:T(8,128)(2,1)S(1)}, bf16[64,2048]{1,0:T(8,128)(2,1)S(1)}, u32[]{:S(2)}, u32[]{:S(2)}) collective-permute-start(bf16[64,2048]{1,0:T(8,128)(2,1)S(1)} %get-tuple-element.198), channel_id=1, source_target_pairs={{0,3},{1,2},{2,1},{3,0},{4,7},{5,6},{6,5},{7,4},{8,11},{9,10},{10,... | collective-permute-start | bytes 786440 | tf_op jit(solution)/shard_map/ppermute | solution.py:430
  95.5 34.8 %collective-permute-start.22 = (bf16[64,2048]{1,0:T(8,128)(2,1)S(1)}, bf16[64,2048]{1,0:T(8,128)(2,1)S(1)}, u32[]{:S(2)}, u32[]{:S(2)}) collective-permute-start(bf16[64,2048]{1,0:T(8,128)(2,1)S(1)} %get-tuple-element.224.refs_0_), channel_id=1, source_target_pairs={{0,1},{1,0},{2,3},{3,2},{4,5},{5,4},{6,7},{7,6},{8,9},{9,8},{10,11... | collective-permute-start | bytes 786440 | tf_op jit(solution)/shard_map/ppermute | solution.py:430
  96.7 33.7 %collective-permute-start.23 = (bf16[64,2048]{1,0:T(8,128)(2,1)S(1)}, bf16[64,2048]{1,0:T(8,128)(2,1)S(1)}, u32[]{:S(2)}, u32[]{:S(2)}) collective-permute-start(bf16[64,2048]{1,0:T(8,128)(2,1)S(1)} %get-tuple-element.224.refs_0_), channel_id=1, source_target_pairs={{0,2},{1,3},{2,0},{3,1},{4,6},{5,7},{6,4},{7,5},{8,10},{9,11},{10,... | collective-permute-start | bytes 786440 | tf_op jit(solution)/shard_map/ppermute | solution.py:430
  100.2 30.8 %collective-permute-start.25 = (bf16[64,2048]{1,0:T(8,128)(2,1)S(1)}, bf16[64,2048]{1,0:T(8,128)(2,1)S(1)}, u32[]{:S(2)}, u32[]{:S(2)}) collective-permute-start(bf16[64,2048]{1,0:T(8,128)(2,1)S(1)} %get-tuple-element.224.refs_0_), channel_id=1, source_target_pairs={{0,4},{4,0},{1,5},{5,1},{2,6},{6,2},{3,7},{7,3},{8,12},{12,8},{9,1... | collective-permute-start | bytes 786440 | tf_op jit(solution)/shard_map/ppermute | solution.py:430
  108.2 27.3 %collective-permute-start.16 = (bf16[64,2048]{1,0:T(8,128)(2,1)S(1)}, bf16[64,2048]{1,0:T(8,128)(2,1)S(1)}, u32[]{:S(2)}, u32[]{:S(2)}) collective-permute-start(bf16[64,2048]{1,0:T(8,128)(2,1)S(1)} %get-tuple-element.201.refs_0_), channel_id=1, source_target_pairs={{0,2},{1,3},{2,0},{3,1},{4,6},{5,7},{6,4},{7,5},{8,10},{9,11},{10,... | collective-permute-start | bytes 786440 | tf_op jit(solution)/shard_map/ppermute | solution.py:430
  130.9 15.8 %collective-permute-start.15 = (bf16[64,2048]{1,0:T(8,128)(2,1)S(1)}, bf16[64,2048]{1,0:T(8,128)(2,1)S(1)}, u32[]{:S(2)}, u32[]{:S(2)}) collective-permute-start(bf16[64,2048]{1,0:T(8,128)(2,1)S(1)} %get-tuple-element.201.refs_0_), channel_id=1, source_target_pairs={{0,1},{1,0},{2,3},{3,2},{4,5},{5,4},{6,7},{7,6},{8,9},{9,8},{10,11... | collective-permute-start | bytes 786440 | tf_op jit(solution)/shard_map/ppermute | solution.py:430
  135.5 16.7 %collective-permute-start.17 = (bf16[64,2048]{1,0:T(8,128)(2,1)S(1)}, bf16[64,2048]{1,0:T(8,128)(2,1)S(1)}, u32[]{:S(2)}, u32[]{:S(2)}) collective-permute-start(bf16[64,2048]{1,0:T(8,128)(2,1)S(1)} %collective-permute-done.16.refs_2_), channel_id=1, source_target_pairs={{0,1},{1,0},{2,3},{3,2},{4,5},{5,4},{6,7},{7,6},{8,9},{9,8},{10,11... | collective-permute-start | bytes 786440 | tf_op jit(solution)/shard_map/ppermute | solution.py:430
  141.1 12.0 %collective-permute-start.28 = (bf16[64,2048]{1,0:T(8,128)(2,1)S(1)}, bf16[64,2048]{1,0:T(8,128)(2,1)S(1)}, u32[]{:S(2)}, u32[]{:S(2)}) collective-permute-start(bf16[64,2048]{1,0:T(8,128)(2,1)S(1)} %collective-permute-done.24.refs_3_), channel_id=1, source_target_pairs={{0,4},{4,0},{1,5},{5,1},{2,6},{6,2},{3,7},{7,3},{8,12},{12,8},{9,1... | collective-permute-start | bytes 786440 | tf_op jit(solution)/shard_map/ppermute | solution.py:430
  143.1 12.2 %collective-permute-start.20 = (bf16[64,2048]{1,0:T(8,128)(2,1)S(1)}, bf16[64,2048]{1,0:T(8,128)(2,1)S(1)}, u32[]{:S(2)}, u32[]{:S(2)}) collective-permute-start(bf16[64,2048]{1,0:T(8,128)(2,1)S(1)} %collective-permute-done.16.refs_2_), channel_id=1, source_target_pairs={{0,4},{4,0},{1,5},{5,1},{2,6},{6,2},{3,7},{7,3},{8,12},{12,8},{9,1... | collective-permute-start | bytes 786440 | tf_op jit(solution)/shard_map/ppermute | solution.py:430
  185.0 13.6 %collective-permute-start.30 = (bf16[64,2048]{1,0:T(8,128)(2,1)S(1)}, bf16[64,2048]{1,0:T(8,128)(2,1)S(1)}, u32[]{:S(2)}, u32[]{:S(2)}) collective-permute-start(bf16[64,2048]{1,0:T(8,128)(2,1)S(1)} %get-tuple-element.212), channel_id=1, source_target_pairs={{0,1},{1,0},{2,3},{3,2},{4,5},{5,4},{6,7},{7,6},{8,9},{9,8},{10,11... | collective-permute-start | bytes 786440 | tf_op jit(solution)/shard_map/ppermute | solution.py:430
  186.6 21.3 %collective-permute-start.31 = (bf16[64,2048]{1,0:T(8,128)(2,1)S(1)}, bf16[64,2048]{1,0:T(8,128)(2,1)S(1)}, u32[]{:S(2)}, u32[]{:S(2)}) collective-permute-start(bf16[64,2048]{1,0:T(8,128)(2,1)S(1)} %get-tuple-element.213), channel_id=1, source_target_pairs={{0,2},{1,3},{2,0},{3,1},{4,6},{5,7},{6,4},{7,5},{8,10},{9,11},{10,... | collective-permute-start | bytes 786440 | tf_op jit(solution)/shard_map/ppermute | solution.py:430
  189.0 18.9 %collective-permute-start.32 = (bf16[64,2048]{1,0:T(8,128)(2,1)S(1)}, bf16[64,2048]{1,0:T(8,128)(2,1)S(1)}, u32[]{:S(2)}, u32[]{:S(2)}) collective-permute-start(bf16[64,2048]{1,0:T(8,128)(2,1)S(1)} %get-tuple-element.214), channel_id=1, source_target_pairs={{0,3},{1,2},{2,1},{3,0},{4,7},{5,6},{6,5},{7,4},{8,11},{9,10},{10,... | collective-permute-start | bytes 786440 | tf_op jit(solution)/shard_map/ppermute | solution.py:430
  208.3 17.7 %collective-permute-start.34 = (bf16[64,2048]{1,0:T(8,128)(2,1)S(1)}, bf16[64,2048]{1,0:T(8,128)(2,1)S(1)}, u32[]{:S(2)}, u32[]{:S(2)}) collective-permute-start(bf16[64,2048]{1,0:T(8,128)(2,1)S(1)} %get-tuple-element.216.refs_0_), channel_id=1, source_target_pairs={{0,2},{1,3},{2,0},{3,1},{4,6},{5,7},{6,4},{7,5},{8,10},{9,11},{10,... | collective-permute-start | bytes 786440 | tf_op jit(solution)/shard_map/ppermute | solution.py:430
  214.5 12.0 %collective-permute-start.33 = (bf16[64,2048]{1,0:T(8,128)(2,1)S(1)}, bf16[64,2048]{1,0:T(8,128)(2,1)S(1)}, u32[]{:S(2)}, u32[]{:S(2)}) collective-permute-start(bf16[64,2048]{1,0:T(8,128)(2,1)S(1)} %get-tuple-element.216.refs_0_), channel_id=1, source_target_pairs={{0,1},{1,0},{2,3},{3,2},{4,5},{5,4},{6,7},{7,6},{8,9},{9,8},{10,11... | collective-permute-start | bytes 786440 | tf_op jit(solution)/shard_map/ppermute | solution.py:430
  250.6 13.0 %collective-permute-start.41 = (bf16[64,2048]{1,0:T(8,128)(2,1)S(1)}, bf16[64,2048]{1,0:T(8,128)(2,1)S(1)}, u32[]{:S(2)}, u32[]{:S(2)}) collective-permute-start(bf16[64,2048]{1,0:T(8,128)(2,1)S(1)} %get-tuple-element.220), channel_id=1, source_target_pairs={{0,1},{1,0},{2,3},{3,2},{4,5},{5,4},{6,7},{7,6},{8,9},{9,8},{10,11... | collective-permute-start | bytes 786440 | tf_op jit(solution)/shard_map/ppermute | solution.py:430
  251.4 21.3 %collective-permute-start.42 = (bf16[64,2048]{1,0:T(8,128)(2,1)S(1)}, bf16[64,2048]{1,0:T(8,128)(2,1)S(1)}, u32[]{:S(2)}, u32[]{:S(2)}) collective-permute-start(bf16[64,2048]{1,0:T(8,128)(2,1)S(1)} %get-tuple-element.221), channel_id=1, source_target_pairs={{0,2},{1,3},{2,0},{3,1},{4,6},{5,7},{6,4},{7,5},{8,10},{9,11},{10,... | collective-permute-start | bytes 786440 | tf_op jit(solution)/shard_map/ppermute | solution.py:430
  252.9 19.8 %collective-permute-start.43 = (bf16[64,2048]{1,0:T(8,128)(2,1)S(1)}, bf16[64,2048]{1,0:T(8,128)(2,1)S(1)}, u32[]{:S(2)}, u32[]{:S(2)}) collective-permute-start(bf16[64,2048]{1,0:T(8,128)(2,1)S(1)} %get-tuple-element.222), channel_id=1, source_target_pairs={{0,3},{1,2},{2,1},{3,0},{4,7},{5,6},{6,5},{7,4},{8,11},{9,10},{10,... | collective-permute-start | bytes 786440 | tf_op jit(solution)/shard_map/ppermute | solution.py:430
  273.1 16.4 %collective-permute-start.45 = (bf16[64,2048]{1,0:T(8,128)(2,1)S(1)}, bf16[64,2048]{1,0:T(8,128)(2,1)S(1)}, u32[]{:S(2)}, u32[]{:S(2)}) collective-permute-start(bf16[64,2048]{1,0:T(8,128)(2,1)S(1)} %get-tuple-element.232.refs_0_), channel_id=1, source_target_pairs={{0,2},{1,3},{2,0},{3,1},{4,6},{5,7},{6,4},{7,5},{8,10},{9,11},{10,... | collective-permute-start | bytes 786440 | tf_op jit(solution)/shard_map/ppermute | solution.py:430
  289.5 29.5 %collective-permute-start.47 = (bf16[64,2048]{1,0:T(8,128)(2,1)S(1)}, bf16[64,2048]{1,0:T(8,128)(2,1)}, u32[]{:S(2)}, u32[]{:S(2)}) collective-permute-start(bf16[64,2048]{1,0:T(8,128)(2,1)S(1)} %get-tuple-element.232.refs_0_), channel_id=1, source_target_pairs={{0,4},{4,0},{1,5},{5,1},{2,6},{6,2},{3,7},{7,3},{8,12},{12,8},{9,1... | collective-permute-start | bytes 786440 | tf_op jit(solution)/shard_map/ppermute | solution.py:430
  289.5 29.5 %collective-permute-start.49 = (bf16[64,2048]{1,0:T(8,128)(2,1)S(1)}, bf16[64,2048]{1,0:T(8,128)(2,1)}, u32[]{:S(2)}, u32[]{:S(2)}) collective-permute-start(bf16[64,2048]{1,0:T(8,128)(2,1)S(1)} %collective-permute-done.45.refs_2_), channel_id=1, source_target_pairs={{0,4},{4,0},{1,5},{5,1},{2,6},{6,2},{3,7},{7,3},{8,12},{12,8},{9,1... | collective-permute-start | bytes 786440 | tf_op jit(solution)/shard_map/ppermute | solution.py:430
  290.0 29.0 %collective-permute-start.48 = (bf16[64,2048]{1,0:T(8,128)(2,1)}, bf16[64,2048]{1,0:T(8,128)(2,1)}, u32[]{:S(2)}, u32[]{:S(2)}) collective-permute-start(bf16[64,2048]{1,0:T(8,128)(2,1)} %collective-permute-done.44.refs_1_), channel_id=1, source_target_pairs={{0,4},{4,0},{1,5},{5,1},{2,6},{6,2},{3,7},{7,3},{8,12},{12,8},{9,1... | collective-permute-start | bytes 786440 | tf_op jit(solution)/shard_map/ppermute | solution.py:430
  296.3 22.7 %collective-permute-start.50 = (bf16[64,2048]{1,0:T(8,128)(2,1)}, bf16[64,2048]{1,0:T(8,128)(2,1)}, u32[]{:S(2)}, u32[]{:S(2)}) collective-permute-start(bf16[64,2048]{1,0:T(8,128)(2,1)} %collective-permute-done.46.refs_3_), channel_id=1, source_target_pairs={{0,4},{4,0},{1,5},{5,1},{2,6},{6,2},{3,7},{7,3},{8,12},{12,8},{9,1... | collective-permute-start | bytes 786440 | tf_op jit(solution)/shard_map/ppermute | solution.py:430
  331.9 28.2 %collective-permute-start.52 = (bf16[64,2048]{1,0:T(8,128)(2,1)}, bf16[64,2048]{1,0:T(8,128)(2,1)}, u32[]{:S(2)}, u32[]{:S(2)}) collective-permute-start(bf16[64,2048]{1,0:T(8,128)(2,1)} %get-tuple-element.240), channel_id=1, source_target_pairs={{0,1},{1,0},{2,3},{3,2},{4,5},{5,4},{6,7},{7,6},{8,9},{9,8},{10,11... | collective-permute-start | bytes 786440 | tf_op jit(solution)/shard_map/ppermute | solution.py:430
  333.4 26.8 %collective-permute-start.53 = (bf16[64,2048]{1,0:T(8,128)(2,1)}, bf16[64,2048]{1,0:T(8,128)(2,1)}, u32[]{:S(2)}, u32[]{:S(2)}) collective-permute-start(bf16[64,2048]{1,0:T(8,128)(2,1)} %get-tuple-element.241), channel_id=1, source_target_pairs={{0,2},{1,3},{2,0},{3,1},{4,6},{5,7},{6,4},{7,5},{8,10},{9,11},{10,... | collective-permute-start | bytes 786440 | tf_op jit(solution)/shard_map/ppermute | solution.py:430
  335.8 24.4 %collective-permute-start.54 = (bf16[64,2048]{1,0:T(8,128)(2,1)}, bf16[64,2048]{1,0:T(8,128)(2,1)}, u32[]{:S(2)}, u32[]{:S(2)}) collective-permute-start(bf16[64,2048]{1,0:T(8,128)(2,1)} %get-tuple-element.242), channel_id=1, source_target_pairs={{0,3},{1,2},{2,1},{3,0},{4,7},{5,6},{6,5},{7,4},{8,11},{9,10},{10,... | collective-permute-start | bytes 786440 | tf_op jit(solution)/shard_map/ppermute | solution.py:430
  360.2 190.2 %reduce-scatter.5.cloned.1.call-start = ((), (), s32[]{:S(2)}) async-start(), calls=%async_computation.8 | async-start | bytes 5242880 | tf_op jit(solution)/shard_map/reduce_scatter | solution.py:606
  365.0 13.5 %collective-permute-start.56 = (bf16[64,2048]{1,0:T(8,128)(2,1)S(1)}, bf16[64,2048]{1,0:T(8,128)(2,1)S(1)}, u32[]{:S(2)}, u32[]{:S(2)}) collective-permute-start(bf16[64,2048]{1,0:T(8,128)(2,1)S(1)} %get-tuple-element.249), channel_id=1, source_target_pairs={{0,1},{1,0},{2,3},{3,2},{4,5},{5,4},{6,7},{7,6},{8,9},{9,8},{10,11... | collective-permute-start | bytes 786440 | tf_op jit(solution)/shard_map/ppermute | solution.py:430
  365.7 21.7 %collective-permute-start.57 = (bf16[64,2048]{1,0:T(8,128)(2,1)S(1)}, bf16[64,2048]{1,0:T(8,128)(2,1)S(1)}, u32[]{:S(2)}, u32[]{:S(2)}) collective-permute-start(bf16[64,2048]{1,0:T(8,128)(2,1)S(1)} %get-tuple-element.250), channel_id=1, source_target_pairs={{0,2},{1,3},{2,0},{3,1},{4,6},{5,7},{6,4},{7,5},{8,10},{9,11},{10,... | collective-permute-start | bytes 786440 | tf_op jit(solution)/shard_map/ppermute | solution.py:430
  369.0 18.4 %collective-permute-start.58 = (bf16[64,2048]{1,0:T(8,128)(2,1)S(1)}, bf16[64,2048]{1,0:T(8,128)(2,1)S(1)}, u32[]{:S(2)}, u32[]{:S(2)}) collective-permute-start(bf16[64,2048]{1,0:T(8,128)(2,1)S(1)} %get-tuple-element.251), channel_id=1, source_target_pairs={{0,3},{1,2},{2,1},{3,0},{4,7},{5,6},{6,5},{7,4},{8,11},{9,10},{10,... | collective-permute-start | bytes 786440 | tf_op jit(solution)/shard_map/ppermute | solution.py:430
  388.9 18.0 %collective-permute-start.60 = (bf16[64,2048]{1,0:T(8,128)(2,1)S(1)}, bf16[64,2048]{1,0:T(8,128)(2,1)S(1)}, u32[]{:S(2)}, u32[]{:S(2)}) collective-permute-start(bf16[64,2048]{1,0:T(8,128)(2,1)S(1)} %get-tuple-element.253.refs_0_), channel_id=1, source_target_pairs={{0,2},{1,3},{2,0},{3,1},{4,6},{5,7},{6,4},{7,5},{8,10},{9,11},{10,... | collective-permute-start | bytes 786440 | tf_op jit(solution)/shard_map/ppermute | solution.py:430
  395.2 12.1 %collective-permute-start.59 = (bf16[64,2048]{1,0:T(8,128)(2,1)S(1)}, bf16[64,2048]{1,0:T(8,128)(2,1)S(1)}, u32[]{:S(2)}, u32[]{:S(2)}) collective-permute-start(bf16[64,2048]{1,0:T(8,128)(2,1)S(1)} %get-tuple-element.253.refs_0_), channel_id=1, source_target_pairs={{0,1},{1,0},{2,3},{3,2},{4,5},{5,4},{6,7},{7,6},{8,9},{9,8},{10,11... | collective-permute-start | bytes 786440 | tf_op jit(solution)/shard_map/ppermute | solution.py:430
  434.3 13.0 %collective-permute-start.67 = (bf16[64,2048]{1,0:T(8,128)(2,1)}, bf16[64,2048]{1,0:T(8,128)(2,1)S(1)}, u32[]{:S(2)}, u32[]{:S(2)}) collective-permute-start(bf16[64,2048]{1,0:T(8,128)(2,1)} %get-tuple-element.260), channel_id=1, source_target_pairs={{0,1},{1,0},{2,3},{3,2},{4,5},{5,4},{6,7},{7,6},{8,9},{9,8},{10,11... | collective-permute-start | bytes 786440 | tf_op jit(solution)/shard_map/ppermute | solution.py:430
  434.5 21.7 %collective-permute-start.68 = (bf16[64,2048]{1,0:T(8,128)(2,1)}, bf16[64,2048]{1,0:T(8,128)(2,1)}, u32[]{:S(2)}, u32[]{:S(2)}) collective-permute-start(bf16[64,2048]{1,0:T(8,128)(2,1)} %get-tuple-element.261), channel_id=1, source_target_pairs={{0,2},{1,3},{2,0},{3,1},{4,6},{5,7},{6,4},{7,5},{8,10},{9,11},{10,... | collective-permute-start | bytes 786440 | tf_op jit(solution)/shard_map/ppermute | solution.py:430
  436.3 19.9 %collective-permute-start.69 = (bf16[64,2048]{1,0:T(8,128)(2,1)}, bf16[64,2048]{1,0:T(8,128)(2,1)}, u32[]{:S(2)}, u32[]{:S(2)}) collective-permute-start(bf16[64,2048]{1,0:T(8,128)(2,1)} %get-tuple-element.262), channel_id=1, source_target_pairs={{0,3},{1,2},{2,1},{3,0},{4,7},{5,6},{6,5},{7,4},{8,11},{9,10},{10,... | collective-permute-start | bytes 786440 | tf_op jit(solution)/shard_map/ppermute | solution.py:430
  456.2 179.9 %reduce-scatter.9.cloned.1.call-start = ((), (), s32[]{:S(2)}) async-start(), calls=%async_computation.10 | async-start | bytes 11141120 | tf_op jit(solution)/shard_map/reduce_scatter | solution.py:606
  461.0 16.5 %collective-permute-start.71 = (bf16[64,2048]{1,0:T(8,128)(2,1)S(1)}, bf16[64,2048]{1,0:T(8,128)(2,1)S(1)}, u32[]{:S(2)}, u32[]{:S(2)}) collective-permute-start(bf16[64,2048]{1,0:T(8,128)(2,1)S(1)} %get-tuple-element.276.refs_0_), channel_id=1, source_target_pairs={{0,2},{1,3},{2,0},{3,1},{4,6},{5,7},{6,4},{7,5},{8,10},{9,11},{10,... | collective-permute-start | bytes 786440 | tf_op jit(solution)/shard_map/ppermute | solution.py:430
  499.6 14.8 %collective-permute-start.78 = (bf16[64,2048]{1,0:T(8,128)(2,1)}, bf16[64,2048]{1,0:T(8,128)(2,1)S(1)}, u32[]{:S(2)}, u32[]{:S(2)}) collective-permute-start(bf16[64,2048]{1,0:T(8,128)(2,1)} %get-tuple-element.281), channel_id=1, source_target_pairs={{0,1},{1,0},{2,3},{3,2},{4,5},{5,4},{6,7},{7,6},{8,9},{9,8},{10,11... | collective-permute-start | bytes 786440 | tf_op jit(solution)/shard_map/ppermute | solution.py:430
  500.4 21.7 %collective-permute-start.79 = (bf16[64,2048]{1,0:T(8,128)(2,1)}, bf16[64,2048]{1,0:T(8,128)(2,1)}, u32[]{:S(2)}, u32[]{:S(2)}) collective-permute-start(bf16[64,2048]{1,0:T(8,128)(2,1)} %get-tuple-element.282), channel_id=1, source_target_pairs={{0,2},{1,3},{2,0},{3,1},{4,6},{5,7},{6,4},{7,5},{8,10},{9,11},{10,... | collective-permute-start | bytes 786440 | tf_op jit(solution)/shard_map/ppermute | solution.py:430
  503.2 18.8 %collective-permute-start.80 = (bf16[64,2048]{1,0:T(8,128)(2,1)}, bf16[64,2048]{1,0:T(8,128)(2,1)}, u32[]{:S(2)}, u32[]{:S(2)}) collective-permute-start(bf16[64,2048]{1,0:T(8,128)(2,1)} %get-tuple-element.283), channel_id=1, source_target_pairs={{0,3},{1,2},{2,1},{3,0},{4,7},{5,6},{6,5},{7,4},{8,11},{9,10},{10,... | collective-permute-start | bytes 786440 | tf_op jit(solution)/shard_map/ppermute | solution.py:430
  522.1 159.4 %reduce-scatter.11.cloned.1.call-start = ((), (), s32[]{:S(2)}) async-start(), calls=%async_computation.11 | async-start | bytes 5242880 | tf_op jit(solution)/shard_map/reduce_scatter | solution.py:606
  525.5 24.8 %collective-permute-start.82 = (bf16[64,2048]{1,0:T(8,128)(2,1)}, bf16[64,2048]{1,0:T(8,128)(2,1)S(1)}, u32[]{:S(2)}, u32[]{:S(2)}) collective-permute-start(bf16[64,2048]{1,0:T(8,128)(2,1)} %get-tuple-element.299.refs_0_), channel_id=1, source_target_pairs={{0,2},{1,3},{2,0},{3,1},{4,6},{5,7},{6,4},{7,5},{8,10},{9,11},{10,... | collective-permute-start | bytes 786440 | tf_op jit(solution)/shard_map/ppermute | solution.py:430
  534.4 27.9 %collective-permute-start.89 = (bf16[256,2176]{1,0:T(8,128)(2,1)}, bf16[256,2176]{1,0:T(8,128)(2,1)}, u32[]{:S(2)}, u32[]{:S(2)}) collective-permute-start(bf16[256,2176]{1,0:T(8,128)(2,1)} %shard_map.230), channel_id=1, source_target_pairs={{0,4},{4,0},{1,5},{5,1},{2,6},{6,2},{3,7},{7,3},{8,12},{12,8},{9,1... | collective-permute-start | bytes 3342344 | tf_op jit(solution)/shard_map/ppermute | solution.py:430
  536.5 17.9 %collective-permute-start.91 = (bf16[64,2048]{1,0:T(8,128)(2,1)}, bf16[64,2048]{1,0:T(8,128)(2,1)S(1)}, u32[]{:S(2)}, u32[]{:S(2)}) collective-permute-start(bf16[64,2048]{1,0:T(8,128)(2,1)} %add_convert_fusion), channel_id=1, source_target_pairs={{0,2},{1,3},{2,0},{3,1},{4,6},{5,7},{6,4},{7,5},{8,10},{9,11},{10,... | collective-permute-start | bytes 786440 | tf_op jit(solution)/shard_map/ppermute | solution.py:430
  536.5 18.2 %collective-permute-start.81 = (bf16[64,2048]{1,0:T(8,128)(2,1)}, bf16[64,2048]{1,0:T(8,128)(2,1)S(1)}, u32[]{:S(2)}, u32[]{:S(2)}) collective-permute-start(bf16[64,2048]{1,0:T(8,128)(2,1)} %get-tuple-element.299.refs_0_), channel_id=1, source_target_pairs={{0,1},{1,0},{2,3},{3,2},{4,5},{5,4},{6,7},{7,6},{8,9},{9,8},{10,11... | collective-permute-start | bytes 786440 | tf_op jit(solution)/shard_map/ppermute | solution.py:430
  538.4 16.5 %collective-permute-start.84 = (bf16[64,2048]{1,0:T(8,128)(2,1)}, bf16[64,2048]{1,0:T(8,128)(2,1)S(1)}, u32[]{:S(2)}, u32[]{:S(2)}) collective-permute-start(bf16[64,2048]{1,0:T(8,128)(2,1)} %get-tuple-element.299.refs_0_), channel_id=1, source_target_pairs={{0,4},{4,0},{1,5},{5,1},{2,6},{6,2},{3,7},{7,3},{8,12},{12,8},{9,1... | collective-permute-start | bytes 786440 | tf_op jit(solution)/shard_map/ppermute | solution.py:430
  560.3 16.0 %collective-permute-start.90 = (bf16[64,2048]{1,0:T(8,128)(2,1)}, bf16[64,2048]{1,0:T(8,128)(2,1)S(1)}, u32[]{:S(2)}, u32[]{:S(2)}) collective-permute-start(bf16[64,2048]{1,0:T(8,128)(2,1)} %add_convert_fusion), channel_id=1, source_target_pairs={{0,1},{1,0},{2,3},{3,2},{4,5},{5,4},{6,7},{7,6},{8,9},{9,8},{10,11... | collective-permute-start | bytes 786440 | tf_op jit(solution)/shard_map/ppermute | solution.py:430
  560.3 16.0 %collective-permute-start.92 = (bf16[64,2048]{1,0:T(8,128)(2,1)S(1)}, bf16[64,2048]{1,0:T(8,128)(2,1)S(1)}, u32[]{:S(2)}, u32[]{:S(2)}) collective-permute-start(bf16[64,2048]{1,0:T(8,128)(2,1)S(1)} %collective-permute-done.91), channel_id=1, source_target_pairs={{0,1},{1,0},{2,3},{3,2},{4,5},{5,4},{6,7},{7,6},{8,9},{9,8},{10,11... | collective-permute-start | bytes 786440 | tf_op jit(solution)/shard_map/ppermute | solution.py:430
  582.3 13.3 %collective-permute-start.94 = (bf16[64,2048]{1,0:T(8,128)(2,1)}, bf16[64,2048]{1,0:T(8,128)(2,1)S(1)}, u32[]{:S(2)}, u32[]{:S(2)}) collective-permute-start(bf16[64,2048]{1,0:T(8,128)(2,1)} %get-tuple-element.323), channel_id=1, source_target_pairs={{0,1},{1,0},{2,3},{3,2},{4,5},{5,4},{6,7},{7,6},{8,9},{9,8},{10,11... | collective-permute-start | bytes 786440 | tf_op jit(solution)/shard_map/ppermute | solution.py:430
  582.3 21.5 %collective-permute-start.95 = (bf16[64,2048]{1,0:T(8,128)(2,1)}, bf16[64,2048]{1,0:T(8,128)(2,1)S(1)}, u32[]{:S(2)}, u32[]{:S(2)}) collective-permute-start(bf16[64,2048]{1,0:T(8,128)(2,1)} %get-tuple-element.324), channel_id=1, source_target_pairs={{0,2},{1,3},{2,0},{3,1},{4,6},{5,7},{6,4},{7,5},{8,10},{9,11},{10,... | collective-permute-start | bytes 786440 | tf_op jit(solution)/shard_map/ppermute | solution.py:430
  584.5 19.3 %collective-permute-start.96 = (bf16[64,2048]{1,0:T(8,128)(2,1)S(1)}, bf16[64,2048]{1,0:T(8,128)(2,1)S(1)}, u32[]{:S(2)}, u32[]{:S(2)}) collective-permute-start(bf16[64,2048]{1,0:T(8,128)(2,1)S(1)} %get-tuple-element.325), channel_id=1, source_target_pairs={{0,3},{1,2},{2,1},{3,0},{4,7},{5,6},{6,5},{7,4},{8,11},{9,10},{10,... | collective-permute-start | bytes 786440 | tf_op jit(solution)/shard_map/ppermute | solution.py:430
  607.0 18.3 %collective-permute-start.98 = (bf16[72,2048]{1,0:T(8,128)(2,1)S(1)}, bf16[72,2048]{1,0:T(8,128)(2,1)S(1)}, u32[]{:S(2)}, u32[]{:S(2)}) collective-permute-start(bf16[72,2048]{1,0:T(8,128)(2,1)S(1)} %concatenate.41), channel_id=1, source_target_pairs={{0,2},{1,3},{2,0},{3,1},{4,6},{5,7},{6,4},{7,5},{8,10},{9,11},{10,... | collective-permute-start | bytes 884744 | tf_op jit(solution)/shard_map/ppermute | solution.py:430
  613.7 17.7 %collective-permute-start.100 = (bf16[128,2048]{1,0:T(8,128)(2,1)S(1)}, bf16[128,2048]{1,0:T(8,128)(2,1)S(1)}, u32[]{:S(2)}, u32[]{:S(2)}) collective-permute-start(bf16[128,2048]{1,0:T(8,128)(2,1)S(1)} %get-tuple-element.414), channel_id=1, source_target_pairs={{0,8},{8,0},{1,9},{9,1},{2,10},{10,2},{3,11},{11,3},{4,12},{12,4},... | collective-permute-start | bytes 1572872 | tf_op jit(solution)/shard_map/ppermute | solution.py:430
  615.2 16.2 %collective-permute-start.97 = (bf16[72,2048]{1,0:T(8,128)(2,1)S(1)}, bf16[72,2048]{1,0:T(8,128)(2,1)}, u32[]{:S(2)}, u32[]{:S(2)}) collective-permute-start(bf16[72,2048]{1,0:T(8,128)(2,1)S(1)} %concatenate.41), channel_id=1, source_target_pairs={{0,1},{1,0},{2,3},{3,2},{4,5},{5,4},{6,7},{7,6},{8,9},{9,8},{10,11... | collective-permute-start | bytes 884744 | tf_op jit(solution)/shard_map/ppermute | solution.py:430
  639.9 23.5 %collective-permute-start.101 = (bf16[137,2048]{1,0:T(8,128)(2,1)}, bf16[137,2048]{1,0:T(8,128)(2,1)S(1)}, u32[]{:S(2)}, u32[]{:S(2)}) collective-permute-start(bf16[137,2048]{1,0:T(8,128)(2,1)} %pad_maximum_fusion.3), channel_id=1, source_target_pairs={{0,8},{8,0},{1,9},{9,1},{2,10},{10,2},{3,11},{11,3},{4,12},{12,4},... | collective-permute-start | bytes 1683464 | tf_op jit(solution)/shard_map/ppermute | solution.py:430
  (153 other events, 1042.9 us)
Sparse Core Ops, SparseCore 0:
  10.5 57.0 all-gather.4
  70.1 97.5 all-gather.6
  170.2 54.3 all-gather.8
  226.9 92.0 all-gather.10
  360.3 90.7 reduce-scatter.6
  456.3 54.7 reduce-scatter.4
  522.2 93.5 reduce-scatter.8
  619.0 62.3 reduce-scatter.10
